TPU v7x, 32 devices: a whole 2x2x4 slice. The times are simulated.
32 devices in a mesh: sub: 8 (over z, y), pln: 4 (over x, core).
Axes of the slice: x: 2, y: 2, z: 4, core: 2. Of those that a mesh axis runs over, the one named last changes fastest.
Arguments:
- labels: int32 [8, 64, 1024], P('pln', None, 'sub'), may hold values from 0 to 3
- levels: float32 [4], replicated, may hold values from 0.1 to 1
- zvec: bfloat16 [64, 8, 64, 1024], P(None, 'pln', None, 'sub'), may hold values from -1 to 1
- resid: float32 [8, 64, 1024], P('pln', None, 'sub'), may hold values from -6 to 6
Outputs:
- coarse_solution: float32 [8, 64], P('sub')
- deflated: float32 [8, 64, 1024], P('pln', None, 'sub')
All inputs are finite; a program needn't handle non-finite values.
Results may differ from a plain program's by a relative error of at most 0.0003.
Values may be sent and summed in bfloat16 or wider, within the bound.
No kernel may reach another device: no remote copies, remote signals or barrier semaphores. Data moves between devices by JAX's collectives and lax.ppermute only.
A program may use at most 128 MiB of HBM per device.

v0:
```python
import jax
import jax.numpy as jnp
from jax import lax
from jax.experimental import pallas as pl
from jax.experimental.pallas import tpu as pltpu
from jax.sharding import PartitionSpec as P

CITERS = 2
STEP = 16
MODES = 8
CHUNK = 16
F32 = jnp.float32
BF16 = jnp.bfloat16
PRECISE = lax.Precision.HIGHEST
NT = (((1,), (1,)), ((), ()))
TN = (((0,), (0,)), ((), ()))
VMEM = pl.BlockSpec(memory_space=pltpu.VMEM)
SMEM = pl.BlockSpec(memory_space=pltpu.SMEM)
HBM = pl.BlockSpec(memory_space=pltpu.HBM)
ANY = pl.BlockSpec(memory_space=pl.ANY)


def call(kernel, outs, specs, scratch=(), flops=0, moved=0, limit=32, aliases=None):
    return pl.pallas_call(
        kernel,
        out_shape=outs,
        in_specs=specs,
        out_specs=[ANY if at in (aliases or {}).values() else VMEM for at in range(len(outs))],
        input_output_aliases=aliases or {},
        scratch_shapes=list(scratch),
        cost_estimate=pl.CostEstimate(flops=flops, bytes_accessed=moved, transcendentals=0),
        compiler_params=pltpu.CompilerParams(vmem_limit_bytes=limit << 20),
    )


def harmonic(left_value, right_value):
    return 2.0 * left_value * right_value / (left_value + right_value)


def coefficients(labels, levels_ref):
    weighted = jnp.zeros(labels.shape, F32)
    for level in range(levels_ref.shape[0]):
        weighted = weighted + jnp.where(labels == level, levels_ref[level], 0.0)
    return weighted


def lane_is(shape, lane):
    return lax.broadcasted_iota(jnp.int32, shape, len(shape) - 1) == lane


def pick_row(lane, width):
    row = lax.broadcasted_iota(jnp.int32, (16, width), 0)
    return ((row == 0) & lane_is((16, width), lane)).astype(BF16)


def stage_kernel(place, labels_far, zvec, inner_near, outer_near, labels, label_sem, sems):
    modes, planes, rows, layers = zvec.shape
    half = rows // 2
    side = lax.rem(place[1], 2)
    start = pl.multiple_of((1 - side) * half, half)
    label_copy = pltpu.make_async_copy(labels_far, labels, label_sem)
    copies = [
        pltpu.make_async_copy(
            zvec.at[:, plane, pl.ds(start, half), :], out.at[pl.ds(0, modes)], sems.at[slot]
        )
        for slot, plane, out in ((1, side, outer_near), (0, 1 - side, inner_near))
    ]
    label_copy.start()
    for copy in copies:
        copy.start()
    label_copy.wait()
    for plane, out in ((side, outer_near), (1 - side, inner_near)):
        out[modes:] = labels[plane].astype(F32).astype(BF16).reshape(rows // half, half, layers)
    for copy in copies:
        copy.wait()


def prepare_kernel(place, labels, held, planes_out, inner_rest, outer_rest, one_pack, two_pack):
    modes, planes, rows, layers = held.shape
    half = rows // 2
    width = planes * rows
    side = lax.rem(place[1], 2)
    odd = lax.rem(place[0], 2) == 1
    one_lane = jnp.where(odd, 0, layers - 1)
    two_lane = jnp.where(odd, layers - 1, 0)
    row = lax.broadcasted_iota(jnp.int32, (16, layers), 0)
    both = ((row == 0) & lane_is((16, layers), one_lane)) | ((row == 1) & lane_is((16, layers), two_lane))
    both = both.astype(BF16)
    flat = labels[...].astype(F32).astype(BF16).reshape(width, layers)
    for out, lane in ((one_pack, one_lane), (two_pack, two_lane)):
        out[modes:] = lax.dot_general(
            pick_row(lane, layers), flat, NT, preferred_element_type=F32
        ).astype(BF16)
    for k in range(0, modes, CHUNK):
        at = slice(k, k + CHUNK)
        ends = lax.dot_general(
            both, held[at].reshape(-1, layers), NT, preferred_element_type=F32
        )
        for out, index in ((one_pack, 0), (two_pack, 1)):
            out[at] = jnp.concatenate(
                [ends[index:index + 1, j * width:(j + 1) * width] for j in range(CHUNK)], axis=0
            ).astype(BF16)
        for slot, plane, rest in ((0, 1 - side, inner_rest), (1, side, outer_rest)):
            planes_out[slot, :, at, :] = jnp.swapaxes(held[at, plane], 0, 1)
            rest[at] = held[at, plane, pl.ds(pl.multiple_of(side * half, half), half), :]


def block_kernel(
    place, levels, labels, resid, here, partial, weights, half_diag, link_y, link_z,
):
    planes, rows, layers = labels.shape
    modes = here.shape[2]
    side = lax.rem(place[1], 2)
    at_edge = (place[1] == 0) | (place[1] == place[2] - 1)
    held = (1 - side, side)
    coef = [coefficients(labels[x], levels) for x in held]
    middle = harmonic(coef[0], coef[1])
    weights[0] = middle
    row = lax.broadcasted_iota(jnp.int32, (rows, layers), 0)
    lane = lax.broadcasted_iota(jnp.int32, (rows, layers), 1)
    for x in range(2):
        c = coef[x]
        up_y = harmonic(c, jnp.where(row == rows - 1, c, pltpu.roll(c, rows - 1, 0)))
        up_z = harmonic(c, pltpu.roll(c, layers - 1, 1))
        down_y = jnp.where(row == 0, c, pltpu.roll(up_y, 1, 0))
        weights[1 + x] = up_y
        weights[3 + x] = up_z
        weights[5 + x] = c
        inner_z = jnp.where(lane == layers - 1, 0.0, up_z)
        total = middle + up_y + down_y + inner_z + pltpu.roll(inner_z, 1, 1)
        if x == 1:
            total = total + jnp.where(at_edge, c, 0.0)
        half_diag[x] = 0.5 * total
        link_y[x] = jnp.where(row == rows - 1, 0.0, up_y)
        link_z[x] = inner_z

    def step(j, carry):
        total, rhs, wide = carry
        for u in range(STEP):
            y = j * STEP + u
            at = pl.ds(y, 1)
            ahead = jnp.minimum(y + 1, rows - 1)
            up = [here[x, ahead].astype(F32) for x in range(2)]
            images = []
            for x in range(2):
                image = (
                    half_diag[x, at, :] * wide[x]
                    - link_y[x, at, :] * up[x]
                    - link_z[x, at, :] * pltpu.roll(wide[x], layers - 1, 1)
                )
                if x == 0:
                    image = image - weights[0, at, :] * wide[1]
                rhs = rhs + resid[held[x], at, :] * wide[x]
                images.append(image.astype(BF16))
            total = total + lax.dot_general(
                jnp.concatenate(images, axis=1),
                jnp.concatenate([here[0, y], here[1, y]], axis=1),
                NT,
                preferred_element_type=F32,
            )
            wide = up
        return total, rhs, wide

    total, rhs, _ = lax.fori_loop(
        0,
        rows // STEP,
        step,
        (
            jnp.zeros((modes, modes), F32),
            jnp.zeros((modes, layers), F32),
            [here[x, 0].astype(F32) for x in range(2)],
        ),
    )
    partial[:modes, :] = total
    partial[modes:, :] = lax.dot_general(
        jnp.ones((8, layers), F32), rhs, NT, precision=PRECISE, preferred_element_type=F32
    )


def join_kernel(
    place, levels, partial, weights, here, inner_got, outer_got, one_pack, two_pack, one_got, two_got,
    out, faces, other_planes,
):
    planes, rows, modes, layers = here.shape
    half = rows // 2
    side = lax.rem(place[1], 2)
    odd = lax.rem(place[0], 2) == 1
    at_edge = (place[1] == 0) | (place[1] == place[2] - 1)
    base = side * half
    for slot, got in ((0, inner_got), (1, outer_got)):
        for k in range(0, modes, CHUNK):
            other_planes[slot, :, k:k + CHUNK, :] = jnp.swapaxes(got[k:k + CHUNK], 0, 1)
    inner_coef, outer_coef = (
        coefficients(got[modes:].astype(F32).reshape(rows, layers), levels)
        for got in (inner_got, outer_got)
    )
    faces[0] = harmonic(weights[5], inner_coef)
    faces[1] = jnp.where(at_edge, weights[6], harmonic(weights[6], outer_coef))

    def step(j, total):
        left, right = [], []
        for u in range(STEP):
            y = j * STEP + u
            at = pl.ds(base + y, 1)
            outer_weight = jnp.where(at_edge, 0.0, faces[1, at, :])
            for weight, own, other in (
                (faces[0, at, :], here[0, base + y], other_planes[0, y]),
                (outer_weight, here[1, base + y], other_planes[1, y]),
            ):
                image = weight * (own.astype(F32) - other.astype(F32))
                left.append(jnp.concatenate([own, other], axis=0))
                right.append(image.astype(BF16))
        return total + lax.dot_general(
            jnp.concatenate(left, axis=1), jnp.concatenate(right, axis=1), NT,
            preferred_element_type=F32,
        )

    cross = lax.fori_loop(0, half // STEP, step, jnp.zeros((2 * modes, modes), F32))
    cross = cross[:modes] - cross[modes:]

    def coef_row(pack):
        return coefficients(pack[modes:modes + 16].astype(F32)[0:1], levels)

    one, two = one_pack[...].astype(F32), two_pack[...].astype(F32)
    one_other, two_other = one_got[...].astype(F32), two_got[...].astype(F32)
    first, last = jnp.where(odd, one, two), jnp.where(odd, two, one)
    next_first = jnp.where(odd, two_other, one_other)
    prev_last = jnp.where(odd, one_other, two_other)
    weight_low = harmonic(coef_row(first), coef_row(prev_last))
    weight_high = harmonic(coef_row(last), coef_row(next_first))

    def product(left, right):
        return lax.dot_general(left, right, NT, precision=PRECISE, preferred_element_type=F32)

    edge_rows = weight_high * last[:modes]
    ends = product(weight_low * first[:modes], first[:modes]) + product(edge_rows, last[:modes])
    square = partial[:modes, :] + 0.5 * (cross + ends)
    square = square + square.T
    upper = -product(edge_rows, next_first[:modes])
    out[:modes, :modes] = square
    out[:modes, modes:] = upper
    out[modes:, :modes] = partial[modes:, :]
    out[modes:, modes:] = jnp.zeros((8, modes), F32)


def sum_kernel(own, one, two, three, inner_rest, outer_rest, out, inner_out, outer_out):
    out[...] = (own[...] + one[...]) + (two[...] + three[...])


def finish_kernel(place, levels, *refs):
    count = len(refs) - 18
    blocks, refs = refs[:count], refs[count:]
    zvec, inner_got, outer_got, inner_last, outer_last, one_got, two_got, weights, faces, resid = refs[:10]
    solution, deflated, direction_ref, image_ref, ahead_ref, spread, sides, ends_ref = refs[10:]
    subs = direction_ref.shape[0]
    modes, planes, rows, layers = zvec.shape
    half = rows // 2
    me = place[0]
    side = lax.rem(place[1], 2)
    odd = lax.rem(me, 2) == 1
    at_edge = (place[1] == 0) | (place[1] == place[2] - 1)
    order = place[3]
    held = (1 - side, side)
    square = (modes, modes)
    eye = lax.broadcasted_iota(jnp.int32, square, 0) == lax.broadcasted_iota(jnp.int32, square, 1)

    def column(row):
        return jnp.sum(jnp.where(eye, row, 0.0), axis=1, keepdims=True)

    def each(body):
        for index, block in enumerate(blocks):
            held_here = block.shape[0]
            if held_here <= 8:
                for entry in range(held_here):
                    body(block.at[entry], jnp.bitwise_xor(order, index * held_here + entry))
            else:
                pl.loop(0, held_here)(lambda entry, block=block: body(block.at[entry], entry))

    def load(block, s):
        direction_ref[pl.ds(s, 1), :] = block[modes:modes + 1, :]

    each(load)

    def turned(rows_of, by):
        by = by % subs
        return jnp.concatenate([rows_of[by:], rows_of[:by]], axis=0)

    def coarse_apply(direction):
        direction_ref[...] = jnp.concatenate([direction, turned(direction, 1)], axis=1)

        def one(block, s):
            values = block[:modes, :]
            pair = direction_ref[pl.ds(s, 1), :]
            ahead = jnp.sum(values * pair, axis=1, keepdims=True)
            ahead_ref[...] = jnp.where(lane_is((modes, 128), s), ahead, ahead_ref[...])
            image_ref[pl.ds(s, 1), :] = jnp.sum(
                values * column(pair[:, :modes]), axis=0, keepdims=True
            )

        each(one)
        return ahead_ref[...].T[:subs] + turned(image_ref[:, modes:], -1)

    def inner(left, right):
        return jnp.sum(jnp.sum(left * right, axis=0, keepdims=True), axis=1, keepdims=True)

    remain = direction_ref[:, :modes]
    direction = remain
    result = jnp.zeros_like(remain)
    norm_now = inner(remain, remain)
    for iteration in range(CITERS):
        image = coarse_apply(direction)
        step_size = norm_now / inner(direction, image)
        result = result + step_size * direction
        if iteration + 1 < CITERS:
            remain = remain - step_size * image
            norm_next = inner(remain, remain)
            direction = remain + (norm_next / norm_now) * direction
            norm_now = norm_next
    direction_ref[:, :modes] = result
    own = direction_ref[pl.ds(me, 1), :modes]
    solution[...] = own
    spread[...] = jnp.broadcast_to(column(own), (modes, layers))
    ahead_column = column(direction_ref[pl.ds(lax.rem(me + 1, subs), 1), :modes])
    behind_column = column(direction_ref[pl.ds(lax.rem(me + subs - 1, subs), 1), :modes])
    at_top = lane_is((modes, layers), layers - 1)
    at_bottom = lane_is((modes, layers), 0)

    def placed(pack, values, precision):
        return lax.dot_general(pack, values, TN, precision=precision, preferred_element_type=F32)

    one_other, two_other = one_got[...].astype(F32), two_got[...].astype(F32)
    next_first = jnp.where(odd, two_other, one_other)
    prev_last = jnp.where(odd, one_other, two_other)
    ends_ref[...] = (
        placed(next_first[:modes], jnp.where(at_top, ahead_column, 0.0), PRECISE)
        + placed(prev_last[:modes], jnp.where(at_bottom, behind_column, 0.0), PRECISE)
    ).reshape(planes, rows, layers)
    end_coef = coefficients(
        placed(next_first[modes:].astype(BF16), pick_row(layers - 1, layers), None)
        + placed(prev_last[modes:].astype(BF16), pick_row(0, layers), None),
        levels,
    ).reshape(planes, rows, layers)

    others = (inner_got, inner_last, outer_got, outer_last)

    def add_mode(j, carry):
        fields, edges = list(carry[0]), list(carry[1])
        for u in range(MODES):
            k = j * MODES + u
            scale = spread[pl.ds(k, 1), :]
            for x in range(2):
                fields[x] = fields[x] + scale * zvec[k, held[x]].astype(F32)
            for index, other in enumerate(others):
                edges[index] = edges[index] + scale * other[k].astype(F32)
        return tuple(fields), tuple(edges)

    zero, short = jnp.zeros((rows, layers), F32), jnp.zeros((half, layers), F32)
    field, edges = lax.fori_loop(0, modes // MODES, add_mode, ((zero, zero), (short,) * 4))
    for slot in range(2):
        sides[slot, pl.ds(pl.multiple_of(side * half, half), half), :] = edges[2 * slot]
        sides[slot, pl.ds(pl.multiple_of((1 - side) * half, half), half), :] = edges[2 * slot + 1]
    row = lax.broadcasted_iota(jnp.int32, (rows, layers), 0)
    lane = lax.broadcasted_iota(jnp.int32, (rows, layers), 1)
    outside = (sides[0], jnp.where(at_edge, 0.0, sides[1]))
    for x in range(2):
        f = field[x]
        c = weights[5 + x]
        end_field = ends_ref[held[x]]
        end_weight = harmonic(c, jnp.where(side == x, end_coef[1], end_coef[0]))
        up_y, up_z = weights[1 + x], weights[3 + x]
        down_y = jnp.where(row == 0, c, pltpu.roll(up_y, 1, 0))
        down_z = jnp.where(lane == 0, end_weight, pltpu.roll(up_z, 1, 1))
        up_z = jnp.where(lane == layers - 1, end_weight, up_z)
        above_y = jnp.where(row == rows - 1, 0.0, pltpu.roll(f, rows - 1, 0))
        below_y = jnp.where(row == 0, 0.0, pltpu.roll(f, 1, 0))
        above_z = jnp.where(lane == layers - 1, end_field, pltpu.roll(f, layers - 1, 1))
        below_z = jnp.where(lane == 0, end_field, pltpu.roll(f, 1, 1))
        image = (
            weights[0] * (f - field[1 - x])
            + faces[x] * (f - outside[x])
            + down_y * (f - below_y)
            + up_y * (f - above_y)
            + down_z * (f - below_z)
            + up_z * (f - above_z)
        )
        deflated[held[x]] = resid[held[x]] - image


def swapped(value, axis, first):
    count = lax.axis_size(axis)
    pairs = []
    for i in range(count):
        up = (i - first) % 2 == 0
        pairs.append((i, (i + 1) % count if up else (i - 1) % count))
    return lax.ppermute(value, axis, pairs)


def swapped_open(value):
    subs, count = lax.axis_size("sub"), lax.axis_size("pln")
    pairs = []
    for s in range(subs):
        for i in range(count):
            if 0 < i < count - 1:
                to = (s, i + 1 if i % 2 else i - 1)
            else:
                to = (s ^ 1, i)
            pairs.append((s * count + i, to[0] * count + to[1]))
    return lax.ppermute(value, ("sub", "pln"), pairs)


def exchanged(value, axis, mask):
    return lax.ppermute(value, axis, [(i, i ^ mask) for i in range(lax.axis_size(axis))])


def gathered(value, axis):
    if lax.axis_size(axis) != 8:
        return [lax.all_gather(value, axis)]
    pair = jnp.stack([value, exchanged(value, axis, 1)])
    return [pair] + [exchanged(pair, axis, mask) for mask in (2, 4, 6)]


def body(labels, levels, zvec, resid):
    modes, planes, rows, layers = zvec.shape
    half = rows // 2
    subs, parts = lax.axis_size("sub"), lax.axis_size("pln")
    shape = jax.ShapeDtypeStruct
    order = lax.axis_index("sub") if subs == 8 else 0
    place = jnp.stack(
        [jnp.int32(v) for v in (lax.axis_index("sub"), lax.axis_index("pln"), parts, order)]
    )
    pack = shape((modes + 16, planes * rows), BF16)
    near = shape((modes + rows // half, half, layers), BF16)
    inner_near, outer_near = call(
        stage_kernel,
        [near, near],
        [SMEM, HBM, HBM],
        [pltpu.VMEM(labels.shape, jnp.int32), pltpu.SemaphoreType.DMA, pltpu.SemaphoreType.DMA((2,))],
        moved=2 << 20,
    )(place, *(pltpu.with_memory_space_constraint(v, pltpu.HBM) for v in (labels, zvec)))
    outer_got = swapped_open(outer_near)
    inner_got = swapped(inner_near, "pln", 0)
    rest = shape((modes, half, layers), BF16)
    here, inner_rest, outer_rest, one_pack, two_pack = call(
        prepare_kernel,
        [shape((planes, rows, modes, layers), BF16), rest, rest, pack, pack],
        [SMEM, VMEM, VMEM],
        flops=10_000_000,
        moved=6 << 20,
    )(place, labels, zvec)
    one_got = swapped(one_pack, "sub", 0)
    two_got = swapped(two_pack, "sub", 1)
    field = (planes, rows, layers)
    partial, weights = call(
        block_kernel,
        [shape((modes + 8, modes), F32), shape((7, rows, layers), F32)],
        [SMEM, SMEM] + [VMEM] * 3,
        [pltpu.VMEM(field, F32)] * 3,
        flops=400_000_000,
        moved=3 << 20,
    )(place, levels, labels, resid, here)
    block, faces = call(
        join_kernel,
        [shape((modes + 8, 2 * modes), F32), shape((2, rows, layers), F32)],
        [SMEM, SMEM] + [VMEM] * 9,
        [pltpu.VMEM((planes, half, modes, layers), BF16)],
        flops=200_000_000,
        moved=2 << 20,
    )(
        place, levels, partial, weights, here, inner_got, outer_got, one_pack, two_pack, one_got, two_got
    )
    if parts == 4:
        block, inner_rest, outer_rest = call(
            sum_kernel,
            [shape(block.shape, F32), rest, rest],
            [VMEM] * 4 + [ANY] * 2,
            aliases={4: 1, 5: 2},
        )(block, *(exchanged(block, "pln", mask) for mask in (1, 2, 3)), inner_rest, outer_rest)
    else:
        block = lax.psum(block, "pln")
    inner_last = swapped(inner_rest, "pln", 0)
    outer_last = swapped_open(outer_rest)
    blocks = gathered(block, "sub")
    return tuple(
        call(
            finish_kernel,
            [shape((1, modes), F32), shape(field, F32)],
            [SMEM, SMEM] + [VMEM] * (10 + len(blocks)),
            [
                pltpu.VMEM((subs, 2 * modes), F32),
                pltpu.VMEM((subs, 2 * modes), F32),
                pltpu.VMEM((modes, 128), F32),
                pltpu.VMEM((modes, layers), F32),
                pltpu.VMEM(field, F32),
                pltpu.VMEM(field, F32),
            ],
            flops=10_000_000,
            moved=5 << 20,
        )(
            place, levels, *blocks, zvec, inner_got, outer_got, inner_last, outer_last, one_got, two_got, weights,
            faces, resid,
        )
    )


def solution(mesh):
    in_specs = (P("pln", None, "sub"), P(), P(None, "pln", None, "sub"), P("pln", None, "sub"))
    out_specs = (P("sub", None), P("pln", None, "sub"))
    return jax.shard_map(body, mesh=mesh, in_specs=in_specs, out_specs=out_specs, check_vma=False)
```

profile of v0, /device:TPU:0, one launch (start us, length us, event | category | flops | bytes accessed | tf_op | source)
XLA Modules:
  0.0 44.3 jit_solution(15917320902181447685)
XLA Ops:
  0.6 0.0 copy-start
  0.6 0.0 copy-start.1
  0.7 0.1 pad_add_fusion.place
  0.7 1.8 %shard_map.61 = (bf16[66,32,128]{2,1,0:T(8,128)(2,1)S(1)}, bf16[66,32,128]{2,1,0:T(8,128)(2,1)S(1)}) custom-call(s32[4]{0:T(128)S(1)} %pad_add_fusion.place, s32[2,64,128]{2,1,0:T(8,128)} %labels_far.1, bf16[64,2,64,128]{3,2,1,0:T(8,128)(2,1)} %refs_4_.1), custom_call_target="tpu_custom_call" | custom-call | bytes 2097152 | tf_op jit(solution)/shard_map/pallas_call | solution.py:433
  2.6 0.5 %collective-permute-start = (bf16[66,32,128]{2,1,0:T(8,128)(2,1)S(1)}, bf16[66,32,128]{2,1,0:T(8,128)(2,1)S(1)}, u32[]{:S(2)}, u32[]{:S(2)}) collective-permute-start(bf16[66,32,128]{2,1,0:T(8,128)(2,1)S(1)} %get-tuple-element.19), channel_id=1, source_target_pairs={{0,1},{1,0},{2,3},{3,2},{4,5},{5,4},{6,7},{7,6},{8,9},{9,8},{10,11... | collective-permute-start | bytes 1622024 | tf_op jit(solution)/shard_map/ppermute | solution.py:395
  3.1 2.6 %collective-permute-start.1 = (bf16[66,32,128]{2,1,0:T(8,128)(2,1)S(1)}, bf16[66,32,128]{2,1,0:T(8,128)(2,1)S(1)}, u32[]{:S(2)}, u32[]{:S(2)}) collective-permute-start(bf16[66,32,128]{2,1,0:T(8,128)(2,1)S(1)} %get-tuple-element.20), channel_id=1, source_target_pairs={{0,4},{1,2},{2,1},{3,7},{4,0},{5,6},{6,5},{7,3},{8,12},{9,10},{10,... | collective-permute-start | bytes 1622024 | tf_op jit(solution)/shard_map/ppermute | solution.py:408
  5.7 2.0 %shard_map.59 = (bf16[2,64,64,128]{3,2,1,0:T(8,128)(2,1)S(1)}, bf16[64,32,128]{2,1,0:T(8,128)(2,1)S(1)}, bf16[64,32,128]{2,1,0:T(8,128)(2,1)S(1)}, bf16[80,128]{1,0:T(8,128)(2,1)S(1)}, bf16[80,128]{1,0:T(8,128)(2,1)S(1)}) custom-call(s32[4]{0:T(128)S(1)} %pad_add_fusion.place, s32[2,64,128]{2,1,0:T(8,128)S(1)} %copy-done.1, bf16[64,2,64,128]{3,2,1,0:T(8,128)(2,1)S(1)} %copy-done), custom_call_target="tpu_custom_call" | custom-call | flops 10000000 | bytes 6291456 | tf_op jit(solution)/shard_map/pallas_call | solution.py:443
  7.7 0.1 collective-permute-start.2
  7.8 5.0 %collective-permute-start.3 = (bf16[80,128]{1,0:T(8,128)(2,1)S(1)}, bf16[80,128]{1,0:T(8,128)(2,1)S(1)}, u32[]{:S(2)}, u32[]{:S(2)}) collective-permute-start(bf16[80,128]{1,0:T(8,128)(2,1)S(1)} %get-tuple-element.22.two_pack), channel_id=1, source_target_pairs={{0,28},{4,8},{8,4},{12,16},{16,12},{20,24},{24,20},{28,0},{1,29},{... | collective-permute-start | bytes 61448 | tf_op jit(solution)/shard_map/ppermute | solution.py:395
  12.8 3.1 %shard_map.60 = (f32[72,64]{1,0:T(8,128)S(1)}, f32[7,64,128]{2,1,0:T(8,128)S(1)}) custom-call(s32[4]{0:T(128)S(1)} %pad_add_fusion.place, f32[4]{0:T(128)S(1)} %copy-done.3, s32[2,64,128]{2,1,0:T(8,128)S(1)} %copy-done.1, f32[2,64,128]{2,1,0:T(8,128)S(1)} %copy-done.2, bf16[2,64,64,128]{3,2,1,0:T(8,128)(2,1)S(1)} %get-tuple-element.16.here), custom_call_target="tpu_custom_call" | custom-call | flops 400000000 | bytes 3145728 | tf_op jit(solution)/shard_map/pallas_call | solution.py:453
  15.9 0.0 collective-permute-done.2.one_got.refs_9_
  15.9 0.0 collective-permute-done.3.two_got.refs_10_
  15.9 0.0 collective-permute-done.inner_got.refs_5_
  16.0 0.0 collective-permute-done.1.outer_got.refs_6_
  16.0 2.2 %shard_map.62 = (f32[72,128]{1,0:T(8,128)S(1)}, f32[2,64,128]{2,1,0:T(8,128)S(1)}) custom-call(s32[4]{0:T(128)S(1)} %pad_add_fusion.place, f32[4]{0:T(128)S(1)} %copy-done.3, f32[72,64]{1,0:T(8,128)S(1)} %get-tuple-element.17.partial, f32[7,64,128]{2,1,0:T(8,128)S(1)} %get-tuple-element.18.weights.refs_11_, ...), custom_call_target="tpu_custom_call" | custom-call | flops 200000000 | bytes 2097152 | tf_op jit(solution)/shard_map/pallas_call | solution.py:461
  18.2 0.8 %collective-permute-start.6 = (f32[72,128]{1,0:T(8,128)S(1)}, f32[72,128]{1,0:T(8,128)S(1)}, u32[]{:S(2)}, u32[]{:S(2)}) collective-permute-start(f32[72,128]{1,0:T(8,128)S(1)} %get-tuple-element.23.own), channel_id=1, source_target_pairs={{0,3},{1,2},{2,1},{3,0},{4,7},{5,6},{6,5},{7,4},{8,11},{9,10},{10,... | collective-permute-start | bytes 110600 | tf_op jit(solution)/shard_map/ppermute | solution.py:412
  18.9 0.5 %collective-permute-start.5 = (f32[72,128]{1,0:T(8,128)S(1)}, f32[72,128]{1,0:T(8,128)S(1)}, u32[]{:S(2)}, u32[]{:S(2)}) collective-permute-start(f32[72,128]{1,0:T(8,128)S(1)} %get-tuple-element.23.own), channel_id=1, source_target_pairs={{0,2},{1,3},{2,0},{3,1},{4,6},{5,7},{6,4},{7,5},{8,10},{9,11},{10,... | collective-permute-start | bytes 110600 | tf_op jit(solution)/shard_map/ppermute | solution.py:412
  19.4 0.7 %collective-permute-start.4 = (f32[72,128]{1,0:T(8,128)S(1)}, f32[72,128]{1,0:T(8,128)S(1)}, u32[]{:S(2)}, u32[]{:S(2)}) collective-permute-start(f32[72,128]{1,0:T(8,128)S(1)} %get-tuple-element.23.own), channel_id=1, source_target_pairs={{0,1},{1,0},{2,3},{3,2},{4,5},{5,4},{6,7},{7,6},{8,9},{9,8},{10,11... | collective-permute-start | bytes 110600 | tf_op jit(solution)/shard_map/ppermute | solution.py:412
  20.1 1.6 %collective-permute-done.6.three = f32[72,128]{1,0:T(8,128)S(1)} collective-permute-done((f32[72,128]{1,0:T(8,128)S(1)}, f32[72,128]{1,0:T(8,128)S(1)}, u32[]{:S(2)}, u32[]{:S(2)}) %collective-permute-start.6) | collective-permute-done | bytes 36896 | tf_op jit(solution)/shard_map/ppermute | solution.py:412
  21.7 1.2 %collective-permute-done.5.two = f32[72,128]{1,0:T(8,128)S(1)} collective-permute-done((f32[72,128]{1,0:T(8,128)S(1)}, f32[72,128]{1,0:T(8,128)S(1)}, u32[]{:S(2)}, u32[]{:S(2)}) %collective-permute-start.5) | collective-permute-done | bytes 36896 | tf_op jit(solution)/shard_map/ppermute | solution.py:412
  22.9 0.0 collective-permute-done.4.one
  22.9 0.1 collective-permute-start.11
  23.0 0.1 collective-permute-start.12
  23.0 2.0 %collective-permute-start.7 = (f32[72,128]{1,0:T(8,128)S(1)}, f32[72,128]{1,0:T(8,128)S(1)}, u32[]{:S(2)}, u32[]{:S(2)}) collective-permute-start(f32[72,128]{1,0:T(8,128)S(1)} %get-tuple-element.26), channel_id=1, source_target_pairs={{0,4},{4,0},{8,12},{12,8},{16,20},{20,16},{24,28},{28,24},{1,5},{5... | collective-permute-start | bytes 110600 | tf_op jit(solution)/shard_map/ppermute | solution.py:412
  25.1 7.9 %collective-permute-done.7 = f32[72,128]{1,0:T(8,128)S(1)} collective-permute-done((f32[72,128]{1,0:T(8,128)S(1)}, f32[72,128]{1,0:T(8,128)S(1)}, u32[]{:S(2)}, u32[]{:S(2)}) %collective-permute-start.7) | collective-permute-done | bytes 36896 | tf_op jit(solution)/shard_map/ppermute | solution.py:412
  33.0 1.6 %collective-permute-start.10 = (f32[2,72,128]{2,1,0:T(8,128)S(1)}, f32[2,72,128]{2,1,0:T(8,128)S(1)}, u32[]{:S(2)}, u32[]{:S(2)}) collective-permute-start(f32[2,72,128]{2,1,0:T(8,128)S(1)} %pad_maximum_fusion.refs_0_), channel_id=1, source_target_pairs={{0,24},{4,28},{8,16},{12,20},{16,8},{20,12},{24,0},{28,4},{1,25},{... | collective-permute-start | bytes 221192 | tf_op jit(solution)/shard_map/ppermute | solution.py:412
  34.6 2.8 %collective-permute-start.8 = (f32[2,72,128]{2,1,0:T(8,128)S(1)}, f32[2,72,128]{2,1,0:T(8,128)S(1)}, u32[]{:S(2)}, u32[]{:S(2)}) collective-permute-start(f32[2,72,128]{2,1,0:T(8,128)S(1)} %pad_maximum_fusion.refs_0_), channel_id=1, source_target_pairs={{0,8},{4,12},{8,0},{12,4},{16,24},{20,28},{24,16},{28,20},{1,9},{5... | collective-permute-start | bytes 221192 | tf_op jit(solution)/shard_map/ppermute | solution.py:412
  37.4 1.8 %collective-permute-done.10.refs_3_ = f32[2,72,128]{2,1,0:T(8,128)S(1)} collective-permute-done((f32[2,72,128]{2,1,0:T(8,128)S(1)}, f32[2,72,128]{2,1,0:T(8,128)S(1)}, u32[]{:S(2)}, u32[]{:S(2)}) %collective-permute-start.10) | collective-permute-done | bytes 73760 | tf_op jit(solution)/shard_map/ppermute | solution.py:412
  39.2 1.6 %collective-permute-done.9.refs_2_ = f32[2,72,128]{2,1,0:T(8,128)S(1)} collective-permute-done((f32[2,72,128]{2,1,0:T(8,128)S(1)}, f32[2,72,128]{2,1,0:T(8,128)S(1)}, u32[]{:S(2)}, u32[]{:S(2)}) %collective-permute-start.9) | collective-permute-done | bytes 73760 | tf_op jit(solution)/shard_map/ppermute | solution.py:412
  40.7 0.0 collective-permute-done.8.refs_1_
  40.7 0.0 collective-permute-done.11.refs_7_
  40.8 3.6 %shard_map.64 = (f32[1,64]{1,0:T(1,128)}, f32[2,64,128]{2,1,0:T(8,128)}) custom-call(s32[4]{0:T(128)S(1)} %pad_add_fusion.place, f32[4]{0:T(128)S(1)} %copy-done.3, f32[2,72,128]{2,1,0:T(8,128)S(1)} %pad_maximum_fusion.refs_0_, f32[2,72,128]{2,1,0:T(8,128)S(1)} %collective-permute-done.8.refs_1_, f32[2,72,128]{2,1,0:T(8,128)S(1)} %collective-permute-done.9.refs_2_, ...), custom_call_target="tpu_custom_call" | custom-call | flops 10000000 | bytes 5242880 | tf_op jit(solution)/shard_map/pallas_call | solution.py:484
  (10 shorter events, 0.0 us)
Async XLA Ops:
  0.6 5.1 %copy-start = (bf16[64,2,64,128]{3,2,1,0:T(8,128)(2,1)S(1)}, bf16[64,2,64,128]{3,2,1,0:T(8,128)(2,1)}, u32[]{:S(2)}) copy-start(bf16[64,2,64,128]{3,2,1,0:T(8,128)(2,1)} %refs_4_.1) | copy-start | bytes 6291460
  0.6 5.1 %copy-start.1 = (s32[2,64,128]{2,1,0:T(8,128)S(1)}, s32[2,64,128]{2,1,0:T(8,128)}, u32[]{:S(2)}) copy-start(s32[2,64,128]{2,1,0:T(8,128)} %labels_far.1) | copy-start | bytes 196612
  0.7 12.1 %copy-start.2 = (f32[2,64,128]{2,1,0:T(8,128)S(1)}, f32[2,64,128]{2,1,0:T(8,128)}, u32[]{:S(2)}) copy-start(f32[2,64,128]{2,1,0:T(8,128)} %refs_13_.1) | copy-start | bytes 196612
  0.7 12.1 %copy-start.3 = (f32[4]{0:T(128)S(1)}, f32[4]{0:T(128)}, u32[]{:S(2)}) copy-start(f32[4]{0:T(128)} %levels.5) | copy-start | bytes 52
  2.6 13.4 %collective-permute-start = (bf16[66,32,128]{2,1,0:T(8,128)(2,1)S(1)}, bf16[66,32,128]{2,1,0:T(8,128)(2,1)S(1)}, u32[]{:S(2)}, u32[]{:S(2)}) collective-permute-start(bf16[66,32,128]{2,1,0:T(8,128)(2,1)S(1)} %get-tuple-element.19), channel_id=1, source_target_pairs={{0,1},{1,0},{2,3},{3,2},{4,5},{5,4},{6,7},{7,6},{8,9},{9,8},{10,11... | collective-permute-start | bytes 1622024 | tf_op jit(solution)/shard_map/ppermute | solution.py:395
  3.1 12.8 %collective-permute-start.1 = (bf16[66,32,128]{2,1,0:T(8,128)(2,1)S(1)}, bf16[66,32,128]{2,1,0:T(8,128)(2,1)S(1)}, u32[]{:S(2)}, u32[]{:S(2)}) collective-permute-start(bf16[66,32,128]{2,1,0:T(8,128)(2,1)S(1)} %get-tuple-element.20), channel_id=1, source_target_pairs={{0,4},{1,2},{2,1},{3,7},{4,0},{5,6},{6,5},{7,3},{8,12},{9,10},{10,... | collective-permute-start | bytes 1622024 | tf_op jit(solution)/shard_map/ppermute | solution.py:408
  7.7 8.2 %collective-permute-start.2 = (bf16[80,128]{1,0:T(8,128)(2,1)S(1)}, bf16[80,128]{1,0:T(8,128)(2,1)S(1)}, u32[]{:S(2)}, u32[]{:S(2)}) collective-permute-start(bf16[80,128]{1,0:T(8,128)(2,1)S(1)} %get-tuple-element.21.one_pack), channel_id=1, source_target_pairs={{0,4},{4,0},{8,12},{12,8},{16,20},{20,16},{24,28},{28,24},{1,5},{5... | collective-permute-start | bytes 61448 | tf_op jit(solution)/shard_map/ppermute | solution.py:395
  7.8 8.1 %collective-permute-start.3 = (bf16[80,128]{1,0:T(8,128)(2,1)S(1)}, bf16[80,128]{1,0:T(8,128)(2,1)S(1)}, u32[]{:S(2)}, u32[]{:S(2)}) collective-permute-start(bf16[80,128]{1,0:T(8,128)(2,1)S(1)} %get-tuple-element.22.two_pack), channel_id=1, source_target_pairs={{0,28},{4,8},{8,4},{12,16},{16,12},{20,24},{24,20},{28,0},{1,29},{... | collective-permute-start | bytes 61448 | tf_op jit(solution)/shard_map/ppermute | solution.py:395
  18.2 3.6 %collective-permute-start.6 = (f32[72,128]{1,0:T(8,128)S(1)}, f32[72,128]{1,0:T(8,128)S(1)}, u32[]{:S(2)}, u32[]{:S(2)}) collective-permute-start(f32[72,128]{1,0:T(8,128)S(1)} %get-tuple-element.23.own), channel_id=1, source_target_pairs={{0,3},{1,2},{2,1},{3,0},{4,7},{5,6},{6,5},{7,4},{8,11},{9,10},{10,... | collective-permute-start | bytes 110600 | tf_op jit(solution)/shard_map/ppermute | solution.py:412
  18.9 4.0 %collective-permute-start.5 = (f32[72,128]{1,0:T(8,128)S(1)}, f32[72,128]{1,0:T(8,128)S(1)}, u32[]{:S(2)}, u32[]{:S(2)}) collective-permute-start(f32[72,128]{1,0:T(8,128)S(1)} %get-tuple-element.23.own), channel_id=1, source_target_pairs={{0,2},{1,3},{2,0},{3,1},{4,6},{5,7},{6,4},{7,5},{8,10},{9,11},{10,... | collective-permute-start | bytes 110600 | tf_op jit(solution)/shard_map/ppermute | solution.py:412
  19.4 3.5 %collective-permute-start.4 = (f32[72,128]{1,0:T(8,128)S(1)}, f32[72,128]{1,0:T(8,128)S(1)}, u32[]{:S(2)}, u32[]{:S(2)}) collective-permute-start(f32[72,128]{1,0:T(8,128)S(1)} %get-tuple-element.23.own), channel_id=1, source_target_pairs={{0,1},{1,0},{2,3},{3,2},{4,5},{5,4},{6,7},{7,6},{8,9},{9,8},{10,11... | collective-permute-start | bytes 110600 | tf_op jit(solution)/shard_map/ppermute | solution.py:412
  22.9 17.9 %collective-permute-start.11 = (bf16[64,32,128]{2,1,0:T(8,128)(2,1)S(1)}, bf16[64,32,128]{2,1,0:T(8,128)(2,1)S(1)}, u32[]{:S(2)}, u32[]{:S(2)}) collective-permute-start(bf16[64,32,128]{2,1,0:T(8,128)(2,1)S(1)} %get-tuple-element.27), channel_id=1, source_target_pairs={{0,1},{1,0},{2,3},{3,2},{4,5},{5,4},{6,7},{7,6},{8,9},{9,8},{10,11... | collective-permute-start | bytes 1572872 | tf_op jit(solution)/shard_map/ppermute | solution.py:395
  23.0 17.8 %collective-permute-start.12 = (bf16[64,32,128]{2,1,0:T(8,128)(2,1)S(1)}, bf16[64,32,128]{2,1,0:T(8,128)(2,1)S(1)}, u32[]{:S(2)}, u32[]{:S(2)}) collective-permute-start(bf16[64,32,128]{2,1,0:T(8,128)(2,1)S(1)} %get-tuple-element.28), channel_id=1, source_target_pairs={{0,4},{1,2},{2,1},{3,7},{4,0},{5,6},{6,5},{7,3},{8,12},{9,10},{10,... | collective-permute-start | bytes 1572872 | tf_op jit(solution)/shard_map/ppermute | solution.py:408
  23.0 10.0 %collective-permute-start.7 = (f32[72,128]{1,0:T(8,128)S(1)}, f32[72,128]{1,0:T(8,128)S(1)}, u32[]{:S(2)}, u32[]{:S(2)}) collective-permute-start(f32[72,128]{1,0:T(8,128)S(1)} %get-tuple-element.26), channel_id=1, source_target_pairs={{0,4},{4,0},{8,12},{12,8},{16,20},{20,16},{24,28},{28,24},{1,5},{5... | collective-permute-start | bytes 110600 | tf_op jit(solution)/shard_map/ppermute | solution.py:412
  33.0 6.2 %collective-permute-start.10 = (f32[2,72,128]{2,1,0:T(8,128)S(1)}, f32[2,72,128]{2,1,0:T(8,128)S(1)}, u32[]{:S(2)}, u32[]{:S(2)}) collective-permute-start(f32[2,72,128]{2,1,0:T(8,128)S(1)} %pad_maximum_fusion.refs_0_), channel_id=1, source_target_pairs={{0,24},{4,28},{8,16},{12,20},{16,8},{20,12},{24,0},{28,4},{1,25},{... | collective-permute-start | bytes 221192 | tf_op jit(solution)/shard_map/ppermute | solution.py:412
  34.6 6.1 %collective-permute-start.9 = (f32[2,72,128]{2,1,0:T(8,128)S(1)}, f32[2,72,128]{2,1,0:T(8,128)S(1)}, u32[]{:S(2)}, u32[]{:S(2)}) collective-permute-start(f32[2,72,128]{2,1,0:T(8,128)S(1)} %pad_maximum_fusion.refs_0_), channel_id=1, source_target_pairs={{0,16},{4,20},{8,24},{12,28},{16,0},{20,4},{24,8},{28,12},{1,17},{... | collective-permute-start | bytes 221192 | tf_op jit(solution)/shard_map/ppermute | solution.py:412
  34.6 6.1 %collective-permute-start.8 = (f32[2,72,128]{2,1,0:T(8,128)S(1)}, f32[2,72,128]{2,1,0:T(8,128)S(1)}, u32[]{:S(2)}, u32[]{:S(2)}) collective-permute-start(f32[2,72,128]{2,1,0:T(8,128)S(1)} %pad_maximum_fusion.refs_0_), channel_id=1, source_target_pairs={{0,8},{4,12},{8,0},{12,4},{16,24},{20,28},{24,16},{28,20},{1,9},{5... | collective-permute-start | bytes 221192 | tf_op jit(solution)/shard_map/ppermute | solution.py:412
where the time goes:
time: 44.5 us; the launch traced here: 44.3 us
  starting transfers between devices  16.7 us (38%)
  waiting for transfers between devices  14.1 us (32%)
  Pallas kernels  12.7 us (29%)
  between operations  0.72 us (2%)
    ppermute x7, waiting for transfers between devices, exchanged(): lax.ppermute(value, axis, [(i, i ^ mask) for i in range(lax.axis_size(axi...  14.1 us
    ppermute x7, starting transfers between devices, exchanged(): lax.ppermute(value, axis, [(i, i ^ mask) for i in range(lax.axis_size(axi...  8.33 us
    ppermute x4, starting transfers between devices, swapped(): return lax.ppermute(value, axis, pairs)  5.69 us
    pallas_call x1, Pallas kernels, body(): call(finish_kernel, [shape((1, modes), F32), shape(field, F32)], [SMEM, S...  3.58 us
    pallas_call x1, Pallas kernels, body(): call(block_kernel, [shape((modes + 8, modes), F32), shape((7, rows, layer...  3.07 us
    ppermute x2, starting transfers between devices, swapped_open(): return lax.ppermute(value, ('sub', 'pln'), pairs)  2.66 us
    pallas_call x1, Pallas kernels, body(): call(join_kernel, [shape((modes + 8, 2 * modes), F32), shape((2, rows, la...  2.18 us
    pallas_call x1, Pallas kernels, body(): call(prepare_kernel, [shape((planes, rows, modes, layers), BF16), rest, r...  2.02 us
  transfers between devices with their start and end apart: 13, of which 5 were waited for; matrix products, arithmetic and copies ran while one was open for 0% of the time, Pallas kernels for 12%

commit v1 on v0

--- a/solution.py
+++ b/solution.py
@@ -53,29 +53,23 @@
     return ((row == 0) & lane_is((16, width), lane)).astype(BF16)
 
 
-def stage_kernel(place, labels_far, zvec, inner_near, outer_near, labels, label_sem, sems):
+def stage_kernel(place, labels_far, zvec, outer_near, labels, label_sem, sem):
     modes, planes, rows, layers = zvec.shape
     half = rows // 2
     side = lax.rem(place[1], 2)
     start = pl.multiple_of((1 - side) * half, half)
     label_copy = pltpu.make_async_copy(labels_far, labels, label_sem)
-    copies = [
-        pltpu.make_async_copy(
-            zvec.at[:, plane, pl.ds(start, half), :], out.at[pl.ds(0, modes)], sems.at[slot]
-        )
-        for slot, plane, out in ((1, side, outer_near), (0, 1 - side, inner_near))
-    ]
+    copy = pltpu.make_async_copy(
+        zvec.at[:, side, pl.ds(start, half), :], outer_near.at[pl.ds(0, modes)], sem
+    )
+    copy.start()
     label_copy.start()
-    for copy in copies:
-        copy.start()
     label_copy.wait()
-    for plane, out in ((side, outer_near), (1 - side, inner_near)):
-        out[modes:] = labels[plane].astype(F32).astype(BF16).reshape(rows // half, half, layers)
-    for copy in copies:
-        copy.wait()
-
-
-def prepare_kernel(place, labels, held, planes_out, inner_rest, outer_rest, one_pack, two_pack):
+    outer_near[modes:] = labels[side].astype(F32).astype(BF16).reshape(rows // half, half, layers)
+    copy.wait()
+
+
+def prepare_kernel(place, labels, held, staged, planes_out, inner_near, one_pack, two_pack):
     modes, planes, rows, layers = held.shape
     half = rows // 2
     width = planes * rows
@@ -100,9 +94,12 @@
             out[at] = jnp.concatenate(
                 [ends[index:index + 1, j * width:(j + 1) * width] for j in range(CHUNK)], axis=0
             ).astype(BF16)
-        for slot, plane, rest in ((0, 1 - side, inner_rest), (1, side, outer_rest)):
+        for slot, plane in ((0, 1 - side), (1, side)):
             planes_out[slot, :, at, :] = jnp.swapaxes(held[at, plane], 0, 1)
-            rest[at] = held[at, plane, pl.ds(pl.multiple_of(side * half, half), half), :]
+        inner_near[at] = held[at, 1 - side, pl.ds(pl.multiple_of((1 - side) * half, half), half), :]
+    inner_near[modes:] = (
+        labels[1 - side].astype(F32).astype(BF16).reshape(rows // half, half, layers)
+    )
 
 
 def block_kernel(
@@ -243,22 +240,14 @@
     out[modes:, modes:] = jnp.zeros((8, modes), F32)
 
 
-def sum_kernel(own, one, two, three, inner_rest, outer_rest, out, inner_out, outer_out):
-    out[...] = (own[...] + one[...]) + (two[...] + three[...])
-
-
-def finish_kernel(place, levels, *refs):
-    count = len(refs) - 18
+def solve_kernel(place, *refs):
+    count = len(refs) - 9
     blocks, refs = refs[:count], refs[count:]
-    zvec, inner_got, outer_got, inner_last, outer_last, one_got, two_got, weights, faces, resid = refs[:10]
-    solution, deflated, direction_ref, image_ref, ahead_ref, spread, sides, ends_ref = refs[10:]
+    zvec, solution, beside, inner_field, outer_field, direction_ref, image_ref, ahead_ref, spread = refs
     subs = direction_ref.shape[0]
     modes, planes, rows, layers = zvec.shape
-    half = rows // 2
     me = place[0]
     side = lax.rem(place[1], 2)
-    odd = lax.rem(me, 2) == 1
-    at_edge = (place[1] == 0) | (place[1] == place[2] - 1)
     order = place[3]
     held = (1 - side, side)
     square = (modes, modes)
@@ -320,8 +309,40 @@
     own = direction_ref[pl.ds(me, 1), :modes]
     solution[...] = own
     spread[...] = jnp.broadcast_to(column(own), (modes, layers))
-    ahead_column = column(direction_ref[pl.ds(lax.rem(me + 1, subs), 1), :modes])
-    behind_column = column(direction_ref[pl.ds(lax.rem(me + subs - 1, subs), 1), :modes])
+    beside[0:1, :] = direction_ref[pl.ds(lax.rem(me + 1, subs), 1), :modes]
+    beside[1:2, :] = direction_ref[pl.ds(lax.rem(me + subs - 1, subs), 1), :modes]
+
+    def add_mode(j, carry):
+        fields = list(carry)
+        for u in range(MODES):
+            k = j * MODES + u
+            scale = spread[pl.ds(k, 1), :]
+            for x in range(2):
+                fields[x] = fields[x] + scale * zvec[k, held[x]].astype(F32)
+        return tuple(fields)
+
+    zero = jnp.zeros((rows, layers), F32)
+    inner_field[...], outer_field[...] = lax.fori_loop(0, modes // MODES, add_mode, (zero, zero))
+
+
+def stencil_kernel(
+    place, levels, beside, inner_field, outer_field, one_got, two_got, weights, faces, resid, inside,
+    ends_ref,
+):
+    rows, layers = inner_field.shape
+    planes = resid.shape[0]
+    modes = beside.shape[1]
+    side = lax.rem(place[1], 2)
+    odd = lax.rem(place[0], 2) == 1
+    held = (1 - side, side)
+    square = (modes, modes)
+    eye = lax.broadcasted_iota(jnp.int32, square, 0) == lax.broadcasted_iota(jnp.int32, square, 1)
+
+    def column(row):
+        return jnp.sum(jnp.where(eye, row, 0.0), axis=1, keepdims=True)
+
+    ahead_column = column(beside[0:1, :])
+    behind_column = column(beside[1:2, :])
     at_top = lane_is((modes, layers), layers - 1)
     at_bottom = lane_is((modes, layers), 0)
 
@@ -340,28 +361,9 @@
         + placed(prev_last[modes:].astype(BF16), pick_row(0, layers), None),
         levels,
     ).reshape(planes, rows, layers)
-
-    others = (inner_got, inner_last, outer_got, outer_last)
-
-    def add_mode(j, carry):
-        fields, edges = list(carry[0]), list(carry[1])
-        for u in range(MODES):
-            k = j * MODES + u
-            scale = spread[pl.ds(k, 1), :]
-            for x in range(2):
-                fields[x] = fields[x] + scale * zvec[k, held[x]].astype(F32)
-            for index, other in enumerate(others):
-                edges[index] = edges[index] + scale * other[k].astype(F32)
-        return tuple(fields), tuple(edges)
-
-    zero, short = jnp.zeros((rows, layers), F32), jnp.zeros((half, layers), F32)
-    field, edges = lax.fori_loop(0, modes // MODES, add_mode, ((zero, zero), (short,) * 4))
-    for slot in range(2):
-        sides[slot, pl.ds(pl.multiple_of(side * half, half), half), :] = edges[2 * slot]
-        sides[slot, pl.ds(pl.multiple_of((1 - side) * half, half), half), :] = edges[2 * slot + 1]
+    field = (inner_field[...], outer_field[...])
     row = lax.broadcasted_iota(jnp.int32, (rows, layers), 0)
     lane = lax.broadcasted_iota(jnp.int32, (rows, layers), 1)
-    outside = (sides[0], jnp.where(at_edge, 0.0, sides[1]))
     for x in range(2):
         f = field[x]
         c = weights[5 + x]
@@ -377,13 +379,20 @@
         below_z = jnp.where(lane == 0, end_field, pltpu.roll(f, 1, 1))
         image = (
             weights[0] * (f - field[1 - x])
-            + faces[x] * (f - outside[x])
+            + faces[x] * f
             + down_y * (f - below_y)
             + up_y * (f - above_y)
             + down_z * (f - below_z)
             + up_z * (f - above_z)
         )
-        deflated[held[x]] = resid[held[x]] - image
+        inside[x] = resid[held[x]] - image
+
+
+def outside_kernel(place, inside, faces, inner_got, outer_got, deflated):
+    side = lax.rem(place[1], 2)
+    at_edge = (place[1] == 0) | (place[1] == place[2] - 1)
+    deflated[1 - side] = inside[0] + faces[0] * inner_got[...]
+    deflated[side] = inside[1] + jnp.where(at_edge, 0.0, faces[1] * outer_got[...])
 
 
 def swapped(value, axis, first):
@@ -412,6 +421,13 @@
     return lax.ppermute(value, axis, [(i, i ^ mask) for i in range(lax.axis_size(axis))])
 
 
+def summed(value, axis):
+    if lax.axis_size(axis) != 4:
+        return lax.psum(value, axis)
+    one, two, three = (exchanged(value, axis, mask) for mask in (1, 2, 3))
+    return (value + one) + (two + three)
+
+
 def gathered(value, axis):
     if lax.axis_size(axis) != 8:
         return [lax.all_gather(value, axis)]
@@ -430,23 +446,22 @@
     )
     pack = shape((modes + 16, planes * rows), BF16)
     near = shape((modes + rows // half, half, layers), BF16)
-    inner_near, outer_near = call(
+    [outer_near] = call(
         stage_kernel,
-        [near, near],
+        [near],
         [SMEM, HBM, HBM],
-        [pltpu.VMEM(labels.shape, jnp.int32), pltpu.SemaphoreType.DMA, pltpu.SemaphoreType.DMA((2,))],
-        moved=2 << 20,
+        [pltpu.VMEM(labels.shape, jnp.int32), pltpu.SemaphoreType.DMA, pltpu.SemaphoreType.DMA],
+        moved=1 << 20,
     )(place, *(pltpu.with_memory_space_constraint(v, pltpu.HBM) for v in (labels, zvec)))
     outer_got = swapped_open(outer_near)
-    inner_got = swapped(inner_near, "pln", 0)
-    rest = shape((modes, half, layers), BF16)
-    here, inner_rest, outer_rest, one_pack, two_pack = call(
+    here, inner_near, one_pack, two_pack = call(
         prepare_kernel,
-        [shape((planes, rows, modes, layers), BF16), rest, rest, pack, pack],
-        [SMEM, VMEM, VMEM],
+        [shape((planes, rows, modes, layers), BF16), near, pack, pack],
+        [SMEM, VMEM, VMEM, ANY],
         flops=10_000_000,
         moved=6 << 20,
-    )(place, labels, zvec)
+    )(place, labels, zvec, outer_near)
+    inner_got = swapped(inner_near, "pln", 0)
     one_got = swapped(one_pack, "sub", 0)
     two_got = swapped(two_pack, "sub", 1)
     field = (planes, rows, layers)
@@ -468,38 +483,35 @@
     )(
         place, levels, partial, weights, here, inner_got, outer_got, one_pack, two_pack, one_got, two_got
     )
-    if parts == 4:
-        block, inner_rest, outer_rest = call(
-            sum_kernel,
-            [shape(block.shape, F32), rest, rest],
-            [VMEM] * 4 + [ANY] * 2,
-            aliases={4: 1, 5: 2},
-        )(block, *(exchanged(block, "pln", mask) for mask in (1, 2, 3)), inner_rest, outer_rest)
-    else:
-        block = lax.psum(block, "pln")
-    inner_last = swapped(inner_rest, "pln", 0)
-    outer_last = swapped_open(outer_rest)
-    blocks = gathered(block, "sub")
-    return tuple(
-        call(
-            finish_kernel,
-            [shape((1, modes), F32), shape(field, F32)],
-            [SMEM, SMEM] + [VMEM] * (10 + len(blocks)),
-            [
-                pltpu.VMEM((subs, 2 * modes), F32),
-                pltpu.VMEM((subs, 2 * modes), F32),
-                pltpu.VMEM((modes, 128), F32),
-                pltpu.VMEM((modes, layers), F32),
-                pltpu.VMEM(field, F32),
-                pltpu.VMEM(field, F32),
-            ],
-            flops=10_000_000,
-            moved=5 << 20,
-        )(
-            place, levels, *blocks, zvec, inner_got, outer_got, inner_last, outer_last, one_got, two_got, weights,
-            faces, resid,
-        )
-    )
+    blocks = gathered(summed(block, "pln"), "sub")
+    plane = shape((rows, layers), F32)
+    solved, beside, inner_field, outer_field = call(
+        solve_kernel,
+        [shape((1, modes), F32), shape((2, modes), F32), plane, plane],
+        [SMEM] + [VMEM] * (1 + len(blocks)),
+        [
+            pltpu.VMEM((subs, 2 * modes), F32),
+            pltpu.VMEM((subs, 2 * modes), F32),
+            pltpu.VMEM((modes, 128), F32),
+            pltpu.VMEM((modes, layers), F32),
+        ],
+        flops=10_000_000,
+        moved=5 << 20,
+    )(place, *blocks, zvec)
+    inner_beside = swapped(inner_field, "pln", 0)
+    outer_beside = swapped(outer_field, "pln", 1)
+    [inside] = call(
+        stencil_kernel,
+        [shape(field, F32)],
+        [SMEM, SMEM] + [VMEM] * 8,
+        [pltpu.VMEM(field, F32)],
+        flops=10_000_000,
+        moved=1 << 20,
+    )(place, levels, beside, inner_field, outer_field, one_got, two_got, weights, faces, resid)
+    [deflated] = call(outside_kernel, [shape(field, F32)], [SMEM] + [VMEM] * 4, moved=1 << 18)(
+        place, inside, faces, inner_beside, outer_beside
+    )
+    return solved, deflated
 
 
 def solution(mesh):

time: 44.5 us -> 44.1 us (level)
  waiting for transfers between devices: 14.1 us -> 11.4 us
  starting transfers between devices: 16.7 us -> 18.1 us
  Pallas kernels: 12.7 us -> 13.6 us
    ppermute x7, waiting for transfers between devices: 14.1 us -> 10.5 us  [exchanged(): lax.ppermute(value, axis, [(i, i ^ mask) for i in range(lax.axis_size(axi...]
    ppermute x4 -> x5, starting transfers between devices: 5.69 us -> 7.12 us  [swapped(): return lax.ppermute(value, axis, pairs)]
    pallas_call x4 -> x5, Pallas kernels: 7.47 us -> 8.36 us  [the longest x1 2.52 us: body(): call(solve_kernel, [shape((1, modes), F32), shape((2, modes), F32), plane...]
    ppermute x4 -> x5, waiting for transfers between devices: 0.03 us -> 0.89 us  [swapped(): return lax.ppermute(value, axis, pairs)]
    ppermute x2 -> x1, starting transfers between devices: 2.66 us -> 2.59 us  [swapped_open(): return lax.ppermute(value, ('sub', 'pln'), pairs)]
  transfers between devices with their start and end apart: 13 -> 13, of which waited for: 5 -> 7; matrix products, arithmetic and copies ran while one was open for 0% -> 0% of each run, Pallas kernels for 12% -> 9%
where the time goes in v1:
time: 44.1 us; the launch traced here: 43.9 us
  starting transfers between devices  18.1 us (41%)
  Pallas kernels  13.6 us (31%)
  waiting for transfers between devices  11.4 us (26%)
  between operations  0.72 us (2%)
    ppermute x7, waiting for transfers between devices, exchanged(): lax.ppermute(value, axis, [(i, i ^ mask) for i in range(lax.axis_size(axi...  10.5 us
    ppermute x7, starting transfers between devices, exchanged(): lax.ppermute(value, axis, [(i, i ^ mask) for i in range(lax.axis_size(axi...  8.34 us
    ppermute x5, starting transfers between devices, swapped(): return lax.ppermute(value, axis, pairs)  7.12 us
    pallas_call x1, Pallas kernels, body(): call(block_kernel, [shape((modes + 8, modes), F32), shape((7, rows, layer...  3.06 us
    ppermute x1, starting transfers between devices, swapped_open(): return lax.ppermute(value, ('sub', 'pln'), pairs)  2.59 us
    pallas_call x1, Pallas kernels, body(): call(solve_kernel, [shape((1, modes), F32), shape((2, modes), F32), plane...  2.52 us
    pallas_call x1, Pallas kernels, body(): call(join_kernel, [shape((modes + 8, 2 * modes), F32), shape((2, rows, la...  2.18 us
    pallas_call x1, Pallas kernels, body(): call(prepare_kernel, [shape((planes, rows, modes, layers), BF16), near, p...  2 us
  transfers between devices with their start and end apart: 13, of which 7 were waited for; matrix products, arithmetic and copies ran while one was open for 0% of the time, Pallas kernels for 9%

profile of v1, /device:TPU:0, one launch (start us, length us, event | category | flops | bytes accessed | tf_op | source)
XLA Modules:
  0.0 43.9 jit_solution(17423187260184925998)
XLA Ops:
  0.6 0.0 copy-start.1
  0.6 0.0 copy-start
  0.7 0.1 pad_add_fusion.place
  0.7 1.7 %shard_map.59.staged = bf16[66,32,128]{2,1,0:T(8,128)(2,1)S(1)} custom-call(s32[4]{0:T(128)S(1)} %pad_add_fusion.place, s32[2,64,128]{2,1,0:T(8,128)} %labels.3, bf16[64,2,64,128]{3,2,1,0:T(8,128)(2,1)} %refs_4_.1), custom_call_target="tpu_custom_call" | custom-call | bytes 1048576 | tf_op jit(solution)/shard_map/pallas_call | solution.py:449
  2.5 2.0 %shard_map.60 = (bf16[2,64,64,128]{3,2,1,0:T(8,128)(2,1)S(1)}, bf16[66,32,128]{2,1,0:T(8,128)(2,1)S(1)}, bf16[80,128]{1,0:T(8,128)(2,1)S(1)}, bf16[80,128]{1,0:T(8,128)(2,1)S(1)}) custom-call(s32[4]{0:T(128)S(1)} %pad_add_fusion.place, s32[2,64,128]{2,1,0:T(8,128)S(1)} %copy-done.1, bf16[64,2,64,128]{3,2,1,0:T(8,128)(2,1)S(1)} %copy-done, ...), custom_call_target="tpu_custom_call" | custom-call | flops 10000000 | bytes 6291456 | tf_op jit(solution)/shard_map/pallas_call | solution.py:457
  4.5 0.5 %collective-permute-start = (bf16[66,32,128]{2,1,0:T(8,128)(2,1)S(1)}, bf16[66,32,128]{2,1,0:T(8,128)(2,1)S(1)}, u32[]{:S(2)}, u32[]{:S(2)}) collective-permute-start(bf16[66,32,128]{2,1,0:T(8,128)(2,1)S(1)} %get-tuple-element.17), channel_id=1, source_target_pairs={{0,1},{1,0},{2,3},{3,2},{4,5},{5,4},{6,7},{7,6},{8,9},{9,8},{10,11... | collective-permute-start | bytes 1622024 | tf_op jit(solution)/shard_map/ppermute | solution.py:404
  5.0 2.6 %collective-permute-start.1 = (bf16[66,32,128]{2,1,0:T(8,128)(2,1)S(1)}, bf16[66,32,128]{2,1,0:T(8,128)(2,1)S(1)}, u32[]{:S(2)}, u32[]{:S(2)}) collective-permute-start(bf16[66,32,128]{2,1,0:T(8,128)(2,1)S(1)} %shard_map.59.staged), channel_id=1, source_target_pairs={{0,4},{1,2},{2,1},{3,7},{4,0},{5,6},{6,5},{7,3},{8,12},{9,10},{10,... | collective-permute-start | bytes 1622024 | tf_op jit(solution)/shard_map/ppermute | solution.py:417
  7.5 0.1 collective-permute-start.2
  7.6 5.0 %collective-permute-start.3 = (bf16[80,128]{1,0:T(8,128)(2,1)S(1)}, bf16[80,128]{1,0:T(8,128)(2,1)S(1)}, u32[]{:S(2)}, u32[]{:S(2)}) collective-permute-start(bf16[80,128]{1,0:T(8,128)(2,1)S(1)} %get-tuple-element.19.two_pack), channel_id=1, source_target_pairs={{0,28},{4,8},{8,4},{12,16},{16,12},{20,24},{24,20},{28,0},{1,29},{... | collective-permute-start | bytes 61448 | tf_op jit(solution)/shard_map/ppermute | solution.py:404
  12.6 3.1 %shard_map.61 = (f32[72,64]{1,0:T(8,128)S(1)}, f32[7,64,128]{2,1,0:T(8,128)S(1)}) custom-call(s32[4]{0:T(128)S(1)} %pad_add_fusion.place, f32[4]{0:T(128)S(1)} %copy-done.3, s32[2,64,128]{2,1,0:T(8,128)S(1)} %copy-done.1, f32[2,64,128]{2,1,0:T(8,128)S(1)} %copy-done.2, bf16[2,64,64,128]{3,2,1,0:T(8,128)(2,1)S(1)} %get-tuple-element.14.here), custom_call_target="tpu_custom_call" | custom-call | flops 400000000 | bytes 3145728 | tf_op jit(solution)/shard_map/pallas_call | solution.py:468
  15.7 0.1 collective-permute-done.2.one_got
  15.8 0.0 collective-permute-done.1.outer_got
  15.8 2.2 %shard_map.62 = (f32[72,128]{1,0:T(8,128)S(1)}, f32[2,64,128]{2,1,0:T(8,128)S(1)}) custom-call(s32[4]{0:T(128)S(1)} %pad_add_fusion.place, f32[4]{0:T(128)S(1)} %copy-done.3, f32[72,64]{1,0:T(8,128)S(1)} %get-tuple-element.15.partial, f32[7,64,128]{2,1,0:T(8,128)S(1)} %get-tuple-element.16.weights, bf16[2,64,64,128]{3,2,1,0:T(8,128)(2,1)S(1)} %get-tuple-element.14.here, ...), custom_call_target="tpu_custom_call" | custom-call | flops 200000000 | bytes 2097152 | tf_op jit(solution)/shard_map/pallas_call | solution.py:476
  18.0 0.6 %collective-permute-start.5 = (f32[72,128]{1,0:T(8,128)S(1)}, f32[72,128]{1,0:T(8,128)S(1)}, u32[]{:S(2)}, u32[]{:S(2)}) collective-permute-start(f32[72,128]{1,0:T(8,128)S(1)} %get-tuple-element.20), channel_id=1, source_target_pairs={{0,2},{1,3},{2,0},{3,1},{4,6},{5,7},{6,4},{7,5},{8,10},{9,11},{10,... | collective-permute-start | bytes 110600 | tf_op jit(solution)/shard_map/ppermute | solution.py:421
  18.5 0.4 collective-permute-start.6
  19.0 1.2 %collective-permute-start.4 = (f32[72,128]{1,0:T(8,128)S(1)}, f32[72,128]{1,0:T(8,128)S(1)}, u32[]{:S(2)}, u32[]{:S(2)}) collective-permute-start(f32[72,128]{1,0:T(8,128)S(1)} %get-tuple-element.20), channel_id=1, source_target_pairs={{0,1},{1,0},{2,3},{3,2},{4,5},{5,4},{6,7},{7,6},{8,9},{9,8},{10,11... | collective-permute-start | bytes 110600 | tf_op jit(solution)/shard_map/ppermute | solution.py:421
  20.2 2.2 %collective-permute-done.5 = f32[72,128]{1,0:T(8,128)S(1)} collective-permute-done((f32[72,128]{1,0:T(8,128)S(1)}, f32[72,128]{1,0:T(8,128)S(1)}, u32[]{:S(2)}, u32[]{:S(2)}) %collective-permute-start.5) | collective-permute-done | bytes 36896 | tf_op jit(solution)/shard_map/ppermute | solution.py:421
  22.3 1.7 %collective-permute-start.7 = (f32[72,128]{1,0:T(8,128)S(1)}, f32[72,128]{1,0:T(8,128)S(1)}, u32[]{:S(2)}, u32[]{:S(2)}) collective-permute-start(f32[72,128]{1,0:T(8,128)S(1)} %add_add_fusion), channel_id=1, source_target_pairs={{0,4},{4,0},{8,12},{12,8},{16,20},{20,16},{24,28},{28,24},{1,5},{5... | collective-permute-start | bytes 110600 | tf_op jit(solution)/shard_map/ppermute | solution.py:421
  24.1 2.3 %collective-permute-done.7 = f32[72,128]{1,0:T(8,128)S(1)} collective-permute-done((f32[72,128]{1,0:T(8,128)S(1)}, f32[72,128]{1,0:T(8,128)S(1)}, u32[]{:S(2)}, u32[]{:S(2)}) %collective-permute-start.7) | collective-permute-done | bytes 36896 | tf_op jit(solution)/shard_map/ppermute | solution.py:421
  26.4 1.7 %collective-permute-start.8 = (f32[2,72,128]{2,1,0:T(8,128)S(1)}, f32[2,72,128]{2,1,0:T(8,128)S(1)}, u32[]{:S(2)}, u32[]{:S(2)}) collective-permute-start(f32[2,72,128]{2,1,0:T(8,128)S(1)} %pad_maximum_fusion.refs_0_), channel_id=1, source_target_pairs={{0,8},{4,12},{8,0},{12,4},{16,24},{20,28},{24,16},{28,20},{1,9},{5... | collective-permute-start | bytes 221192 | tf_op jit(solution)/shard_map/ppermute | solution.py:421
  28.1 2.6 %collective-permute-start.9 = (f32[2,72,128]{2,1,0:T(8,128)S(1)}, f32[2,72,128]{2,1,0:T(8,128)S(1)}, u32[]{:S(2)}, u32[]{:S(2)}) collective-permute-start(f32[2,72,128]{2,1,0:T(8,128)S(1)} %pad_maximum_fusion.refs_0_), channel_id=1, source_target_pairs={{0,16},{4,20},{8,24},{12,28},{16,0},{20,4},{24,8},{28,12},{1,17},{... | collective-permute-start | bytes 221192 | tf_op jit(solution)/shard_map/ppermute | solution.py:421
  30.7 0.1 collective-permute-start.10
  30.8 0.7 %collective-permute-done.8.refs_1_ = f32[2,72,128]{2,1,0:T(8,128)S(1)} collective-permute-done((f32[2,72,128]{2,1,0:T(8,128)S(1)}, f32[2,72,128]{2,1,0:T(8,128)S(1)}, u32[]{:S(2)}, u32[]{:S(2)}) %collective-permute-start.8) | collective-permute-done | bytes 73760 | tf_op jit(solution)/shard_map/ppermute | solution.py:421
  31.4 3.7 %collective-permute-done.9.refs_2_ = f32[2,72,128]{2,1,0:T(8,128)S(1)} collective-permute-done((f32[2,72,128]{2,1,0:T(8,128)S(1)}, f32[2,72,128]{2,1,0:T(8,128)S(1)}, u32[]{:S(2)}, u32[]{:S(2)}) %collective-permute-start.9) | collective-permute-done | bytes 73760 | tf_op jit(solution)/shard_map/ppermute | solution.py:421
  35.1 1.7 %collective-permute-done.10.refs_3_ = f32[2,72,128]{2,1,0:T(8,128)S(1)} collective-permute-done((f32[2,72,128]{2,1,0:T(8,128)S(1)}, f32[2,72,128]{2,1,0:T(8,128)S(1)}, u32[]{:S(2)}, u32[]{:S(2)}) %collective-permute-start.10) | collective-permute-done | bytes 73760 | tf_op jit(solution)/shard_map/ppermute | solution.py:421
  36.9 2.5 %shard_map.63 = (f32[1,64]{1,0:T(1,128)}, f32[2,64]{1,0:T(2,128)S(1)}, f32[64,128]{1,0:T(8,128)S(1)}, f32[64,128]{1,0:T(8,128)S(1)}) custom-call(s32[4]{0:T(128)S(1)} %pad_add_fusion.place, f32[2,72,128]{2,1,0:T(8,128)S(1)} %pad_maximum_fusion.refs_0_, f32[2,72,128]{2,1,0:T(8,128)S(1)} %collective-permute-done.8.refs_1_, ...), custom_call_target="tpu_custom_call" | custom-call | flops 10000000 | bytes 5242880 | tf_op jit(solution)/shard_map/pallas_call | solution.py:488
  39.4 0.0 collective-permute-start.11
  39.4 1.6 %collective-permute-start.12 = (f32[64,128]{1,0:T(8,128)S(1)}, f32[64,128]{1,0:T(8,128)S(1)}, u32[]{:S(2)}, u32[]{:S(2)}) collective-permute-start(f32[64,128]{1,0:T(8,128)S(1)} %get-tuple-element.24.outer_field), channel_id=1, source_target_pairs={{0,3},{1,2},{2,1},{3,0},{4,7},{5,6},{6,5},{7,4},{8,11},{9,10},{10,... | collective-permute-start | bytes 98312 | tf_op jit(solution)/shard_map/ppermute | solution.py:404
  40.9 1.0 %shard_map.64.inside = f32[2,64,128]{2,1,0:T(8,128)S(1)} custom-call(s32[4]{0:T(128)S(1)} %pad_add_fusion.place, f32[4]{0:T(128)S(1)} %copy-done.3, f32[2,64]{1,0:T(2,128)S(1)} %get-tuple-element.22.beside, f32[64,128]{1,0:T(8,128)S(1)} %get-tuple-element.23.inner_field, f32[64,128]{1,0:T(8,128)S(1)} %get-tuple-element.24.outer_field, ...), custom_call_target="tpu_custom_call" | custom-call | flops 10000000 | bytes 1048576 | tf_op jit(solution)/shard_map/pallas_call | solution.py:503
  41.9 0.0 collective-permute-done.11.inner_got
  41.9 0.8 %collective-permute-done.12.outer_got = f32[64,128]{1,0:T(8,128)S(1)} collective-permute-done((f32[64,128]{1,0:T(8,128)S(1)}, f32[64,128]{1,0:T(8,128)S(1)}, u32[]{:S(2)}, u32[]{:S(2)}) %collective-permute-start.12) | collective-permute-done | bytes 32800 | tf_op jit(solution)/shard_map/ppermute | solution.py:404
  42.7 1.2 %shard_map.65 = f32[2,64,128]{2,1,0:T(8,128)} custom-call(s32[4]{0:T(128)S(1)} %pad_add_fusion.place, f32[2,64,128]{2,1,0:T(8,128)S(1)} %shard_map.64.inside, f32[2,64,128]{2,1,0:T(8,128)S(1)} %get-tuple-element.25.faces, f32[64,128]{1,0:T(8,128)S(1)} %collective-permute-done.11.inner_got, f32[64,128]{1,0:T(8,128)S(1)} %collective-permute-done.12.outer_got), custom_call_target="tpu_custom_call" | custom-call | bytes 262144 | tf_op jit(solution)/shard_map/pallas_call | solution.py:511
  (12 shorter events, 0.0 us)
Async XLA Ops:
  0.6 1.8 %copy-start.1 = (s32[2,64,128]{2,1,0:T(8,128)S(1)}, s32[2,64,128]{2,1,0:T(8,128)}, u32[]{:S(2)}) copy-start(s32[2,64,128]{2,1,0:T(8,128)} %labels.3) | copy-start | bytes 196612
  0.6 1.8 %copy-start = (bf16[64,2,64,128]{3,2,1,0:T(8,128)(2,1)S(1)}, bf16[64,2,64,128]{3,2,1,0:T(8,128)(2,1)}, u32[]{:S(2)}) copy-start(bf16[64,2,64,128]{3,2,1,0:T(8,128)(2,1)} %refs_4_.1) | copy-start | bytes 6291460
  0.7 11.9 %copy-start.2 = (f32[2,64,128]{2,1,0:T(8,128)S(1)}, f32[2,64,128]{2,1,0:T(8,128)}, u32[]{:S(2)}) copy-start(f32[2,64,128]{2,1,0:T(8,128)} %resid.3) | copy-start | bytes 196612
  0.7 11.9 %copy-start.3 = (f32[4]{0:T(128)S(1)}, f32[4]{0:T(128)}, u32[]{:S(2)}) copy-start(f32[4]{0:T(128)} %levels.5) | copy-start | bytes 52
  4.5 11.3 %collective-permute-start = (bf16[66,32,128]{2,1,0:T(8,128)(2,1)S(1)}, bf16[66,32,128]{2,1,0:T(8,128)(2,1)S(1)}, u32[]{:S(2)}, u32[]{:S(2)}) collective-permute-start(bf16[66,32,128]{2,1,0:T(8,128)(2,1)S(1)} %get-tuple-element.17), channel_id=1, source_target_pairs={{0,1},{1,0},{2,3},{3,2},{4,5},{5,4},{6,7},{7,6},{8,9},{9,8},{10,11... | collective-permute-start | bytes 1622024 | tf_op jit(solution)/shard_map/ppermute | solution.py:404
  5.0 10.8 %collective-permute-start.1 = (bf16[66,32,128]{2,1,0:T(8,128)(2,1)S(1)}, bf16[66,32,128]{2,1,0:T(8,128)(2,1)S(1)}, u32[]{:S(2)}, u32[]{:S(2)}) collective-permute-start(bf16[66,32,128]{2,1,0:T(8,128)(2,1)S(1)} %shard_map.59.staged), channel_id=1, source_target_pairs={{0,4},{1,2},{2,1},{3,7},{4,0},{5,6},{6,5},{7,3},{8,12},{9,10},{10,... | collective-permute-start | bytes 1622024 | tf_op jit(solution)/shard_map/ppermute | solution.py:417
  7.5 8.2 %collective-permute-start.2 = (bf16[80,128]{1,0:T(8,128)(2,1)S(1)}, bf16[80,128]{1,0:T(8,128)(2,1)S(1)}, u32[]{:S(2)}, u32[]{:S(2)}) collective-permute-start(bf16[80,128]{1,0:T(8,128)(2,1)S(1)} %get-tuple-element.18.one_pack), channel_id=1, source_target_pairs={{0,4},{4,0},{8,12},{12,8},{16,20},{20,16},{24,28},{28,24},{1,5},{5... | collective-permute-start | bytes 61448 | tf_op jit(solution)/shard_map/ppermute | solution.py:404
  7.6 8.1 %collective-permute-start.3 = (bf16[80,128]{1,0:T(8,128)(2,1)S(1)}, bf16[80,128]{1,0:T(8,128)(2,1)S(1)}, u32[]{:S(2)}, u32[]{:S(2)}) collective-permute-start(bf16[80,128]{1,0:T(8,128)(2,1)S(1)} %get-tuple-element.19.two_pack), channel_id=1, source_target_pairs={{0,28},{4,8},{8,4},{12,16},{16,12},{20,24},{24,20},{28,0},{1,29},{... | collective-permute-start | bytes 61448 | tf_op jit(solution)/shard_map/ppermute | solution.py:404
  18.0 4.4 %collective-permute-start.5 = (f32[72,128]{1,0:T(8,128)S(1)}, f32[72,128]{1,0:T(8,128)S(1)}, u32[]{:S(2)}, u32[]{:S(2)}) collective-permute-start(f32[72,128]{1,0:T(8,128)S(1)} %get-tuple-element.20), channel_id=1, source_target_pairs={{0,2},{1,3},{2,0},{3,1},{4,6},{5,7},{6,4},{7,5},{8,10},{9,11},{10,... | collective-permute-start | bytes 110600 | tf_op jit(solution)/shard_map/ppermute | solution.py:421
  18.5 3.8 %collective-permute-start.6 = (f32[72,128]{1,0:T(8,128)S(1)}, f32[72,128]{1,0:T(8,128)S(1)}, u32[]{:S(2)}, u32[]{:S(2)}) collective-permute-start(f32[72,128]{1,0:T(8,128)S(1)} %get-tuple-element.20), channel_id=1, source_target_pairs={{0,3},{1,2},{2,1},{3,0},{4,7},{5,6},{6,5},{7,4},{8,11},{9,10},{10,... | collective-permute-start | bytes 110600 | tf_op jit(solution)/shard_map/ppermute | solution.py:421
  19.0 3.3 %collective-permute-start.4 = (f32[72,128]{1,0:T(8,128)S(1)}, f32[72,128]{1,0:T(8,128)S(1)}, u32[]{:S(2)}, u32[]{:S(2)}) collective-permute-start(f32[72,128]{1,0:T(8,128)S(1)} %get-tuple-element.20), channel_id=1, source_target_pairs={{0,1},{1,0},{2,3},{3,2},{4,5},{5,4},{6,7},{7,6},{8,9},{9,8},{10,11... | collective-permute-start | bytes 110600 | tf_op jit(solution)/shard_map/ppermute | solution.py:421
  22.3 4.0 %collective-permute-start.7 = (f32[72,128]{1,0:T(8,128)S(1)}, f32[72,128]{1,0:T(8,128)S(1)}, u32[]{:S(2)}, u32[]{:S(2)}) collective-permute-start(f32[72,128]{1,0:T(8,128)S(1)} %add_add_fusion), channel_id=1, source_target_pairs={{0,4},{4,0},{8,12},{12,8},{16,20},{20,16},{24,28},{28,24},{1,5},{5... | collective-permute-start | bytes 110600 | tf_op jit(solution)/shard_map/ppermute | solution.py:421
  26.4 5.1 %collective-permute-start.8 = (f32[2,72,128]{2,1,0:T(8,128)S(1)}, f32[2,72,128]{2,1,0:T(8,128)S(1)}, u32[]{:S(2)}, u32[]{:S(2)}) collective-permute-start(f32[2,72,128]{2,1,0:T(8,128)S(1)} %pad_maximum_fusion.refs_0_), channel_id=1, source_target_pairs={{0,8},{4,12},{8,0},{12,4},{16,24},{20,28},{24,16},{28,20},{1,9},{5... | collective-permute-start | bytes 221192 | tf_op jit(solution)/shard_map/ppermute | solution.py:421
  28.1 7.0 %collective-permute-start.9 = (f32[2,72,128]{2,1,0:T(8,128)S(1)}, f32[2,72,128]{2,1,0:T(8,128)S(1)}, u32[]{:S(2)}, u32[]{:S(2)}) collective-permute-start(f32[2,72,128]{2,1,0:T(8,128)S(1)} %pad_maximum_fusion.refs_0_), channel_id=1, source_target_pairs={{0,16},{4,20},{8,24},{12,28},{16,0},{20,4},{24,8},{28,12},{1,17},{... | collective-permute-start | bytes 221192 | tf_op jit(solution)/shard_map/ppermute | solution.py:421
  30.7 6.2 %collective-permute-start.10 = (f32[2,72,128]{2,1,0:T(8,128)S(1)}, f32[2,72,128]{2,1,0:T(8,128)S(1)}, u32[]{:S(2)}, u32[]{:S(2)}) collective-permute-start(f32[2,72,128]{2,1,0:T(8,128)S(1)} %pad_maximum_fusion.refs_0_), channel_id=1, source_target_pairs={{0,24},{4,28},{8,16},{12,20},{16,8},{20,12},{24,0},{28,4},{1,25},{... | collective-permute-start | bytes 221192 | tf_op jit(solution)/shard_map/ppermute | solution.py:421
  39.4 2.5 %collective-permute-start.11 = (f32[64,128]{1,0:T(8,128)S(1)}, f32[64,128]{1,0:T(8,128)S(1)}, u32[]{:S(2)}, u32[]{:S(2)}) collective-permute-start(f32[64,128]{1,0:T(8,128)S(1)} %get-tuple-element.23.inner_field), channel_id=1, source_target_pairs={{0,1},{1,0},{2,3},{3,2},{4,5},{5,4},{6,7},{7,6},{8,9},{9,8},{10,11... | collective-permute-start | bytes 98312 | tf_op jit(solution)/shard_map/ppermute | solution.py:404
  39.4 3.3 %collective-permute-start.12 = (f32[64,128]{1,0:T(8,128)S(1)}, f32[64,128]{1,0:T(8,128)S(1)}, u32[]{:S(2)}, u32[]{:S(2)}) collective-permute-start(f32[64,128]{1,0:T(8,128)S(1)} %get-tuple-element.24.outer_field), channel_id=1, source_target_pairs={{0,3},{1,2},{2,1},{3,0},{4,7},{5,6},{6,5},{7,4},{8,11},{9,10},{10,... | collective-permute-start | bytes 98312 | tf_op jit(solution)/shard_map/ppermute | solution.py:404

commit v2 on v0

--- a/solution.py
+++ b/solution.py
@@ -53,7 +53,7 @@
     return ((row == 0) & lane_is((16, width), lane)).astype(BF16)
 
 
-def stage_kernel(place, labels_far, zvec, inner_near, outer_near, labels, label_sem, sems):
+def stage_kernel(place, labels_far, zvec, inner_send, outer_near, labels, label_sem, sems):
     modes, planes, rows, layers = zvec.shape
     half = rows // 2
     side = lax.rem(place[1], 2)
@@ -61,21 +61,21 @@
     label_copy = pltpu.make_async_copy(labels_far, labels, label_sem)
     copies = [
         pltpu.make_async_copy(
-            zvec.at[:, plane, pl.ds(start, half), :], out.at[pl.ds(0, modes)], sems.at[slot]
-        )
-        for slot, plane, out in ((1, side, outer_near), (0, 1 - side, inner_near))
+            zvec.at[:, side, pl.ds(start, half), :], outer_near.at[pl.ds(0, modes)], sems.at[0]
+        ),
+        pltpu.make_async_copy(zvec.at[:, 1 - side], inner_send.at[pl.ds(0, modes)], sems.at[1]),
     ]
     label_copy.start()
     for copy in copies:
         copy.start()
     label_copy.wait()
-    for plane, out in ((side, outer_near), (1 - side, inner_near)):
-        out[modes:] = labels[plane].astype(F32).astype(BF16).reshape(rows // half, half, layers)
+    outer_near[modes:] = labels[side].astype(F32).astype(BF16).reshape(rows // half, half, layers)
+    inner_send[modes] = labels[1 - side].astype(F32).astype(BF16)
     for copy in copies:
         copy.wait()
 
 
-def prepare_kernel(place, labels, held, planes_out, inner_rest, outer_rest, one_pack, two_pack):
+def prepare_kernel(place, labels, held, planes_out, outer_rest, one_pack, two_pack):
     modes, planes, rows, layers = held.shape
     half = rows // 2
     width = planes * rows
@@ -100,9 +100,9 @@
             out[at] = jnp.concatenate(
                 [ends[index:index + 1, j * width:(j + 1) * width] for j in range(CHUNK)], axis=0
             ).astype(BF16)
-        for slot, plane, rest in ((0, 1 - side, inner_rest), (1, side, outer_rest)):
+        for slot, plane in ((0, 1 - side), (1, side)):
             planes_out[slot, :, at, :] = jnp.swapaxes(held[at, plane], 0, 1)
-            rest[at] = held[at, plane, pl.ds(pl.multiple_of(side * half, half), half), :]
+        outer_rest[at] = held[at, side, pl.ds(pl.multiple_of(side * half, half), half), :]
 
 
 def block_kernel(
@@ -177,46 +177,43 @@
     )
 
 
-def join_kernel(
-    place, levels, partial, weights, here, inner_got, outer_got, one_pack, two_pack, one_got, two_got,
-    out, faces, other_planes,
+def turn(got, start, out):
+    half, modes, layers = out.shape
+    for k in range(0, modes, CHUNK):
+        out[:, k:k + CHUNK, :] = jnp.swapaxes(got[k:k + CHUNK, pl.ds(start, half), :], 0, 1)
+
+
+def face_product(weight_ref, base, own, other):
+    half, modes, layers = other.shape
+
+    def step(j, total):
+        left, right = [], []
+        for u in range(STEP):
+            y = j * STEP + u
+            weight = weight_ref[pl.ds(base + y, 1), :]
+            image = weight * (own[base + y].astype(F32) - other[y].astype(F32))
+            left.append(jnp.concatenate([own[base + y], other[y]], axis=0))
+            right.append(image.astype(BF16))
+        return total + lax.dot_general(
+            jnp.concatenate(left, axis=1), jnp.concatenate(right, axis=1), NT,
+            preferred_element_type=F32,
+        )
+
+    total = lax.fori_loop(0, half // STEP, step, jnp.zeros((2 * modes, modes), F32))
+    return total[:modes] - total[modes:]
+
+
+def inner_kernel(
+    place, levels, partial, weights, here, inner_got, one_pack, two_pack, one_got, two_got, out, face, turned,
 ):
     planes, rows, modes, layers = here.shape
     half = rows // 2
     side = lax.rem(place[1], 2)
     odd = lax.rem(place[0], 2) == 1
-    at_edge = (place[1] == 0) | (place[1] == place[2] - 1)
-    base = side * half
-    for slot, got in ((0, inner_got), (1, outer_got)):
-        for k in range(0, modes, CHUNK):
-            other_planes[slot, :, k:k + CHUNK, :] = jnp.swapaxes(got[k:k + CHUNK], 0, 1)
-    inner_coef, outer_coef = (
-        coefficients(got[modes:].astype(F32).reshape(rows, layers), levels)
-        for got in (inner_got, outer_got)
-    )
-    faces[0] = harmonic(weights[5], inner_coef)
-    faces[1] = jnp.where(at_edge, weights[6], harmonic(weights[6], outer_coef))
-
-    def step(j, total):
-        left, right = [], []
-        for u in range(STEP):
-            y = j * STEP + u
-            at = pl.ds(base + y, 1)
-            outer_weight = jnp.where(at_edge, 0.0, faces[1, at, :])
-            for weight, own, other in (
-                (faces[0, at, :], here[0, base + y], other_planes[0, y]),
-                (outer_weight, here[1, base + y], other_planes[1, y]),
-            ):
-                image = weight * (own.astype(F32) - other.astype(F32))
-                left.append(jnp.concatenate([own, other], axis=0))
-                right.append(image.astype(BF16))
-        return total + lax.dot_general(
-            jnp.concatenate(left, axis=1), jnp.concatenate(right, axis=1), NT,
-            preferred_element_type=F32,
-        )
-
-    cross = lax.fori_loop(0, half // STEP, step, jnp.zeros((2 * modes, modes), F32))
-    cross = cross[:modes] - cross[modes:]
+    base = pl.multiple_of(side * half, half)
+    turn(inner_got, base, turned)
+    face[...] = harmonic(weights[5], coefficients(inner_got[modes].astype(F32), levels))
+    cross = face_product(face, base, here.at[0], turned)
 
     def coef_row(pack):
         return coefficients(pack[modes:modes + 16].astype(F32)[0:1], levels)
@@ -234,24 +231,64 @@
 
     edge_rows = weight_high * last[:modes]
     ends = product(weight_low * first[:modes], first[:modes]) + product(edge_rows, last[:modes])
-    square = partial[:modes, :] + 0.5 * (cross + ends)
-    square = square + square.T
-    upper = -product(edge_rows, next_first[:modes])
-    out[:modes, :modes] = square
-    out[:modes, modes:] = upper
+    out[:modes, :modes] = partial[:modes, :] + 0.5 * (cross + ends)
+    out[:modes, modes:] = -product(edge_rows, next_first[:modes])
     out[modes:, :modes] = partial[modes:, :]
     out[modes:, modes:] = jnp.zeros((8, modes), F32)
 
 
-def sum_kernel(own, one, two, three, inner_rest, outer_rest, out, inner_out, outer_out):
-    out[...] = (own[...] + one[...]) + (two[...] + three[...])
+def outer_kernel(place, levels, block, weights, here, outer_got, out, face, turned, face_here):
+    planes, rows, modes, layers = here.shape
+    half = rows // 2
+    side = lax.rem(place[1], 2)
+    at_edge = (place[1] == 0) | (place[1] == place[2] - 1)
+    base = pl.multiple_of(side * half, half)
+    turn(outer_got, 0, turned)
+    coef = coefficients(outer_got[modes:].astype(F32).reshape(rows, layers), levels)
+    between = harmonic(weights[6], coef)
+    face[...] = jnp.where(at_edge, weights[6], between)
+    face_here[...] = jnp.where(at_edge, 0.0, between)
+    cross = face_product(face_here, base, here.at[1], turned)
+    square = block[:modes, :modes] + 0.5 * cross
+    out[:modes, :modes] = square + square.T
+    out[:modes, modes:] = block[:modes, modes:]
+    out[modes:, :] = block[modes:, :]
+
+
+def sum_kernel(own, one, two, three, outer_rest, out, outer_out):
+    modes = own.shape[1] // 2
+    total = (own[...] + one[...]) + (two[...] + three[...])
+    encode(total, modes, out)
+
+
+def encode(total, modes, out):
+    row = lax.broadcasted_iota(jnp.int32, (modes, 2 * modes), 0)
+    lane = lax.broadcasted_iota(jnp.int32, (modes, 2 * modes), 1)
+    values = total[:modes]
+    high = values.astype(BF16).astype(F32)
+    low = values - high
+    out[:modes] = jnp.where((lane <= row) | (lane >= modes), high, low).astype(BF16)
+    diagonal = lane == row
+    right = total[modes:modes + 1]
+    parts = []
+    for _ in range(3):
+        part = right.astype(BF16).astype(F32)
+        parts.append(part)
+        right = right - part
+    for part in (high, low):
+        parts.append(jnp.sum(jnp.where(diagonal, part, 0.0), axis=0, keepdims=True))
+    rows = lax.broadcasted_iota(jnp.int32, (16, 2 * modes), 0)
+    extra = jnp.zeros((16, 2 * modes), F32)
+    for index, part in enumerate(parts):
+        extra = jnp.where(rows == index, part, extra)
+    out[modes:] = extra.astype(BF16)
 
 
 def finish_kernel(place, levels, *refs):
-    count = len(refs) - 18
+    count = len(refs) - 19
     blocks, refs = refs[:count], refs[count:]
-    zvec, inner_got, outer_got, inner_last, outer_last, one_got, two_got, weights, faces, resid = refs[:10]
-    solution, deflated, direction_ref, image_ref, ahead_ref, spread, sides, ends_ref = refs[10:]
+    zvec, inner_got, outer_got, outer_last, one_got, two_got, weights, inner_face, outer_face, resid = refs[:10]
+    solution, deflated, direction_ref, image_ref, ahead_ref, spread, outer_field, ends_ref, fix_ref = refs[10:]
     subs = direction_ref.shape[0]
     modes, planes, rows, layers = zvec.shape
     half = rows // 2
@@ -277,9 +314,12 @@
                 pl.loop(0, held_here)(lambda entry, block=block: body(block.at[entry], entry))
 
     def load(block, s):
-        direction_ref[pl.ds(s, 1), :] = block[modes:modes + 1, :]
+        extra = block[modes:modes + 16, :].astype(F32)
+        direction_ref[pl.ds(s, 1), :] = (extra[0:1] + extra[1:2]) + extra[2:3]
+        fix_ref[pl.ds(s, 1), :] = extra[4:5] - extra[3:4]
 
     each(load)
+    fix = fix_ref[:, :modes]
 
     def turned(rows_of, by):
         by = by % subs
@@ -289,7 +329,7 @@
         direction_ref[...] = jnp.concatenate([direction, turned(direction, 1)], axis=1)
 
         def one(block, s):
-            values = block[:modes, :]
+            values = block[:modes, :].astype(F32)
             pair = direction_ref[pl.ds(s, 1), :]
             ahead = jnp.sum(values * pair, axis=1, keepdims=True)
             ahead_ref[...] = jnp.where(lane_is((modes, 128), s), ahead, ahead_ref[...])
@@ -298,7 +338,9 @@
             )
 
         each(one)
-        return ahead_ref[...].T[:subs] + turned(image_ref[:, modes:], -1)
+        image = image_ref[...]
+        square_part = ahead_ref[...].T[:subs] + image[:, :modes] + fix * direction
+        return square_part + turned(image[:, modes:], -1)
 
     def inner(left, right):
         return jnp.sum(jnp.sum(left * right, axis=0, keepdims=True), axis=1, keepdims=True)
@@ -341,27 +383,25 @@
         levels,
     ).reshape(planes, rows, layers)
 
-    others = (inner_got, inner_last, outer_got, outer_last)
-
     def add_mode(j, carry):
-        fields, edges = list(carry[0]), list(carry[1])
+        fields, near, last = list(carry[0]), carry[1], carry[2]
         for u in range(MODES):
             k = j * MODES + u
             scale = spread[pl.ds(k, 1), :]
-            for x in range(2):
-                fields[x] = fields[x] + scale * zvec[k, held[x]].astype(F32)
-            for index, other in enumerate(others):
-                edges[index] = edges[index] + scale * other[k].astype(F32)
-        return tuple(fields), tuple(edges)
+            for x, plane in enumerate((zvec[k, held[0]], zvec[k, held[1]], inner_got[k])):
+                fields[x] = fields[x] + scale * plane.astype(F32)
+            near = near + scale * outer_got[k].astype(F32)
+            last = last + scale * outer_last[k].astype(F32)
+        return tuple(fields), near, last
 
     zero, short = jnp.zeros((rows, layers), F32), jnp.zeros((half, layers), F32)
-    field, edges = lax.fori_loop(0, modes // MODES, add_mode, ((zero, zero), (short,) * 4))
-    for slot in range(2):
-        sides[slot, pl.ds(pl.multiple_of(side * half, half), half), :] = edges[2 * slot]
-        sides[slot, pl.ds(pl.multiple_of((1 - side) * half, half), half), :] = edges[2 * slot + 1]
+    field, near, last = lax.fori_loop(0, modes // MODES, add_mode, ((zero,) * 3, short, short))
+    outer_field[pl.ds(pl.multiple_of(side * half, half), half), :] = near
+    outer_field[pl.ds(pl.multiple_of((1 - side) * half, half), half), :] = last
+    outside = (field[2], jnp.where(at_edge, 0.0, outer_field[...]))
+    faces = (inner_face[...], outer_face[...])
     row = lax.broadcasted_iota(jnp.int32, (rows, layers), 0)
     lane = lax.broadcasted_iota(jnp.int32, (rows, layers), 1)
-    outside = (sides[0], jnp.where(at_edge, 0.0, sides[1]))
     for x in range(2):
         f = field[x]
         c = weights[5 + x]
@@ -395,17 +435,11 @@
     return lax.ppermute(value, axis, pairs)
 
 
-def swapped_open(value):
-    subs, count = lax.axis_size("sub"), lax.axis_size("pln")
+def swapped_open(value, axis):
     pairs = []
-    for s in range(subs):
-        for i in range(count):
-            if 0 < i < count - 1:
-                to = (s, i + 1 if i % 2 else i - 1)
-            else:
-                to = (s ^ 1, i)
-            pairs.append((s * count + i, to[0] * count + to[1]))
-    return lax.ppermute(value, ("sub", "pln"), pairs)
+    for i in range(1, lax.axis_size(axis) - 1):
+        pairs.append((i, i + 1 if i % 2 else i - 1))
+    return lax.ppermute(value, axis, pairs)
 
 
 def exchanged(value, axis, mask):
@@ -429,20 +463,19 @@
         [jnp.int32(v) for v in (lax.axis_index("sub"), lax.axis_index("pln"), parts, order)]
     )
     pack = shape((modes + 16, planes * rows), BF16)
-    near = shape((modes + rows // half, half, layers), BF16)
-    inner_near, outer_near = call(
+    inner_send, outer_near = call(
         stage_kernel,
-        [near, near],
+        [shape((modes + 1, rows, layers), BF16), shape((modes + rows // half, half, layers), BF16)],
         [SMEM, HBM, HBM],
         [pltpu.VMEM(labels.shape, jnp.int32), pltpu.SemaphoreType.DMA, pltpu.SemaphoreType.DMA((2,))],
         moved=2 << 20,
     )(place, *(pltpu.with_memory_space_constraint(v, pltpu.HBM) for v in (labels, zvec)))
-    outer_got = swapped_open(outer_near)
-    inner_got = swapped(inner_near, "pln", 0)
+    outer_got = swapped_open(outer_near, "pln")
+    inner_got = swapped(inner_send, "pln", 0)
     rest = shape((modes, half, layers), BF16)
-    here, inner_rest, outer_rest, one_pack, two_pack = call(
+    here, outer_rest, one_pack, two_pack = call(
         prepare_kernel,
-        [shape((planes, rows, modes, layers), BF16), rest, rest, pack, pack],
+        [shape((planes, rows, modes, layers), BF16), rest, pack, pack],
         [SMEM, VMEM, VMEM],
         flops=10_000_000,
         moved=6 << 20,
@@ -450,36 +483,44 @@
     one_got = swapped(one_pack, "sub", 0)
     two_got = swapped(two_pack, "sub", 1)
     field = (planes, rows, layers)
+    plane = (rows, layers)
+    block_shape = shape((modes + 8, 2 * modes), F32)
     partial, weights = call(
         block_kernel,
-        [shape((modes + 8, modes), F32), shape((7, rows, layers), F32)],
+        [shape((modes + 8, modes), F32), shape((7,) + plane, F32)],
         [SMEM, SMEM] + [VMEM] * 3,
         [pltpu.VMEM(field, F32)] * 3,
         flops=400_000_000,
         moved=3 << 20,
     )(place, levels, labels, resid, here)
-    block, faces = call(
-        join_kernel,
-        [shape((modes + 8, 2 * modes), F32), shape((2, rows, layers), F32)],
-        [SMEM, SMEM] + [VMEM] * 9,
-        [pltpu.VMEM((planes, half, modes, layers), BF16)],
-        flops=200_000_000,
-        moved=2 << 20,
-    )(
-        place, levels, partial, weights, here, inner_got, outer_got, one_pack, two_pack, one_got, two_got
-    )
+    turned = pltpu.VMEM((half, modes, layers), BF16)
+    block, inner_face = call(
+        inner_kernel,
+        [block_shape, shape(plane, F32)],
+        [SMEM, SMEM] + [VMEM] * 8,
+        [turned],
+        flops=100_000_000,
+        moved=1 << 20,
+    )(place, levels, partial, weights, here, inner_got, one_pack, two_pack, one_got, two_got)
+    block, outer_face = call(
+        outer_kernel,
+        [block_shape, shape(plane, F32)],
+        [SMEM, SMEM] + [VMEM] * 4,
+        [turned, pltpu.VMEM(plane, F32)],
+        flops=100_000_000,
+        moved=1 << 20,
+    )(place, levels, block, weights, here, outer_got)
+    packed = shape((modes + 16, 2 * modes), BF16)
     if parts == 4:
-        block, inner_rest, outer_rest = call(
-            sum_kernel,
-            [shape(block.shape, F32), rest, rest],
-            [VMEM] * 4 + [ANY] * 2,
-            aliases={4: 1, 5: 2},
-        )(block, *(exchanged(block, "pln", mask) for mask in (1, 2, 3)), inner_rest, outer_rest)
+        others = [exchanged(block, "pln", mask) for mask in (1, 2, 3)]
     else:
         block = lax.psum(block, "pln")
-    inner_last = swapped(inner_rest, "pln", 0)
-    outer_last = swapped_open(outer_rest)
-    blocks = gathered(block, "sub")
+        others = [jnp.zeros_like(block)] * 3
+    packed, outer_rest = call(
+        sum_kernel, [packed, rest], [VMEM] * 4 + [ANY], aliases={4: 1}
+    )(block, *others, outer_rest)
+    blocks = gathered(packed, "sub")
+    outer_last = swapped_open(outer_rest, "pln")
     return tuple(
         call(
             finish_kernel,
@@ -490,14 +531,15 @@
                 pltpu.VMEM((subs, 2 * modes), F32),
                 pltpu.VMEM((modes, 128), F32),
                 pltpu.VMEM((modes, layers), F32),
+                pltpu.VMEM(plane, F32),
                 pltpu.VMEM(field, F32),
-                pltpu.VMEM(field, F32),
+                pltpu.VMEM((subs, 2 * modes), F32),
             ],
             flops=10_000_000,
             moved=5 << 20,
         )(
-            place, levels, *blocks, zvec, inner_got, outer_got, inner_last, outer_last, one_got, two_got, weights,
-            faces, resid,
+            place, levels, *blocks, zvec, inner_got, outer_got, outer_last, one_got, two_got, weights,
+            inner_face, outer_face, resid,
         )
     )
 

time: 44.5 us -> 41.2 us (0.926)
  waiting for transfers between devices: 14.1 us -> 9.92 us
  Pallas kernels: 12.7 us -> 13.9 us
    ppermute x7, waiting for transfers between devices: 14.1 us -> 9.88 us  [exchanged(): lax.ppermute(value, axis, [(i, i ^ mask) for i in range(lax.axis_size(axi...]
    ppermute x2, starting transfers between devices: 2.66 us -> 1.38 us  [swapped_open(): return lax.ppermute(value, axis, pairs)]
    pallas_call x5 -> x6, Pallas kernels: 9.14 us -> 10.2 us  [the longest x1 3.06 us: body(): call(block_kernel, [shape((modes + 8, modes), F32), shape((7,) + plane, F...]
    ppermute x4 -> x3, starting transfers between devices: 5.69 us -> 6.66 us  [swapped(): return lax.ppermute(value, axis, pairs)]
  transfers between devices with their start and end apart: 13 -> 12, of which waited for: 5 -> 4; matrix products, arithmetic and copies ran while one was open for 0% -> 0% of each run, Pallas kernels for 12% -> 16%
where the time goes in v2:
time: 41.2 us; the launch traced here: 41.1 us
  starting transfers between devices  16.5 us (40%)
  Pallas kernels  13.9 us (34%)
  waiting for transfers between devices  9.92 us (24%)
  between operations  0.73 us (2%)
    ppermute x7, waiting for transfers between devices, exchanged(): lax.ppermute(value, axis, [(i, i ^ mask) for i in range(lax.axis_size(axi...  9.88 us
    ppermute x7, starting transfers between devices, exchanged(): lax.ppermute(value, axis, [(i, i ^ mask) for i in range(lax.axis_size(axi...  8.42 us
    ppermute x3, starting transfers between devices, swapped(): return lax.ppermute(value, axis, pairs)  6.66 us
    pallas_call x1, Pallas kernels, body(): call(finish_kernel, [shape((1, modes), F32), shape(field, F32)], [SMEM, S...  3.61 us
    pallas_call x1, Pallas kernels, body(): call(block_kernel, [shape((modes + 8, modes), F32), shape((7,) + plane, F...  3.06 us
    pallas_call x1, Pallas kernels, body(): call(stage_kernel, [shape((modes + 1, rows, layers), BF16), shape((modes...  2.03 us
    pallas_call x1, Pallas kernels, body(): call(prepare_kernel, [shape((planes, rows, modes, layers), BF16), rest, p...  2.01 us
    pallas_call x1, Pallas kernels, body(): call(inner_kernel, [block_shape, shape(plane, F32)], [SMEM, SMEM] + [VMEM...  1.7 us
  transfers between devices with their start and end apart: 12, of which 4 were waited for; matrix products, arithmetic and copies ran while one was open for 0% of the time, Pallas kernels for 16%

profile of v2, /device:TPU:0, one launch (start us, length us, event | category | flops | bytes accessed | tf_op | source)
XLA Modules:
  0.0 41.1 jit_solution(11034944790013903079)
XLA Ops:
  0.6 0.0 copy-start
  0.6 0.0 copy-start.1
  0.7 0.1 pad_add_fusion.place
  0.7 2.0 %shard_map.61 = (bf16[65,64,128]{2,1,0:T(8,128)(2,1)S(1)}, bf16[66,32,128]{2,1,0:T(8,128)(2,1)S(1)}) custom-call(s32[4]{0:T(128)S(1)} %pad_add_fusion.place, s32[2,64,128]{2,1,0:T(8,128)} %labels_far.1, bf16[64,2,64,128]{3,2,1,0:T(8,128)(2,1)} %refs_4_.1), custom_call_target="tpu_custom_call" | custom-call | bytes 2097152 | tf_op jit(solution)/shard_map/pallas_call | solution.py:466
  2.8 0.5 %collective-permute-start = (bf16[65,64,128]{2,1,0:T(8,128)(2,1)S(1)}, bf16[65,64,128]{2,1,0:T(8,128)(2,1)S(1)}, u32[]{:S(2)}, u32[]{:S(2)}) collective-permute-start(bf16[65,64,128]{2,1,0:T(8,128)(2,1)S(1)} %get-tuple-element.19), channel_id=1, source_target_pairs={{0,1},{1,0},{2,3},{3,2},{4,5},{5,4},{6,7},{7,6},{8,9},{9,8},{10,11... | collective-permute-start | bytes 3194888 | tf_op jit(solution)/shard_map/ppermute | solution.py:435
  3.3 0.7 %collective-permute-start.3 = (bf16[66,32,128]{2,1,0:T(8,128)(2,1)S(1)}, bf16[66,32,128]{2,1,0:T(8,128)(2,1)S(1)}, u32[]{:S(2)}, u32[]{:S(2)}) collective-permute-start(bf16[66,32,128]{2,1,0:T(8,128)(2,1)S(1)} %get-tuple-element.23), channel_id=1, source_target_pairs={{1,2},{2,1},{5,6},{6,5},{9,10},{10,9},{13,14},{14,13},{17,18},{18,... | collective-permute-start | bytes 1622024 | tf_op jit(solution)/shard_map/ppermute | solution.py:442
  4.0 2.0 %shard_map.59 = (bf16[2,64,64,128]{3,2,1,0:T(8,128)(2,1)S(1)}, bf16[64,32,128]{2,1,0:T(8,128)(2,1)S(1)}, bf16[80,128]{1,0:T(8,128)(2,1)S(1)}, bf16[80,128]{1,0:T(8,128)(2,1)S(1)}) custom-call(s32[4]{0:T(128)S(1)} %pad_add_fusion.place, s32[2,64,128]{2,1,0:T(8,128)S(1)} %copy-done.1, bf16[64,2,64,128]{3,2,1,0:T(8,128)(2,1)S(1)} %copy-done), custom_call_target="tpu_custom_call" | custom-call | flops 10000000 | bytes 6291456 | tf_op jit(solution)/shard_map/pallas_call | solution.py:476
  6.0 2.6 %collective-permute-start.1 = (bf16[80,128]{1,0:T(8,128)(2,1)S(1)}, bf16[80,128]{1,0:T(8,128)(2,1)S(1)}, u32[]{:S(2)}, u32[]{:S(2)}) collective-permute-start(bf16[80,128]{1,0:T(8,128)(2,1)S(1)} %get-tuple-element.20.one_pack), channel_id=1, source_target_pairs={{0,4},{4,0},{8,12},{12,8},{16,20},{20,16},{24,28},{28,24},{1,5},{5... | collective-permute-start | bytes 61448 | tf_op jit(solution)/shard_map/ppermute | solution.py:435
  8.6 3.5 %collective-permute-start.2 = (bf16[80,128]{1,0:T(8,128)(2,1)S(1)}, bf16[80,128]{1,0:T(8,128)(2,1)S(1)}, u32[]{:S(2)}, u32[]{:S(2)}) collective-permute-start(bf16[80,128]{1,0:T(8,128)(2,1)S(1)} %get-tuple-element.21.two_pack), channel_id=1, source_target_pairs={{0,28},{4,8},{8,4},{12,16},{16,12},{20,24},{24,20},{28,0},{1,29},{... | collective-permute-start | bytes 61448 | tf_op jit(solution)/shard_map/ppermute | solution.py:435
  12.2 3.1 %shard_map.60 = (f32[72,64]{1,0:T(8,128)S(1)}, f32[7,64,128]{2,1,0:T(8,128)S(1)}) custom-call(s32[4]{0:T(128)S(1)} %pad_add_fusion.place, f32[4]{0:T(128)S(1)} %copy-done.3, s32[2,64,128]{2,1,0:T(8,128)S(1)} %copy-done.1, f32[2,64,128]{2,1,0:T(8,128)S(1)} %copy-done.2, bf16[2,64,64,128]{3,2,1,0:T(8,128)(2,1)S(1)} %get-tuple-element.16.here), custom_call_target="tpu_custom_call" | custom-call | flops 400000000 | bytes 3145728 | tf_op jit(solution)/shard_map/pallas_call | solution.py:488
  15.2 0.0 collective-permute-done.1.one_got.refs_8_
  15.2 0.0 collective-permute-done.2.two_got.refs_9_
  15.2 0.0 collective-permute-done.inner_got.refs_5_
  15.3 1.7 %shard_map.62 = (f32[72,128]{1,0:T(8,128)S(1)}, f32[64,128]{1,0:T(8,128)S(1)}) custom-call(s32[4]{0:T(128)S(1)} %pad_add_fusion.place, f32[4]{0:T(128)S(1)} %copy-done.3, f32[72,64]{1,0:T(8,128)S(1)} %get-tuple-element.17.partial, f32[7,64,128]{2,1,0:T(8,128)S(1)} %get-tuple-element.18.weights.refs_10_, bf16[2,64,64,128]{3,2,1,0:T(8,128)(2,1)S(1)} %get-tuple-element.16.here, ...), custom_call_target="tpu_custom_call" | custom-call | flops 100000000 | bytes 1048576 | tf_op jit(solution)/shard_map/pallas_call | solution.py:497
  17.0 0.0 collective-permute-done.3.outer_got.refs_6_
  17.0 1.4 %shard_map.63 = (f32[72,128]{1,0:T(8,128)S(1)}, f32[64,128]{1,0:T(8,128)S(1)}) custom-call(s32[4]{0:T(128)S(1)} %pad_add_fusion.place, f32[4]{0:T(128)S(1)} %copy-done.3, f32[72,128]{1,0:T(8,128)S(1)} %get-tuple-element.22.block, f32[7,64,128]{2,1,0:T(8,128)S(1)} %get-tuple-element.18.weights.refs_10_, bf16[2,64,64,128]{3,2,1,0:T(8,128)(2,1)S(1)} %get-tuple-element.16.here, ...), custom_call_target="tpu_custom_call" | custom-call | flops 100000000 | bytes 1048576 | tf_op jit(solution)/shard_map/pallas_call | solution.py:505
  18.4 1.1 %collective-permute-start.6 = (f32[72,128]{1,0:T(8,128)S(1)}, f32[72,128]{1,0:T(8,128)S(1)}, u32[]{:S(2)}, u32[]{:S(2)}) collective-permute-start(f32[72,128]{1,0:T(8,128)S(1)} %get-tuple-element.24.own), channel_id=1, source_target_pairs={{0,3},{1,2},{2,1},{3,0},{4,7},{5,6},{6,5},{7,4},{8,11},{9,10},{10,... | collective-permute-start | bytes 110600 | tf_op jit(solution)/shard_map/ppermute | solution.py:446
  19.5 2.9 %collective-permute-start.5 = (f32[72,128]{1,0:T(8,128)S(1)}, f32[72,128]{1,0:T(8,128)S(1)}, u32[]{:S(2)}, u32[]{:S(2)}) collective-permute-start(f32[72,128]{1,0:T(8,128)S(1)} %get-tuple-element.24.own), channel_id=1, source_target_pairs={{0,2},{1,3},{2,0},{3,1},{4,6},{5,7},{6,4},{7,5},{8,10},{9,11},{10,... | collective-permute-start | bytes 110600 | tf_op jit(solution)/shard_map/ppermute | solution.py:446
  22.4 0.0 collective-permute-start.4
  22.4 0.0 collective-permute-done.6.three
  22.4 2.5 %collective-permute-done.5.two = f32[72,128]{1,0:T(8,128)S(1)} collective-permute-done((f32[72,128]{1,0:T(8,128)S(1)}, f32[72,128]{1,0:T(8,128)S(1)}, u32[]{:S(2)}, u32[]{:S(2)}) %collective-permute-start.5) | collective-permute-done | bytes 36896 | tf_op jit(solution)/shard_map/ppermute | solution.py:446
  24.9 0.0 collective-permute-done.4.one
  24.9 0.7 %collective-permute-start.11 = (bf16[64,32,128]{2,1,0:T(8,128)(2,1)S(1)}, bf16[64,32,128]{2,1,0:T(8,128)(2,1)S(1)}, u32[]{:S(2)}, u32[]{:S(2)}) collective-permute-start(bf16[64,32,128]{2,1,0:T(8,128)(2,1)S(1)} %get-tuple-element.27), channel_id=1, source_target_pairs={{1,2},{2,1},{5,6},{6,5},{9,10},{10,9},{13,14},{14,13},{17,18},{18,... | collective-permute-start | bytes 1572872 | tf_op jit(solution)/shard_map/ppermute | solution.py:442
  25.6 0.1 collective-permute-start.7
  25.7 3.8 %collective-permute-done.7 = bf16[80,128]{1,0:T(8,128)(2,1)S(1)} collective-permute-done((bf16[80,128]{1,0:T(8,128)(2,1)S(1)}, bf16[80,128]{1,0:T(8,128)(2,1)S(1)}, u32[]{:S(2)}, u32[]{:S(2)}) %collective-permute-start.7) | collective-permute-done | bytes 20512 | tf_op jit(solution)/shard_map/ppermute | solution.py:446
  29.5 1.1 %collective-permute-start.10 = (bf16[2,80,128]{2,1,0:T(8,128)(2,1)S(1)}, bf16[2,80,128]{2,1,0:T(8,128)(2,1)S(1)}, u32[]{:S(2)}, u32[]{:S(2)}) collective-permute-start(bf16[2,80,128]{2,1,0:T(8,128)(2,1)S(1)} %pad_maximum_fusion.refs_0_), channel_id=1, source_target_pairs={{0,24},{4,28},{8,16},{12,20},{16,8},{20,12},{24,0},{28,4},{1,25},{... | collective-permute-start | bytes 122888 | tf_op jit(solution)/shard_map/ppermute | solution.py:446
  30.6 0.0 collective-permute-start.9
  30.6 3.3 %collective-permute-start.8 = (bf16[2,80,128]{2,1,0:T(8,128)(2,1)S(1)}, bf16[2,80,128]{2,1,0:T(8,128)(2,1)S(1)}, u32[]{:S(2)}, u32[]{:S(2)}) collective-permute-start(bf16[2,80,128]{2,1,0:T(8,128)(2,1)S(1)} %pad_maximum_fusion.refs_0_), channel_id=1, source_target_pairs={{0,8},{4,12},{8,0},{12,4},{16,24},{20,28},{24,16},{28,20},{1,9},{5... | collective-permute-start | bytes 122888 | tf_op jit(solution)/shard_map/ppermute | solution.py:446
  33.9 1.4 %collective-permute-done.10.refs_3_ = bf16[2,80,128]{2,1,0:T(8,128)(2,1)S(1)} collective-permute-done((bf16[2,80,128]{2,1,0:T(8,128)(2,1)S(1)}, bf16[2,80,128]{2,1,0:T(8,128)(2,1)S(1)}, u32[]{:S(2)}, u32[]{:S(2)}) %collective-permute-start.10) | collective-permute-done | bytes 40992 | tf_op jit(solution)/shard_map/ppermute | solution.py:446
  35.3 2.1 %collective-permute-done.9.refs_2_ = bf16[2,80,128]{2,1,0:T(8,128)(2,1)S(1)} collective-permute-done((bf16[2,80,128]{2,1,0:T(8,128)(2,1)S(1)}, bf16[2,80,128]{2,1,0:T(8,128)(2,1)S(1)}, u32[]{:S(2)}, u32[]{:S(2)}) %collective-permute-start.9) | collective-permute-done | bytes 40992 | tf_op jit(solution)/shard_map/ppermute | solution.py:446
  37.4 0.0 collective-permute-done.8.refs_1_
  37.5 3.6 %shard_map.65 = (f32[1,64]{1,0:T(1,128)}, f32[2,64,128]{2,1,0:T(8,128)}) custom-call(s32[4]{0:T(128)S(1)} %pad_add_fusion.place, f32[4]{0:T(128)S(1)} %copy-done.3, bf16[2,80,128]{2,1,0:T(8,128)(2,1)S(1)} %pad_maximum_fusion.refs_0_, bf16[2,80,128]{2,1,0:T(8,128)(2,1)S(1)} %collective-permute-done.8.refs_1_, ...), custom_call_target="tpu_custom_call" | custom-call | flops 10000000 | bytes 5242880 | tf_op jit(solution)/shard_map/pallas_call | solution.py:525
  (9 shorter events, 0.1 us)
Async XLA Ops:
  0.6 3.4 %copy-start = (bf16[64,2,64,128]{3,2,1,0:T(8,128)(2,1)S(1)}, bf16[64,2,64,128]{3,2,1,0:T(8,128)(2,1)}, u32[]{:S(2)}) copy-start(bf16[64,2,64,128]{3,2,1,0:T(8,128)(2,1)} %refs_4_.1) | copy-start | bytes 6291460
  0.6 3.4 %copy-start.1 = (s32[2,64,128]{2,1,0:T(8,128)S(1)}, s32[2,64,128]{2,1,0:T(8,128)}, u32[]{:S(2)}) copy-start(s32[2,64,128]{2,1,0:T(8,128)} %labels_far.1) | copy-start | bytes 196612
  0.7 11.4 %copy-start.2 = (f32[2,64,128]{2,1,0:T(8,128)S(1)}, f32[2,64,128]{2,1,0:T(8,128)}, u32[]{:S(2)}) copy-start(f32[2,64,128]{2,1,0:T(8,128)} %refs_13_.1) | copy-start | bytes 196612
  0.7 11.4 %copy-start.3 = (f32[4]{0:T(128)S(1)}, f32[4]{0:T(128)}, u32[]{:S(2)}) copy-start(f32[4]{0:T(128)} %levels.7) | copy-start | bytes 52
  2.8 12.5 %collective-permute-start = (bf16[65,64,128]{2,1,0:T(8,128)(2,1)S(1)}, bf16[65,64,128]{2,1,0:T(8,128)(2,1)S(1)}, u32[]{:S(2)}, u32[]{:S(2)}) collective-permute-start(bf16[65,64,128]{2,1,0:T(8,128)(2,1)S(1)} %get-tuple-element.19), channel_id=1, source_target_pairs={{0,1},{1,0},{2,3},{3,2},{4,5},{5,4},{6,7},{7,6},{8,9},{9,8},{10,11... | collective-permute-start | bytes 3194888 | tf_op jit(solution)/shard_map/ppermute | solution.py:435
  3.3 13.7 %collective-permute-start.3 = (bf16[66,32,128]{2,1,0:T(8,128)(2,1)S(1)}, bf16[66,32,128]{2,1,0:T(8,128)(2,1)S(1)}, u32[]{:S(2)}, u32[]{:S(2)}) collective-permute-start(bf16[66,32,128]{2,1,0:T(8,128)(2,1)S(1)} %get-tuple-element.23), channel_id=1, source_target_pairs={{1,2},{2,1},{5,6},{6,5},{9,10},{10,9},{13,14},{14,13},{17,18},{18,... | collective-permute-start | bytes 1622024 | tf_op jit(solution)/shard_map/ppermute | solution.py:442
  6.0 9.2 %collective-permute-start.1 = (bf16[80,128]{1,0:T(8,128)(2,1)S(1)}, bf16[80,128]{1,0:T(8,128)(2,1)S(1)}, u32[]{:S(2)}, u32[]{:S(2)}) collective-permute-start(bf16[80,128]{1,0:T(8,128)(2,1)S(1)} %get-tuple-element.20.one_pack), channel_id=1, source_target_pairs={{0,4},{4,0},{8,12},{12,8},{16,20},{20,16},{24,28},{28,24},{1,5},{5... | collective-permute-start | bytes 61448 | tf_op jit(solution)/shard_map/ppermute | solution.py:435
  8.6 6.6 %collective-permute-start.2 = (bf16[80,128]{1,0:T(8,128)(2,1)S(1)}, bf16[80,128]{1,0:T(8,128)(2,1)S(1)}, u32[]{:S(2)}, u32[]{:S(2)}) collective-permute-start(bf16[80,128]{1,0:T(8,128)(2,1)S(1)} %get-tuple-element.21.two_pack), channel_id=1, source_target_pairs={{0,28},{4,8},{8,4},{12,16},{16,12},{20,24},{24,20},{28,0},{1,29},{... | collective-permute-start | bytes 61448 | tf_op jit(solution)/shard_map/ppermute | solution.py:435
  18.4 4.0 %collective-permute-start.6 = (f32[72,128]{1,0:T(8,128)S(1)}, f32[72,128]{1,0:T(8,128)S(1)}, u32[]{:S(2)}, u32[]{:S(2)}) collective-permute-start(f32[72,128]{1,0:T(8,128)S(1)} %get-tuple-element.24.own), channel_id=1, source_target_pairs={{0,3},{1,2},{2,1},{3,0},{4,7},{5,6},{6,5},{7,4},{8,11},{9,10},{10,... | collective-permute-start | bytes 110600 | tf_op jit(solution)/shard_map/ppermute | solution.py:446
  19.5 5.4 %collective-permute-start.5 = (f32[72,128]{1,0:T(8,128)S(1)}, f32[72,128]{1,0:T(8,128)S(1)}, u32[]{:S(2)}, u32[]{:S(2)}) collective-permute-start(f32[72,128]{1,0:T(8,128)S(1)} %get-tuple-element.24.own), channel_id=1, source_target_pairs={{0,2},{1,3},{2,0},{3,1},{4,6},{5,7},{6,4},{7,5},{8,10},{9,11},{10,... | collective-permute-start | bytes 110600 | tf_op jit(solution)/shard_map/ppermute | solution.py:446
  22.4 2.6 %collective-permute-start.4 = (f32[72,128]{1,0:T(8,128)S(1)}, f32[72,128]{1,0:T(8,128)S(1)}, u32[]{:S(2)}, u32[]{:S(2)}) collective-permute-start(f32[72,128]{1,0:T(8,128)S(1)} %get-tuple-element.24.own), channel_id=1, source_target_pairs={{0,1},{1,0},{2,3},{3,2},{4,5},{5,4},{6,7},{7,6},{8,9},{9,8},{10,11... | collective-permute-start | bytes 110600 | tf_op jit(solution)/shard_map/ppermute | solution.py:446
  24.9 12.5 %collective-permute-start.11 = (bf16[64,32,128]{2,1,0:T(8,128)(2,1)S(1)}, bf16[64,32,128]{2,1,0:T(8,128)(2,1)S(1)}, u32[]{:S(2)}, u32[]{:S(2)}) collective-permute-start(bf16[64,32,128]{2,1,0:T(8,128)(2,1)S(1)} %get-tuple-element.27), channel_id=1, source_target_pairs={{1,2},{2,1},{5,6},{6,5},{9,10},{10,9},{13,14},{14,13},{17,18},{18,... | collective-permute-start | bytes 1572872 | tf_op jit(solution)/shard_map/ppermute | solution.py:442
  25.6 3.8 %collective-permute-start.7 = (bf16[80,128]{1,0:T(8,128)(2,1)S(1)}, bf16[80,128]{1,0:T(8,128)(2,1)S(1)}, u32[]{:S(2)}, u32[]{:S(2)}) collective-permute-start(bf16[80,128]{1,0:T(8,128)(2,1)S(1)} %get-tuple-element.26), channel_id=1, source_target_pairs={{0,4},{4,0},{8,12},{12,8},{16,20},{20,16},{24,28},{28,24},{1,5},{5... | collective-permute-start | bytes 61448 | tf_op jit(solution)/shard_map/ppermute | solution.py:446
  29.5 5.8 %collective-permute-start.10 = (bf16[2,80,128]{2,1,0:T(8,128)(2,1)S(1)}, bf16[2,80,128]{2,1,0:T(8,128)(2,1)S(1)}, u32[]{:S(2)}, u32[]{:S(2)}) collective-permute-start(bf16[2,80,128]{2,1,0:T(8,128)(2,1)S(1)} %pad_maximum_fusion.refs_0_), channel_id=1, source_target_pairs={{0,24},{4,28},{8,16},{12,20},{16,8},{20,12},{24,0},{28,4},{1,25},{... | collective-permute-start | bytes 122888 | tf_op jit(solution)/shard_map/ppermute | solution.py:446
  30.6 6.8 %collective-permute-start.9 = (bf16[2,80,128]{2,1,0:T(8,128)(2,1)S(1)}, bf16[2,80,128]{2,1,0:T(8,128)(2,1)S(1)}, u32[]{:S(2)}, u32[]{:S(2)}) collective-permute-start(bf16[2,80,128]{2,1,0:T(8,128)(2,1)S(1)} %pad_maximum_fusion.refs_0_), channel_id=1, source_target_pairs={{0,16},{4,20},{8,24},{12,28},{16,0},{20,4},{24,8},{28,12},{1,17},{... | collective-permute-start | bytes 122888 | tf_op jit(solution)/shard_map/ppermute | solution.py:446
  30.6 6.8 %collective-permute-start.8 = (bf16[2,80,128]{2,1,0:T(8,128)(2,1)S(1)}, bf16[2,80,128]{2,1,0:T(8,128)(2,1)S(1)}, u32[]{:S(2)}, u32[]{:S(2)}) collective-permute-start(bf16[2,80,128]{2,1,0:T(8,128)(2,1)S(1)} %pad_maximum_fusion.refs_0_), channel_id=1, source_target_pairs={{0,8},{4,12},{8,0},{12,4},{16,24},{20,28},{24,16},{28,20},{1,9},{5... | collective-permute-start | bytes 122888 | tf_op jit(solution)/shard_map/ppermute | solution.py:446

commit v3 on v2

--- a/solution.py
+++ b/solution.py
@@ -203,44 +203,25 @@
     return total[:modes] - total[modes:]
 
 
-def inner_kernel(
-    place, levels, partial, weights, here, inner_got, one_pack, two_pack, one_got, two_got, out, face, turned,
+def inner_kernel(place, levels, partial, weights, here, inner_got, out, face, turned):
+    planes, rows, modes, layers = here.shape
+    half = rows // 2
+    side = lax.rem(place[1], 2)
+    base = pl.multiple_of(side * half, half)
+    turn(inner_got, base, turned)
+    face[...] = harmonic(weights[5], coefficients(inner_got[modes].astype(F32), levels))
+    out[:modes, :] = partial[:modes, :] + 0.5 * face_product(face, base, here.at[0], turned)
+    out[modes:, :] = partial[modes:, :]
+
+
+def outer_kernel(
+    place, levels, partial, weights, here, outer_got, one_pack, two_pack, one_got, two_got,
+    out, face, turned, face_here,
 ):
     planes, rows, modes, layers = here.shape
     half = rows // 2
     side = lax.rem(place[1], 2)
     odd = lax.rem(place[0], 2) == 1
-    base = pl.multiple_of(side * half, half)
-    turn(inner_got, base, turned)
-    face[...] = harmonic(weights[5], coefficients(inner_got[modes].astype(F32), levels))
-    cross = face_product(face, base, here.at[0], turned)
-
-    def coef_row(pack):
-        return coefficients(pack[modes:modes + 16].astype(F32)[0:1], levels)
-
-    one, two = one_pack[...].astype(F32), two_pack[...].astype(F32)
-    one_other, two_other = one_got[...].astype(F32), two_got[...].astype(F32)
-    first, last = jnp.where(odd, one, two), jnp.where(odd, two, one)
-    next_first = jnp.where(odd, two_other, one_other)
-    prev_last = jnp.where(odd, one_other, two_other)
-    weight_low = harmonic(coef_row(first), coef_row(prev_last))
-    weight_high = harmonic(coef_row(last), coef_row(next_first))
-
-    def product(left, right):
-        return lax.dot_general(left, right, NT, precision=PRECISE, preferred_element_type=F32)
-
-    edge_rows = weight_high * last[:modes]
-    ends = product(weight_low * first[:modes], first[:modes]) + product(edge_rows, last[:modes])
-    out[:modes, :modes] = partial[:modes, :] + 0.5 * (cross + ends)
-    out[:modes, modes:] = -product(edge_rows, next_first[:modes])
-    out[modes:, :modes] = partial[modes:, :]
-    out[modes:, modes:] = jnp.zeros((8, modes), F32)
-
-
-def outer_kernel(place, levels, block, weights, here, outer_got, out, face, turned, face_here):
-    planes, rows, modes, layers = here.shape
-    half = rows // 2
-    side = lax.rem(place[1], 2)
     at_edge = (place[1] == 0) | (place[1] == place[2] - 1)
     base = pl.multiple_of(side * half, half)
     turn(outer_got, 0, turned)
@@ -249,10 +230,64 @@
     face[...] = jnp.where(at_edge, weights[6], between)
     face_here[...] = jnp.where(at_edge, 0.0, between)
     cross = face_product(face_here, base, here.at[1], turned)
-    square = block[:modes, :modes] + 0.5 * cross
+
+    def coef_row(pack):
+        return coefficients(pack[modes:modes + 16].astype(F32)[0:1], levels)
+
+    one, two = one_pack[...].astype(F32), two_pack[...].astype(F32)
+    one_other, two_other = one_got[...].astype(F32), two_got[...].astype(F32)
+    first, last = jnp.where(odd, one, two), jnp.where(odd, two, one)
+    next_first = jnp.where(odd, two_other, one_other)
+    prev_last = jnp.where(odd, one_other, two_other)
+    weight_low = harmonic(coef_row(first), coef_row(prev_last))
+    weight_high = harmonic(coef_row(last), coef_row(next_first))
+
+    def product(left, right):
+        return lax.dot_general(left, right, NT, precision=PRECISE, preferred_element_type=F32)
+
+    edge_rows = weight_high * last[:modes]
+    ends = product(weight_low * first[:modes], first[:modes]) + product(edge_rows, last[:modes])
+    square = partial[:modes, :] + 0.5 * (cross + ends)
     out[:modes, :modes] = square + square.T
-    out[:modes, modes:] = block[:modes, modes:]
-    out[modes:, :] = block[modes:, :]
+    out[:modes, modes:] = -product(edge_rows, next_first[:modes])
+    out[modes:, :modes] = partial[modes:, :]
+    out[modes:, modes:] = jnp.zeros((8, modes), F32)
+
+
+def terms_kernel(
+    place, levels, pair, one_got, two_got, weights, inner_face, outer_face, terms, picked, coef_ref
+):
+    modes, width = picked.shape[1:]
+    rows, layers = inner_face.shape
+    side = lax.rem(place[1], 2)
+    odd = lax.rem(place[0], 2) == 1
+    one_other, two_other = one_got[...].astype(F32), two_got[...].astype(F32)
+    next_first = jnp.where(odd, two_other, one_other)
+    prev_last = jnp.where(odd, one_other, two_other)
+    picked[0] = next_first[:modes]
+    picked[1] = prev_last[:modes]
+    end_labels = lax.dot_general(
+        next_first[modes:].astype(BF16), pick_row(layers - 1, layers), TN, preferred_element_type=F32
+    ) + lax.dot_general(
+        prev_last[modes:].astype(BF16), pick_row(0, layers), TN, preferred_element_type=F32
+    )
+    coef_ref[...] = coefficients(end_labels, levels).reshape(width // rows, rows, layers)
+    row = lax.broadcasted_iota(jnp.int32, (rows, layers), 0)
+    lane = lax.broadcasted_iota(jnp.int32, (rows, layers), 1)
+    for x, face in enumerate((inner_face, outer_face)):
+        c = weights[5 + x]
+        end_weight = harmonic(c, coef_ref[1 - side if x == 0 else side])
+        up_y, up_z = weights[1 + x], weights[3 + x]
+        down_y = jnp.where(row == 0, c, pltpu.roll(up_y, 1, 0))
+        down_z = pltpu.roll(up_z, 1, 1)
+        total = face[...] + weights[0] + up_y + down_y
+        total = total + jnp.where(lane == layers - 1, end_weight, up_z)
+        terms[x, 0] = total + jnp.where(lane == 0, end_weight, down_z)
+        terms[x, 1] = jnp.where(row == 0, 0.0, down_y)
+        terms[x, 2] = jnp.where(row == rows - 1, 0.0, up_y)
+        terms[x, 3] = jnp.where(lane == 0, 0.0, down_z)
+        terms[x, 4] = jnp.where(lane == layers - 1, 0.0, up_z)
+        terms[x, 5] = end_weight
 
 
 def sum_kernel(own, one, two, three, outer_rest, out, outer_out):
@@ -284,11 +319,11 @@
     out[modes:] = extra.astype(BF16)
 
 
-def finish_kernel(place, levels, *refs):
-    count = len(refs) - 19
+def finish_kernel(place, *refs):
+    count = len(refs) - 18
     blocks, refs = refs[:count], refs[count:]
-    zvec, inner_got, outer_got, outer_last, one_got, two_got, weights, inner_face, outer_face, resid = refs[:10]
-    solution, deflated, direction_ref, image_ref, ahead_ref, spread, outer_field, ends_ref, fix_ref = refs[10:]
+    zvec, inner_got, outer_got, outer_last, picked, terms, middle, inner_face, outer_face, resid = refs[:10]
+    solution, deflated, direction_ref, image_ref, ahead_ref, spread, outer_field, fix_ref = refs[10:]
     subs = direction_ref.shape[0]
     modes, planes, rows, layers = zvec.shape
     half = rows // 2
@@ -367,21 +402,14 @@
     at_top = lane_is((modes, layers), layers - 1)
     at_bottom = lane_is((modes, layers), 0)
 
-    def placed(pack, values, precision):
-        return lax.dot_general(pack, values, TN, precision=precision, preferred_element_type=F32)
-
-    one_other, two_other = one_got[...].astype(F32), two_got[...].astype(F32)
-    next_first = jnp.where(odd, two_other, one_other)
-    prev_last = jnp.where(odd, one_other, two_other)
-    ends_ref[...] = (
-        placed(next_first[:modes], jnp.where(at_top, ahead_column, 0.0), PRECISE)
-        + placed(prev_last[:modes], jnp.where(at_bottom, behind_column, 0.0), PRECISE)
-    ).reshape(planes, rows, layers)
-    end_coef = coefficients(
-        placed(next_first[modes:].astype(BF16), pick_row(layers - 1, layers), None)
-        + placed(prev_last[modes:].astype(BF16), pick_row(0, layers), None),
-        levels,
-    ).reshape(planes, rows, layers)
+    def placed(pack, values):
+        return lax.dot_general(
+            pack, values, TN, precision=PRECISE, preferred_element_type=F32
+        ).reshape(planes, rows, layers)
+
+    ends = placed(picked[0], jnp.where(at_top, ahead_column, 0.0)) + placed(
+        picked[1], jnp.where(at_bottom, behind_column, 0.0)
+    )
 
     def add_mode(j, carry):
         fields, near, last = list(carry[0]), carry[1], carry[2]
@@ -400,28 +428,18 @@
     outer_field[pl.ds(pl.multiple_of((1 - side) * half, half), half), :] = last
     outside = (field[2], jnp.where(at_edge, 0.0, outer_field[...]))
     faces = (inner_face[...], outer_face[...])
-    row = lax.broadcasted_iota(jnp.int32, (rows, layers), 0)
-    lane = lax.broadcasted_iota(jnp.int32, (rows, layers), 1)
     for x in range(2):
         f = field[x]
-        c = weights[5 + x]
-        end_field = ends_ref[held[x]]
-        end_weight = harmonic(c, jnp.where(side == x, end_coef[1], end_coef[0]))
-        up_y, up_z = weights[1 + x], weights[3 + x]
-        down_y = jnp.where(row == 0, c, pltpu.roll(up_y, 1, 0))
-        down_z = jnp.where(lane == 0, end_weight, pltpu.roll(up_z, 1, 1))
-        up_z = jnp.where(lane == layers - 1, end_weight, up_z)
-        above_y = jnp.where(row == rows - 1, 0.0, pltpu.roll(f, rows - 1, 0))
-        below_y = jnp.where(row == 0, 0.0, pltpu.roll(f, 1, 0))
-        above_z = jnp.where(lane == layers - 1, end_field, pltpu.roll(f, layers - 1, 1))
-        below_z = jnp.where(lane == 0, end_field, pltpu.roll(f, 1, 1))
+        end_field = jnp.where(side == x, ends[1], ends[0])
         image = (
-            weights[0] * (f - field[1 - x])
-            + faces[x] * (f - outside[x])
-            + down_y * (f - below_y)
-            + up_y * (f - above_y)
-            + down_z * (f - below_z)
-            + up_z * (f - above_z)
+            terms[x, 0] * f
+            - middle[0] * field[1 - x]
+            - faces[x] * outside[x]
+            - terms[x, 1] * pltpu.roll(f, 1, 0)
+            - terms[x, 2] * pltpu.roll(f, rows - 1, 0)
+            - terms[x, 3] * pltpu.roll(f, 1, 1)
+            - terms[x, 4] * pltpu.roll(f, layers - 1, 1)
+            - terms[x, 5] * end_field
         )
         deflated[held[x]] = resid[held[x]] - image
 
@@ -435,11 +453,24 @@
     return lax.ppermute(value, axis, pairs)
 
 
-def swapped_open(value, axis):
+def swapped_open(value):
     pairs = []
-    for i in range(1, lax.axis_size(axis) - 1):
+    for i in range(1, lax.axis_size("pln") - 1):
         pairs.append((i, i + 1 if i % 2 else i - 1))
-    return lax.ppermute(value, axis, pairs)
+    return lax.ppermute(value, "pln", pairs)
+
+
+def swapped_all(value):
+    subs, count = lax.axis_size("sub"), lax.axis_size("pln")
+    pairs = []
+    for s in range(subs):
+        for i in range(count):
+            if 0 < i < count - 1:
+                to = (s, i + 1 if i % 2 else i - 1)
+            else:
+                to = (s ^ 1, i)
+            pairs.append((s * count + i, to[0] * count + to[1]))
+    return lax.ppermute(value, ("sub", "pln"), pairs)
 
 
 def exchanged(value, axis, mask):
@@ -470,7 +501,7 @@
         [pltpu.VMEM(labels.shape, jnp.int32), pltpu.SemaphoreType.DMA, pltpu.SemaphoreType.DMA((2,))],
         moved=2 << 20,
     )(place, *(pltpu.with_memory_space_constraint(v, pltpu.HBM) for v in (labels, zvec)))
-    outer_got = swapped_open(outer_near, "pln")
+    outer_got = swapped_all(outer_near)
     inner_got = swapped(inner_send, "pln", 0)
     rest = shape((modes, half, layers), BF16)
     here, outer_rest, one_pack, two_pack = call(
@@ -484,7 +515,6 @@
     two_got = swapped(two_pack, "sub", 1)
     field = (planes, rows, layers)
     plane = (rows, layers)
-    block_shape = shape((modes + 8, 2 * modes), F32)
     partial, weights = call(
         block_kernel,
         [shape((modes + 8, modes), F32), shape((7,) + plane, F32)],
@@ -494,22 +524,22 @@
         moved=3 << 20,
     )(place, levels, labels, resid, here)
     turned = pltpu.VMEM((half, modes, layers), BF16)
-    block, inner_face = call(
+    partial, inner_face = call(
         inner_kernel,
-        [block_shape, shape(plane, F32)],
-        [SMEM, SMEM] + [VMEM] * 8,
+        [shape((modes + 8, modes), F32), shape(plane, F32)],
+        [SMEM, SMEM] + [VMEM] * 4,
         [turned],
         flops=100_000_000,
         moved=1 << 20,
-    )(place, levels, partial, weights, here, inner_got, one_pack, two_pack, one_got, two_got)
+    )(place, levels, partial, weights, here, inner_got)
     block, outer_face = call(
         outer_kernel,
-        [block_shape, shape(plane, F32)],
-        [SMEM, SMEM] + [VMEM] * 4,
+        [shape((modes + 8, 2 * modes), F32), shape(plane, F32)],
+        [SMEM, SMEM] + [VMEM] * 8,
         [turned, pltpu.VMEM(plane, F32)],
         flops=100_000_000,
         moved=1 << 20,
-    )(place, levels, block, weights, here, outer_got)
+    )(place, levels, partial, weights, here, outer_got, one_pack, two_pack, one_got, two_got)
     packed = shape((modes + 16, 2 * modes), BF16)
     if parts == 4:
         others = [exchanged(block, "pln", mask) for mask in (1, 2, 3)]
@@ -520,26 +550,33 @@
         sum_kernel, [packed, rest], [VMEM] * 4 + [ANY], aliases={4: 1}
     )(block, *others, outer_rest)
     blocks = gathered(packed, "sub")
-    outer_last = swapped_open(outer_rest, "pln")
+    outer_last = swapped_open(outer_rest)
+    terms, picked = call(
+        terms_kernel,
+        [shape((planes, 6) + plane, F32), shape((2, modes, planes * rows), F32)],
+        [SMEM, SMEM, ANY] + [VMEM] * 5,
+        [pltpu.VMEM(field, F32)],
+        flops=1_000_000,
+        moved=64 << 20,
+    )(place, levels, blocks[0], one_got, two_got, weights, inner_face, outer_face)
     return tuple(
         call(
             finish_kernel,
             [shape((1, modes), F32), shape(field, F32)],
-            [SMEM, SMEM] + [VMEM] * (10 + len(blocks)),
+            [SMEM] + [VMEM] * (10 + len(blocks)),
             [
                 pltpu.VMEM((subs, 2 * modes), F32),
                 pltpu.VMEM((subs, 2 * modes), F32),
                 pltpu.VMEM((modes, 128), F32),
                 pltpu.VMEM((modes, layers), F32),
                 pltpu.VMEM(plane, F32),
-                pltpu.VMEM(field, F32),
                 pltpu.VMEM((subs, 2 * modes), F32),
             ],
             flops=10_000_000,
             moved=5 << 20,
         )(
-            place, levels, *blocks, zvec, inner_got, outer_got, outer_last, one_got, two_got, weights,
-            inner_face, outer_face, resid,
+            place, *blocks, zvec, inner_got, outer_got, outer_last, picked, terms, weights, inner_face,
+            outer_face, resid,
         )
     )
 

time: 41.2 us -> 39.5 us (0.959)
  waiting for transfers between devices: 9.92 us -> 8.6 us
  starting transfers between devices: 16.5 us -> 15.3 us
  Pallas kernels: 13.9 us -> 14.6 us
    ppermute x7, starting transfers between devices: 8.42 us -> 6.38 us  [exchanged(): lax.ppermute(value, axis, [(i, i ^ mask) for i in range(lax.axis_size(axi...]
    ppermute x2, starting transfers between devices: 1.38 us -> 3.29 us  [the longest x1 2.59 us: swapped_all(): return lax.ppermute(value, ('sub', 'pln'), pairs)]
    ppermute x7, waiting for transfers between devices: 9.88 us -> 8.58 us  [exchanged(): lax.ppermute(value, axis, [(i, i ^ mask) for i in range(lax.axis_size(axi...]
    ppermute x3, starting transfers between devices: 6.66 us -> 5.64 us  [swapped(): return lax.ppermute(value, axis, pairs)]
    pallas_call x3 -> x4, Pallas kernels: 6.73 us -> 7.43 us  [the longest x1 3.54 us: body(): call(finish_kernel, [shape((1, modes), F32), shape(field, F32)], [SMEM] +...]
  transfers between devices with their start and end apart: 12 -> 12, of which waited for: 4 -> 5; matrix products, arithmetic and copies ran while one was open for 0% -> 0% of each run, Pallas kernels for 16% -> 18%
where the time goes in v3:
time: 39.5 us; the launch traced here: 39.3 us
  starting transfers between devices  15.3 us (39%)
  Pallas kernels  14.6 us (37%)
  waiting for transfers between devices  8.6 us (22%)
  between operations  0.73 us (2%)
    ppermute x7, waiting for transfers between devices, exchanged(): lax.ppermute(value, axis, [(i, i ^ mask) for i in range(lax.axis_size(axi...  8.58 us
    ppermute x7, starting transfers between devices, exchanged(): lax.ppermute(value, axis, [(i, i ^ mask) for i in range(lax.axis_size(axi...  6.38 us
    ppermute x3, starting transfers between devices, swapped(): return lax.ppermute(value, axis, pairs)  5.64 us
    pallas_call x1, Pallas kernels, body(): call(finish_kernel, [shape((1, modes), F32), shape(field, F32)], [SMEM] +...  3.54 us
    pallas_call x1, Pallas kernels, body(): call(block_kernel, [shape((modes + 8, modes), F32), shape((7,) + plane, F...  3.06 us
    ppermute x1, starting transfers between devices, swapped_all(): return lax.ppermute(value, ('sub', 'pln'), pairs)  2.59 us
    pallas_call x1, Pallas kernels, body(): call(stage_kernel, [shape((modes + 1, rows, layers), BF16), shape((modes...  2.03 us
    pallas_call x1, Pallas kernels, body(): call(prepare_kernel, [shape((planes, rows, modes, layers), BF16), rest, p...  2 us
  transfers between devices with their start and end apart: 12, of which 5 were waited for; matrix products, arithmetic and copies ran while one was open for 0% of the time, Pallas kernels for 18%

profile of v3, /device:TPU:0, one launch (start us, length us, event | category | flops | bytes accessed | tf_op | source)
XLA Modules:
  0.0 39.3 jit_solution(4756491953599425676)
XLA Ops:
  0.6 0.0 copy-start
  0.6 0.0 copy-start.1
  0.7 0.1 pad_add_fusion.place
  0.7 2.0 %shard_map.61 = (bf16[65,64,128]{2,1,0:T(8,128)(2,1)S(1)}, bf16[66,32,128]{2,1,0:T(8,128)(2,1)S(1)}) custom-call(s32[4]{0:T(128)S(1)} %pad_add_fusion.place, s32[2,64,128]{2,1,0:T(8,128)} %labels_far.1, bf16[64,2,64,128]{3,2,1,0:T(8,128)(2,1)} %refs_4_.1), custom_call_target="tpu_custom_call" | custom-call | bytes 2097152 | tf_op jit(solution)/shard_map/pallas_call | solution.py:497
  2.8 0.5 %collective-permute-start = (bf16[65,64,128]{2,1,0:T(8,128)(2,1)S(1)}, bf16[65,64,128]{2,1,0:T(8,128)(2,1)S(1)}, u32[]{:S(2)}, u32[]{:S(2)}) collective-permute-start(bf16[65,64,128]{2,1,0:T(8,128)(2,1)S(1)} %get-tuple-element.21), channel_id=1, source_target_pairs={{0,1},{1,0},{2,3},{3,2},{4,5},{5,4},{6,7},{7,6},{8,9},{9,8},{10,11... | collective-permute-start | bytes 3194888 | tf_op jit(solution)/shard_map/ppermute | solution.py:453
  3.3 2.6 %collective-permute-start.1 = (bf16[66,32,128]{2,1,0:T(8,128)(2,1)S(1)}, bf16[66,32,128]{2,1,0:T(8,128)(2,1)S(1)}, u32[]{:S(2)}, u32[]{:S(2)}) collective-permute-start(bf16[66,32,128]{2,1,0:T(8,128)(2,1)S(1)} %get-tuple-element.23), channel_id=1, source_target_pairs={{0,4},{1,2},{2,1},{3,7},{4,0},{5,6},{6,5},{7,3},{8,12},{9,10},{10,... | collective-permute-start | bytes 1622024 | tf_op jit(solution)/shard_map/ppermute | solution.py:473
  5.9 2.0 %shard_map.59 = (bf16[2,64,64,128]{3,2,1,0:T(8,128)(2,1)S(1)}, bf16[64,32,128]{2,1,0:T(8,128)(2,1)S(1)}, bf16[80,128]{1,0:T(8,128)(2,1)S(1)}, bf16[80,128]{1,0:T(8,128)(2,1)S(1)}) custom-call(s32[4]{0:T(128)S(1)} %pad_add_fusion.place, s32[2,64,128]{2,1,0:T(8,128)S(1)} %copy-done.1, bf16[64,2,64,128]{3,2,1,0:T(8,128)(2,1)S(1)} %copy-done), custom_call_target="tpu_custom_call" | custom-call | flops 10000000 | bytes 6291456 | tf_op jit(solution)/shard_map/pallas_call | solution.py:507
  7.9 0.1 collective-permute-start.2
  8.0 5.0 %collective-permute-start.3 = (bf16[80,128]{1,0:T(8,128)(2,1)S(1)}, bf16[80,128]{1,0:T(8,128)(2,1)S(1)}, u32[]{:S(2)}, u32[]{:S(2)}) collective-permute-start(bf16[80,128]{1,0:T(8,128)(2,1)S(1)} %get-tuple-element.25.two_pack), channel_id=1, source_target_pairs={{0,28},{4,8},{8,4},{12,16},{16,12},{20,24},{24,20},{28,0},{1,29},{... | collective-permute-start | bytes 61448 | tf_op jit(solution)/shard_map/ppermute | solution.py:453
  13.0 3.1 %shard_map.60 = (f32[72,64]{1,0:T(8,128)S(1)}, f32[7,64,128]{2,1,0:T(8,128)S(1)}) custom-call(s32[4]{0:T(128)S(1)} %pad_add_fusion.place, f32[4]{0:T(128)S(1)} %copy-done.3, s32[2,64,128]{2,1,0:T(8,128)S(1)} %copy-done.1, f32[2,64,128]{2,1,0:T(8,128)S(1)} %copy-done.2, bf16[2,64,64,128]{3,2,1,0:T(8,128)(2,1)S(1)} %get-tuple-element.18.here), custom_call_target="tpu_custom_call" | custom-call | flops 400000000 | bytes 3145728 | tf_op jit(solution)/shard_map/pallas_call | solution.py:518
  16.1 0.0 collective-permute-done.inner_got.refs_5_
  16.1 1.4 %shard_map.62 = (f32[72,64]{1,0:T(8,128)S(1)}, f32[64,128]{1,0:T(8,128)S(1)}) custom-call(s32[4]{0:T(128)S(1)} %pad_add_fusion.place, f32[4]{0:T(128)S(1)} %copy-done.3, f32[72,64]{1,0:T(8,128)S(1)} %get-tuple-element.19.partial, f32[7,64,128]{2,1,0:T(8,128)S(1)} %get-tuple-element.20.weights.refs_10_, bf16[2,64,64,128]{3,2,1,0:T(8,128)(2,1)S(1)} %get-tuple-element.18.here, ...), custom_call_target="tpu_custom_call" | custom-call | flops 100000000 | bytes 1048576 | tf_op jit(solution)/shard_map/pallas_call | solution.py:527
  17.5 0.0 collective-permute-done.2.one_got
  17.5 0.0 collective-permute-done.1.outer_got.refs_6_
  17.5 1.7 %shard_map.63 = (f32[72,128]{1,0:T(8,128)S(1)}, f32[64,128]{1,0:T(8,128)S(1)}) custom-call(s32[4]{0:T(128)S(1)} %pad_add_fusion.place, f32[4]{0:T(128)S(1)} %copy-done.3, f32[72,64]{1,0:T(8,128)S(1)} %get-tuple-element.22.partial, f32[7,64,128]{2,1,0:T(8,128)S(1)} %get-tuple-element.20.weights.refs_10_, bf16[2,64,64,128]{3,2,1,0:T(8,128)(2,1)S(1)} %get-tuple-element.18.here, ...), custom_call_target="tpu_custom_call" | custom-call | flops 100000000 | bytes 1048576 | tf_op jit(solution)/shard_map/pallas_call | solution.py:535
  19.2 0.7 %collective-permute-start.6 = (f32[72,128]{1,0:T(8,128)S(1)}, f32[72,128]{1,0:T(8,128)S(1)}, u32[]{:S(2)}, u32[]{:S(2)}) collective-permute-start(f32[72,128]{1,0:T(8,128)S(1)} %get-tuple-element.26.own), channel_id=1, source_target_pairs={{0,3},{1,2},{2,1},{3,0},{4,7},{5,6},{6,5},{7,4},{8,11},{9,10},{10,... | collective-permute-start | bytes 110600 | tf_op jit(solution)/shard_map/ppermute | solution.py:477
  20.0 0.5 %collective-permute-start.5 = (f32[72,128]{1,0:T(8,128)S(1)}, f32[72,128]{1,0:T(8,128)S(1)}, u32[]{:S(2)}, u32[]{:S(2)}) collective-permute-start(f32[72,128]{1,0:T(8,128)S(1)} %get-tuple-element.26.own), channel_id=1, source_target_pairs={{0,2},{1,3},{2,0},{3,1},{4,6},{5,7},{6,4},{7,5},{8,10},{9,11},{10,... | collective-permute-start | bytes 110600 | tf_op jit(solution)/shard_map/ppermute | solution.py:477
  20.4 0.7 %collective-permute-start.4 = (f32[72,128]{1,0:T(8,128)S(1)}, f32[72,128]{1,0:T(8,128)S(1)}, u32[]{:S(2)}, u32[]{:S(2)}) collective-permute-start(f32[72,128]{1,0:T(8,128)S(1)} %get-tuple-element.26.own), channel_id=1, source_target_pairs={{0,1},{1,0},{2,3},{3,2},{4,5},{5,4},{6,7},{7,6},{8,9},{9,8},{10,11... | collective-permute-start | bytes 110600 | tf_op jit(solution)/shard_map/ppermute | solution.py:477
  21.2 1.6 %collective-permute-done.6.three = f32[72,128]{1,0:T(8,128)S(1)} collective-permute-done((f32[72,128]{1,0:T(8,128)S(1)}, f32[72,128]{1,0:T(8,128)S(1)}, u32[]{:S(2)}, u32[]{:S(2)}) %collective-permute-start.6) | collective-permute-done | bytes 36896 | tf_op jit(solution)/shard_map/ppermute | solution.py:477
  22.8 1.2 %collective-permute-done.5.two = f32[72,128]{1,0:T(8,128)S(1)} collective-permute-done((f32[72,128]{1,0:T(8,128)S(1)}, f32[72,128]{1,0:T(8,128)S(1)}, u32[]{:S(2)}, u32[]{:S(2)}) %collective-permute-start.5) | collective-permute-done | bytes 36896 | tf_op jit(solution)/shard_map/ppermute | solution.py:477
  23.9 0.0 collective-permute-done.4.one
  24.0 0.7 %collective-permute-start.11 = (bf16[64,32,128]{2,1,0:T(8,128)(2,1)S(1)}, bf16[64,32,128]{2,1,0:T(8,128)(2,1)S(1)}, u32[]{:S(2)}, u32[]{:S(2)}) collective-permute-start(bf16[64,32,128]{2,1,0:T(8,128)(2,1)S(1)} %get-tuple-element.29), channel_id=1, source_target_pairs={{1,2},{2,1},{5,6},{6,5},{9,10},{10,9},{13,14},{14,13},{17,18},{18,... | collective-permute-start | bytes 1572872 | tf_op jit(solution)/shard_map/ppermute | solution.py:460
  24.7 0.1 collective-permute-start.7
  24.7 3.8 %collective-permute-done.7 = bf16[80,128]{1,0:T(8,128)(2,1)S(1)} collective-permute-done((bf16[80,128]{1,0:T(8,128)(2,1)S(1)}, bf16[80,128]{1,0:T(8,128)(2,1)S(1)}, u32[]{:S(2)}, u32[]{:S(2)}) %collective-permute-start.7) | collective-permute-done | bytes 20512 | tf_op jit(solution)/shard_map/ppermute | solution.py:477
  28.5 0.5 %collective-permute-start.10 = (bf16[2,80,128]{2,1,0:T(8,128)(2,1)S(1)}, bf16[2,80,128]{2,1,0:T(8,128)(2,1)S(1)}, u32[]{:S(2)}, u32[]{:S(2)}) collective-permute-start(bf16[2,80,128]{2,1,0:T(8,128)(2,1)S(1)} %pad_maximum_fusion.pair.refs_0_), channel_id=1, source_target_pairs={{0,24},{4,28},{8,16},{12,20},{16,8},{20,12},{24,0},{28,4},{1,25},{... | collective-permute-start | bytes 122888 | tf_op jit(solution)/shard_map/ppermute | solution.py:477
  29.0 0.0 collective-permute-start.9
  29.0 3.9 %collective-permute-start.8 = (bf16[2,80,128]{2,1,0:T(8,128)(2,1)S(1)}, bf16[2,80,128]{2,1,0:T(8,128)(2,1)S(1)}, u32[]{:S(2)}, u32[]{:S(2)}) collective-permute-start(bf16[2,80,128]{2,1,0:T(8,128)(2,1)S(1)} %pad_maximum_fusion.pair.refs_0_), channel_id=1, source_target_pairs={{0,8},{4,12},{8,0},{12,4},{16,24},{20,28},{24,16},{28,20},{1,9},{5... | collective-permute-start | bytes 122888 | tf_op jit(solution)/shard_map/ppermute | solution.py:477
  32.9 0.8 %shard_map.65 = (f32[2,6,64,128]{3,2,1,0:T(8,128)S(1)}, f32[2,64,128]{2,1,0:T(8,128)S(1)}) custom-call(s32[4]{0:T(128)S(1)} %pad_add_fusion.place, f32[4]{0:T(128)S(1)} %copy-done.3, bf16[2,80,128]{2,1,0:T(8,128)(2,1)S(1)} %pad_maximum_fusion.pair.refs_0_, bf16[80,128]{1,0:T(8,128)(2,1)S(1)} %collective-permute-done.2.one_got, ...), custom_call_target="tpu_custom_call" | custom-call | flops 1000000 | bytes 67108864 | tf_op jit(solution)/shard_map/pallas_call | solution.py:554
  33.7 1.1 %collective-permute-done.10.refs_3_ = bf16[2,80,128]{2,1,0:T(8,128)(2,1)S(1)} collective-permute-done((bf16[2,80,128]{2,1,0:T(8,128)(2,1)S(1)}, bf16[2,80,128]{2,1,0:T(8,128)(2,1)S(1)}, u32[]{:S(2)}, u32[]{:S(2)}) %collective-permute-start.10) | collective-permute-done | bytes 40992 | tf_op jit(solution)/shard_map/ppermute | solution.py:477
  34.9 0.9 %collective-permute-done.9.refs_2_ = bf16[2,80,128]{2,1,0:T(8,128)(2,1)S(1)} collective-permute-done((bf16[2,80,128]{2,1,0:T(8,128)(2,1)S(1)}, bf16[2,80,128]{2,1,0:T(8,128)(2,1)S(1)}, u32[]{:S(2)}, u32[]{:S(2)}) %collective-permute-start.9) | collective-permute-done | bytes 40992 | tf_op jit(solution)/shard_map/ppermute | solution.py:477
  35.8 0.0 collective-permute-done.8.refs_1_
  35.8 3.5 %shard_map.66 = (f32[1,64]{1,0:T(1,128)}, f32[2,64,128]{2,1,0:T(8,128)}) custom-call(s32[4]{0:T(128)S(1)} %pad_add_fusion.place, bf16[2,80,128]{2,1,0:T(8,128)(2,1)S(1)} %pad_maximum_fusion.pair.refs_0_, bf16[2,80,128]{2,1,0:T(8,128)(2,1)S(1)} %collective-permute-done.8.refs_1_, bf16[2,80,128]{2,1,0:T(8,128)(2,1)S(1)} %collective-permute-done.9.refs_2_, ...), custom_call_target="tpu_custom_call" | custom-call | flops 10000000 | bytes 5242880 | tf_op jit(solution)/shard_map/pallas_call | solution.py:563
  (10 shorter events, 0.1 us)
Async XLA Ops:
  0.6 5.3 %copy-start = (bf16[64,2,64,128]{3,2,1,0:T(8,128)(2,1)S(1)}, bf16[64,2,64,128]{3,2,1,0:T(8,128)(2,1)}, u32[]{:S(2)}) copy-start(bf16[64,2,64,128]{3,2,1,0:T(8,128)(2,1)} %refs_4_.1) | copy-start | bytes 6291460
  0.6 5.3 %copy-start.1 = (s32[2,64,128]{2,1,0:T(8,128)S(1)}, s32[2,64,128]{2,1,0:T(8,128)}, u32[]{:S(2)}) copy-start(s32[2,64,128]{2,1,0:T(8,128)} %labels_far.1) | copy-start | bytes 196612
  0.7 12.3 %copy-start.2 = (f32[2,64,128]{2,1,0:T(8,128)S(1)}, f32[2,64,128]{2,1,0:T(8,128)}, u32[]{:S(2)}) copy-start(f32[2,64,128]{2,1,0:T(8,128)} %refs_13_.1) | copy-start | bytes 196612
  0.7 12.3 %copy-start.3 = (f32[4]{0:T(128)S(1)}, f32[4]{0:T(128)}, u32[]{:S(2)}) copy-start(f32[4]{0:T(128)} %levels.7) | copy-start | bytes 52
  2.8 13.3 %collective-permute-start = (bf16[65,64,128]{2,1,0:T(8,128)(2,1)S(1)}, bf16[65,64,128]{2,1,0:T(8,128)(2,1)S(1)}, u32[]{:S(2)}, u32[]{:S(2)}) collective-permute-start(bf16[65,64,128]{2,1,0:T(8,128)(2,1)S(1)} %get-tuple-element.21), channel_id=1, source_target_pairs={{0,1},{1,0},{2,3},{3,2},{4,5},{5,4},{6,7},{7,6},{8,9},{9,8},{10,11... | collective-permute-start | bytes 3194888 | tf_op jit(solution)/shard_map/ppermute | solution.py:453
  3.3 14.2 %collective-permute-start.1 = (bf16[66,32,128]{2,1,0:T(8,128)(2,1)S(1)}, bf16[66,32,128]{2,1,0:T(8,128)(2,1)S(1)}, u32[]{:S(2)}, u32[]{:S(2)}) collective-permute-start(bf16[66,32,128]{2,1,0:T(8,128)(2,1)S(1)} %get-tuple-element.23), channel_id=1, source_target_pairs={{0,4},{1,2},{2,1},{3,7},{4,0},{5,6},{6,5},{7,3},{8,12},{9,10},{10,... | collective-permute-start | bytes 1622024 | tf_op jit(solution)/shard_map/ppermute | solution.py:473
  7.9 9.6 %collective-permute-start.2 = (bf16[80,128]{1,0:T(8,128)(2,1)S(1)}, bf16[80,128]{1,0:T(8,128)(2,1)S(1)}, u32[]{:S(2)}, u32[]{:S(2)}) collective-permute-start(bf16[80,128]{1,0:T(8,128)(2,1)S(1)} %get-tuple-element.24.one_pack), channel_id=1, source_target_pairs={{0,4},{4,0},{8,12},{12,8},{16,20},{20,16},{24,28},{28,24},{1,5},{5... | collective-permute-start | bytes 61448 | tf_op jit(solution)/shard_map/ppermute | solution.py:453
  8.0 9.5 %collective-permute-start.3 = (bf16[80,128]{1,0:T(8,128)(2,1)S(1)}, bf16[80,128]{1,0:T(8,128)(2,1)S(1)}, u32[]{:S(2)}, u32[]{:S(2)}) collective-permute-start(bf16[80,128]{1,0:T(8,128)(2,1)S(1)} %get-tuple-element.25.two_pack), channel_id=1, source_target_pairs={{0,28},{4,8},{8,4},{12,16},{16,12},{20,24},{24,20},{28,0},{1,29},{... | collective-permute-start | bytes 61448 | tf_op jit(solution)/shard_map/ppermute | solution.py:453
  19.2 3.5 %collective-permute-start.6 = (f32[72,128]{1,0:T(8,128)S(1)}, f32[72,128]{1,0:T(8,128)S(1)}, u32[]{:S(2)}, u32[]{:S(2)}) collective-permute-start(f32[72,128]{1,0:T(8,128)S(1)} %get-tuple-element.26.own), channel_id=1, source_target_pairs={{0,3},{1,2},{2,1},{3,0},{4,7},{5,6},{6,5},{7,4},{8,11},{9,10},{10,... | collective-permute-start | bytes 110600 | tf_op jit(solution)/shard_map/ppermute | solution.py:477
  20.0 4.0 %collective-permute-start.5 = (f32[72,128]{1,0:T(8,128)S(1)}, f32[72,128]{1,0:T(8,128)S(1)}, u32[]{:S(2)}, u32[]{:S(2)}) collective-permute-start(f32[72,128]{1,0:T(8,128)S(1)} %get-tuple-element.26.own), channel_id=1, source_target_pairs={{0,2},{1,3},{2,0},{3,1},{4,6},{5,7},{6,4},{7,5},{8,10},{9,11},{10,... | collective-permute-start | bytes 110600 | tf_op jit(solution)/shard_map/ppermute | solution.py:477
  20.4 3.5 %collective-permute-start.4 = (f32[72,128]{1,0:T(8,128)S(1)}, f32[72,128]{1,0:T(8,128)S(1)}, u32[]{:S(2)}, u32[]{:S(2)}) collective-permute-start(f32[72,128]{1,0:T(8,128)S(1)} %get-tuple-element.26.own), channel_id=1, source_target_pairs={{0,1},{1,0},{2,3},{3,2},{4,5},{5,4},{6,7},{7,6},{8,9},{9,8},{10,11... | collective-permute-start | bytes 110600 | tf_op jit(solution)/shard_map/ppermute | solution.py:477
  24.0 11.8 %collective-permute-start.11 = (bf16[64,32,128]{2,1,0:T(8,128)(2,1)S(1)}, bf16[64,32,128]{2,1,0:T(8,128)(2,1)S(1)}, u32[]{:S(2)}, u32[]{:S(2)}) collective-permute-start(bf16[64,32,128]{2,1,0:T(8,128)(2,1)S(1)} %get-tuple-element.29), channel_id=1, source_target_pairs={{1,2},{2,1},{5,6},{6,5},{9,10},{10,9},{13,14},{14,13},{17,18},{18,... | collective-permute-start | bytes 1572872 | tf_op jit(solution)/shard_map/ppermute | solution.py:460
  24.7 3.8 %collective-permute-start.7 = (bf16[80,128]{1,0:T(8,128)(2,1)S(1)}, bf16[80,128]{1,0:T(8,128)(2,1)S(1)}, u32[]{:S(2)}, u32[]{:S(2)}) collective-permute-start(bf16[80,128]{1,0:T(8,128)(2,1)S(1)} %get-tuple-element.28), channel_id=1, source_target_pairs={{0,4},{4,0},{8,12},{12,8},{16,20},{20,16},{24,28},{28,24},{1,5},{5... | collective-permute-start | bytes 61448 | tf_op jit(solution)/shard_map/ppermute | solution.py:477
  28.5 6.3 %collective-permute-start.10 = (bf16[2,80,128]{2,1,0:T(8,128)(2,1)S(1)}, bf16[2,80,128]{2,1,0:T(8,128)(2,1)S(1)}, u32[]{:S(2)}, u32[]{:S(2)}) collective-permute-start(bf16[2,80,128]{2,1,0:T(8,128)(2,1)S(1)} %pad_maximum_fusion.pair.refs_0_), channel_id=1, source_target_pairs={{0,24},{4,28},{8,16},{12,20},{16,8},{20,12},{24,0},{28,4},{1,25},{... | collective-permute-start | bytes 122888 | tf_op jit(solution)/shard_map/ppermute | solution.py:477
  29.0 6.8 %collective-permute-start.9 = (bf16[2,80,128]{2,1,0:T(8,128)(2,1)S(1)}, bf16[2,80,128]{2,1,0:T(8,128)(2,1)S(1)}, u32[]{:S(2)}, u32[]{:S(2)}) collective-permute-start(bf16[2,80,128]{2,1,0:T(8,128)(2,1)S(1)} %pad_maximum_fusion.pair.refs_0_), channel_id=1, source_target_pairs={{0,16},{4,20},{8,24},{12,28},{16,0},{20,4},{24,8},{28,12},{1,17},{... | collective-permute-start | bytes 122888 | tf_op jit(solution)/shard_map/ppermute | solution.py:477
  29.0 6.8 %collective-permute-start.8 = (bf16[2,80,128]{2,1,0:T(8,128)(2,1)S(1)}, bf16[2,80,128]{2,1,0:T(8,128)(2,1)S(1)}, u32[]{:S(2)}, u32[]{:S(2)}) collective-permute-start(bf16[2,80,128]{2,1,0:T(8,128)(2,1)S(1)} %pad_maximum_fusion.pair.refs_0_), channel_id=1, source_target_pairs={{0,8},{4,12},{8,0},{12,4},{16,24},{20,28},{24,16},{28,20},{1,9},{5... | collective-permute-start | bytes 122888 | tf_op jit(solution)/shard_map/ppermute | solution.py:477

commit v4 on v3

--- a/solution.py
+++ b/solution.py
@@ -53,29 +53,34 @@
     return ((row == 0) & lane_is((16, width), lane)).astype(BF16)
 
 
-def stage_kernel(place, labels_far, zvec, inner_send, outer_near, labels, label_sem, sems):
+def stage_kernel(place, labels_far, zvec, outer_near, labels, label_sem, sem):
     modes, planes, rows, layers = zvec.shape
     half = rows // 2
     side = lax.rem(place[1], 2)
     start = pl.multiple_of((1 - side) * half, half)
     label_copy = pltpu.make_async_copy(labels_far, labels, label_sem)
-    copies = [
-        pltpu.make_async_copy(
-            zvec.at[:, side, pl.ds(start, half), :], outer_near.at[pl.ds(0, modes)], sems.at[0]
-        ),
-        pltpu.make_async_copy(zvec.at[:, 1 - side], inner_send.at[pl.ds(0, modes)], sems.at[1]),
-    ]
+    copy = pltpu.make_async_copy(
+        zvec.at[:, side, pl.ds(start, half), :], outer_near.at[pl.ds(0, modes)], sem
+    )
+    copy.start()
     label_copy.start()
-    for copy in copies:
-        copy.start()
     label_copy.wait()
     outer_near[modes:] = labels[side].astype(F32).astype(BF16).reshape(rows // half, half, layers)
+    copy.wait()
+
+
+def plane_kernel(place, labels, held, staged, inner_send):
+    modes = held.shape[0]
+    side = lax.rem(place[1], 2)
+    inner_send[:modes] = held[:, 1 - side]
     inner_send[modes] = labels[1 - side].astype(F32).astype(BF16)
-    for copy in copies:
-        copy.wait()
-
-
-def prepare_kernel(place, labels, held, planes_out, outer_rest, one_pack, two_pack):
+
+
+def release_kernel(after, outer_rest, outer_out):
+    pass
+
+
+def prepare_kernel(place, labels, held, staged, planes_out, outer_rest, one_pack, two_pack):
     modes, planes, rows, layers = held.shape
     half = rows // 2
     width = planes * rows
@@ -290,7 +295,7 @@
         terms[x, 5] = end_weight
 
 
-def sum_kernel(own, one, two, three, outer_rest, out, outer_out):
+def sum_kernel(own, one, two, three, out):
     modes = own.shape[1] // 2
     total = (own[...] + one[...]) + (two[...] + three[...])
     encode(total, modes, out)
@@ -320,10 +325,10 @@
 
 
 def finish_kernel(place, *refs):
-    count = len(refs) - 18
+    count = len(refs) - 17
     blocks, refs = refs[:count], refs[count:]
     zvec, inner_got, outer_got, outer_last, picked, terms, middle, inner_face, outer_face, resid = refs[:10]
-    solution, deflated, direction_ref, image_ref, ahead_ref, spread, outer_field, fix_ref = refs[10:]
+    solution, deflated, direction_ref, image_ref, spread, outer_field, fix_ref = refs[10:]
     subs = direction_ref.shape[0]
     modes, planes, rows, layers = zvec.shape
     half = rows // 2
@@ -339,21 +344,26 @@
     def column(row):
         return jnp.sum(jnp.where(eye, row, 0.0), axis=1, keepdims=True)
 
-    def each(body):
+    def each(body, carry):
         for index, block in enumerate(blocks):
             held_here = block.shape[0]
             if held_here <= 8:
                 for entry in range(held_here):
-                    body(block.at[entry], jnp.bitwise_xor(order, index * held_here + entry))
+                    s = jnp.bitwise_xor(order, index * held_here + entry)
+                    carry = body(block.at[entry], s, carry)
             else:
-                pl.loop(0, held_here)(lambda entry, block=block: body(block.at[entry], entry))
-
-    def load(block, s):
+                carry = lax.fori_loop(
+                    0, held_here, lambda entry, c, block=block: body(block.at[entry], entry, c), carry
+                )
+        return carry
+
+    def load(block, s, carry):
         extra = block[modes:modes + 16, :].astype(F32)
         direction_ref[pl.ds(s, 1), :] = (extra[0:1] + extra[1:2]) + extra[2:3]
         fix_ref[pl.ds(s, 1), :] = extra[4:5] - extra[3:4]
-
-    each(load)
+        return carry
+
+    each(load, 0)
     fix = fix_ref[:, :modes]
 
     def turned(rows_of, by):
@@ -363,18 +373,18 @@
     def coarse_apply(direction):
         direction_ref[...] = jnp.concatenate([direction, turned(direction, 1)], axis=1)
 
-        def one(block, s):
+        def one(block, s, carry):
             values = block[:modes, :].astype(F32)
             pair = direction_ref[pl.ds(s, 1), :]
             ahead = jnp.sum(values * pair, axis=1, keepdims=True)
-            ahead_ref[...] = jnp.where(lane_is((modes, 128), s), ahead, ahead_ref[...])
             image_ref[pl.ds(s, 1), :] = jnp.sum(
                 values * column(pair[:, :modes]), axis=0, keepdims=True
             )
-
-        each(one)
+            return jnp.where(lane_is((modes, 128), s), ahead, carry)
+
+        ahead_all = each(one, jnp.zeros((modes, 128), F32))
         image = image_ref[...]
-        square_part = ahead_ref[...].T[:subs] + image[:, :modes] + fix * direction
+        square_part = ahead_all.T[:subs] + image[:, :modes] + fix * direction
         return square_part + turned(image[:, modes:], -1)
 
     def inner(left, right):
@@ -494,23 +504,26 @@
         [jnp.int32(v) for v in (lax.axis_index("sub"), lax.axis_index("pln"), parts, order)]
     )
     pack = shape((modes + 16, planes * rows), BF16)
-    inner_send, outer_near = call(
+    [outer_near] = call(
         stage_kernel,
-        [shape((modes + 1, rows, layers), BF16), shape((modes + rows // half, half, layers), BF16)],
+        [shape((modes + rows // half, half, layers), BF16)],
         [SMEM, HBM, HBM],
-        [pltpu.VMEM(labels.shape, jnp.int32), pltpu.SemaphoreType.DMA, pltpu.SemaphoreType.DMA((2,))],
-        moved=2 << 20,
+        [pltpu.VMEM(labels.shape, jnp.int32), pltpu.SemaphoreType.DMA, pltpu.SemaphoreType.DMA],
+        moved=1 << 20,
     )(place, *(pltpu.with_memory_space_constraint(v, pltpu.HBM) for v in (labels, zvec)))
     outer_got = swapped_all(outer_near)
+    [inner_send] = call(
+        plane_kernel, [shape((modes + 1, rows, layers), BF16)], [SMEM, VMEM, VMEM, ANY], moved=2 << 20
+    )(place, labels, zvec, outer_near)
     inner_got = swapped(inner_send, "pln", 0)
     rest = shape((modes, half, layers), BF16)
     here, outer_rest, one_pack, two_pack = call(
         prepare_kernel,
         [shape((planes, rows, modes, layers), BF16), rest, pack, pack],
-        [SMEM, VMEM, VMEM],
+        [SMEM, VMEM, VMEM, ANY],
         flops=10_000_000,
         moved=6 << 20,
-    )(place, labels, zvec)
+    )(place, labels, zvec, inner_send)
     one_got = swapped(one_pack, "sub", 0)
     two_got = swapped(two_pack, "sub", 1)
     field = (planes, rows, layers)
@@ -546,9 +559,8 @@
     else:
         block = lax.psum(block, "pln")
         others = [jnp.zeros_like(block)] * 3
-    packed, outer_rest = call(
-        sum_kernel, [packed, rest], [VMEM] * 4 + [ANY], aliases={4: 1}
-    )(block, *others, outer_rest)
+    [packed] = call(sum_kernel, [packed], [VMEM] * 4)(block, *others)
+    [outer_rest] = call(release_kernel, [rest], [ANY] * 2, aliases={1: 0})(packed, outer_rest)
     blocks = gathered(packed, "sub")
     outer_last = swapped_open(outer_rest)
     terms, picked = call(
@@ -556,8 +568,9 @@
         [shape((planes, 6) + plane, F32), shape((2, modes, planes * rows), F32)],
         [SMEM, SMEM, ANY] + [VMEM] * 5,
         [pltpu.VMEM(field, F32)],
-        flops=1_000_000,
-        moved=64 << 20,
+
+        flops=1 << 33,
+        moved=1 << 20,
     )(place, levels, blocks[0], one_got, two_got, weights, inner_face, outer_face)
     return tuple(
         call(
@@ -567,7 +580,6 @@
             [
                 pltpu.VMEM((subs, 2 * modes), F32),
                 pltpu.VMEM((subs, 2 * modes), F32),
-                pltpu.VMEM((modes, 128), F32),
                 pltpu.VMEM((modes, layers), F32),
                 pltpu.VMEM(plane, F32),
                 pltpu.VMEM((subs, 2 * modes), F32),

time: 39.5 us -> 38.3 us (0.970)
  waiting for transfers between devices: 8.6 us -> 7.11 us
    ppermute x7, waiting for transfers between devices: 8.58 us -> 7.1 us  [exchanged(): lax.ppermute(value, axis, [(i, i ^ mask) for i in range(lax.axis_size(axi...]
    pallas_call x2 -> x4, Pallas kernels: 2.06 us -> 2.32 us  [the longest x1 1.67 us: body(): call(stage_kernel, [shape((modes + rows // half, half, layers), BF16)], [...]
  transfers between devices with their start and end apart: 12 -> 12, of which waited for: 5 -> 5; matrix products, arithmetic and copies ran while one was open for 0% -> 0% of each run, Pallas kernels for 18% -> 19%
where the time goes in v4:
time: 38.3 us; the launch traced here: 38.1 us
  starting transfers between devices  15.3 us (40%)
  Pallas kernels  14.8 us (39%)
  waiting for transfers between devices  7.11 us (19%)
  between operations  0.78 us (2%)
    ppermute x7, waiting for transfers between devices, exchanged(): lax.ppermute(value, axis, [(i, i ^ mask) for i in range(lax.axis_size(axi...  7.1 us
    ppermute x7, starting transfers between devices, exchanged(): lax.ppermute(value, axis, [(i, i ^ mask) for i in range(lax.axis_size(axi...  6.38 us
    ppermute x3, starting transfers between devices, swapped(): return lax.ppermute(value, axis, pairs)  5.64 us
    pallas_call x1, Pallas kernels, body(): call(finish_kernel, [shape((1, modes), F32), shape(field, F32)], [SMEM] +...  3.53 us
    pallas_call x1, Pallas kernels, body(): call(block_kernel, [shape((modes + 8, modes), F32), shape((7,) + plane, F...  3.07 us
    ppermute x1, starting transfers between devices, swapped_all(): return lax.ppermute(value, ('sub', 'pln'), pairs)  2.59 us
    pallas_call x1, Pallas kernels, body(): call(prepare_kernel, [shape((planes, rows, modes, layers), BF16), rest, p...  2 us
    pallas_call x1, Pallas kernels, body(): call(outer_kernel, [shape((modes + 8, 2 * modes), F32), shape(plane, F32)...  1.72 us
  transfers between devices with their start and end apart: 12, of which 5 were waited for; matrix products, arithmetic and copies ran while one was open for 0% of the time, Pallas kernels for 19%

profile of v4, /device:TPU:0, one launch (start us, length us, event | category | flops | bytes accessed | tf_op | source)
XLA Modules:
  0.0 38.1 jit_solution(14608658084747909556)
XLA Ops:
  0.6 0.0 copy-start
  0.6 0.0 copy-start.1
  0.7 0.1 pad_add_fusion.place
  0.7 1.7 %shard_map.59.staged = bf16[66,32,128]{2,1,0:T(8,128)(2,1)S(1)} custom-call(s32[4]{0:T(128)S(1)} %pad_add_fusion.place, s32[2,64,128]{2,1,0:T(8,128)} %labels.5, bf16[64,2,64,128]{3,2,1,0:T(8,128)(2,1)} %refs_4_.1), custom_call_target="tpu_custom_call" | custom-call | bytes 1048576 | tf_op jit(solution)/shard_map/pallas_call | solution.py:507
  2.4 0.6 %shard_map.60.staged = bf16[65,64,128]{2,1,0:T(8,128)(2,1)S(1)} custom-call(s32[4]{0:T(128)S(1)} %pad_add_fusion.place, s32[2,64,128]{2,1,0:T(8,128)S(1)} %copy-done.1, bf16[64,2,64,128]{3,2,1,0:T(8,128)(2,1)S(1)} %copy-done, bf16[66,32,128]{2,1,0:T(8,128)(2,1)S(1)} %shard_map.59.staged), custom_call_target="tpu_custom_call" | custom-call | bytes 2097152 | tf_op jit(solution)/shard_map/pallas_call | solution.py:515
  3.1 0.0 copy-start.2
  3.1 0.0 copy-start.3
  3.1 0.5 %collective-permute-start = (bf16[65,64,128]{2,1,0:T(8,128)(2,1)S(1)}, bf16[65,64,128]{2,1,0:T(8,128)(2,1)S(1)}, u32[]{:S(2)}, u32[]{:S(2)}) collective-permute-start(bf16[65,64,128]{2,1,0:T(8,128)(2,1)S(1)} %shard_map.60.staged), channel_id=1, source_target_pairs={{0,1},{1,0},{2,3},{3,2},{4,5},{5,4},{6,7},{7,6},{8,9},{9,8},{10,11... | collective-permute-start | bytes 3194888 | tf_op jit(solution)/shard_map/ppermute | solution.py:463
  3.6 2.6 %collective-permute-start.1 = (bf16[66,32,128]{2,1,0:T(8,128)(2,1)S(1)}, bf16[66,32,128]{2,1,0:T(8,128)(2,1)S(1)}, u32[]{:S(2)}, u32[]{:S(2)}) collective-permute-start(bf16[66,32,128]{2,1,0:T(8,128)(2,1)S(1)} %shard_map.59.staged), channel_id=1, source_target_pairs={{0,4},{1,2},{2,1},{3,7},{4,0},{5,6},{6,5},{7,3},{8,12},{9,10},{10,... | collective-permute-start | bytes 1622024 | tf_op jit(solution)/shard_map/ppermute | solution.py:483
  6.2 2.0 %shard_map.61 = (bf16[2,64,64,128]{3,2,1,0:T(8,128)(2,1)S(1)}, bf16[64,32,128]{2,1,0:T(8,128)(2,1)S(1)}, bf16[80,128]{1,0:T(8,128)(2,1)S(1)}, bf16[80,128]{1,0:T(8,128)(2,1)S(1)}) custom-call(s32[4]{0:T(128)S(1)} %pad_add_fusion.place, s32[2,64,128]{2,1,0:T(8,128)S(1)} %copy-done.1, bf16[64,2,64,128]{3,2,1,0:T(8,128)(2,1)S(1)} %copy-done, ...), custom_call_target="tpu_custom_call" | custom-call | flops 10000000 | bytes 6291456 | tf_op jit(solution)/shard_map/pallas_call | solution.py:520
  8.2 0.1 collective-permute-start.2
  8.3 5.0 %collective-permute-start.3 = (bf16[80,128]{1,0:T(8,128)(2,1)S(1)}, bf16[80,128]{1,0:T(8,128)(2,1)S(1)}, u32[]{:S(2)}, u32[]{:S(2)}) collective-permute-start(bf16[80,128]{1,0:T(8,128)(2,1)S(1)} %get-tuple-element.19.two_pack), channel_id=1, source_target_pairs={{0,28},{4,8},{8,4},{12,16},{16,12},{20,24},{24,20},{28,0},{1,29},{... | collective-permute-start | bytes 61448 | tf_op jit(solution)/shard_map/ppermute | solution.py:463
  13.3 3.1 %shard_map.62 = (f32[72,64]{1,0:T(8,128)S(1)}, f32[7,64,128]{2,1,0:T(8,128)S(1)}) custom-call(s32[4]{0:T(128)S(1)} %pad_add_fusion.place, f32[4]{0:T(128)S(1)} %copy-done.3, s32[2,64,128]{2,1,0:T(8,128)S(1)} %copy-done.1, f32[2,64,128]{2,1,0:T(8,128)S(1)} %copy-done.2, bf16[2,64,64,128]{3,2,1,0:T(8,128)(2,1)S(1)} %get-tuple-element.14.here), custom_call_target="tpu_custom_call" | custom-call | flops 400000000 | bytes 3145728 | tf_op jit(solution)/shard_map/pallas_call | solution.py:531
  16.4 0.0 collective-permute-done.inner_got.refs_5_
  16.4 1.4 %shard_map.63 = (f32[72,64]{1,0:T(8,128)S(1)}, f32[64,128]{1,0:T(8,128)S(1)}) custom-call(s32[4]{0:T(128)S(1)} %pad_add_fusion.place, f32[4]{0:T(128)S(1)} %copy-done.3, f32[72,64]{1,0:T(8,128)S(1)} %get-tuple-element.15.partial, f32[7,64,128]{2,1,0:T(8,128)S(1)} %get-tuple-element.16.weights.refs_10_, bf16[2,64,64,128]{3,2,1,0:T(8,128)(2,1)S(1)} %get-tuple-element.14.here, ...), custom_call_target="tpu_custom_call" | custom-call | flops 100000000 | bytes 1048576 | tf_op jit(solution)/shard_map/pallas_call | solution.py:540
  17.8 0.0 collective-permute-done.3.two_got
  17.8 1.7 %shard_map.64 = (f32[72,128]{1,0:T(8,128)S(1)}, f32[64,128]{1,0:T(8,128)S(1)}) custom-call(s32[4]{0:T(128)S(1)} %pad_add_fusion.place, f32[4]{0:T(128)S(1)} %copy-done.3, f32[72,64]{1,0:T(8,128)S(1)} %get-tuple-element.17.partial, f32[7,64,128]{2,1,0:T(8,128)S(1)} %get-tuple-element.16.weights.refs_10_, bf16[2,64,64,128]{3,2,1,0:T(8,128)(2,1)S(1)} %get-tuple-element.14.here, ...), custom_call_target="tpu_custom_call" | custom-call | flops 100000000 | bytes 1048576 | tf_op jit(solution)/shard_map/pallas_call | solution.py:548
  19.5 0.8 %collective-permute-start.6 = (f32[72,128]{1,0:T(8,128)S(1)}, f32[72,128]{1,0:T(8,128)S(1)}, u32[]{:S(2)}, u32[]{:S(2)}) collective-permute-start(f32[72,128]{1,0:T(8,128)S(1)} %get-tuple-element.20.own), channel_id=1, source_target_pairs={{0,3},{1,2},{2,1},{3,0},{4,7},{5,6},{6,5},{7,4},{8,11},{9,10},{10,... | collective-permute-start | bytes 110600 | tf_op jit(solution)/shard_map/ppermute | solution.py:487
  20.3 0.5 %collective-permute-start.5 = (f32[72,128]{1,0:T(8,128)S(1)}, f32[72,128]{1,0:T(8,128)S(1)}, u32[]{:S(2)}, u32[]{:S(2)}) collective-permute-start(f32[72,128]{1,0:T(8,128)S(1)} %get-tuple-element.20.own), channel_id=1, source_target_pairs={{0,2},{1,3},{2,0},{3,1},{4,6},{5,7},{6,4},{7,5},{8,10},{9,11},{10,... | collective-permute-start | bytes 110600 | tf_op jit(solution)/shard_map/ppermute | solution.py:487
  20.8 0.7 %collective-permute-start.4 = (f32[72,128]{1,0:T(8,128)S(1)}, f32[72,128]{1,0:T(8,128)S(1)}, u32[]{:S(2)}, u32[]{:S(2)}) collective-permute-start(f32[72,128]{1,0:T(8,128)S(1)} %get-tuple-element.20.own), channel_id=1, source_target_pairs={{0,1},{1,0},{2,3},{3,2},{4,5},{5,4},{6,7},{7,6},{8,9},{9,8},{10,11... | collective-permute-start | bytes 110600 | tf_op jit(solution)/shard_map/ppermute | solution.py:487
  21.5 1.6 %collective-permute-done.6.three = f32[72,128]{1,0:T(8,128)S(1)} collective-permute-done((f32[72,128]{1,0:T(8,128)S(1)}, f32[72,128]{1,0:T(8,128)S(1)}, u32[]{:S(2)}, u32[]{:S(2)}) %collective-permute-start.6) | collective-permute-done | bytes 36896 | tf_op jit(solution)/shard_map/ppermute | solution.py:487
  23.1 1.2 %collective-permute-done.5.two = f32[72,128]{1,0:T(8,128)S(1)} collective-permute-done((f32[72,128]{1,0:T(8,128)S(1)}, f32[72,128]{1,0:T(8,128)S(1)}, u32[]{:S(2)}, u32[]{:S(2)}) %collective-permute-start.5) | collective-permute-done | bytes 36896 | tf_op jit(solution)/shard_map/ppermute | solution.py:487
  24.3 0.1 collective-permute-start.7
  24.4 0.7 %collective-permute-start.11 = (bf16[64,32,128]{2,1,0:T(8,128)(2,1)S(1)}, bf16[64,32,128]{2,1,0:T(8,128)(2,1)S(1)}, u32[]{:S(2)}, u32[]{:S(2)}) collective-permute-start(bf16[64,32,128]{2,1,0:T(8,128)(2,1)S(1)} %shard_map.66), channel_id=1, source_target_pairs={{1,2},{2,1},{5,6},{6,5},{9,10},{10,9},{13,14},{14,13},{17,18},{18,... | collective-permute-start | bytes 1572872 | tf_op jit(solution)/shard_map/ppermute | solution.py:470
  25.1 3.1 %collective-permute-done.7 = bf16[80,128]{1,0:T(8,128)(2,1)S(1)} collective-permute-done((bf16[80,128]{1,0:T(8,128)(2,1)S(1)}, bf16[80,128]{1,0:T(8,128)(2,1)S(1)}, u32[]{:S(2)}, u32[]{:S(2)}) %collective-permute-start.7) | collective-permute-done | bytes 20512 | tf_op jit(solution)/shard_map/ppermute | solution.py:487
  28.1 0.4 %collective-permute-start.10 = (bf16[2,80,128]{2,1,0:T(8,128)(2,1)S(1)}, bf16[2,80,128]{2,1,0:T(8,128)(2,1)S(1)}, u32[]{:S(2)}, u32[]{:S(2)}) collective-permute-start(bf16[2,80,128]{2,1,0:T(8,128)(2,1)S(1)} %pad_maximum_fusion.pair.refs_0_), channel_id=1, source_target_pairs={{0,24},{4,28},{8,16},{12,20},{16,8},{20,12},{24,0},{28,4},{1,25},{... | collective-permute-start | bytes 122888 | tf_op jit(solution)/shard_map/ppermute | solution.py:487
  28.6 0.0 collective-permute-start.9
  28.6 3.9 %collective-permute-start.8 = (bf16[2,80,128]{2,1,0:T(8,128)(2,1)S(1)}, bf16[2,80,128]{2,1,0:T(8,128)(2,1)S(1)}, u32[]{:S(2)}, u32[]{:S(2)}) collective-permute-start(bf16[2,80,128]{2,1,0:T(8,128)(2,1)S(1)} %pad_maximum_fusion.pair.refs_0_), channel_id=1, source_target_pairs={{0,8},{4,12},{8,0},{12,4},{16,24},{20,28},{24,16},{28,20},{1,9},{5... | collective-permute-start | bytes 122888 | tf_op jit(solution)/shard_map/ppermute | solution.py:487
  32.5 0.8 %shard_map.67 = (f32[2,6,64,128]{3,2,1,0:T(8,128)S(1)}, f32[2,64,128]{2,1,0:T(8,128)S(1)}) custom-call(s32[4]{0:T(128)S(1)} %pad_add_fusion.place, f32[4]{0:T(128)S(1)} %copy-done.3, bf16[2,80,128]{2,1,0:T(8,128)(2,1)S(1)} %pad_maximum_fusion.pair.refs_0_, bf16[80,128]{1,0:T(8,128)(2,1)S(1)} %collective-permute-done.2.one_got, ...), custom_call_target="tpu_custom_call" | custom-call | flops 8589934592 | bytes 1048576 | tf_op jit(solution)/shard_map/pallas_call | solution.py:566
  33.3 0.9 %collective-permute-done.10.refs_3_ = bf16[2,80,128]{2,1,0:T(8,128)(2,1)S(1)} collective-permute-done((bf16[2,80,128]{2,1,0:T(8,128)(2,1)S(1)}, bf16[2,80,128]{2,1,0:T(8,128)(2,1)S(1)}, u32[]{:S(2)}, u32[]{:S(2)}) %collective-permute-start.10) | collective-permute-done | bytes 40992 | tf_op jit(solution)/shard_map/ppermute | solution.py:487
  34.2 0.3 collective-permute-done.8.refs_1_
  34.6 3.5 %shard_map.68 = (f32[1,64]{1,0:T(1,128)}, f32[2,64,128]{2,1,0:T(8,128)}) custom-call(s32[4]{0:T(128)S(1)} %pad_add_fusion.place, bf16[2,80,128]{2,1,0:T(8,128)(2,1)S(1)} %pad_maximum_fusion.pair.refs_0_, bf16[2,80,128]{2,1,0:T(8,128)(2,1)S(1)} %collective-permute-done.8.refs_1_, bf16[2,80,128]{2,1,0:T(8,128)(2,1)S(1)} %collective-permute-done.9.refs_2_, ...), custom_call_target="tpu_custom_call" | custom-call | flops 10000000 | bytes 5242880 | tf_op jit(solution)/shard_map/pallas_call | solution.py:576
  (12 shorter events, 0.1 us)
Async XLA Ops:
  0.6 1.8 %copy-start = (bf16[64,2,64,128]{3,2,1,0:T(8,128)(2,1)S(1)}, bf16[64,2,64,128]{3,2,1,0:T(8,128)(2,1)}, u32[]{:S(2)}) copy-start(bf16[64,2,64,128]{3,2,1,0:T(8,128)(2,1)} %refs_4_.1) | copy-start | bytes 6291460
  0.6 1.8 %copy-start.1 = (s32[2,64,128]{2,1,0:T(8,128)S(1)}, s32[2,64,128]{2,1,0:T(8,128)}, u32[]{:S(2)}) copy-start(s32[2,64,128]{2,1,0:T(8,128)} %labels.5) | copy-start | bytes 196612
  3.1 10.3 %copy-start.2 = (f32[2,64,128]{2,1,0:T(8,128)S(1)}, f32[2,64,128]{2,1,0:T(8,128)}, u32[]{:S(2)}) copy-start(f32[2,64,128]{2,1,0:T(8,128)} %refs_13_.1) | copy-start | bytes 196612
  3.1 10.2 %copy-start.3 = (f32[4]{0:T(128)S(1)}, f32[4]{0:T(128)}, u32[]{:S(2)}) copy-start(f32[4]{0:T(128)} %levels.7) | copy-start | bytes 52
  3.1 13.3 %collective-permute-start = (bf16[65,64,128]{2,1,0:T(8,128)(2,1)S(1)}, bf16[65,64,128]{2,1,0:T(8,128)(2,1)S(1)}, u32[]{:S(2)}, u32[]{:S(2)}) collective-permute-start(bf16[65,64,128]{2,1,0:T(8,128)(2,1)S(1)} %shard_map.60.staged), channel_id=1, source_target_pairs={{0,1},{1,0},{2,3},{3,2},{4,5},{5,4},{6,7},{7,6},{8,9},{9,8},{10,11... | collective-permute-start | bytes 3194888 | tf_op jit(solution)/shard_map/ppermute | solution.py:463
  3.6 14.2 %collective-permute-start.1 = (bf16[66,32,128]{2,1,0:T(8,128)(2,1)S(1)}, bf16[66,32,128]{2,1,0:T(8,128)(2,1)S(1)}, u32[]{:S(2)}, u32[]{:S(2)}) collective-permute-start(bf16[66,32,128]{2,1,0:T(8,128)(2,1)S(1)} %shard_map.59.staged), channel_id=1, source_target_pairs={{0,4},{1,2},{2,1},{3,7},{4,0},{5,6},{6,5},{7,3},{8,12},{9,10},{10,... | collective-permute-start | bytes 1622024 | tf_op jit(solution)/shard_map/ppermute | solution.py:483
  8.2 9.6 %collective-permute-start.2 = (bf16[80,128]{1,0:T(8,128)(2,1)S(1)}, bf16[80,128]{1,0:T(8,128)(2,1)S(1)}, u32[]{:S(2)}, u32[]{:S(2)}) collective-permute-start(bf16[80,128]{1,0:T(8,128)(2,1)S(1)} %get-tuple-element.18.one_pack), channel_id=1, source_target_pairs={{0,4},{4,0},{8,12},{12,8},{16,20},{20,16},{24,28},{28,24},{1,5},{5... | collective-permute-start | bytes 61448 | tf_op jit(solution)/shard_map/ppermute | solution.py:463
  8.3 9.5 %collective-permute-start.3 = (bf16[80,128]{1,0:T(8,128)(2,1)S(1)}, bf16[80,128]{1,0:T(8,128)(2,1)S(1)}, u32[]{:S(2)}, u32[]{:S(2)}) collective-permute-start(bf16[80,128]{1,0:T(8,128)(2,1)S(1)} %get-tuple-element.19.two_pack), channel_id=1, source_target_pairs={{0,28},{4,8},{8,4},{12,16},{16,12},{20,24},{24,20},{28,0},{1,29},{... | collective-permute-start | bytes 61448 | tf_op jit(solution)/shard_map/ppermute | solution.py:463
  19.5 3.5 %collective-permute-start.6 = (f32[72,128]{1,0:T(8,128)S(1)}, f32[72,128]{1,0:T(8,128)S(1)}, u32[]{:S(2)}, u32[]{:S(2)}) collective-permute-start(f32[72,128]{1,0:T(8,128)S(1)} %get-tuple-element.20.own), channel_id=1, source_target_pairs={{0,3},{1,2},{2,1},{3,0},{4,7},{5,6},{6,5},{7,4},{8,11},{9,10},{10,... | collective-permute-start | bytes 110600 | tf_op jit(solution)/shard_map/ppermute | solution.py:487
  20.3 4.0 %collective-permute-start.5 = (f32[72,128]{1,0:T(8,128)S(1)}, f32[72,128]{1,0:T(8,128)S(1)}, u32[]{:S(2)}, u32[]{:S(2)}) collective-permute-start(f32[72,128]{1,0:T(8,128)S(1)} %get-tuple-element.20.own), channel_id=1, source_target_pairs={{0,2},{1,3},{2,0},{3,1},{4,6},{5,7},{6,4},{7,5},{8,10},{9,11},{10,... | collective-permute-start | bytes 110600 | tf_op jit(solution)/shard_map/ppermute | solution.py:487
  20.8 3.5 %collective-permute-start.4 = (f32[72,128]{1,0:T(8,128)S(1)}, f32[72,128]{1,0:T(8,128)S(1)}, u32[]{:S(2)}, u32[]{:S(2)}) collective-permute-start(f32[72,128]{1,0:T(8,128)S(1)} %get-tuple-element.20.own), channel_id=1, source_target_pairs={{0,1},{1,0},{2,3},{3,2},{4,5},{5,4},{6,7},{7,6},{8,9},{9,8},{10,11... | collective-permute-start | bytes 110600 | tf_op jit(solution)/shard_map/ppermute | solution.py:487
  24.3 3.8 %collective-permute-start.7 = (bf16[80,128]{1,0:T(8,128)(2,1)S(1)}, bf16[80,128]{1,0:T(8,128)(2,1)S(1)}, u32[]{:S(2)}, u32[]{:S(2)}) collective-permute-start(bf16[80,128]{1,0:T(8,128)(2,1)S(1)} %shard_map.65.after), channel_id=1, source_target_pairs={{0,4},{4,0},{8,12},{12,8},{16,20},{20,16},{24,28},{28,24},{1,5},{5... | collective-permute-start | bytes 61448 | tf_op jit(solution)/shard_map/ppermute | solution.py:487
  24.4 10.2 %collective-permute-start.11 = (bf16[64,32,128]{2,1,0:T(8,128)(2,1)S(1)}, bf16[64,32,128]{2,1,0:T(8,128)(2,1)S(1)}, u32[]{:S(2)}, u32[]{:S(2)}) collective-permute-start(bf16[64,32,128]{2,1,0:T(8,128)(2,1)S(1)} %shard_map.66), channel_id=1, source_target_pairs={{1,2},{2,1},{5,6},{6,5},{9,10},{10,9},{13,14},{14,13},{17,18},{18,... | collective-permute-start | bytes 1572872 | tf_op jit(solution)/shard_map/ppermute | solution.py:470
  28.1 6.1 %collective-permute-start.10 = (bf16[2,80,128]{2,1,0:T(8,128)(2,1)S(1)}, bf16[2,80,128]{2,1,0:T(8,128)(2,1)S(1)}, u32[]{:S(2)}, u32[]{:S(2)}) collective-permute-start(bf16[2,80,128]{2,1,0:T(8,128)(2,1)S(1)} %pad_maximum_fusion.pair.refs_0_), channel_id=1, source_target_pairs={{0,24},{4,28},{8,16},{12,20},{16,8},{20,12},{24,0},{28,4},{1,25},{... | collective-permute-start | bytes 122888 | tf_op jit(solution)/shard_map/ppermute | solution.py:487
  28.6 5.7 %collective-permute-start.9 = (bf16[2,80,128]{2,1,0:T(8,128)(2,1)S(1)}, bf16[2,80,128]{2,1,0:T(8,128)(2,1)S(1)}, u32[]{:S(2)}, u32[]{:S(2)}) collective-permute-start(bf16[2,80,128]{2,1,0:T(8,128)(2,1)S(1)} %pad_maximum_fusion.pair.refs_0_), channel_id=1, source_target_pairs={{0,16},{4,20},{8,24},{12,28},{16,0},{20,4},{24,8},{28,12},{1,17},{... | collective-permute-start | bytes 122888 | tf_op jit(solution)/shard_map/ppermute | solution.py:487
  28.6 6.0 %collective-permute-start.8 = (bf16[2,80,128]{2,1,0:T(8,128)(2,1)S(1)}, bf16[2,80,128]{2,1,0:T(8,128)(2,1)S(1)}, u32[]{:S(2)}, u32[]{:S(2)}) collective-permute-start(bf16[2,80,128]{2,1,0:T(8,128)(2,1)S(1)} %pad_maximum_fusion.pair.refs_0_), channel_id=1, source_target_pairs={{0,8},{4,12},{8,0},{12,4},{16,24},{20,28},{24,16},{28,20},{1,9},{5... | collective-permute-start | bytes 122888 | tf_op jit(solution)/shard_map/ppermute | solution.py:487

commit v5 on v3

--- a/solution.py
+++ b/solution.py
@@ -73,6 +73,10 @@
     inner_send[modes] = labels[1 - side].astype(F32).astype(BF16)
     for copy in copies:
         copy.wait()
+
+
+def release_kernel(after, outer_rest, outer_out):
+    pass
 
 
 def prepare_kernel(place, labels, held, planes_out, outer_rest, one_pack, two_pack):
@@ -290,10 +294,14 @@
         terms[x, 5] = end_weight
 
 
-def sum_kernel(own, one, two, three, outer_rest, out, outer_out):
+def pair_kernel(own, across, beside, oblique, out):
     modes = own.shape[1] // 2
-    total = (own[...] + one[...]) + (two[...] + three[...])
-    encode(total, modes, out)
+    encode(own[...] + across[...], modes, out.at[0])
+    encode(beside[...] + oblique[...], modes, out.at[1])
+
+
+def single_kernel(own, out):
+    encode(own[...], own.shape[1] // 2, out)
 
 
 def encode(total, modes, out):
@@ -320,10 +328,10 @@
 
 
 def finish_kernel(place, *refs):
-    count = len(refs) - 18
+    count = len(refs) - 17
     blocks, refs = refs[:count], refs[count:]
     zvec, inner_got, outer_got, outer_last, picked, terms, middle, inner_face, outer_face, resid = refs[:10]
-    solution, deflated, direction_ref, image_ref, ahead_ref, spread, outer_field, fix_ref = refs[10:]
+    solution, deflated, direction_ref, image_ref, spread, outer_field, fix_ref = refs[10:]
     subs = direction_ref.shape[0]
     modes, planes, rows, layers = zvec.shape
     half = rows // 2
@@ -339,21 +347,26 @@
     def column(row):
         return jnp.sum(jnp.where(eye, row, 0.0), axis=1, keepdims=True)
 
-    def each(body):
+    def each(body, carry):
         for index, block in enumerate(blocks):
             held_here = block.shape[0]
             if held_here <= 8:
                 for entry in range(held_here):
-                    body(block.at[entry], jnp.bitwise_xor(order, index * held_here + entry))
+                    s = jnp.bitwise_xor(order, index * held_here + entry)
+                    carry = body(block.at[entry], s, carry)
             else:
-                pl.loop(0, held_here)(lambda entry, block=block: body(block.at[entry], entry))
-
-    def load(block, s):
+                carry = lax.fori_loop(
+                    0, held_here, lambda entry, c, block=block: body(block.at[entry], entry, c), carry
+                )
+        return carry
+
+    def load(block, s, carry):
         extra = block[modes:modes + 16, :].astype(F32)
         direction_ref[pl.ds(s, 1), :] = (extra[0:1] + extra[1:2]) + extra[2:3]
         fix_ref[pl.ds(s, 1), :] = extra[4:5] - extra[3:4]
-
-    each(load)
+        return carry
+
+    each(load, 0)
     fix = fix_ref[:, :modes]
 
     def turned(rows_of, by):
@@ -363,18 +376,18 @@
     def coarse_apply(direction):
         direction_ref[...] = jnp.concatenate([direction, turned(direction, 1)], axis=1)
 
-        def one(block, s):
+        def one(block, s, carry):
             values = block[:modes, :].astype(F32)
             pair = direction_ref[pl.ds(s, 1), :]
             ahead = jnp.sum(values * pair, axis=1, keepdims=True)
-            ahead_ref[...] = jnp.where(lane_is((modes, 128), s), ahead, ahead_ref[...])
             image_ref[pl.ds(s, 1), :] = jnp.sum(
                 values * column(pair[:, :modes]), axis=0, keepdims=True
             )
-
-        each(one)
+            return jnp.where(lane_is((modes, 128), s), ahead, carry)
+
+        ahead_all = each(one, jnp.zeros((modes, 128), F32))
         image = image_ref[...]
-        square_part = ahead_ref[...].T[:subs] + image[:, :modes] + fix * direction
+        square_part = ahead_all.T[:subs] + image[:, :modes] + fix * direction
         return square_part + turned(image[:, modes:], -1)
 
     def inner(left, right):
@@ -399,17 +412,20 @@
     spread[...] = jnp.broadcast_to(column(own), (modes, layers))
     ahead_column = column(direction_ref[pl.ds(lax.rem(me + 1, subs), 1), :modes])
     behind_column = column(direction_ref[pl.ds(lax.rem(me + subs - 1, subs), 1), :modes])
-    at_top = lane_is((modes, layers), layers - 1)
-    at_bottom = lane_is((modes, layers), 0)
-
-    def placed(pack, values):
-        return lax.dot_general(
-            pack, values, TN, precision=PRECISE, preferred_element_type=F32
-        ).reshape(planes, rows, layers)
-
-    ends = placed(picked[0], jnp.where(at_top, ahead_column, 0.0)) + placed(
-        picked[1], jnp.where(at_bottom, behind_column, 0.0)
-    )
+    ahead_row = jnp.sum(ahead_column * picked[0], axis=0, keepdims=True)
+    behind_row = jnp.sum(behind_column * picked[1], axis=0, keepdims=True)
+    width = planes * rows
+    both_rows = jnp.where(
+        lax.broadcasted_iota(jnp.int32, (8, width), 0) == 0,
+        jnp.broadcast_to(ahead_row, (8, width)),
+        jnp.broadcast_to(behind_row, (8, width)),
+    )
+    columns = both_rows.T
+    ends = jnp.where(
+        lane_is((width, layers), layers - 1),
+        columns[:, 0:1],
+        jnp.where(lane_is((width, layers), 0), columns[:, 1:2], 0.0),
+    ).reshape(planes, rows, layers)
 
     def add_mode(j, carry):
         fields, near, last = list(carry[0]), carry[1], carry[2]
@@ -453,13 +469,6 @@
     return lax.ppermute(value, axis, pairs)
 
 
-def swapped_open(value):
-    pairs = []
-    for i in range(1, lax.axis_size("pln") - 1):
-        pairs.append((i, i + 1 if i % 2 else i - 1))
-    return lax.ppermute(value, "pln", pairs)
-
-
 def swapped_all(value):
     subs, count = lax.axis_size("sub"), lax.axis_size("pln")
     pairs = []
@@ -477,11 +486,12 @@
     return lax.ppermute(value, axis, [(i, i ^ mask) for i in range(lax.axis_size(axis))])
 
 
-def gathered(value, axis):
-    if lax.axis_size(axis) != 8:
-        return [lax.all_gather(value, axis)]
-    pair = jnp.stack([value, exchanged(value, axis, 1)])
-    return [pair] + [exchanged(pair, axis, mask) for mask in (2, 4, 6)]
+def partner(value, sub_mask, pln_mask):
+    subs, count = lax.axis_size("sub"), lax.axis_size("pln")
+    pairs = [
+        (s * count + p, (s ^ sub_mask) * count + (p ^ pln_mask)) for s in range(subs) for p in range(count)
+    ]
+    return lax.ppermute(value, ("sub", "pln"), pairs)
 
 
 def body(labels, levels, zvec, resid):
@@ -540,24 +550,25 @@
         flops=100_000_000,
         moved=1 << 20,
     )(place, levels, partial, weights, here, outer_got, one_pack, two_pack, one_got, two_got)
-    packed = shape((modes + 16, 2 * modes), BF16)
-    if parts == 4:
-        others = [exchanged(block, "pln", mask) for mask in (1, 2, 3)]
+    packed = (modes + 16, 2 * modes)
+    if parts == 4 and subs == 8:
+        block = block + exchanged(block, "pln", 1)
+        others = [partner(block, *masks) for masks in ((0, 2), (1, 0), (1, 2))]
+        [pair] = call(pair_kernel, [shape((2,) + packed, BF16)], [VMEM] * 4)(block, *others)
+        blocks = [pair] + [exchanged(pair, "sub", mask) for mask in (2, 4, 6)]
     else:
-        block = lax.psum(block, "pln")
-        others = [jnp.zeros_like(block)] * 3
-    packed, outer_rest = call(
-        sum_kernel, [packed, rest], [VMEM] * 4 + [ANY], aliases={4: 1}
-    )(block, *others, outer_rest)
-    blocks = gathered(packed, "sub")
-    outer_last = swapped_open(outer_rest)
+        [single] = call(single_kernel, [shape(packed, BF16)], [VMEM])(lax.psum(block, "pln"))
+        blocks = [lax.all_gather(single, "sub")]
+    [outer_rest] = call(release_kernel, [rest], [ANY] * 2, aliases={1: 0})(block, outer_rest)
+    outer_last = swapped_all(outer_rest)
     terms, picked = call(
         terms_kernel,
         [shape((planes, 6) + plane, F32), shape((2, modes, planes * rows), F32)],
         [SMEM, SMEM, ANY] + [VMEM] * 5,
         [pltpu.VMEM(field, F32)],
-        flops=1_000_000,
-        moved=64 << 20,
+
+        flops=1 << 33,
+        moved=1 << 20,
     )(place, levels, blocks[0], one_got, two_got, weights, inner_face, outer_face)
     return tuple(
         call(
@@ -567,7 +578,6 @@
             [
                 pltpu.VMEM((subs, 2 * modes), F32),
                 pltpu.VMEM((subs, 2 * modes), F32),
-                pltpu.VMEM((modes, 128), F32),
                 pltpu.VMEM((modes, layers), F32),
                 pltpu.VMEM(plane, F32),
                 pltpu.VMEM((subs, 2 * modes), F32),

time: 39.5 us -> 36.8 us (0.932)
  waiting for transfers between devices: 8.6 us -> 5.08 us
  starting transfers between devices: 15.3 us -> 16.2 us
    ppermute x7 -> x4, waiting for transfers between devices: 8.58 us -> 2.37 us  [exchanged(): lax.ppermute(value, axis, [(i, i ^ mask) for i in range(lax.axis_size(axi...]
    ppermute x1 -> x3, starting transfers between devices: 0.69 us -> 3.48 us  [partner(): return lax.ppermute(value, ('sub', 'pln'), pairs)]
    ppermute x1 -> x3, waiting for transfers between devices: 0.01 us -> 2.66 us  [partner(): return lax.ppermute(value, ('sub', 'pln'), pairs)]
    ppermute x7 -> x4, starting transfers between devices: 6.38 us -> 4.52 us  [exchanged(): lax.ppermute(value, axis, [(i, i ^ mask) for i in range(lax.axis_size(axi...]
    ppermute x1 -> x2, starting transfers between devices: 2.59 us -> 2.6 us  [swapped_all(): return lax.ppermute(value, ('sub', 'pln'), pairs)]
  transfers between devices with their start and end apart: 12 -> 12, of which waited for: 5 -> 5; matrix products, arithmetic and copies ran while one was open for 0% -> 0% of each run, Pallas kernels for 18% -> 20%
where the time goes in v5:
time: 36.8 us; the launch traced here: 36.7 us
  starting transfers between devices  16.2 us (44%)
  Pallas kernels  14.5 us (39%)
  waiting for transfers between devices  5.08 us (14%)
  between operations  0.73 us (2%)
    ppermute x3, starting transfers between devices, swapped(): return lax.ppermute(value, axis, pairs)  5.64 us
    ppermute x4, starting transfers between devices, exchanged(): lax.ppermute(value, axis, [(i, i ^ mask) for i in range(lax.axis_size(axi...  4.52 us
    pallas_call x1, Pallas kernels, body(): call(finish_kernel, [shape((1, modes), F32), shape(field, F32)], [SMEM] +...  3.5 us
    ppermute x3, starting transfers between devices, partner(): return lax.ppermute(value, ('sub', 'pln'), pairs)  3.48 us
    pallas_call x1, Pallas kernels, body(): call(block_kernel, [shape((modes + 8, modes), F32), shape((7,) + plane, F...  3.06 us
    ppermute x3, waiting for transfers between devices, partner(): return lax.ppermute(value, ('sub', 'pln'), pairs)  2.66 us
    ppermute x2, starting transfers between devices, swapped_all(): return lax.ppermute(value, ('sub', 'pln'), pairs)  2.6 us
    ppermute x4, waiting for transfers between devices, exchanged(): lax.ppermute(value, axis, [(i, i ^ mask) for i in range(lax.axis_size(axi...  2.37 us
  transfers between devices with their start and end apart: 12, of which 5 were waited for; matrix products, arithmetic and copies ran while one was open for 0% of the time, Pallas kernels for 20%

profile of v5, /device:TPU:0, one launch (start us, length us, event | category | flops | bytes accessed | tf_op | source)
XLA Modules:
  0.0 36.7 jit_solution(11152281988389189800)
XLA Ops:
  0.6 0.0 copy-start
  0.6 0.0 copy-start.1
  0.7 0.1 pad_add_fusion.place
  0.7 2.0 %shard_map.61 = (bf16[65,64,128]{2,1,0:T(8,128)(2,1)S(1)}, bf16[66,32,128]{2,1,0:T(8,128)(2,1)S(1)}) custom-call(s32[4]{0:T(128)S(1)} %pad_add_fusion.place, s32[2,64,128]{2,1,0:T(8,128)} %labels_far.1, bf16[64,2,64,128]{3,2,1,0:T(8,128)(2,1)} %refs_4_.1), custom_call_target="tpu_custom_call" | custom-call | bytes 2097152 | tf_op jit(solution)/shard_map/pallas_call | solution.py:507
  2.8 0.5 %collective-permute-start = (bf16[65,64,128]{2,1,0:T(8,128)(2,1)S(1)}, bf16[65,64,128]{2,1,0:T(8,128)(2,1)S(1)}, u32[]{:S(2)}, u32[]{:S(2)}) collective-permute-start(bf16[65,64,128]{2,1,0:T(8,128)(2,1)S(1)} %get-tuple-element.19), channel_id=1, source_target_pairs={{0,1},{1,0},{2,3},{3,2},{4,5},{5,4},{6,7},{7,6},{8,9},{9,8},{10,11... | collective-permute-start | bytes 3194888 | tf_op jit(solution)/shard_map/ppermute | solution.py:469
  3.3 2.6 %collective-permute-start.1 = (bf16[66,32,128]{2,1,0:T(8,128)(2,1)S(1)}, bf16[66,32,128]{2,1,0:T(8,128)(2,1)S(1)}, u32[]{:S(2)}, u32[]{:S(2)}) collective-permute-start(bf16[66,32,128]{2,1,0:T(8,128)(2,1)S(1)} %get-tuple-element.21), channel_id=1, source_target_pairs={{0,4},{1,2},{2,1},{3,7},{4,0},{5,6},{6,5},{7,3},{8,12},{9,10},{10,... | collective-permute-start | bytes 1622024 | tf_op jit(solution)/shard_map/ppermute | solution.py:482
  5.9 2.0 %shard_map.59 = (bf16[2,64,64,128]{3,2,1,0:T(8,128)(2,1)S(1)}, bf16[64,32,128]{2,1,0:T(8,128)(2,1)S(1)}, bf16[80,128]{1,0:T(8,128)(2,1)S(1)}, bf16[80,128]{1,0:T(8,128)(2,1)S(1)}) custom-call(s32[4]{0:T(128)S(1)} %pad_add_fusion.place, s32[2,64,128]{2,1,0:T(8,128)S(1)} %copy-done.1, bf16[64,2,64,128]{3,2,1,0:T(8,128)(2,1)S(1)} %copy-done), custom_call_target="tpu_custom_call" | custom-call | flops 10000000 | bytes 6291456 | tf_op jit(solution)/shard_map/pallas_call | solution.py:517
  7.9 0.1 collective-permute-start.2
  8.0 5.0 %collective-permute-start.3 = (bf16[80,128]{1,0:T(8,128)(2,1)S(1)}, bf16[80,128]{1,0:T(8,128)(2,1)S(1)}, u32[]{:S(2)}, u32[]{:S(2)}) collective-permute-start(bf16[80,128]{1,0:T(8,128)(2,1)S(1)} %get-tuple-element.23.two_pack), channel_id=1, source_target_pairs={{0,28},{4,8},{8,4},{12,16},{16,12},{20,24},{24,20},{28,0},{1,29},{... | collective-permute-start | bytes 61448 | tf_op jit(solution)/shard_map/ppermute | solution.py:469
  13.0 3.1 %shard_map.60 = (f32[72,64]{1,0:T(8,128)S(1)}, f32[7,64,128]{2,1,0:T(8,128)S(1)}) custom-call(s32[4]{0:T(128)S(1)} %pad_add_fusion.place, f32[4]{0:T(128)S(1)} %copy-done.3, s32[2,64,128]{2,1,0:T(8,128)S(1)} %copy-done.1, f32[2,64,128]{2,1,0:T(8,128)S(1)} %copy-done.2, bf16[2,64,64,128]{3,2,1,0:T(8,128)(2,1)S(1)} %get-tuple-element.16.here), custom_call_target="tpu_custom_call" | custom-call | flops 400000000 | bytes 3145728 | tf_op jit(solution)/shard_map/pallas_call | solution.py:528
  16.1 0.0 collective-permute-done.inner_got.refs_5_
  16.1 1.4 %shard_map.62 = (f32[72,64]{1,0:T(8,128)S(1)}, f32[64,128]{1,0:T(8,128)S(1)}) custom-call(s32[4]{0:T(128)S(1)} %pad_add_fusion.place, f32[4]{0:T(128)S(1)} %copy-done.3, f32[72,64]{1,0:T(8,128)S(1)} %get-tuple-element.17.partial, f32[7,64,128]{2,1,0:T(8,128)S(1)} %get-tuple-element.18.weights.refs_10_, bf16[2,64,64,128]{3,2,1,0:T(8,128)(2,1)S(1)} %get-tuple-element.16.here, ...), custom_call_target="tpu_custom_call" | custom-call | flops 100000000 | bytes 1048576 | tf_op jit(solution)/shard_map/pallas_call | solution.py:537
  17.5 0.0 collective-permute-done.2.one_got
  17.5 0.0 collective-permute-done.3.two_got
  17.5 0.0 collective-permute-done.1.outer_got.refs_6_
  17.5 1.7 %shard_map.63 = (f32[72,128]{1,0:T(8,128)S(1)}, f32[64,128]{1,0:T(8,128)S(1)}) custom-call(s32[4]{0:T(128)S(1)} %pad_add_fusion.place, f32[4]{0:T(128)S(1)} %copy-done.3, f32[72,64]{1,0:T(8,128)S(1)} %get-tuple-element.20.partial, f32[7,64,128]{2,1,0:T(8,128)S(1)} %get-tuple-element.18.weights.refs_10_, bf16[2,64,64,128]{3,2,1,0:T(8,128)(2,1)S(1)} %get-tuple-element.16.here, ...), custom_call_target="tpu_custom_call" | custom-call | flops 100000000 | bytes 1048576 | tf_op jit(solution)/shard_map/pallas_call | solution.py:545
  19.2 0.1 collective-permute-start.4
  19.3 1.2 %collective-permute-done.4 = f32[72,128]{1,0:T(8,128)S(1)} collective-permute-done((f32[72,128]{1,0:T(8,128)S(1)}, f32[72,128]{1,0:T(8,128)S(1)}, u32[]{:S(2)}, u32[]{:S(2)}) %collective-permute-start.4) | collective-permute-done | bytes 36896 | tf_op jit(solution)/shard_map/ppermute | solution.py:486
  20.5 2.2 %collective-permute-start.6 = (f32[72,128]{1,0:T(8,128)S(1)}, f32[72,128]{1,0:T(8,128)S(1)}, u32[]{:S(2)}, u32[]{:S(2)}) collective-permute-start(f32[72,128]{1,0:T(8,128)S(1)} %add.3.own.after), channel_id=1, source_target_pairs={{0,4},{1,5},{2,6},{3,7},{4,0},{5,1},{6,2},{7,3},{8,12},{9,13},{10,... | collective-permute-start | bytes 110600 | tf_op jit(solution)/shard_map/ppermute | solution.py:494
  22.7 1.3 %collective-permute-start.5 = (f32[72,128]{1,0:T(8,128)S(1)}, f32[72,128]{1,0:T(8,128)S(1)}, u32[]{:S(2)}, u32[]{:S(2)}) collective-permute-start(f32[72,128]{1,0:T(8,128)S(1)} %add.3.own.after), channel_id=1, source_target_pairs={{0,2},{1,3},{2,0},{3,1},{4,6},{5,7},{6,4},{7,5},{8,10},{9,11},{10,... | collective-permute-start | bytes 110600 | tf_op jit(solution)/shard_map/ppermute | solution.py:494
  24.0 0.0 collective-permute-start.11
  24.0 1.6 %collective-permute-done.7.oblique = f32[72,128]{1,0:T(8,128)S(1)} collective-permute-done((f32[72,128]{1,0:T(8,128)S(1)}, f32[72,128]{1,0:T(8,128)S(1)}, u32[]{:S(2)}, u32[]{:S(2)}) %collective-permute-start.7) | collective-permute-done | bytes 36896 | tf_op jit(solution)/shard_map/ppermute | solution.py:494
  25.6 0.0 collective-permute-done.6.beside
  25.6 1.1 %collective-permute-done.5.across = f32[72,128]{1,0:T(8,128)S(1)} collective-permute-done((f32[72,128]{1,0:T(8,128)S(1)}, f32[72,128]{1,0:T(8,128)S(1)}, u32[]{:S(2)}, u32[]{:S(2)}) %collective-permute-start.5) | collective-permute-done | bytes 36896 | tf_op jit(solution)/shard_map/ppermute | solution.py:494
  26.7 0.5 %collective-permute-start.10 = (bf16[2,80,128]{2,1,0:T(8,128)(2,1)S(1)}, bf16[2,80,128]{2,1,0:T(8,128)(2,1)S(1)}, u32[]{:S(2)}, u32[]{:S(2)}) collective-permute-start(bf16[2,80,128]{2,1,0:T(8,128)(2,1)S(1)} %shard_map.64.pair.refs_0_), channel_id=1, source_target_pairs={{0,24},{4,28},{8,16},{12,20},{16,8},{20,12},{24,0},{28,4},{1,25},{... | collective-permute-start | bytes 122888 | tf_op jit(solution)/shard_map/ppermute | solution.py:486
  27.2 0.0 collective-permute-start.9
  27.2 3.9 %collective-permute-start.8 = (bf16[2,80,128]{2,1,0:T(8,128)(2,1)S(1)}, bf16[2,80,128]{2,1,0:T(8,128)(2,1)S(1)}, u32[]{:S(2)}, u32[]{:S(2)}) collective-permute-start(bf16[2,80,128]{2,1,0:T(8,128)(2,1)S(1)} %shard_map.64.pair.refs_0_), channel_id=1, source_target_pairs={{0,8},{4,12},{8,0},{12,4},{16,24},{20,28},{24,16},{28,20},{1,9},{5... | collective-permute-start | bytes 122888 | tf_op jit(solution)/shard_map/ppermute | solution.py:486
  31.2 0.8 %shard_map.66 = (f32[2,6,64,128]{3,2,1,0:T(8,128)S(1)}, f32[2,64,128]{2,1,0:T(8,128)S(1)}) custom-call(s32[4]{0:T(128)S(1)} %pad_add_fusion.place, f32[4]{0:T(128)S(1)} %copy-done.3, bf16[2,80,128]{2,1,0:T(8,128)(2,1)S(1)} %shard_map.64.pair.refs_0_, bf16[80,128]{1,0:T(8,128)(2,1)S(1)} %collective-permute-done.2.one_got, ...), custom_call_target="tpu_custom_call" | custom-call | flops 8589934592 | bytes 1048576 | tf_op jit(solution)/shard_map/pallas_call | solution.py:564
  32.0 0.6 %collective-permute-done.10.refs_3_ = bf16[2,80,128]{2,1,0:T(8,128)(2,1)S(1)} collective-permute-done((bf16[2,80,128]{2,1,0:T(8,128)(2,1)S(1)}, bf16[2,80,128]{2,1,0:T(8,128)(2,1)S(1)}, u32[]{:S(2)}, u32[]{:S(2)}) %collective-permute-start.10) | collective-permute-done | bytes 40992 | tf_op jit(solution)/shard_map/ppermute | solution.py:486
  32.6 0.6 %collective-permute-done.8.refs_1_ = bf16[2,80,128]{2,1,0:T(8,128)(2,1)S(1)} collective-permute-done((bf16[2,80,128]{2,1,0:T(8,128)(2,1)S(1)}, bf16[2,80,128]{2,1,0:T(8,128)(2,1)S(1)}, u32[]{:S(2)}, u32[]{:S(2)}) %collective-permute-start.8) | collective-permute-done | bytes 40992 | tf_op jit(solution)/shard_map/ppermute | solution.py:486
  33.1 0.0 collective-permute-done.11.refs_7_
  33.2 3.5 %shard_map.67 = (f32[1,64]{1,0:T(1,128)}, f32[2,64,128]{2,1,0:T(8,128)}) custom-call(s32[4]{0:T(128)S(1)} %pad_add_fusion.place, bf16[2,80,128]{2,1,0:T(8,128)(2,1)S(1)} %shard_map.64.pair.refs_0_, bf16[2,80,128]{2,1,0:T(8,128)(2,1)S(1)} %collective-permute-done.8.refs_1_, bf16[2,80,128]{2,1,0:T(8,128)(2,1)S(1)} %collective-permute-done.9.refs_2_, ...), custom_call_target="tpu_custom_call" | custom-call | flops 10000000 | bytes 5242880 | tf_op jit(solution)/shard_map/pallas_call | solution.py:574
  (11 shorter events, 0.1 us)
Async XLA Ops:
  0.6 5.3 %copy-start = (bf16[64,2,64,128]{3,2,1,0:T(8,128)(2,1)S(1)}, bf16[64,2,64,128]{3,2,1,0:T(8,128)(2,1)}, u32[]{:S(2)}) copy-start(bf16[64,2,64,128]{3,2,1,0:T(8,128)(2,1)} %refs_4_.1) | copy-start | bytes 6291460
  0.6 5.3 %copy-start.1 = (s32[2,64,128]{2,1,0:T(8,128)S(1)}, s32[2,64,128]{2,1,0:T(8,128)}, u32[]{:S(2)}) copy-start(s32[2,64,128]{2,1,0:T(8,128)} %labels_far.1) | copy-start | bytes 196612
  0.7 12.3 %copy-start.2 = (f32[2,64,128]{2,1,0:T(8,128)S(1)}, f32[2,64,128]{2,1,0:T(8,128)}, u32[]{:S(2)}) copy-start(f32[2,64,128]{2,1,0:T(8,128)} %refs_13_.1) | copy-start | bytes 196612
  0.7 12.3 %copy-start.3 = (f32[4]{0:T(128)S(1)}, f32[4]{0:T(128)}, u32[]{:S(2)}) copy-start(f32[4]{0:T(128)} %levels.7) | copy-start | bytes 52
  2.8 13.3 %collective-permute-start = (bf16[65,64,128]{2,1,0:T(8,128)(2,1)S(1)}, bf16[65,64,128]{2,1,0:T(8,128)(2,1)S(1)}, u32[]{:S(2)}, u32[]{:S(2)}) collective-permute-start(bf16[65,64,128]{2,1,0:T(8,128)(2,1)S(1)} %get-tuple-element.19), channel_id=1, source_target_pairs={{0,1},{1,0},{2,3},{3,2},{4,5},{5,4},{6,7},{7,6},{8,9},{9,8},{10,11... | collective-permute-start | bytes 3194888 | tf_op jit(solution)/shard_map/ppermute | solution.py:469
  3.3 14.2 %collective-permute-start.1 = (bf16[66,32,128]{2,1,0:T(8,128)(2,1)S(1)}, bf16[66,32,128]{2,1,0:T(8,128)(2,1)S(1)}, u32[]{:S(2)}, u32[]{:S(2)}) collective-permute-start(bf16[66,32,128]{2,1,0:T(8,128)(2,1)S(1)} %get-tuple-element.21), channel_id=1, source_target_pairs={{0,4},{1,2},{2,1},{3,7},{4,0},{5,6},{6,5},{7,3},{8,12},{9,10},{10,... | collective-permute-start | bytes 1622024 | tf_op jit(solution)/shard_map/ppermute | solution.py:482
  7.9 9.6 %collective-permute-start.2 = (bf16[80,128]{1,0:T(8,128)(2,1)S(1)}, bf16[80,128]{1,0:T(8,128)(2,1)S(1)}, u32[]{:S(2)}, u32[]{:S(2)}) collective-permute-start(bf16[80,128]{1,0:T(8,128)(2,1)S(1)} %get-tuple-element.22.one_pack), channel_id=1, source_target_pairs={{0,4},{4,0},{8,12},{12,8},{16,20},{20,16},{24,28},{28,24},{1,5},{5... | collective-permute-start | bytes 61448 | tf_op jit(solution)/shard_map/ppermute | solution.py:469
  8.0 9.5 %collective-permute-start.3 = (bf16[80,128]{1,0:T(8,128)(2,1)S(1)}, bf16[80,128]{1,0:T(8,128)(2,1)S(1)}, u32[]{:S(2)}, u32[]{:S(2)}) collective-permute-start(bf16[80,128]{1,0:T(8,128)(2,1)S(1)} %get-tuple-element.23.two_pack), channel_id=1, source_target_pairs={{0,28},{4,8},{8,4},{12,16},{16,12},{20,24},{24,20},{28,0},{1,29},{... | collective-permute-start | bytes 61448 | tf_op jit(solution)/shard_map/ppermute | solution.py:469
  19.2 1.3 %collective-permute-start.4 = (f32[72,128]{1,0:T(8,128)S(1)}, f32[72,128]{1,0:T(8,128)S(1)}, u32[]{:S(2)}, u32[]{:S(2)}) collective-permute-start(f32[72,128]{1,0:T(8,128)S(1)} %get-tuple-element.24), channel_id=1, source_target_pairs={{0,1},{1,0},{2,3},{3,2},{4,5},{5,4},{6,7},{7,6},{8,9},{9,8},{10,11... | collective-permute-start | bytes 110600 | tf_op jit(solution)/shard_map/ppermute | solution.py:486
  20.5 5.1 %collective-permute-start.7 = (f32[72,128]{1,0:T(8,128)S(1)}, f32[72,128]{1,0:T(8,128)S(1)}, u32[]{:S(2)}, u32[]{:S(2)}) collective-permute-start(f32[72,128]{1,0:T(8,128)S(1)} %add.3.own.after), channel_id=1, source_target_pairs={{0,6},{1,7},{2,4},{3,5},{4,2},{5,3},{6,0},{7,1},{8,14},{9,15},{10,... | collective-permute-start | bytes 110600 | tf_op jit(solution)/shard_map/ppermute | solution.py:494
  20.5 5.1 %collective-permute-start.6 = (f32[72,128]{1,0:T(8,128)S(1)}, f32[72,128]{1,0:T(8,128)S(1)}, u32[]{:S(2)}, u32[]{:S(2)}) collective-permute-start(f32[72,128]{1,0:T(8,128)S(1)} %add.3.own.after), channel_id=1, source_target_pairs={{0,4},{1,5},{2,6},{3,7},{4,0},{5,1},{6,2},{7,3},{8,12},{9,13},{10,... | collective-permute-start | bytes 110600 | tf_op jit(solution)/shard_map/ppermute | solution.py:494
  22.7 4.0 %collective-permute-start.5 = (f32[72,128]{1,0:T(8,128)S(1)}, f32[72,128]{1,0:T(8,128)S(1)}, u32[]{:S(2)}, u32[]{:S(2)}) collective-permute-start(f32[72,128]{1,0:T(8,128)S(1)} %add.3.own.after), channel_id=1, source_target_pairs={{0,2},{1,3},{2,0},{3,1},{4,6},{5,7},{6,4},{7,5},{8,10},{9,11},{10,... | collective-permute-start | bytes 110600 | tf_op jit(solution)/shard_map/ppermute | solution.py:494
  24.0 9.2 %collective-permute-start.11 = (bf16[64,32,128]{2,1,0:T(8,128)(2,1)S(1)}, bf16[64,32,128]{2,1,0:T(8,128)(2,1)S(1)}, u32[]{:S(2)}, u32[]{:S(2)}) collective-permute-start(bf16[64,32,128]{2,1,0:T(8,128)(2,1)S(1)} %shard_map.65), channel_id=1, source_target_pairs={{0,4},{1,2},{2,1},{3,7},{4,0},{5,6},{6,5},{7,3},{8,12},{9,10},{10,... | collective-permute-start | bytes 1572872 | tf_op jit(solution)/shard_map/ppermute | solution.py:482
  26.7 5.9 %collective-permute-start.10 = (bf16[2,80,128]{2,1,0:T(8,128)(2,1)S(1)}, bf16[2,80,128]{2,1,0:T(8,128)(2,1)S(1)}, u32[]{:S(2)}, u32[]{:S(2)}) collective-permute-start(bf16[2,80,128]{2,1,0:T(8,128)(2,1)S(1)} %shard_map.64.pair.refs_0_), channel_id=1, source_target_pairs={{0,24},{4,28},{8,16},{12,20},{16,8},{20,12},{24,0},{28,4},{1,25},{... | collective-permute-start | bytes 122888 | tf_op jit(solution)/shard_map/ppermute | solution.py:486
  27.2 5.4 %collective-permute-start.9 = (bf16[2,80,128]{2,1,0:T(8,128)(2,1)S(1)}, bf16[2,80,128]{2,1,0:T(8,128)(2,1)S(1)}, u32[]{:S(2)}, u32[]{:S(2)}) collective-permute-start(bf16[2,80,128]{2,1,0:T(8,128)(2,1)S(1)} %shard_map.64.pair.refs_0_), channel_id=1, source_target_pairs={{0,16},{4,20},{8,24},{12,28},{16,0},{20,4},{24,8},{28,12},{1,17},{... | collective-permute-start | bytes 122888 | tf_op jit(solution)/shard_map/ppermute | solution.py:486
  27.2 5.9 %collective-permute-start.8 = (bf16[2,80,128]{2,1,0:T(8,128)(2,1)S(1)}, bf16[2,80,128]{2,1,0:T(8,128)(2,1)S(1)}, u32[]{:S(2)}, u32[]{:S(2)}) collective-permute-start(bf16[2,80,128]{2,1,0:T(8,128)(2,1)S(1)} %shard_map.64.pair.refs_0_), channel_id=1, source_target_pairs={{0,8},{4,12},{8,0},{12,4},{16,24},{20,28},{24,16},{28,20},{1,9},{5... | collective-permute-start | bytes 122888 | tf_op jit(solution)/shard_map/ppermute | solution.py:486

commit v6 on v5

--- a/solution.py
+++ b/solution.py
@@ -79,7 +79,7 @@
     pass
 
 
-def prepare_kernel(place, labels, held, planes_out, outer_rest, one_pack, two_pack):
+def prepare_kernel(place, labels, held, outer_rest, one_pack, two_pack):
     modes, planes, rows, layers = held.shape
     half = rows // 2
     width = planes * rows
@@ -104,19 +104,20 @@
             out[at] = jnp.concatenate(
                 [ends[index:index + 1, j * width:(j + 1) * width] for j in range(CHUNK)], axis=0
             ).astype(BF16)
-        for slot, plane in ((0, 1 - side), (1, side)):
-            planes_out[slot, :, at, :] = jnp.swapaxes(held[at, plane], 0, 1)
         outer_rest[at] = held[at, side, pl.ds(pl.multiple_of(side * half, half), half), :]
 
 
 def block_kernel(
-    place, levels, labels, resid, here, partial, weights, half_diag, link_y, link_z,
+    place, levels, labels, resid, zvec, after, partial, weights, here, half_diag, link_y, link_z,
 ):
     planes, rows, layers = labels.shape
     modes = here.shape[2]
     side = lax.rem(place[1], 2)
     at_edge = (place[1] == 0) | (place[1] == place[2] - 1)
     held = (1 - side, side)
+    for slot, plane in enumerate(held):
+        for k in range(0, modes, CHUNK):
+            here[slot, :, k:k + CHUNK, :] = jnp.swapaxes(zvec[k:k + CHUNK, plane], 0, 1)
     coef = [coefficients(labels[x], levels) for x in held]
     middle = harmonic(coef[0], coef[1])
     weights[0] = middle
@@ -218,14 +219,10 @@
     out[modes:, :] = partial[modes:, :]
 
 
-def outer_kernel(
-    place, levels, partial, weights, here, outer_got, one_pack, two_pack, one_got, two_got,
-    out, face, turned, face_here,
-):
+def outer_kernel(place, levels, partial, weights, here, outer_got, out, face, turned, face_here):
     planes, rows, modes, layers = here.shape
     half = rows // 2
     side = lax.rem(place[1], 2)
-    odd = lax.rem(place[0], 2) == 1
     at_edge = (place[1] == 0) | (place[1] == place[2] - 1)
     base = pl.multiple_of(side * half, half)
     turn(outer_got, 0, turned)
@@ -233,7 +230,13 @@
     between = harmonic(weights[6], coef)
     face[...] = jnp.where(at_edge, weights[6], between)
     face_here[...] = jnp.where(at_edge, 0.0, between)
-    cross = face_product(face_here, base, here.at[1], turned)
+    out[:modes, :] = partial[:modes, :] + 0.5 * face_product(face_here, base, here.at[1], turned)
+    out[modes:, :] = partial[modes:, :]
+
+
+def ends_kernel(place, levels, partial, one_pack, two_pack, one_got, two_got, out):
+    modes = partial.shape[1]
+    odd = lax.rem(place[0], 2) == 1
 
     def coef_row(pack):
         return coefficients(pack[modes:modes + 16].astype(F32)[0:1], levels)
@@ -251,7 +254,7 @@
 
     edge_rows = weight_high * last[:modes]
     ends = product(weight_low * first[:modes], first[:modes]) + product(edge_rows, last[:modes])
-    square = partial[:modes, :] + 0.5 * (cross + ends)
+    square = partial[:modes, :] + 0.5 * ends
     out[:modes, :modes] = square + square.T
     out[:modes, modes:] = -product(edge_rows, next_first[:modes])
     out[modes:, :modes] = partial[modes:, :]
@@ -514,9 +517,9 @@
     outer_got = swapped_all(outer_near)
     inner_got = swapped(inner_send, "pln", 0)
     rest = shape((modes, half, layers), BF16)
-    here, outer_rest, one_pack, two_pack = call(
+    outer_rest, one_pack, two_pack = call(
         prepare_kernel,
-        [shape((planes, rows, modes, layers), BF16), rest, pack, pack],
+        [rest, pack, pack],
         [SMEM, VMEM, VMEM],
         flops=10_000_000,
         moved=6 << 20,
@@ -525,14 +528,18 @@
     two_got = swapped(two_pack, "sub", 1)
     field = (planes, rows, layers)
     plane = (rows, layers)
-    partial, weights = call(
+    partial, weights, here = call(
         block_kernel,
-        [shape((modes + 8, modes), F32), shape((7,) + plane, F32)],
-        [SMEM, SMEM] + [VMEM] * 3,
+        [
+            shape((modes + 8, modes), F32),
+            shape((7,) + plane, F32),
+            shape((planes, rows, modes, layers), BF16),
+        ],
+        [SMEM, SMEM] + [VMEM] * 3 + [ANY],
         [pltpu.VMEM(field, F32)] * 3,
         flops=400_000_000,
         moved=3 << 20,
-    )(place, levels, labels, resid, here)
+    )(place, levels, labels, resid, zvec, one_pack)
     turned = pltpu.VMEM((half, modes, layers), BF16)
     partial, inner_face = call(
         inner_kernel,
@@ -542,14 +549,17 @@
         flops=100_000_000,
         moved=1 << 20,
     )(place, levels, partial, weights, here, inner_got)
-    block, outer_face = call(
+    partial, outer_face = call(
         outer_kernel,
-        [shape((modes + 8, 2 * modes), F32), shape(plane, F32)],
-        [SMEM, SMEM] + [VMEM] * 8,
+        [shape((modes + 8, modes), F32), shape(plane, F32)],
+        [SMEM, SMEM] + [VMEM] * 4,
         [turned, pltpu.VMEM(plane, F32)],
         flops=100_000_000,
         moved=1 << 20,
-    )(place, levels, partial, weights, here, outer_got, one_pack, two_pack, one_got, two_got)
+    )(place, levels, partial, weights, here, outer_got)
+    [block] = call(
+        ends_kernel, [shape((modes + 8, 2 * modes), F32)], [SMEM, SMEM] + [VMEM] * 5, flops=10_000_000
+    )(place, levels, partial, one_pack, two_pack, one_got, two_got)
     packed = (modes + 16, 2 * modes)
     if parts == 4 and subs == 8:
         block = block + exchanged(block, "pln", 1)

time: 36.8 us -> 37.1 us (level)
  waiting for transfers between devices: 5.08 us -> 3.71 us
  starting transfers between devices: 16.2 us -> 17.3 us
  Pallas kernels: 14.5 us -> 15.1 us
    ppermute x2, starting transfers between devices: 2.6 us -> 4.33 us  [swapped_all(): return lax.ppermute(value, ('sub', 'pln'), pairs)]
    ppermute x3, starting transfers between devices: 5.64 us -> 4.1 us  [swapped(): return lax.ppermute(value, axis, pairs)]
    ppermute x3, waiting for transfers between devices: 2.66 us -> 1.27 us  [partner(): return lax.ppermute(value, ('sub', 'pln'), pairs)]
    ppermute x4, starting transfers between devices: 4.52 us -> 5.34 us  [exchanged(): lax.ppermute(value, axis, [(i, i ^ mask) for i in range(lax.axis_size(axi...]
    pallas_call x1, Pallas kernels: 3.06 us -> 3.88 us  [body(): call(block_kernel, [shape((modes + 8, modes), F32), shape((7,) + plane, F...]
    pallas_call x2 -> x3, Pallas kernels: 3.73 us -> 3.49 us  [the longest x1 1.33 us: body(): call(outer_kernel, [shape((modes + 8, modes), F32), shape(plane, F32)], [...]
  transfers between devices with their start and end apart: 12 -> 12, of which waited for: 5 -> 4; matrix products, arithmetic and copies ran while one was open for 0% -> 0% of each run, Pallas kernels for 20% -> 23%
where the time goes in v6:
time: 37.1 us; the launch traced here: 36.9 us
  starting transfers between devices  17.3 us (47%)
  Pallas kernels  15.1 us (41%)
  waiting for transfers between devices  3.71 us (10%)
  between operations  0.73 us (2%)
    ppermute x4, starting transfers between devices, exchanged(): lax.ppermute(value, axis, [(i, i ^ mask) for i in range(lax.axis_size(axi...  5.34 us
    ppermute x2, starting transfers between devices, swapped_all(): return lax.ppermute(value, ('sub', 'pln'), pairs)  4.33 us
    ppermute x3, starting transfers between devices, swapped(): return lax.ppermute(value, axis, pairs)  4.1 us
    pallas_call x1, Pallas kernels, body(): call(block_kernel, [shape((modes + 8, modes), F32), shape((7,) + plane, F...  3.88 us
    pallas_call x1, Pallas kernels, body(): call(finish_kernel, [shape((1, modes), F32), shape(field, F32)], [SMEM] +...  3.5 us
    ppermute x3, starting transfers between devices, partner(): return lax.ppermute(value, ('sub', 'pln'), pairs)  3.49 us
    ppermute x4, waiting for transfers between devices, exchanged(): lax.ppermute(value, axis, [(i, i ^ mask) for i in range(lax.axis_size(axi...  2.43 us
    pallas_call x1, Pallas kernels, body(): call(stage_kernel, [shape((modes + 1, rows, layers), BF16), shape((modes...  2.03 us
  transfers between devices with their start and end apart: 12, of which 4 were waited for; matrix products, arithmetic and copies ran while one was open for 0% of the time, Pallas kernels for 23%

profile of v6, /device:TPU:0, one launch (start us, length us, event | category | flops | bytes accessed | tf_op | source)
XLA Modules:
  0.0 36.9 jit_solution(4899580622212692004)
XLA Ops:
  0.6 0.0 copy-start
  0.6 0.0 copy-start.1
  0.7 0.1 pad_add_fusion.place
  0.7 2.0 %shard_map.61 = (bf16[65,64,128]{2,1,0:T(8,128)(2,1)S(1)}, bf16[66,32,128]{2,1,0:T(8,128)(2,1)S(1)}) custom-call(s32[4]{0:T(128)S(1)} %pad_add_fusion.place, s32[2,64,128]{2,1,0:T(8,128)} %labels_far.1, bf16[64,2,64,128]{3,2,1,0:T(8,128)(2,1)} %refs_4_.1), custom_call_target="tpu_custom_call" | custom-call | bytes 2097152 | tf_op jit(solution)/shard_map/pallas_call | solution.py:510
  2.8 0.5 %collective-permute-start = (bf16[65,64,128]{2,1,0:T(8,128)(2,1)S(1)}, bf16[65,64,128]{2,1,0:T(8,128)(2,1)S(1)}, u32[]{:S(2)}, u32[]{:S(2)}) collective-permute-start(bf16[65,64,128]{2,1,0:T(8,128)(2,1)S(1)} %get-tuple-element.20), channel_id=1, source_target_pairs={{0,1},{1,0},{2,3},{3,2},{4,5},{5,4},{6,7},{7,6},{8,9},{9,8},{10,11... | collective-permute-start | bytes 3194888 | tf_op jit(solution)/shard_map/ppermute | solution.py:472
  3.3 2.6 %collective-permute-start.1 = (bf16[66,32,128]{2,1,0:T(8,128)(2,1)S(1)}, bf16[66,32,128]{2,1,0:T(8,128)(2,1)S(1)}, u32[]{:S(2)}, u32[]{:S(2)}) collective-permute-start(bf16[66,32,128]{2,1,0:T(8,128)(2,1)S(1)} %get-tuple-element.22), channel_id=1, source_target_pairs={{0,4},{1,2},{2,1},{3,7},{4,0},{5,6},{6,5},{7,3},{8,12},{9,10},{10,... | collective-permute-start | bytes 1622024 | tf_op jit(solution)/shard_map/ppermute | solution.py:485
  5.9 1.2 %shard_map.59 = (bf16[64,32,128]{2,1,0:T(8,128)(2,1)S(1)}, bf16[80,128]{1,0:T(8,128)(2,1)S(1)}, bf16[80,128]{1,0:T(8,128)(2,1)S(1)}) custom-call(s32[4]{0:T(128)S(1)} %pad_add_fusion.place, s32[2,64,128]{2,1,0:T(8,128)S(1)} %copy-done.1, bf16[64,2,64,128]{3,2,1,0:T(8,128)(2,1)S(1)} %copy-done), custom_call_target="tpu_custom_call" | custom-call | flops 10000000 | bytes 6291456 | tf_op jit(solution)/shard_map/pallas_call | solution.py:520
  7.1 3.6 %collective-permute-start.3 = (bf16[80,128]{1,0:T(8,128)(2,1)S(1)}, bf16[80,128]{1,0:T(8,128)(2,1)S(1)}, u32[]{:S(2)}, u32[]{:S(2)}) collective-permute-start(bf16[80,128]{1,0:T(8,128)(2,1)S(1)} %get-tuple-element.24.two_pack), channel_id=1, source_target_pairs={{0,28},{4,8},{8,4},{12,16},{16,12},{20,24},{24,20},{28,0},{1,29},{... | collective-permute-start | bytes 61448 | tf_op jit(solution)/shard_map/ppermute | solution.py:472
  10.7 0.0 collective-permute-start.2
  10.7 3.9 %shard_map.60 = (f32[72,64]{1,0:T(8,128)S(1)}, f32[7,64,128]{2,1,0:T(8,128)S(1)}, bf16[2,64,64,128]{3,2,1,0:T(8,128)(2,1)S(1)}) custom-call(s32[4]{0:T(128)S(1)} %pad_add_fusion.place, f32[4]{0:T(128)S(1)} %copy-done.3, s32[2,64,128]{2,1,0:T(8,128)S(1)} %copy-done.1, f32[2,64,128]{2,1,0:T(8,128)S(1)} %copy-done.2, bf16[64,2,64,128]{3,2,1,0:T(8,128)(2,1)S(1)} %copy-done, ...), custom_call_target="tpu_custom_call" | custom-call | flops 400000000 | bytes 3145728 | tf_op jit(solution)/shard_map/pallas_call | solution.py:531
  14.6 0.0 collective-permute-done.inner_got.refs_5_
  14.6 1.4 %shard_map.62 = (f32[72,64]{1,0:T(8,128)S(1)}, f32[64,128]{1,0:T(8,128)S(1)}) custom-call(s32[4]{0:T(128)S(1)} %pad_add_fusion.place, f32[4]{0:T(128)S(1)} %copy-done.3, f32[72,64]{1,0:T(8,128)S(1)} %get-tuple-element.17.partial, f32[7,64,128]{2,1,0:T(8,128)S(1)} %get-tuple-element.18.weights.refs_10_, bf16[2,64,64,128]{3,2,1,0:T(8,128)(2,1)S(1)} %get-tuple-element.19.here, ...), custom_call_target="tpu_custom_call" | custom-call | flops 100000000 | bytes 1048576 | tf_op jit(solution)/shard_map/pallas_call | solution.py:544
  16.0 1.3 %shard_map.63 = (f32[72,64]{1,0:T(8,128)S(1)}, f32[64,128]{1,0:T(8,128)S(1)}) custom-call(s32[4]{0:T(128)S(1)} %pad_add_fusion.place, f32[4]{0:T(128)S(1)} %copy-done.3, f32[72,64]{1,0:T(8,128)S(1)} %get-tuple-element.21.partial, f32[7,64,128]{2,1,0:T(8,128)S(1)} %get-tuple-element.18.weights.refs_10_, bf16[2,64,64,128]{3,2,1,0:T(8,128)(2,1)S(1)} %get-tuple-element.19.here, ...), custom_call_target="tpu_custom_call" | custom-call | flops 100000000 | bytes 1048576 | tf_op jit(solution)/shard_map/pallas_call | solution.py:552
  17.3 0.0 collective-permute-done.3.two_got
  17.3 0.0 collective-permute-done.2.one_got
  17.3 0.9 %shard_map.64 = f32[72,128]{1,0:T(8,128)S(1)} custom-call(s32[4]{0:T(128)S(1)} %pad_add_fusion.place, f32[4]{0:T(128)S(1)} %copy-done.3, f32[72,64]{1,0:T(8,128)S(1)} %get-tuple-element.23.partial, bf16[80,128]{1,0:T(8,128)(2,1)S(1)} %get-tuple-element.16.after.one_pack, bf16[80,128]{1,0:T(8,128)(2,1)S(1)} %get-tuple-element.24.two_pack, ...), custom_call_target="tpu_custom_call" | custom-call | flops 10000000 | tf_op jit(solution)/shard_map/pallas_call | solution.py:560
  18.3 0.9 %collective-permute-start.4 = (f32[72,128]{1,0:T(8,128)S(1)}, f32[72,128]{1,0:T(8,128)S(1)}, u32[]{:S(2)}, u32[]{:S(2)}) collective-permute-start(f32[72,128]{1,0:T(8,128)S(1)} %shard_map.64), channel_id=1, source_target_pairs={{0,1},{1,0},{2,3},{3,2},{4,5},{5,4},{6,7},{7,6},{8,9},{9,8},{10,11... | collective-permute-start | bytes 110600 | tf_op jit(solution)/shard_map/ppermute | solution.py:489
  19.2 0.9 %collective-permute-done.4 = f32[72,128]{1,0:T(8,128)S(1)} collective-permute-done((f32[72,128]{1,0:T(8,128)S(1)}, f32[72,128]{1,0:T(8,128)S(1)}, u32[]{:S(2)}, u32[]{:S(2)}) %collective-permute-start.4) | collective-permute-done | bytes 36896 | tf_op jit(solution)/shard_map/ppermute | solution.py:489
  20.0 2.5 %collective-permute-start.7 = (f32[72,128]{1,0:T(8,128)S(1)}, f32[72,128]{1,0:T(8,128)S(1)}, u32[]{:S(2)}, u32[]{:S(2)}) collective-permute-start(f32[72,128]{1,0:T(8,128)S(1)} %add.3.own.after), channel_id=1, source_target_pairs={{0,6},{1,7},{2,4},{3,5},{4,2},{5,3},{6,0},{7,1},{8,14},{9,15},{10,... | collective-permute-start | bytes 110600 | tf_op jit(solution)/shard_map/ppermute | solution.py:497
  22.6 1.0 %collective-permute-start.5 = (f32[72,128]{1,0:T(8,128)S(1)}, f32[72,128]{1,0:T(8,128)S(1)}, u32[]{:S(2)}, u32[]{:S(2)}) collective-permute-start(f32[72,128]{1,0:T(8,128)S(1)} %add.3.own.after), channel_id=1, source_target_pairs={{0,2},{1,3},{2,0},{3,1},{4,6},{5,7},{6,4},{7,5},{8,10},{9,11},{10,... | collective-permute-start | bytes 110600 | tf_op jit(solution)/shard_map/ppermute | solution.py:497
  23.5 1.7 %collective-permute-start.11 = (bf16[64,32,128]{2,1,0:T(8,128)(2,1)S(1)}, bf16[64,32,128]{2,1,0:T(8,128)(2,1)S(1)}, u32[]{:S(2)}, u32[]{:S(2)}) collective-permute-start(bf16[64,32,128]{2,1,0:T(8,128)(2,1)S(1)} %shard_map.66), channel_id=1, source_target_pairs={{0,4},{1,2},{2,1},{3,7},{4,0},{5,6},{6,5},{7,3},{8,12},{9,10},{10,... | collective-permute-start | bytes 1572872 | tf_op jit(solution)/shard_map/ppermute | solution.py:485
  25.3 1.3 %collective-permute-done.6.beside = f32[72,128]{1,0:T(8,128)S(1)} collective-permute-done((f32[72,128]{1,0:T(8,128)S(1)}, f32[72,128]{1,0:T(8,128)S(1)}, u32[]{:S(2)}, u32[]{:S(2)}) %collective-permute-start.6) | collective-permute-done | bytes 36896 | tf_op jit(solution)/shard_map/ppermute | solution.py:497
  26.5 0.0 collective-permute-done.5.across
  26.6 1.0 %collective-permute-start.10 = (bf16[2,80,128]{2,1,0:T(8,128)(2,1)S(1)}, bf16[2,80,128]{2,1,0:T(8,128)(2,1)S(1)}, u32[]{:S(2)}, u32[]{:S(2)}) collective-permute-start(bf16[2,80,128]{2,1,0:T(8,128)(2,1)S(1)} %shard_map.65.pair.refs_0_), channel_id=1, source_target_pairs={{0,24},{4,28},{8,16},{12,20},{16,8},{20,12},{24,0},{28,4},{1,25},{... | collective-permute-start | bytes 122888 | tf_op jit(solution)/shard_map/ppermute | solution.py:489
  27.6 0.8 %collective-permute-start.9 = (bf16[2,80,128]{2,1,0:T(8,128)(2,1)S(1)}, bf16[2,80,128]{2,1,0:T(8,128)(2,1)S(1)}, u32[]{:S(2)}, u32[]{:S(2)}) collective-permute-start(bf16[2,80,128]{2,1,0:T(8,128)(2,1)S(1)} %shard_map.65.pair.refs_0_), channel_id=1, source_target_pairs={{0,16},{4,20},{8,24},{12,28},{16,0},{20,4},{24,8},{28,12},{1,17},{... | collective-permute-start | bytes 122888 | tf_op jit(solution)/shard_map/ppermute | solution.py:489
  28.4 2.7 %collective-permute-start.8 = (bf16[2,80,128]{2,1,0:T(8,128)(2,1)S(1)}, bf16[2,80,128]{2,1,0:T(8,128)(2,1)S(1)}, u32[]{:S(2)}, u32[]{:S(2)}) collective-permute-start(bf16[2,80,128]{2,1,0:T(8,128)(2,1)S(1)} %shard_map.65.pair.refs_0_), channel_id=1, source_target_pairs={{0,8},{4,12},{8,0},{12,4},{16,24},{20,28},{24,16},{28,20},{1,9},{5... | collective-permute-start | bytes 122888 | tf_op jit(solution)/shard_map/ppermute | solution.py:489
  31.0 0.8 %shard_map.67 = (f32[2,6,64,128]{3,2,1,0:T(8,128)S(1)}, f32[2,64,128]{2,1,0:T(8,128)S(1)}) custom-call(s32[4]{0:T(128)S(1)} %pad_add_fusion.place, f32[4]{0:T(128)S(1)} %copy-done.3, bf16[2,80,128]{2,1,0:T(8,128)(2,1)S(1)} %shard_map.65.pair.refs_0_, bf16[80,128]{1,0:T(8,128)(2,1)S(1)} %collective-permute-done.2.one_got, ...), custom_call_target="tpu_custom_call" | custom-call | flops 8589934592 | bytes 1048576 | tf_op jit(solution)/shard_map/pallas_call | solution.py:574
  31.8 0.7 %collective-permute-done.10.refs_3_ = bf16[2,80,128]{2,1,0:T(8,128)(2,1)S(1)} collective-permute-done((bf16[2,80,128]{2,1,0:T(8,128)(2,1)S(1)}, bf16[2,80,128]{2,1,0:T(8,128)(2,1)S(1)}, u32[]{:S(2)}, u32[]{:S(2)}) %collective-permute-start.10) | collective-permute-done | bytes 40992 | tf_op jit(solution)/shard_map/ppermute | solution.py:489
  32.5 0.9 %collective-permute-done.9.refs_2_ = bf16[2,80,128]{2,1,0:T(8,128)(2,1)S(1)} collective-permute-done((bf16[2,80,128]{2,1,0:T(8,128)(2,1)S(1)}, bf16[2,80,128]{2,1,0:T(8,128)(2,1)S(1)}, u32[]{:S(2)}, u32[]{:S(2)}) %collective-permute-start.9) | collective-permute-done | bytes 40992 | tf_op jit(solution)/shard_map/ppermute | solution.py:489
  33.4 0.0 collective-permute-done.8.refs_1_
  33.4 0.0 collective-permute-done.11.refs_7_
  33.4 3.5 %shard_map.68 = (f32[1,64]{1,0:T(1,128)}, f32[2,64,128]{2,1,0:T(8,128)}) custom-call(s32[4]{0:T(128)S(1)} %pad_add_fusion.place, bf16[2,80,128]{2,1,0:T(8,128)(2,1)S(1)} %shard_map.65.pair.refs_0_, bf16[2,80,128]{2,1,0:T(8,128)(2,1)S(1)} %collective-permute-done.8.refs_1_, bf16[2,80,128]{2,1,0:T(8,128)(2,1)S(1)} %collective-permute-done.9.refs_2_, ...), custom_call_target="tpu_custom_call" | custom-call | flops 10000000 | bytes 5242880 | tf_op jit(solution)/shard_map/pallas_call | solution.py:584
  (12 shorter events, 0.1 us)
Async XLA Ops:
  0.6 5.3 %copy-start = (bf16[64,2,64,128]{3,2,1,0:T(8,128)(2,1)S(1)}, bf16[64,2,64,128]{3,2,1,0:T(8,128)(2,1)}, u32[]{:S(2)}) copy-start(bf16[64,2,64,128]{3,2,1,0:T(8,128)(2,1)} %refs_4_.1) | copy-start | bytes 6291460
  0.6 5.3 %copy-start.1 = (s32[2,64,128]{2,1,0:T(8,128)S(1)}, s32[2,64,128]{2,1,0:T(8,128)}, u32[]{:S(2)}) copy-start(s32[2,64,128]{2,1,0:T(8,128)} %labels_far.1) | copy-start | bytes 196612
  0.7 10.0 %copy-start.2 = (f32[2,64,128]{2,1,0:T(8,128)S(1)}, f32[2,64,128]{2,1,0:T(8,128)}, u32[]{:S(2)}) copy-start(f32[2,64,128]{2,1,0:T(8,128)} %refs_13_.1) | copy-start | bytes 196612
  0.7 10.0 %copy-start.3 = (f32[4]{0:T(128)S(1)}, f32[4]{0:T(128)}, u32[]{:S(2)}) copy-start(f32[4]{0:T(128)} %levels.9) | copy-start | bytes 52
  2.8 11.8 %collective-permute-start = (bf16[65,64,128]{2,1,0:T(8,128)(2,1)S(1)}, bf16[65,64,128]{2,1,0:T(8,128)(2,1)S(1)}, u32[]{:S(2)}, u32[]{:S(2)}) collective-permute-start(bf16[65,64,128]{2,1,0:T(8,128)(2,1)S(1)} %get-tuple-element.20), channel_id=1, source_target_pairs={{0,1},{1,0},{2,3},{3,2},{4,5},{5,4},{6,7},{7,6},{8,9},{9,8},{10,11... | collective-permute-start | bytes 3194888 | tf_op jit(solution)/shard_map/ppermute | solution.py:472
  3.3 12.7 %collective-permute-start.1 = (bf16[66,32,128]{2,1,0:T(8,128)(2,1)S(1)}, bf16[66,32,128]{2,1,0:T(8,128)(2,1)S(1)}, u32[]{:S(2)}, u32[]{:S(2)}) collective-permute-start(bf16[66,32,128]{2,1,0:T(8,128)(2,1)S(1)} %get-tuple-element.22), channel_id=1, source_target_pairs={{0,4},{1,2},{2,1},{3,7},{4,0},{5,6},{6,5},{7,3},{8,12},{9,10},{10,... | collective-permute-start | bytes 1622024 | tf_op jit(solution)/shard_map/ppermute | solution.py:485
  7.1 10.2 %collective-permute-start.3 = (bf16[80,128]{1,0:T(8,128)(2,1)S(1)}, bf16[80,128]{1,0:T(8,128)(2,1)S(1)}, u32[]{:S(2)}, u32[]{:S(2)}) collective-permute-start(bf16[80,128]{1,0:T(8,128)(2,1)S(1)} %get-tuple-element.24.two_pack), channel_id=1, source_target_pairs={{0,28},{4,8},{8,4},{12,16},{16,12},{20,24},{24,20},{28,0},{1,29},{... | collective-permute-start | bytes 61448 | tf_op jit(solution)/shard_map/ppermute | solution.py:472
  10.7 6.6 %collective-permute-start.2 = (bf16[80,128]{1,0:T(8,128)(2,1)S(1)}, bf16[80,128]{1,0:T(8,128)(2,1)S(1)}, u32[]{:S(2)}, u32[]{:S(2)}) collective-permute-start(bf16[80,128]{1,0:T(8,128)(2,1)S(1)} %get-tuple-element.16.after.one_pack), channel_id=1, source_target_pairs={{0,4},{4,0},{8,12},{12,8},{16,20},{20,16},{24,28},{28,24},{1,5},{5... | collective-permute-start | bytes 61448 | tf_op jit(solution)/shard_map/ppermute | solution.py:472
  18.3 1.8 %collective-permute-start.4 = (f32[72,128]{1,0:T(8,128)S(1)}, f32[72,128]{1,0:T(8,128)S(1)}, u32[]{:S(2)}, u32[]{:S(2)}) collective-permute-start(f32[72,128]{1,0:T(8,128)S(1)} %shard_map.64), channel_id=1, source_target_pairs={{0,1},{1,0},{2,3},{3,2},{4,5},{5,4},{6,7},{7,6},{8,9},{9,8},{10,11... | collective-permute-start | bytes 110600 | tf_op jit(solution)/shard_map/ppermute | solution.py:489
  20.0 5.2 %collective-permute-start.7 = (f32[72,128]{1,0:T(8,128)S(1)}, f32[72,128]{1,0:T(8,128)S(1)}, u32[]{:S(2)}, u32[]{:S(2)}) collective-permute-start(f32[72,128]{1,0:T(8,128)S(1)} %add.3.own.after), channel_id=1, source_target_pairs={{0,6},{1,7},{2,4},{3,5},{4,2},{5,3},{6,0},{7,1},{8,14},{9,15},{10,... | collective-permute-start | bytes 110600 | tf_op jit(solution)/shard_map/ppermute | solution.py:497
  22.6 4.0 %collective-permute-start.6 = (f32[72,128]{1,0:T(8,128)S(1)}, f32[72,128]{1,0:T(8,128)S(1)}, u32[]{:S(2)}, u32[]{:S(2)}) collective-permute-start(f32[72,128]{1,0:T(8,128)S(1)} %add.3.own.after), channel_id=1, source_target_pairs={{0,4},{1,5},{2,6},{3,7},{4,0},{5,1},{6,2},{7,3},{8,12},{9,13},{10,... | collective-permute-start | bytes 110600 | tf_op jit(solution)/shard_map/ppermute | solution.py:497
  22.6 4.0 %collective-permute-start.5 = (f32[72,128]{1,0:T(8,128)S(1)}, f32[72,128]{1,0:T(8,128)S(1)}, u32[]{:S(2)}, u32[]{:S(2)}) collective-permute-start(f32[72,128]{1,0:T(8,128)S(1)} %add.3.own.after), channel_id=1, source_target_pairs={{0,2},{1,3},{2,0},{3,1},{4,6},{5,7},{6,4},{7,5},{8,10},{9,11},{10,... | collective-permute-start | bytes 110600 | tf_op jit(solution)/shard_map/ppermute | solution.py:497
  23.5 9.9 %collective-permute-start.11 = (bf16[64,32,128]{2,1,0:T(8,128)(2,1)S(1)}, bf16[64,32,128]{2,1,0:T(8,128)(2,1)S(1)}, u32[]{:S(2)}, u32[]{:S(2)}) collective-permute-start(bf16[64,32,128]{2,1,0:T(8,128)(2,1)S(1)} %shard_map.66), channel_id=1, source_target_pairs={{0,4},{1,2},{2,1},{3,7},{4,0},{5,6},{6,5},{7,3},{8,12},{9,10},{10,... | collective-permute-start | bytes 1572872 | tf_op jit(solution)/shard_map/ppermute | solution.py:485
  26.6 5.9 %collective-permute-start.10 = (bf16[2,80,128]{2,1,0:T(8,128)(2,1)S(1)}, bf16[2,80,128]{2,1,0:T(8,128)(2,1)S(1)}, u32[]{:S(2)}, u32[]{:S(2)}) collective-permute-start(bf16[2,80,128]{2,1,0:T(8,128)(2,1)S(1)} %shard_map.65.pair.refs_0_), channel_id=1, source_target_pairs={{0,24},{4,28},{8,16},{12,20},{16,8},{20,12},{24,0},{28,4},{1,25},{... | collective-permute-start | bytes 122888 | tf_op jit(solution)/shard_map/ppermute | solution.py:489
  27.6 5.8 %collective-permute-start.9 = (bf16[2,80,128]{2,1,0:T(8,128)(2,1)S(1)}, bf16[2,80,128]{2,1,0:T(8,128)(2,1)S(1)}, u32[]{:S(2)}, u32[]{:S(2)}) collective-permute-start(bf16[2,80,128]{2,1,0:T(8,128)(2,1)S(1)} %shard_map.65.pair.refs_0_), channel_id=1, source_target_pairs={{0,16},{4,20},{8,24},{12,28},{16,0},{20,4},{24,8},{28,12},{1,17},{... | collective-permute-start | bytes 122888 | tf_op jit(solution)/shard_map/ppermute | solution.py:489
  28.4 5.0 %collective-permute-start.8 = (bf16[2,80,128]{2,1,0:T(8,128)(2,1)S(1)}, bf16[2,80,128]{2,1,0:T(8,128)(2,1)S(1)}, u32[]{:S(2)}, u32[]{:S(2)}) collective-permute-start(bf16[2,80,128]{2,1,0:T(8,128)(2,1)S(1)} %shard_map.65.pair.refs_0_), channel_id=1, source_target_pairs={{0,8},{4,12},{8,0},{12,4},{16,24},{20,28},{24,16},{28,20},{1,9},{5... | collective-permute-start | bytes 122888 | tf_op jit(solution)/shard_map/ppermute | solution.py:489

commit v7 on v5

--- a/solution.py
+++ b/solution.py
@@ -79,7 +79,7 @@
     pass
 
 
-def prepare_kernel(place, labels, held, planes_out, outer_rest, one_pack, two_pack):
+def prepare_kernel(place, labels, held, outer_rest, one_pack, two_pack):
     modes, planes, rows, layers = held.shape
     half = rows // 2
     width = planes * rows
@@ -104,19 +104,25 @@
             out[at] = jnp.concatenate(
                 [ends[index:index + 1, j * width:(j + 1) * width] for j in range(CHUNK)], axis=0
             ).astype(BF16)
-        for slot, plane in ((0, 1 - side), (1, side)):
-            planes_out[slot, :, at, :] = jnp.swapaxes(held[at, plane], 0, 1)
         outer_rest[at] = held[at, side, pl.ds(pl.multiple_of(side * half, half), half), :]
 
 
 def block_kernel(
-    place, levels, labels, resid, here, partial, weights, half_diag, link_y, link_z,
+    place, levels, labels, resid, zvec, after, partial, weights, here, half_diag, link_y, link_z,
 ):
     planes, rows, layers = labels.shape
     modes = here.shape[2]
     side = lax.rem(place[1], 2)
     at_edge = (place[1] == 0) | (place[1] == place[2] - 1)
     held = (1 - side, side)
+
+    def turn_rows(start):
+        for slot, plane in enumerate(held):
+            for k in range(0, modes, CHUNK):
+                block = zvec[k:k + CHUNK, plane, pl.ds(start, STEP), :]
+                here[slot, pl.ds(start, STEP), k:k + CHUNK, :] = jnp.swapaxes(block, 0, 1)
+
+    turn_rows(0)
     coef = [coefficients(labels[x], levels) for x in held]
     middle = harmonic(coef[0], coef[1])
     weights[0] = middle
@@ -140,6 +146,7 @@
 
     def step(j, carry):
         total, rhs, wide = carry
+        turn_rows(pl.multiple_of(jnp.minimum((j + 1) * STEP, rows - STEP), STEP))
         for u in range(STEP):
             y = j * STEP + u
             at = pl.ds(y, 1)
@@ -225,7 +232,6 @@
     planes, rows, modes, layers = here.shape
     half = rows // 2
     side = lax.rem(place[1], 2)
-    odd = lax.rem(place[0], 2) == 1
     at_edge = (place[1] == 0) | (place[1] == place[2] - 1)
     base = pl.multiple_of(side * half, half)
     turn(outer_got, 0, turned)
@@ -234,6 +240,7 @@
     face[...] = jnp.where(at_edge, weights[6], between)
     face_here[...] = jnp.where(at_edge, 0.0, between)
     cross = face_product(face_here, base, here.at[1], turned)
+    odd = lax.rem(place[0], 2) == 1
 
     def coef_row(pack):
         return coefficients(pack[modes:modes + 16].astype(F32)[0:1], levels)
@@ -247,10 +254,15 @@
     weight_high = harmonic(coef_row(last), coef_row(next_first))
 
     def product(left, right):
-        return lax.dot_general(left, right, NT, precision=PRECISE, preferred_element_type=F32)
+        return lax.dot_general(
+            left.astype(BF16), right.astype(BF16), NT, preferred_element_type=F32
+        )
 
     edge_rows = weight_high * last[:modes]
-    ends = product(weight_low * first[:modes], first[:modes]) + product(edge_rows, last[:modes])
+    ends = product(
+        jnp.concatenate([weight_low * first[:modes], edge_rows], axis=1),
+        jnp.concatenate([first[:modes], last[:modes]], axis=1),
+    )
     square = partial[:modes, :] + 0.5 * (cross + ends)
     out[:modes, :modes] = square + square.T
     out[:modes, modes:] = -product(edge_rows, next_first[:modes])
@@ -328,10 +340,10 @@
 
 
 def finish_kernel(place, *refs):
-    count = len(refs) - 17
+    count = len(refs) - 15
     blocks, refs = refs[:count], refs[count:]
     zvec, inner_got, outer_got, outer_last, picked, terms, middle, inner_face, outer_face, resid = refs[:10]
-    solution, deflated, direction_ref, image_ref, spread, outer_field, fix_ref = refs[10:]
+    solution, deflated, direction_ref, spread, outer_field = refs[10:]
     subs = direction_ref.shape[0]
     modes, planes, rows, layers = zvec.shape
     half = rows // 2
@@ -360,40 +372,54 @@
                 )
         return carry
 
+    def row_is(s, width):
+        return lax.broadcasted_iota(jnp.int32, (subs, width), 0) == s
+
     def load(block, s, carry):
         extra = block[modes:modes + 16, :].astype(F32)
-        direction_ref[pl.ds(s, 1), :] = (extra[0:1] + extra[1:2]) + extra[2:3]
-        fix_ref[pl.ds(s, 1), :] = extra[4:5] - extra[3:4]
-        return carry
-
-    each(load, 0)
-    fix = fix_ref[:, :modes]
+        right = (extra[0:1] + extra[1:2]) + extra[2:3]
+        here = row_is(s, 2 * modes)
+        return jnp.where(here, right, carry[0]), jnp.where(here, extra[4:5] - extra[3:4], carry[1])
+
+    empty = jnp.zeros((subs, 2 * modes), F32)
+    right_side, fix = each(load, (empty, empty))
+    fix = fix[:, :modes]
 
     def turned(rows_of, by):
         by = by % subs
         return jnp.concatenate([rows_of[by:], rows_of[:by]], axis=0)
 
+    def in_parts(value):
+        parts = []
+        for _ in range(3):
+            part = value.astype(BF16)
+            parts.append(part.astype(F32))
+            value = value - parts[-1]
+        return jnp.concatenate(parts, axis=0).astype(BF16)
+
+    def joined(value):
+        return (value[:subs] + value[subs:2 * subs]) + value[2 * subs:]
+
     def coarse_apply(direction):
-        direction_ref[...] = jnp.concatenate([direction, turned(direction, 1)], axis=1)
+        pairs = in_parts(jnp.concatenate([direction, turned(direction, 1)], axis=1))
+        single = pairs[:, :modes]
 
         def one(block, s, carry):
-            values = block[:modes, :].astype(F32)
-            pair = direction_ref[pl.ds(s, 1), :]
-            ahead = jnp.sum(values * pair, axis=1, keepdims=True)
-            image_ref[pl.ds(s, 1), :] = jnp.sum(
-                values * column(pair[:, :modes]), axis=0, keepdims=True
+            values = block[:modes, :]
+            ahead = lax.dot_general(pairs, values, NT, preferred_element_type=F32)
+            image = jnp.dot(single, values, preferred_element_type=F32)
+            return (
+                jnp.where(row_is(s, modes), joined(ahead), carry[0]),
+                jnp.where(row_is(s, 2 * modes), joined(image), carry[1]),
             )
-            return jnp.where(lane_is((modes, 128), s), ahead, carry)
-
-        ahead_all = each(one, jnp.zeros((modes, 128), F32))
-        image = image_ref[...]
-        square_part = ahead_all.T[:subs] + image[:, :modes] + fix * direction
-        return square_part + turned(image[:, modes:], -1)
+
+        ahead, image = each(one, (jnp.zeros((subs, modes), F32), empty))
+        return ahead + image[:, :modes] + fix * direction + turned(image[:, modes:], -1)
 
     def inner(left, right):
         return jnp.sum(jnp.sum(left * right, axis=0, keepdims=True), axis=1, keepdims=True)
 
-    remain = direction_ref[:, :modes]
+    remain = right_side[:, :modes]
     direction = remain
     result = jnp.zeros_like(remain)
     norm_now = inner(remain, remain)
@@ -406,12 +432,12 @@
             norm_next = inner(remain, remain)
             direction = remain + (norm_next / norm_now) * direction
             norm_now = norm_next
-    direction_ref[:, :modes] = result
-    own = direction_ref[pl.ds(me, 1), :modes]
+    direction_ref[...] = result
+    own = direction_ref[pl.ds(me, 1), :]
     solution[...] = own
     spread[...] = jnp.broadcast_to(column(own), (modes, layers))
-    ahead_column = column(direction_ref[pl.ds(lax.rem(me + 1, subs), 1), :modes])
-    behind_column = column(direction_ref[pl.ds(lax.rem(me + subs - 1, subs), 1), :modes])
+    ahead_column = column(direction_ref[pl.ds(lax.rem(me + 1, subs), 1), :])
+    behind_column = column(direction_ref[pl.ds(lax.rem(me + subs - 1, subs), 1), :])
     ahead_row = jnp.sum(ahead_column * picked[0], axis=0, keepdims=True)
     behind_row = jnp.sum(behind_column * picked[1], axis=0, keepdims=True)
     width = planes * rows
@@ -514,9 +540,9 @@
     outer_got = swapped_all(outer_near)
     inner_got = swapped(inner_send, "pln", 0)
     rest = shape((modes, half, layers), BF16)
-    here, outer_rest, one_pack, two_pack = call(
+    outer_rest, one_pack, two_pack = call(
         prepare_kernel,
-        [shape((planes, rows, modes, layers), BF16), rest, pack, pack],
+        [rest, pack, pack],
         [SMEM, VMEM, VMEM],
         flops=10_000_000,
         moved=6 << 20,
@@ -525,14 +551,18 @@
     two_got = swapped(two_pack, "sub", 1)
     field = (planes, rows, layers)
     plane = (rows, layers)
-    partial, weights = call(
+    partial, weights, here = call(
         block_kernel,
-        [shape((modes + 8, modes), F32), shape((7,) + plane, F32)],
-        [SMEM, SMEM] + [VMEM] * 3,
+        [
+            shape((modes + 8, modes), F32),
+            shape((7,) + plane, F32),
+            shape((planes, rows, modes, layers), BF16),
+        ],
+        [SMEM, SMEM] + [VMEM] * 3 + [ANY],
         [pltpu.VMEM(field, F32)] * 3,
         flops=400_000_000,
         moved=3 << 20,
-    )(place, levels, labels, resid, here)
+    )(place, levels, labels, resid, zvec, one_pack)
     turned = pltpu.VMEM((half, modes, layers), BF16)
     partial, inner_face = call(
         inner_kernel,
@@ -576,11 +606,9 @@
             [shape((1, modes), F32), shape(field, F32)],
             [SMEM] + [VMEM] * (10 + len(blocks)),
             [
-                pltpu.VMEM((subs, 2 * modes), F32),
-                pltpu.VMEM((subs, 2 * modes), F32),
+                pltpu.VMEM((subs, modes), F32),
                 pltpu.VMEM((modes, layers), F32),
                 pltpu.VMEM(plane, F32),
-                pltpu.VMEM((subs, 2 * modes), F32),
             ],
             flops=10_000_000,
             moved=5 << 20,

time: 36.8 us -> 36.5 us (level)
  waiting for transfers between devices: 5.08 us -> 3.72 us
  starting transfers between devices: 16.2 us -> 17.3 us
    ppermute x2, starting transfers between devices: 2.6 us -> 4.33 us  [swapped_all(): return lax.ppermute(value, ('sub', 'pln'), pairs)]
    ppermute x3, starting transfers between devices: 5.64 us -> 4.1 us  [swapped(): return lax.ppermute(value, axis, pairs)]
    ppermute x3, waiting for transfers between devices: 2.66 us -> 1.27 us  [partner(): return lax.ppermute(value, ('sub', 'pln'), pairs)]
    pallas_call x1, Pallas kernels: 3.06 us -> 4.02 us  [body(): call(block_kernel, [shape((modes + 8, modes), F32), shape((7,) + plane, F...]
    ppermute x4, starting transfers between devices: 4.52 us -> 5.34 us  [exchanged(): lax.ppermute(value, axis, [(i, i ^ mask) for i in range(lax.axis_size(axi...]
    pallas_call x1, Pallas kernels: 2 us -> 1.23 us  [body(): call(prepare_kernel, [rest, pack, pack], [SMEM, VMEM, VMEM], flops=100000...]
  transfers between devices with their start and end apart: 12 -> 12, of which waited for: 5 -> 4; matrix products, arithmetic and copies ran while one was open for 0% -> 0% of each run, Pallas kernels for 20% -> 20%
where the time goes in v7:
time: 36.5 us; the launch traced here: 36.4 us
  starting transfers between devices  17.3 us (47%)
  Pallas kernels  14.6 us (40%)
  waiting for transfers between devices  3.72 us (10%)
  between operations  0.72 us (2%)
    ppermute x4, starting transfers between devices, exchanged(): lax.ppermute(value, axis, [(i, i ^ mask) for i in range(lax.axis_size(axi...  5.34 us
    ppermute x2, starting transfers between devices, swapped_all(): return lax.ppermute(value, ('sub', 'pln'), pairs)  4.33 us
    ppermute x3, starting transfers between devices, swapped(): return lax.ppermute(value, axis, pairs)  4.1 us
    pallas_call x1, Pallas kernels, body(): call(block_kernel, [shape((modes + 8, modes), F32), shape((7,) + plane, F...  4.02 us
    pallas_call x1, Pallas kernels, body(): call(finish_kernel, [shape((1, modes), F32), shape(field, F32)], [SMEM] +...  3.53 us
    ppermute x3, starting transfers between devices, partner(): return lax.ppermute(value, ('sub', 'pln'), pairs)  3.49 us
    ppermute x4, waiting for transfers between devices, exchanged(): lax.ppermute(value, axis, [(i, i ^ mask) for i in range(lax.axis_size(axi...  2.43 us
    pallas_call x1, Pallas kernels, body(): call(stage_kernel, [shape((modes + 1, rows, layers), BF16), shape((modes...  2.03 us
  transfers between devices with their start and end apart: 12, of which 4 were waited for; matrix products, arithmetic and copies ran while one was open for 0% of the time, Pallas kernels for 20%

profile of v7, /device:TPU:0, one launch (start us, length us, event | category | flops | bytes accessed | tf_op | source)
XLA Modules:
  0.0 36.4 jit_solution(12423126562855151898)
XLA Ops:
  0.6 0.0 copy-start
  0.6 0.0 copy-start.1
  0.7 0.1 pad_add_fusion.place
  0.7 2.0 %shard_map.61 = (bf16[65,64,128]{2,1,0:T(8,128)(2,1)S(1)}, bf16[66,32,128]{2,1,0:T(8,128)(2,1)S(1)}) custom-call(s32[4]{0:T(128)S(1)} %pad_add_fusion.place, s32[2,64,128]{2,1,0:T(8,128)} %labels_far.1, bf16[64,2,64,128]{3,2,1,0:T(8,128)(2,1)} %refs_4_.1), custom_call_target="tpu_custom_call" | custom-call | bytes 2097152 | tf_op jit(solution)/shard_map/pallas_call | solution.py:533
  2.8 0.5 %collective-permute-start = (bf16[65,64,128]{2,1,0:T(8,128)(2,1)S(1)}, bf16[65,64,128]{2,1,0:T(8,128)(2,1)S(1)}, u32[]{:S(2)}, u32[]{:S(2)}) collective-permute-start(bf16[65,64,128]{2,1,0:T(8,128)(2,1)S(1)} %get-tuple-element.20), channel_id=1, source_target_pairs={{0,1},{1,0},{2,3},{3,2},{4,5},{5,4},{6,7},{7,6},{8,9},{9,8},{10,11... | collective-permute-start | bytes 3194888 | tf_op jit(solution)/shard_map/ppermute | solution.py:495
  3.3 2.6 %collective-permute-start.1 = (bf16[66,32,128]{2,1,0:T(8,128)(2,1)S(1)}, bf16[66,32,128]{2,1,0:T(8,128)(2,1)S(1)}, u32[]{:S(2)}, u32[]{:S(2)}) collective-permute-start(bf16[66,32,128]{2,1,0:T(8,128)(2,1)S(1)} %get-tuple-element.22), channel_id=1, source_target_pairs={{0,4},{1,2},{2,1},{3,7},{4,0},{5,6},{6,5},{7,3},{8,12},{9,10},{10,... | collective-permute-start | bytes 1622024 | tf_op jit(solution)/shard_map/ppermute | solution.py:508
  5.9 1.2 %shard_map.59 = (bf16[64,32,128]{2,1,0:T(8,128)(2,1)S(1)}, bf16[80,128]{1,0:T(8,128)(2,1)S(1)}, bf16[80,128]{1,0:T(8,128)(2,1)S(1)}) custom-call(s32[4]{0:T(128)S(1)} %pad_add_fusion.place, s32[2,64,128]{2,1,0:T(8,128)S(1)} %copy-done.1, bf16[64,2,64,128]{3,2,1,0:T(8,128)(2,1)S(1)} %copy-done), custom_call_target="tpu_custom_call" | custom-call | flops 10000000 | bytes 6291456 | tf_op jit(solution)/shard_map/pallas_call | solution.py:543
  7.1 3.6 %collective-permute-start.3 = (bf16[80,128]{1,0:T(8,128)(2,1)S(1)}, bf16[80,128]{1,0:T(8,128)(2,1)S(1)}, u32[]{:S(2)}, u32[]{:S(2)}) collective-permute-start(bf16[80,128]{1,0:T(8,128)(2,1)S(1)} %get-tuple-element.23.two_pack), channel_id=1, source_target_pairs={{0,28},{4,8},{8,4},{12,16},{16,12},{20,24},{24,20},{28,0},{1,29},{... | collective-permute-start | bytes 61448 | tf_op jit(solution)/shard_map/ppermute | solution.py:495
  10.7 0.0 collective-permute-start.2
  10.7 4.0 %shard_map.60 = (f32[72,64]{1,0:T(8,128)S(1)}, f32[7,64,128]{2,1,0:T(8,128)S(1)}, bf16[2,64,64,128]{3,2,1,0:T(8,128)(2,1)S(1)}) custom-call(s32[4]{0:T(128)S(1)} %pad_add_fusion.place, f32[4]{0:T(128)S(1)} %copy-done.3, s32[2,64,128]{2,1,0:T(8,128)S(1)} %copy-done.1, f32[2,64,128]{2,1,0:T(8,128)S(1)} %copy-done.2, bf16[64,2,64,128]{3,2,1,0:T(8,128)(2,1)S(1)} %copy-done, ...), custom_call_target="tpu_custom_call" | custom-call | flops 400000000 | bytes 3145728 | tf_op jit(solution)/shard_map/pallas_call | solution.py:554
  14.7 0.0 collective-permute-done.inner_got.refs_5_
  14.7 1.4 %shard_map.62 = (f32[72,64]{1,0:T(8,128)S(1)}, f32[64,128]{1,0:T(8,128)S(1)}) custom-call(s32[4]{0:T(128)S(1)} %pad_add_fusion.place, f32[4]{0:T(128)S(1)} %copy-done.3, f32[72,64]{1,0:T(8,128)S(1)} %get-tuple-element.17.partial, f32[7,64,128]{2,1,0:T(8,128)S(1)} %get-tuple-element.18.weights.refs_10_, bf16[2,64,64,128]{3,2,1,0:T(8,128)(2,1)S(1)} %get-tuple-element.19.here, ...), custom_call_target="tpu_custom_call" | custom-call | flops 100000000 | bytes 1048576 | tf_op jit(solution)/shard_map/pallas_call | solution.py:567
  16.1 0.0 collective-permute-done.3.two_got
  16.1 0.0 collective-permute-done.2.one_got
  16.1 1.6 %shard_map.63 = (f32[72,128]{1,0:T(8,128)S(1)}, f32[64,128]{1,0:T(8,128)S(1)}) custom-call(s32[4]{0:T(128)S(1)} %pad_add_fusion.place, f32[4]{0:T(128)S(1)} %copy-done.3, f32[72,64]{1,0:T(8,128)S(1)} %get-tuple-element.21.partial, f32[7,64,128]{2,1,0:T(8,128)S(1)} %get-tuple-element.18.weights.refs_10_, bf16[2,64,64,128]{3,2,1,0:T(8,128)(2,1)S(1)} %get-tuple-element.19.here, ...), custom_call_target="tpu_custom_call" | custom-call | flops 100000000 | bytes 1048576 | tf_op jit(solution)/shard_map/pallas_call | solution.py:575
  17.7 0.9 %collective-permute-start.4 = (f32[72,128]{1,0:T(8,128)S(1)}, f32[72,128]{1,0:T(8,128)S(1)}, u32[]{:S(2)}, u32[]{:S(2)}) collective-permute-start(f32[72,128]{1,0:T(8,128)S(1)} %get-tuple-element.24), channel_id=1, source_target_pairs={{0,1},{1,0},{2,3},{3,2},{4,5},{5,4},{6,7},{7,6},{8,9},{9,8},{10,11... | collective-permute-start | bytes 110600 | tf_op jit(solution)/shard_map/ppermute | solution.py:512
  18.6 0.9 %collective-permute-done.4 = f32[72,128]{1,0:T(8,128)S(1)} collective-permute-done((f32[72,128]{1,0:T(8,128)S(1)}, f32[72,128]{1,0:T(8,128)S(1)}, u32[]{:S(2)}, u32[]{:S(2)}) %collective-permute-start.4) | collective-permute-done | bytes 36896 | tf_op jit(solution)/shard_map/ppermute | solution.py:512
  19.5 2.5 %collective-permute-start.7 = (f32[72,128]{1,0:T(8,128)S(1)}, f32[72,128]{1,0:T(8,128)S(1)}, u32[]{:S(2)}, u32[]{:S(2)}) collective-permute-start(f32[72,128]{1,0:T(8,128)S(1)} %add.3.own.after), channel_id=1, source_target_pairs={{0,6},{1,7},{2,4},{3,5},{4,2},{5,3},{6,0},{7,1},{8,14},{9,15},{10,... | collective-permute-start | bytes 110600 | tf_op jit(solution)/shard_map/ppermute | solution.py:520
  22.0 0.0 collective-permute-start.6
  22.0 0.9 %collective-permute-start.5 = (f32[72,128]{1,0:T(8,128)S(1)}, f32[72,128]{1,0:T(8,128)S(1)}, u32[]{:S(2)}, u32[]{:S(2)}) collective-permute-start(f32[72,128]{1,0:T(8,128)S(1)} %add.3.own.after), channel_id=1, source_target_pairs={{0,2},{1,3},{2,0},{3,1},{4,6},{5,7},{6,4},{7,5},{8,10},{9,11},{10,... | collective-permute-start | bytes 110600 | tf_op jit(solution)/shard_map/ppermute | solution.py:520
  23.0 1.7 %collective-permute-start.11 = (bf16[64,32,128]{2,1,0:T(8,128)(2,1)S(1)}, bf16[64,32,128]{2,1,0:T(8,128)(2,1)S(1)}, u32[]{:S(2)}, u32[]{:S(2)}) collective-permute-start(bf16[64,32,128]{2,1,0:T(8,128)(2,1)S(1)} %shard_map.65), channel_id=1, source_target_pairs={{0,4},{1,2},{2,1},{3,7},{4,0},{5,6},{6,5},{7,3},{8,12},{9,10},{10,... | collective-permute-start | bytes 1572872 | tf_op jit(solution)/shard_map/ppermute | solution.py:508
  24.7 1.3 %collective-permute-done.6.beside = f32[72,128]{1,0:T(8,128)S(1)} collective-permute-done((f32[72,128]{1,0:T(8,128)S(1)}, f32[72,128]{1,0:T(8,128)S(1)}, u32[]{:S(2)}, u32[]{:S(2)}) %collective-permute-start.6) | collective-permute-done | bytes 36896 | tf_op jit(solution)/shard_map/ppermute | solution.py:520
  26.0 0.0 collective-permute-done.5.across
  26.0 1.0 %collective-permute-start.10 = (bf16[2,80,128]{2,1,0:T(8,128)(2,1)S(1)}, bf16[2,80,128]{2,1,0:T(8,128)(2,1)S(1)}, u32[]{:S(2)}, u32[]{:S(2)}) collective-permute-start(bf16[2,80,128]{2,1,0:T(8,128)(2,1)S(1)} %shard_map.64.pair.refs_0_), channel_id=1, source_target_pairs={{0,24},{4,28},{8,16},{12,20},{16,8},{20,12},{24,0},{28,4},{1,25},{... | collective-permute-start | bytes 122888 | tf_op jit(solution)/shard_map/ppermute | solution.py:512
  27.0 0.8 %collective-permute-start.9 = (bf16[2,80,128]{2,1,0:T(8,128)(2,1)S(1)}, bf16[2,80,128]{2,1,0:T(8,128)(2,1)S(1)}, u32[]{:S(2)}, u32[]{:S(2)}) collective-permute-start(bf16[2,80,128]{2,1,0:T(8,128)(2,1)S(1)} %shard_map.64.pair.refs_0_), channel_id=1, source_target_pairs={{0,16},{4,20},{8,24},{12,28},{16,0},{20,4},{24,8},{28,12},{1,17},{... | collective-permute-start | bytes 122888 | tf_op jit(solution)/shard_map/ppermute | solution.py:512
  27.8 2.7 %collective-permute-start.8 = (bf16[2,80,128]{2,1,0:T(8,128)(2,1)S(1)}, bf16[2,80,128]{2,1,0:T(8,128)(2,1)S(1)}, u32[]{:S(2)}, u32[]{:S(2)}) collective-permute-start(bf16[2,80,128]{2,1,0:T(8,128)(2,1)S(1)} %shard_map.64.pair.refs_0_), channel_id=1, source_target_pairs={{0,8},{4,12},{8,0},{12,4},{16,24},{20,28},{24,16},{28,20},{1,9},{5... | collective-permute-start | bytes 122888 | tf_op jit(solution)/shard_map/ppermute | solution.py:512
  30.5 0.8 %shard_map.66 = (f32[2,6,64,128]{3,2,1,0:T(8,128)S(1)}, f32[2,64,128]{2,1,0:T(8,128)S(1)}) custom-call(s32[4]{0:T(128)S(1)} %pad_add_fusion.place, f32[4]{0:T(128)S(1)} %copy-done.3, bf16[2,80,128]{2,1,0:T(8,128)(2,1)S(1)} %shard_map.64.pair.refs_0_, bf16[80,128]{1,0:T(8,128)(2,1)S(1)} %collective-permute-done.2.one_got, ...), custom_call_target="tpu_custom_call" | custom-call | flops 8589934592 | bytes 1048576 | tf_op jit(solution)/shard_map/pallas_call | solution.py:594
  31.3 0.7 %collective-permute-done.10.refs_3_ = bf16[2,80,128]{2,1,0:T(8,128)(2,1)S(1)} collective-permute-done((bf16[2,80,128]{2,1,0:T(8,128)(2,1)S(1)}, bf16[2,80,128]{2,1,0:T(8,128)(2,1)S(1)}, u32[]{:S(2)}, u32[]{:S(2)}) %collective-permute-start.10) | collective-permute-done | bytes 40992 | tf_op jit(solution)/shard_map/ppermute | solution.py:512
  31.9 0.9 %collective-permute-done.9.refs_2_ = bf16[2,80,128]{2,1,0:T(8,128)(2,1)S(1)} collective-permute-done((bf16[2,80,128]{2,1,0:T(8,128)(2,1)S(1)}, bf16[2,80,128]{2,1,0:T(8,128)(2,1)S(1)}, u32[]{:S(2)}, u32[]{:S(2)}) %collective-permute-start.9) | collective-permute-done | bytes 40992 | tf_op jit(solution)/shard_map/ppermute | solution.py:512
  32.8 0.0 collective-permute-done.8.refs_1_
  32.9 0.0 collective-permute-done.11.refs_7_
  32.9 3.5 %shard_map.67 = (f32[1,64]{1,0:T(1,128)}, f32[2,64,128]{2,1,0:T(8,128)}) custom-call(s32[4]{0:T(128)S(1)} %pad_add_fusion.place, bf16[2,80,128]{2,1,0:T(8,128)(2,1)S(1)} %shard_map.64.pair.refs_0_, bf16[2,80,128]{2,1,0:T(8,128)(2,1)S(1)} %collective-permute-done.8.refs_1_, bf16[2,80,128]{2,1,0:T(8,128)(2,1)S(1)} %collective-permute-done.9.refs_2_, ...), custom_call_target="tpu_custom_call" | custom-call | flops 10000000 | bytes 5242880 | tf_op jit(solution)/shard_map/pallas_call | solution.py:604
  (11 shorter events, 0.1 us)
Async XLA Ops:
  0.6 5.3 %copy-start = (bf16[64,2,64,128]{3,2,1,0:T(8,128)(2,1)S(1)}, bf16[64,2,64,128]{3,2,1,0:T(8,128)(2,1)}, u32[]{:S(2)}) copy-start(bf16[64,2,64,128]{3,2,1,0:T(8,128)(2,1)} %refs_4_.1) | copy-start | bytes 6291460
  0.6 5.3 %copy-start.1 = (s32[2,64,128]{2,1,0:T(8,128)S(1)}, s32[2,64,128]{2,1,0:T(8,128)}, u32[]{:S(2)}) copy-start(s32[2,64,128]{2,1,0:T(8,128)} %labels_far.1) | copy-start | bytes 196612
  0.7 10.0 %copy-start.2 = (f32[2,64,128]{2,1,0:T(8,128)S(1)}, f32[2,64,128]{2,1,0:T(8,128)}, u32[]{:S(2)}) copy-start(f32[2,64,128]{2,1,0:T(8,128)} %refs_13_.1) | copy-start | bytes 196612
  0.7 10.0 %copy-start.3 = (f32[4]{0:T(128)S(1)}, f32[4]{0:T(128)}, u32[]{:S(2)}) copy-start(f32[4]{0:T(128)} %levels.7) | copy-start | bytes 52
  2.8 12.0 %collective-permute-start = (bf16[65,64,128]{2,1,0:T(8,128)(2,1)S(1)}, bf16[65,64,128]{2,1,0:T(8,128)(2,1)S(1)}, u32[]{:S(2)}, u32[]{:S(2)}) collective-permute-start(bf16[65,64,128]{2,1,0:T(8,128)(2,1)S(1)} %get-tuple-element.20), channel_id=1, source_target_pairs={{0,1},{1,0},{2,3},{3,2},{4,5},{5,4},{6,7},{7,6},{8,9},{9,8},{10,11... | collective-permute-start | bytes 3194888 | tf_op jit(solution)/shard_map/ppermute | solution.py:495
  3.3 12.8 %collective-permute-start.1 = (bf16[66,32,128]{2,1,0:T(8,128)(2,1)S(1)}, bf16[66,32,128]{2,1,0:T(8,128)(2,1)S(1)}, u32[]{:S(2)}, u32[]{:S(2)}) collective-permute-start(bf16[66,32,128]{2,1,0:T(8,128)(2,1)S(1)} %get-tuple-element.22), channel_id=1, source_target_pairs={{0,4},{1,2},{2,1},{3,7},{4,0},{5,6},{6,5},{7,3},{8,12},{9,10},{10,... | collective-permute-start | bytes 1622024 | tf_op jit(solution)/shard_map/ppermute | solution.py:508
  7.1 9.0 %collective-permute-start.3 = (bf16[80,128]{1,0:T(8,128)(2,1)S(1)}, bf16[80,128]{1,0:T(8,128)(2,1)S(1)}, u32[]{:S(2)}, u32[]{:S(2)}) collective-permute-start(bf16[80,128]{1,0:T(8,128)(2,1)S(1)} %get-tuple-element.23.two_pack), channel_id=1, source_target_pairs={{0,28},{4,8},{8,4},{12,16},{16,12},{20,24},{24,20},{28,0},{1,29},{... | collective-permute-start | bytes 61448 | tf_op jit(solution)/shard_map/ppermute | solution.py:495
  10.7 5.4 %collective-permute-start.2 = (bf16[80,128]{1,0:T(8,128)(2,1)S(1)}, bf16[80,128]{1,0:T(8,128)(2,1)S(1)}, u32[]{:S(2)}, u32[]{:S(2)}) collective-permute-start(bf16[80,128]{1,0:T(8,128)(2,1)S(1)} %get-tuple-element.16.after.one_pack), channel_id=1, source_target_pairs={{0,4},{4,0},{8,12},{12,8},{16,20},{20,16},{24,28},{28,24},{1,5},{5... | collective-permute-start | bytes 61448 | tf_op jit(solution)/shard_map/ppermute | solution.py:495
  17.7 1.8 %collective-permute-start.4 = (f32[72,128]{1,0:T(8,128)S(1)}, f32[72,128]{1,0:T(8,128)S(1)}, u32[]{:S(2)}, u32[]{:S(2)}) collective-permute-start(f32[72,128]{1,0:T(8,128)S(1)} %get-tuple-element.24), channel_id=1, source_target_pairs={{0,1},{1,0},{2,3},{3,2},{4,5},{5,4},{6,7},{7,6},{8,9},{9,8},{10,11... | collective-permute-start | bytes 110600 | tf_op jit(solution)/shard_map/ppermute | solution.py:512
  19.5 5.2 %collective-permute-start.7 = (f32[72,128]{1,0:T(8,128)S(1)}, f32[72,128]{1,0:T(8,128)S(1)}, u32[]{:S(2)}, u32[]{:S(2)}) collective-permute-start(f32[72,128]{1,0:T(8,128)S(1)} %add.3.own.after), channel_id=1, source_target_pairs={{0,6},{1,7},{2,4},{3,5},{4,2},{5,3},{6,0},{7,1},{8,14},{9,15},{10,... | collective-permute-start | bytes 110600 | tf_op jit(solution)/shard_map/ppermute | solution.py:520
  22.0 4.0 %collective-permute-start.6 = (f32[72,128]{1,0:T(8,128)S(1)}, f32[72,128]{1,0:T(8,128)S(1)}, u32[]{:S(2)}, u32[]{:S(2)}) collective-permute-start(f32[72,128]{1,0:T(8,128)S(1)} %add.3.own.after), channel_id=1, source_target_pairs={{0,4},{1,5},{2,6},{3,7},{4,0},{5,1},{6,2},{7,3},{8,12},{9,13},{10,... | collective-permute-start | bytes 110600 | tf_op jit(solution)/shard_map/ppermute | solution.py:520
  22.0 4.0 %collective-permute-start.5 = (f32[72,128]{1,0:T(8,128)S(1)}, f32[72,128]{1,0:T(8,128)S(1)}, u32[]{:S(2)}, u32[]{:S(2)}) collective-permute-start(f32[72,128]{1,0:T(8,128)S(1)} %add.3.own.after), channel_id=1, source_target_pairs={{0,2},{1,3},{2,0},{3,1},{4,6},{5,7},{6,4},{7,5},{8,10},{9,11},{10,... | collective-permute-start | bytes 110600 | tf_op jit(solution)/shard_map/ppermute | solution.py:520
  23.0 9.9 %collective-permute-start.11 = (bf16[64,32,128]{2,1,0:T(8,128)(2,1)S(1)}, bf16[64,32,128]{2,1,0:T(8,128)(2,1)S(1)}, u32[]{:S(2)}, u32[]{:S(2)}) collective-permute-start(bf16[64,32,128]{2,1,0:T(8,128)(2,1)S(1)} %shard_map.65), channel_id=1, source_target_pairs={{0,4},{1,2},{2,1},{3,7},{4,0},{5,6},{6,5},{7,3},{8,12},{9,10},{10,... | collective-permute-start | bytes 1572872 | tf_op jit(solution)/shard_map/ppermute | solution.py:508
  26.0 5.9 %collective-permute-start.10 = (bf16[2,80,128]{2,1,0:T(8,128)(2,1)S(1)}, bf16[2,80,128]{2,1,0:T(8,128)(2,1)S(1)}, u32[]{:S(2)}, u32[]{:S(2)}) collective-permute-start(bf16[2,80,128]{2,1,0:T(8,128)(2,1)S(1)} %shard_map.64.pair.refs_0_), channel_id=1, source_target_pairs={{0,24},{4,28},{8,16},{12,20},{16,8},{20,12},{24,0},{28,4},{1,25},{... | collective-permute-start | bytes 122888 | tf_op jit(solution)/shard_map/ppermute | solution.py:512
  27.0 5.8 %collective-permute-start.9 = (bf16[2,80,128]{2,1,0:T(8,128)(2,1)S(1)}, bf16[2,80,128]{2,1,0:T(8,128)(2,1)S(1)}, u32[]{:S(2)}, u32[]{:S(2)}) collective-permute-start(bf16[2,80,128]{2,1,0:T(8,128)(2,1)S(1)} %shard_map.64.pair.refs_0_), channel_id=1, source_target_pairs={{0,16},{4,20},{8,24},{12,28},{16,0},{20,4},{24,8},{28,12},{1,17},{... | collective-permute-start | bytes 122888 | tf_op jit(solution)/shard_map/ppermute | solution.py:512
  27.8 5.1 %collective-permute-start.8 = (bf16[2,80,128]{2,1,0:T(8,128)(2,1)S(1)}, bf16[2,80,128]{2,1,0:T(8,128)(2,1)S(1)}, u32[]{:S(2)}, u32[]{:S(2)}) collective-permute-start(bf16[2,80,128]{2,1,0:T(8,128)(2,1)S(1)} %shard_map.64.pair.refs_0_), channel_id=1, source_target_pairs={{0,8},{4,12},{8,0},{12,4},{16,24},{20,28},{24,16},{28,20},{1,9},{5... | collective-permute-start | bytes 122888 | tf_op jit(solution)/shard_map/ppermute | solution.py:512

commit v8 on v7

--- a/solution.py
+++ b/solution.py
@@ -583,9 +583,9 @@
     packed = (modes + 16, 2 * modes)
     if parts == 4 and subs == 8:
         block = block + exchanged(block, "pln", 1)
-        others = [partner(block, *masks) for masks in ((0, 2), (1, 0), (1, 2))]
+        others = [partner(block, *masks) for masks in ((0, 3), (1, 1), (1, 3))]
         [pair] = call(pair_kernel, [shape((2,) + packed, BF16)], [VMEM] * 4)(block, *others)
-        blocks = [pair] + [exchanged(pair, "sub", mask) for mask in (2, 4, 6)]
+        blocks = [pair] + [partner(pair, mask, 1) for mask in (2, 4, 6)]
     else:
         [single] = call(single_kernel, [shape(packed, BF16)], [VMEM])(lax.psum(block, "pln"))
         blocks = [lax.all_gather(single, "sub")]

time: 36.5 us -> 36.4 us (level)
  starting transfers between devices: 17.3 us -> 16.6 us
  waiting for transfers between devices: 3.72 us -> 4.2 us
    ppermute x4 -> x1, starting transfers between devices: 5.34 us -> 0.89 us  [exchanged(): lax.ppermute(value, axis, [(i, i ^ mask) for i in range(lax.axis_size(axi...]
    ppermute x3 -> x6, starting transfers between devices: 3.49 us -> 7.29 us  [partner(): return lax.ppermute(value, ('sub', 'pln'), pairs)]
    ppermute x3 -> x6, waiting for transfers between devices: 1.27 us -> 3.32 us  [partner(): return lax.ppermute(value, ('sub', 'pln'), pairs)]
    ppermute x4 -> x1, waiting for transfers between devices: 2.43 us -> 0.87 us  [exchanged(): lax.ppermute(value, axis, [(i, i ^ mask) for i in range(lax.axis_size(axi...]
  transfers between devices with their start and end apart: 12 -> 12, of which waited for: 4 -> 4; matrix products, arithmetic and copies ran while one was open for 0% -> 0% of each run, Pallas kernels for 20% -> 21%
where the time goes in v8:
time: 36.4 us; the launch traced here: 36.2 us
  starting transfers between devices  16.6 us (46%)
  Pallas kernels  14.6 us (40%)
  waiting for transfers between devices  4.2 us (12%)
  between operations  0.72 us (2%)
    ppermute x6, starting transfers between devices, partner(): return lax.ppermute(value, ('sub', 'pln'), pairs)  7.29 us
    ppermute x2, starting transfers between devices, swapped_all(): return lax.ppermute(value, ('sub', 'pln'), pairs)  4.33 us
    ppermute x3, starting transfers between devices, swapped(): return lax.ppermute(value, axis, pairs)  4.1 us
    pallas_call x1, Pallas kernels, body(): call(block_kernel, [shape((modes + 8, modes), F32), shape((7,) + plane, F...  4.02 us
    pallas_call x1, Pallas kernels, body(): call(finish_kernel, [shape((1, modes), F32), shape(field, F32)], [SMEM] +...  3.53 us
    ppermute x6, waiting for transfers between devices, partner(): return lax.ppermute(value, ('sub', 'pln'), pairs)  3.32 us
    pallas_call x1, Pallas kernels, body(): call(stage_kernel, [shape((modes + 1, rows, layers), BF16), shape((modes...  2.03 us
    pallas_call x1, Pallas kernels, body(): call(outer_kernel, [shape((modes + 8, 2 * modes), F32), shape(plane, F32)...  1.58 us
  transfers between devices with their start and end apart: 12, of which 4 were waited for; matrix products, arithmetic and copies ran while one was open for 0% of the time, Pallas kernels for 21%

profile of v8, /device:TPU:0, one launch (start us, length us, event | category | flops | bytes accessed | tf_op | source)
XLA Modules:
  0.0 36.2 jit_solution(2717706232357897364)
XLA Ops:
  0.6 0.0 copy-start
  0.6 0.0 copy-start.1
  0.7 0.1 pad_add_fusion.place
  0.7 2.0 %shard_map.61 = (bf16[65,64,128]{2,1,0:T(8,128)(2,1)S(1)}, bf16[66,32,128]{2,1,0:T(8,128)(2,1)S(1)}) custom-call(s32[4]{0:T(128)S(1)} %pad_add_fusion.place, s32[2,64,128]{2,1,0:T(8,128)} %labels_far.1, bf16[64,2,64,128]{3,2,1,0:T(8,128)(2,1)} %refs_4_.1), custom_call_target="tpu_custom_call" | custom-call | bytes 2097152 | tf_op jit(solution)/shard_map/pallas_call | solution.py:533
  2.8 0.5 %collective-permute-start = (bf16[65,64,128]{2,1,0:T(8,128)(2,1)S(1)}, bf16[65,64,128]{2,1,0:T(8,128)(2,1)S(1)}, u32[]{:S(2)}, u32[]{:S(2)}) collective-permute-start(bf16[65,64,128]{2,1,0:T(8,128)(2,1)S(1)} %get-tuple-element.20), channel_id=1, source_target_pairs={{0,1},{1,0},{2,3},{3,2},{4,5},{5,4},{6,7},{7,6},{8,9},{9,8},{10,11... | collective-permute-start | bytes 3194888 | tf_op jit(solution)/shard_map/ppermute | solution.py:495
  3.3 2.6 %collective-permute-start.1 = (bf16[66,32,128]{2,1,0:T(8,128)(2,1)S(1)}, bf16[66,32,128]{2,1,0:T(8,128)(2,1)S(1)}, u32[]{:S(2)}, u32[]{:S(2)}) collective-permute-start(bf16[66,32,128]{2,1,0:T(8,128)(2,1)S(1)} %get-tuple-element.22), channel_id=1, source_target_pairs={{0,4},{1,2},{2,1},{3,7},{4,0},{5,6},{6,5},{7,3},{8,12},{9,10},{10,... | collective-permute-start | bytes 1622024 | tf_op jit(solution)/shard_map/ppermute | solution.py:508
  5.9 1.2 %shard_map.59 = (bf16[64,32,128]{2,1,0:T(8,128)(2,1)S(1)}, bf16[80,128]{1,0:T(8,128)(2,1)S(1)}, bf16[80,128]{1,0:T(8,128)(2,1)S(1)}) custom-call(s32[4]{0:T(128)S(1)} %pad_add_fusion.place, s32[2,64,128]{2,1,0:T(8,128)S(1)} %copy-done.1, bf16[64,2,64,128]{3,2,1,0:T(8,128)(2,1)S(1)} %copy-done), custom_call_target="tpu_custom_call" | custom-call | flops 10000000 | bytes 6291456 | tf_op jit(solution)/shard_map/pallas_call | solution.py:543
  7.1 3.6 %collective-permute-start.3 = (bf16[80,128]{1,0:T(8,128)(2,1)S(1)}, bf16[80,128]{1,0:T(8,128)(2,1)S(1)}, u32[]{:S(2)}, u32[]{:S(2)}) collective-permute-start(bf16[80,128]{1,0:T(8,128)(2,1)S(1)} %get-tuple-element.23.two_pack), channel_id=1, source_target_pairs={{0,28},{4,8},{8,4},{12,16},{16,12},{20,24},{24,20},{28,0},{1,29},{... | collective-permute-start | bytes 61448 | tf_op jit(solution)/shard_map/ppermute | solution.py:495
  10.7 0.0 collective-permute-start.2
  10.7 4.0 %shard_map.60 = (f32[72,64]{1,0:T(8,128)S(1)}, f32[7,64,128]{2,1,0:T(8,128)S(1)}, bf16[2,64,64,128]{3,2,1,0:T(8,128)(2,1)S(1)}) custom-call(s32[4]{0:T(128)S(1)} %pad_add_fusion.place, f32[4]{0:T(128)S(1)} %copy-done.3, s32[2,64,128]{2,1,0:T(8,128)S(1)} %copy-done.1, f32[2,64,128]{2,1,0:T(8,128)S(1)} %copy-done.2, bf16[64,2,64,128]{3,2,1,0:T(8,128)(2,1)S(1)} %copy-done, ...), custom_call_target="tpu_custom_call" | custom-call | flops 400000000 | bytes 3145728 | tf_op jit(solution)/shard_map/pallas_call | solution.py:554
  14.7 0.0 collective-permute-done.inner_got.refs_5_
  14.7 1.4 %shard_map.62 = (f32[72,64]{1,0:T(8,128)S(1)}, f32[64,128]{1,0:T(8,128)S(1)}) custom-call(s32[4]{0:T(128)S(1)} %pad_add_fusion.place, f32[4]{0:T(128)S(1)} %copy-done.3, f32[72,64]{1,0:T(8,128)S(1)} %get-tuple-element.17.partial, f32[7,64,128]{2,1,0:T(8,128)S(1)} %get-tuple-element.18.weights.refs_10_, bf16[2,64,64,128]{3,2,1,0:T(8,128)(2,1)S(1)} %get-tuple-element.19.here, ...), custom_call_target="tpu_custom_call" | custom-call | flops 100000000 | bytes 1048576 | tf_op jit(solution)/shard_map/pallas_call | solution.py:567
  16.1 0.0 collective-permute-done.3.two_got
  16.1 0.0 collective-permute-done.2.one_got
  16.1 0.0 collective-permute-done.1.outer_got.refs_6_
  16.1 1.6 %shard_map.63 = (f32[72,128]{1,0:T(8,128)S(1)}, f32[64,128]{1,0:T(8,128)S(1)}) custom-call(s32[4]{0:T(128)S(1)} %pad_add_fusion.place, f32[4]{0:T(128)S(1)} %copy-done.3, f32[72,64]{1,0:T(8,128)S(1)} %get-tuple-element.21.partial, f32[7,64,128]{2,1,0:T(8,128)S(1)} %get-tuple-element.18.weights.refs_10_, bf16[2,64,64,128]{3,2,1,0:T(8,128)(2,1)S(1)} %get-tuple-element.19.here, ...), custom_call_target="tpu_custom_call" | custom-call | flops 100000000 | bytes 1048576 | tf_op jit(solution)/shard_map/pallas_call | solution.py:575
  17.7 0.9 %collective-permute-start.4 = (f32[72,128]{1,0:T(8,128)S(1)}, f32[72,128]{1,0:T(8,128)S(1)}, u32[]{:S(2)}, u32[]{:S(2)}) collective-permute-start(f32[72,128]{1,0:T(8,128)S(1)} %get-tuple-element.24), channel_id=1, source_target_pairs={{0,1},{1,0},{2,3},{3,2},{4,5},{5,4},{6,7},{7,6},{8,9},{9,8},{10,11... | collective-permute-start | bytes 110600 | tf_op jit(solution)/shard_map/ppermute | solution.py:512
  18.6 0.9 %collective-permute-done.4 = f32[72,128]{1,0:T(8,128)S(1)} collective-permute-done((f32[72,128]{1,0:T(8,128)S(1)}, f32[72,128]{1,0:T(8,128)S(1)}, u32[]{:S(2)}, u32[]{:S(2)}) %collective-permute-start.4) | collective-permute-done | bytes 36896 | tf_op jit(solution)/shard_map/ppermute | solution.py:512
  19.5 2.3 %collective-permute-start.7 = (f32[72,128]{1,0:T(8,128)S(1)}, f32[72,128]{1,0:T(8,128)S(1)}, u32[]{:S(2)}, u32[]{:S(2)}) collective-permute-start(f32[72,128]{1,0:T(8,128)S(1)} %add.3.own.after), channel_id=1, source_target_pairs={{0,7},{1,6},{2,5},{3,4},{4,3},{5,2},{6,1},{7,0},{8,15},{9,14},{10,... | collective-permute-start | bytes 110600 | tf_op jit(solution)/shard_map/ppermute | solution.py:520
  21.8 0.0 collective-permute-start.6
  21.8 0.9 %collective-permute-start.5 = (f32[72,128]{1,0:T(8,128)S(1)}, f32[72,128]{1,0:T(8,128)S(1)}, u32[]{:S(2)}, u32[]{:S(2)}) collective-permute-start(f32[72,128]{1,0:T(8,128)S(1)} %add.3.own.after), channel_id=1, source_target_pairs={{0,3},{1,2},{2,1},{3,0},{4,7},{5,6},{6,5},{7,4},{8,11},{9,10},{10,... | collective-permute-start | bytes 110600 | tf_op jit(solution)/shard_map/ppermute | solution.py:520
  22.7 1.7 %collective-permute-start.11 = (bf16[64,32,128]{2,1,0:T(8,128)(2,1)S(1)}, bf16[64,32,128]{2,1,0:T(8,128)(2,1)S(1)}, u32[]{:S(2)}, u32[]{:S(2)}) collective-permute-start(bf16[64,32,128]{2,1,0:T(8,128)(2,1)S(1)} %shard_map.65), channel_id=1, source_target_pairs={{0,4},{1,2},{2,1},{3,7},{4,0},{5,6},{6,5},{7,3},{8,12},{9,10},{10,... | collective-permute-start | bytes 1572872 | tf_op jit(solution)/shard_map/ppermute | solution.py:508
  24.4 0.0 collective-permute-done.7.oblique
  24.4 0.8 %collective-permute-done.6.beside = f32[72,128]{1,0:T(8,128)S(1)} collective-permute-done((f32[72,128]{1,0:T(8,128)S(1)}, f32[72,128]{1,0:T(8,128)S(1)}, u32[]{:S(2)}, u32[]{:S(2)}) %collective-permute-start.6) | collective-permute-done | bytes 36896 | tf_op jit(solution)/shard_map/ppermute | solution.py:520
  25.2 0.0 collective-permute-done.5.across
  25.2 1.1 %collective-permute-start.10 = (bf16[2,80,128]{2,1,0:T(8,128)(2,1)S(1)}, bf16[2,80,128]{2,1,0:T(8,128)(2,1)S(1)}, u32[]{:S(2)}, u32[]{:S(2)}) collective-permute-start(bf16[2,80,128]{2,1,0:T(8,128)(2,1)S(1)} %shard_map.64.pair.refs_0_), channel_id=1, source_target_pairs={{0,25},{1,24},{2,27},{3,26},{4,29},{5,28},{6,31},{7,30},{8,17},{9,... | collective-permute-start | bytes 122888 | tf_op jit(solution)/shard_map/ppermute | solution.py:520
  26.3 0.3 collective-permute-start.9
  26.7 2.7 %collective-permute-start.8 = (bf16[2,80,128]{2,1,0:T(8,128)(2,1)S(1)}, bf16[2,80,128]{2,1,0:T(8,128)(2,1)S(1)}, u32[]{:S(2)}, u32[]{:S(2)}) collective-permute-start(bf16[2,80,128]{2,1,0:T(8,128)(2,1)S(1)} %shard_map.64.pair.refs_0_), channel_id=1, source_target_pairs={{0,9},{1,8},{2,11},{3,10},{4,13},{5,12},{6,15},{7,14},{8,1},{9,0},... | collective-permute-start | bytes 122888 | tf_op jit(solution)/shard_map/ppermute | solution.py:520
  29.3 0.8 %shard_map.66 = (f32[2,6,64,128]{3,2,1,0:T(8,128)S(1)}, f32[2,64,128]{2,1,0:T(8,128)S(1)}) custom-call(s32[4]{0:T(128)S(1)} %pad_add_fusion.place, f32[4]{0:T(128)S(1)} %copy-done.3, bf16[2,80,128]{2,1,0:T(8,128)(2,1)S(1)} %shard_map.64.pair.refs_0_, bf16[80,128]{1,0:T(8,128)(2,1)S(1)} %collective-permute-done.2.one_got, ...), custom_call_target="tpu_custom_call" | custom-call | flops 8589934592 | bytes 1048576 | tf_op jit(solution)/shard_map/pallas_call | solution.py:594
  30.1 0.4 %collective-permute-done.10.refs_3_ = bf16[2,80,128]{2,1,0:T(8,128)(2,1)S(1)} collective-permute-done((bf16[2,80,128]{2,1,0:T(8,128)(2,1)S(1)}, bf16[2,80,128]{2,1,0:T(8,128)(2,1)S(1)}, u32[]{:S(2)}, u32[]{:S(2)}) %collective-permute-start.10) | collective-permute-done | bytes 40992 | tf_op jit(solution)/shard_map/ppermute | solution.py:520
  30.5 2.2 %collective-permute-done.9.refs_2_ = bf16[2,80,128]{2,1,0:T(8,128)(2,1)S(1)} collective-permute-done((bf16[2,80,128]{2,1,0:T(8,128)(2,1)S(1)}, bf16[2,80,128]{2,1,0:T(8,128)(2,1)S(1)}, u32[]{:S(2)}, u32[]{:S(2)}) %collective-permute-start.9) | collective-permute-done | bytes 40992 | tf_op jit(solution)/shard_map/ppermute | solution.py:520
  32.7 3.5 %shard_map.67 = (f32[1,64]{1,0:T(1,128)}, f32[2,64,128]{2,1,0:T(8,128)}) custom-call(s32[4]{0:T(128)S(1)} %pad_add_fusion.place, bf16[2,80,128]{2,1,0:T(8,128)(2,1)S(1)} %shard_map.64.pair.refs_0_, bf16[2,80,128]{2,1,0:T(8,128)(2,1)S(1)} %collective-permute-done.8.refs_1_, bf16[2,80,128]{2,1,0:T(8,128)(2,1)S(1)} %collective-permute-done.9.refs_2_, ...), custom_call_target="tpu_custom_call" | custom-call | flops 10000000 | bytes 5242880 | tf_op jit(solution)/shard_map/pallas_call | solution.py:604
  (11 shorter events, 0.1 us)
Async XLA Ops:
  0.6 5.3 %copy-start = (bf16[64,2,64,128]{3,2,1,0:T(8,128)(2,1)S(1)}, bf16[64,2,64,128]{3,2,1,0:T(8,128)(2,1)}, u32[]{:S(2)}) copy-start(bf16[64,2,64,128]{3,2,1,0:T(8,128)(2,1)} %refs_4_.1) | copy-start | bytes 6291460
  0.6 5.3 %copy-start.1 = (s32[2,64,128]{2,1,0:T(8,128)S(1)}, s32[2,64,128]{2,1,0:T(8,128)}, u32[]{:S(2)}) copy-start(s32[2,64,128]{2,1,0:T(8,128)} %labels_far.1) | copy-start | bytes 196612
  0.7 10.0 %copy-start.2 = (f32[2,64,128]{2,1,0:T(8,128)S(1)}, f32[2,64,128]{2,1,0:T(8,128)}, u32[]{:S(2)}) copy-start(f32[2,64,128]{2,1,0:T(8,128)} %refs_13_.1) | copy-start | bytes 196612
  0.7 10.0 %copy-start.3 = (f32[4]{0:T(128)S(1)}, f32[4]{0:T(128)}, u32[]{:S(2)}) copy-start(f32[4]{0:T(128)} %levels.7) | copy-start | bytes 52
  2.8 12.0 %collective-permute-start = (bf16[65,64,128]{2,1,0:T(8,128)(2,1)S(1)}, bf16[65,64,128]{2,1,0:T(8,128)(2,1)S(1)}, u32[]{:S(2)}, u32[]{:S(2)}) collective-permute-start(bf16[65,64,128]{2,1,0:T(8,128)(2,1)S(1)} %get-tuple-element.20), channel_id=1, source_target_pairs={{0,1},{1,0},{2,3},{3,2},{4,5},{5,4},{6,7},{7,6},{8,9},{9,8},{10,11... | collective-permute-start | bytes 3194888 | tf_op jit(solution)/shard_map/ppermute | solution.py:495
  3.3 12.8 %collective-permute-start.1 = (bf16[66,32,128]{2,1,0:T(8,128)(2,1)S(1)}, bf16[66,32,128]{2,1,0:T(8,128)(2,1)S(1)}, u32[]{:S(2)}, u32[]{:S(2)}) collective-permute-start(bf16[66,32,128]{2,1,0:T(8,128)(2,1)S(1)} %get-tuple-element.22), channel_id=1, source_target_pairs={{0,4},{1,2},{2,1},{3,7},{4,0},{5,6},{6,5},{7,3},{8,12},{9,10},{10,... | collective-permute-start | bytes 1622024 | tf_op jit(solution)/shard_map/ppermute | solution.py:508
  7.1 9.0 %collective-permute-start.3 = (bf16[80,128]{1,0:T(8,128)(2,1)S(1)}, bf16[80,128]{1,0:T(8,128)(2,1)S(1)}, u32[]{:S(2)}, u32[]{:S(2)}) collective-permute-start(bf16[80,128]{1,0:T(8,128)(2,1)S(1)} %get-tuple-element.23.two_pack), channel_id=1, source_target_pairs={{0,28},{4,8},{8,4},{12,16},{16,12},{20,24},{24,20},{28,0},{1,29},{... | collective-permute-start | bytes 61448 | tf_op jit(solution)/shard_map/ppermute | solution.py:495
  10.7 5.4 %collective-permute-start.2 = (bf16[80,128]{1,0:T(8,128)(2,1)S(1)}, bf16[80,128]{1,0:T(8,128)(2,1)S(1)}, u32[]{:S(2)}, u32[]{:S(2)}) collective-permute-start(bf16[80,128]{1,0:T(8,128)(2,1)S(1)} %get-tuple-element.16.after.one_pack), channel_id=1, source_target_pairs={{0,4},{4,0},{8,12},{12,8},{16,20},{20,16},{24,28},{28,24},{1,5},{5... | collective-permute-start | bytes 61448 | tf_op jit(solution)/shard_map/ppermute | solution.py:495
  17.7 1.8 %collective-permute-start.4 = (f32[72,128]{1,0:T(8,128)S(1)}, f32[72,128]{1,0:T(8,128)S(1)}, u32[]{:S(2)}, u32[]{:S(2)}) collective-permute-start(f32[72,128]{1,0:T(8,128)S(1)} %get-tuple-element.24), channel_id=1, source_target_pairs={{0,1},{1,0},{2,3},{3,2},{4,5},{5,4},{6,7},{7,6},{8,9},{9,8},{10,11... | collective-permute-start | bytes 110600 | tf_op jit(solution)/shard_map/ppermute | solution.py:512
  19.5 4.9 %collective-permute-start.7 = (f32[72,128]{1,0:T(8,128)S(1)}, f32[72,128]{1,0:T(8,128)S(1)}, u32[]{:S(2)}, u32[]{:S(2)}) collective-permute-start(f32[72,128]{1,0:T(8,128)S(1)} %add.3.own.after), channel_id=1, source_target_pairs={{0,7},{1,6},{2,5},{3,4},{4,3},{5,2},{6,1},{7,0},{8,15},{9,14},{10,... | collective-permute-start | bytes 110600 | tf_op jit(solution)/shard_map/ppermute | solution.py:520
  21.8 3.4 %collective-permute-start.6 = (f32[72,128]{1,0:T(8,128)S(1)}, f32[72,128]{1,0:T(8,128)S(1)}, u32[]{:S(2)}, u32[]{:S(2)}) collective-permute-start(f32[72,128]{1,0:T(8,128)S(1)} %add.3.own.after), channel_id=1, source_target_pairs={{0,5},{1,4},{2,7},{3,6},{4,1},{5,0},{6,3},{7,2},{8,13},{9,12},{10,... | collective-permute-start | bytes 110600 | tf_op jit(solution)/shard_map/ppermute | solution.py:520
  21.8 3.4 %collective-permute-start.5 = (f32[72,128]{1,0:T(8,128)S(1)}, f32[72,128]{1,0:T(8,128)S(1)}, u32[]{:S(2)}, u32[]{:S(2)}) collective-permute-start(f32[72,128]{1,0:T(8,128)S(1)} %add.3.own.after), channel_id=1, source_target_pairs={{0,3},{1,2},{2,1},{3,0},{4,7},{5,6},{6,5},{7,4},{8,11},{9,10},{10,... | collective-permute-start | bytes 110600 | tf_op jit(solution)/shard_map/ppermute | solution.py:520
  22.7 10.0 %collective-permute-start.11 = (bf16[64,32,128]{2,1,0:T(8,128)(2,1)S(1)}, bf16[64,32,128]{2,1,0:T(8,128)(2,1)S(1)}, u32[]{:S(2)}, u32[]{:S(2)}) collective-permute-start(bf16[64,32,128]{2,1,0:T(8,128)(2,1)S(1)} %shard_map.65), channel_id=1, source_target_pairs={{0,4},{1,2},{2,1},{3,7},{4,0},{5,6},{6,5},{7,3},{8,12},{9,10},{10,... | collective-permute-start | bytes 1572872 | tf_op jit(solution)/shard_map/ppermute | solution.py:508
  25.2 5.3 %collective-permute-start.10 = (bf16[2,80,128]{2,1,0:T(8,128)(2,1)S(1)}, bf16[2,80,128]{2,1,0:T(8,128)(2,1)S(1)}, u32[]{:S(2)}, u32[]{:S(2)}) collective-permute-start(bf16[2,80,128]{2,1,0:T(8,128)(2,1)S(1)} %shard_map.64.pair.refs_0_), channel_id=1, source_target_pairs={{0,25},{1,24},{2,27},{3,26},{4,29},{5,28},{6,31},{7,30},{8,17},{9,... | collective-permute-start | bytes 122888 | tf_op jit(solution)/shard_map/ppermute | solution.py:520
  26.3 6.3 %collective-permute-start.9 = (bf16[2,80,128]{2,1,0:T(8,128)(2,1)S(1)}, bf16[2,80,128]{2,1,0:T(8,128)(2,1)S(1)}, u32[]{:S(2)}, u32[]{:S(2)}) collective-permute-start(bf16[2,80,128]{2,1,0:T(8,128)(2,1)S(1)} %shard_map.64.pair.refs_0_), channel_id=1, source_target_pairs={{0,17},{1,16},{2,19},{3,18},{4,21},{5,20},{6,23},{7,22},{8,25},{9,... | collective-permute-start | bytes 122888 | tf_op jit(solution)/shard_map/ppermute | solution.py:520
  26.7 6.0 %collective-permute-start.8 = (bf16[2,80,128]{2,1,0:T(8,128)(2,1)S(1)}, bf16[2,80,128]{2,1,0:T(8,128)(2,1)S(1)}, u32[]{:S(2)}, u32[]{:S(2)}) collective-permute-start(bf16[2,80,128]{2,1,0:T(8,128)(2,1)S(1)} %shard_map.64.pair.refs_0_), channel_id=1, source_target_pairs={{0,9},{1,8},{2,11},{3,10},{4,13},{5,12},{6,15},{7,14},{8,1},{9,0},... | collective-permute-start | bytes 122888 | tf_op jit(solution)/shard_map/ppermute | solution.py:520

commit v9 on v8

--- a/solution.py
+++ b/solution.py
@@ -351,7 +351,6 @@
     side = lax.rem(place[1], 2)
     odd = lax.rem(me, 2) == 1
     at_edge = (place[1] == 0) | (place[1] == place[2] - 1)
-    order = place[3]
     held = (1 - side, side)
     square = (modes, modes)
     eye = lax.broadcasted_iota(jnp.int32, square, 0) == lax.broadcasted_iota(jnp.int32, square, 1)
@@ -364,7 +363,7 @@
             held_here = block.shape[0]
             if held_here <= 8:
                 for entry in range(held_here):
-                    s = jnp.bitwise_xor(order, index * held_here + entry)
+                    s = jnp.bitwise_xor(place[3 + index], entry)
                     carry = body(block.at[entry], s, carry)
             else:
                 carry = lax.fori_loop(
@@ -520,15 +519,25 @@
     return lax.ppermute(value, ("sub", "pln"), pairs)
 
 
+FAR = (4, 6)
+
+
+def far_partner(value):
+    subs, count = lax.axis_size("sub"), lax.axis_size("pln")
+    pairs = [(s * count + p, (s ^ FAR[p % 2]) * count + p) for s in range(subs) for p in range(count)]
+    return lax.ppermute(value, ("sub", "pln"), pairs)
+
+
 def body(labels, levels, zvec, resid):
     modes, planes, rows, layers = zvec.shape
     half = rows // 2
     subs, parts = lax.axis_size("sub"), lax.axis_size("pln")
     shape = jax.ShapeDtypeStruct
-    order = lax.axis_index("sub") if subs == 8 else 0
-    place = jnp.stack(
-        [jnp.int32(v) for v in (lax.axis_index("sub"), lax.axis_index("pln"), parts, order)]
-    )
+    at_sub, at_pln = lax.axis_index("sub"), lax.axis_index("pln")
+    core = at_pln % 2
+    masks = (0, FAR[0] + core * (FAR[1] - FAR[0]), 2, FAR[1] + core * (FAR[0] - FAR[1]))
+    orders = [at_sub ^ mask for mask in masks] if parts == 4 and subs == 8 else [0] * 4
+    place = jnp.stack([jnp.int32(v) for v in (at_sub, at_pln, parts, *orders)])
     pack = shape((modes + 16, planes * rows), BF16)
     inner_send, outer_near = call(
         stage_kernel,
@@ -585,7 +594,8 @@
         block = block + exchanged(block, "pln", 1)
         others = [partner(block, *masks) for masks in ((0, 3), (1, 1), (1, 3))]
         [pair] = call(pair_kernel, [shape((2,) + packed, BF16)], [VMEM] * 4)(block, *others)
-        blocks = [pair] + [partner(pair, mask, 1) for mask in (2, 4, 6)]
+        far = far_partner(pair)
+        blocks = [pair, far, partner(pair, 2, 1), exchanged(far, "pln", 1)]
     else:
         [single] = call(single_kernel, [shape(packed, BF16)], [VMEM])(lax.psum(block, "pln"))
         blocks = [lax.all_gather(single, "sub")]

time: 36.4 us -> 39.4 us (1.082)
  waiting for transfers between devices: 4.2 us -> 10.2 us
  starting transfers between devices: 16.6 us -> 13.6 us
    ppermute x2, waiting for transfers between devices: 0.01 us -> 3.73 us  [swapped_all(): return lax.ppermute(value, ('sub', 'pln'), pairs)]
    ppermute x6 -> x4, starting transfers between devices: 7.29 us -> 3.88 us  [partner(): return lax.ppermute(value, ('sub', 'pln'), pairs)]
    ppermute x0 -> x1, waiting for transfers between devices: none -> 2.63 us  [far_partner(): return lax.ppermute(value, ('sub', 'pln'), pairs)]
    ppermute x0 -> x1, starting transfers between devices: none -> 1.29 us  [far_partner(): return lax.ppermute(value, ('sub', 'pln'), pairs)]
    ppermute x2, starting transfers between devices: 4.33 us -> 3.48 us  [swapped_all(): return lax.ppermute(value, ('sub', 'pln'), pairs)]
    ppermute x6 -> x4, waiting for transfers between devices: 3.32 us -> 2.52 us  [partner(): return lax.ppermute(value, ('sub', 'pln'), pairs)]
    ppermute x1 -> x2, waiting for transfers between devices: 0.87 us -> 1.27 us  [exchanged(): lax.ppermute(value, axis, [(i, i ^ mask) for i in range(lax.axis_size(axi...]
    ppermute x1 -> x2, starting transfers between devices: 0.89 us -> 0.89 us  [exchanged(): lax.ppermute(value, axis, [(i, i ^ mask) for i in range(lax.axis_size(axi...]
  transfers between devices with their start and end apart: 12 -> 12, of which waited for: 4 -> 6; matrix products, arithmetic and copies ran while one was open for 0% -> 0% of each run, Pallas kernels for 21% -> 19%
where the time goes in v9:
time: 39.4 us; the launch traced here: 39.2 us
  Pallas kernels  14.6 us (37%)
  starting transfers between devices  13.6 us (35%)
  waiting for transfers between devices  10.2 us (26%)
  between operations  0.74 us (2%)
    ppermute x3, starting transfers between devices, swapped(): return lax.ppermute(value, axis, pairs)  4.1 us
    pallas_call x1, Pallas kernels, body(): call(block_kernel, [shape((modes + 8, modes), F32), shape((7,) + plane, F...  4.02 us
    ppermute x4, starting transfers between devices, partner(): return lax.ppermute(value, ('sub', 'pln'), pairs)  3.88 us
    ppermute x2, waiting for transfers between devices, swapped_all(): return lax.ppermute(value, ('sub', 'pln'), pairs)  3.73 us
    pallas_call x1, Pallas kernels, body(): call(finish_kernel, [shape((1, modes), F32), shape(field, F32)], [SMEM] +...  3.53 us
    ppermute x2, starting transfers between devices, swapped_all(): return lax.ppermute(value, ('sub', 'pln'), pairs)  3.48 us
    ppermute x1, waiting for transfers between devices, far_partner(): return lax.ppermute(value, ('sub', 'pln'), pairs)  2.63 us
    ppermute x4, waiting for transfers between devices, partner(): return lax.ppermute(value, ('sub', 'pln'), pairs)  2.52 us
  transfers between devices with their start and end apart: 12, of which 6 were waited for; matrix products, arithmetic and copies ran while one was open for 0% of the time, Pallas kernels for 19%

profile of v9, /device:TPU:0, one launch (start us, length us, event | category | flops | bytes accessed | tf_op | source)
XLA Modules:
  0.0 39.2 jit_solution(8007761549746349729)
XLA Ops:
  0.6 0.0 copy-start
  0.6 0.0 copy-start.1
  0.7 0.1 stack.24.place
  0.8 2.0 %shard_map.61 = (bf16[65,64,128]{2,1,0:T(8,128)(2,1)S(1)}, bf16[66,32,128]{2,1,0:T(8,128)(2,1)S(1)}) custom-call(s32[7]{0:T(128)S(1)} %stack.24.place, s32[2,64,128]{2,1,0:T(8,128)} %labels_far.1, bf16[64,2,64,128]{3,2,1,0:T(8,128)(2,1)} %refs_4_.1), custom_call_target="tpu_custom_call" | custom-call | bytes 2097152 | tf_op jit(solution)/shard_map/pallas_call | solution.py:542
  2.8 0.5 %collective-permute-start = (bf16[65,64,128]{2,1,0:T(8,128)(2,1)S(1)}, bf16[65,64,128]{2,1,0:T(8,128)(2,1)S(1)}, u32[]{:S(2)}, u32[]{:S(2)}) collective-permute-start(bf16[65,64,128]{2,1,0:T(8,128)(2,1)S(1)} %get-tuple-element.20), channel_id=1, source_target_pairs={{0,1},{1,0},{2,3},{3,2},{4,5},{5,4},{6,7},{7,6},{8,9},{9,8},{10,11... | collective-permute-start | bytes 3194888 | tf_op jit(solution)/shard_map/ppermute | solution.py:494
  3.3 2.6 %collective-permute-start.1 = (bf16[66,32,128]{2,1,0:T(8,128)(2,1)S(1)}, bf16[66,32,128]{2,1,0:T(8,128)(2,1)S(1)}, u32[]{:S(2)}, u32[]{:S(2)}) collective-permute-start(bf16[66,32,128]{2,1,0:T(8,128)(2,1)S(1)} %get-tuple-element.22), channel_id=1, source_target_pairs={{0,4},{1,2},{2,1},{3,7},{4,0},{5,6},{6,5},{7,3},{8,12},{9,10},{10,... | collective-permute-start | bytes 1622024 | tf_op jit(solution)/shard_map/ppermute | solution.py:507
  5.9 1.2 %shard_map.59 = (bf16[64,32,128]{2,1,0:T(8,128)(2,1)S(1)}, bf16[80,128]{1,0:T(8,128)(2,1)S(1)}, bf16[80,128]{1,0:T(8,128)(2,1)S(1)}) custom-call(s32[7]{0:T(128)S(1)} %stack.24.place, s32[2,64,128]{2,1,0:T(8,128)S(1)} %copy-done.1, bf16[64,2,64,128]{3,2,1,0:T(8,128)(2,1)S(1)} %copy-done), custom_call_target="tpu_custom_call" | custom-call | flops 10000000 | bytes 6291456 | tf_op jit(solution)/shard_map/pallas_call | solution.py:552
  7.1 3.6 %collective-permute-start.3 = (bf16[80,128]{1,0:T(8,128)(2,1)S(1)}, bf16[80,128]{1,0:T(8,128)(2,1)S(1)}, u32[]{:S(2)}, u32[]{:S(2)}) collective-permute-start(bf16[80,128]{1,0:T(8,128)(2,1)S(1)} %get-tuple-element.23.two_pack), channel_id=1, source_target_pairs={{0,28},{4,8},{8,4},{12,16},{16,12},{20,24},{24,20},{28,0},{1,29},{... | collective-permute-start | bytes 61448 | tf_op jit(solution)/shard_map/ppermute | solution.py:494
  10.7 0.0 collective-permute-start.2
  10.7 4.0 %shard_map.60 = (f32[72,64]{1,0:T(8,128)S(1)}, f32[7,64,128]{2,1,0:T(8,128)S(1)}, bf16[2,64,64,128]{3,2,1,0:T(8,128)(2,1)S(1)}) custom-call(s32[7]{0:T(128)S(1)} %stack.24.place, f32[4]{0:T(128)S(1)} %copy-done.3, s32[2,64,128]{2,1,0:T(8,128)S(1)} %copy-done.1, f32[2,64,128]{2,1,0:T(8,128)S(1)} %copy-done.2, bf16[64,2,64,128]{3,2,1,0:T(8,128)(2,1)S(1)} %copy-done, ...), custom_call_target="tpu_custom_call" | custom-call | flops 400000000 | bytes 3145728 | tf_op jit(solution)/shard_map/pallas_call | solution.py:563
  14.7 0.0 collective-permute-done.inner_got.refs_5_
  14.7 1.4 %shard_map.62 = (f32[72,64]{1,0:T(8,128)S(1)}, f32[64,128]{1,0:T(8,128)S(1)}) custom-call(s32[7]{0:T(128)S(1)} %stack.24.place, f32[4]{0:T(128)S(1)} %copy-done.3, f32[72,64]{1,0:T(8,128)S(1)} %get-tuple-element.17.partial, f32[7,64,128]{2,1,0:T(8,128)S(1)} %get-tuple-element.18.weights.refs_10_, bf16[2,64,64,128]{3,2,1,0:T(8,128)(2,1)S(1)} %get-tuple-element.19.here, ...), custom_call_target="tpu_custom_call" | custom-call | flops 100000000 | bytes 1048576 | tf_op jit(solution)/shard_map/pallas_call | solution.py:576
  16.1 0.0 collective-permute-done.3.two_got
  16.1 0.0 collective-permute-done.2.one_got
  16.1 0.0 collective-permute-done.1.outer_got.refs_6_
  16.1 1.6 %shard_map.63 = (f32[72,128]{1,0:T(8,128)S(1)}, f32[64,128]{1,0:T(8,128)S(1)}) custom-call(s32[7]{0:T(128)S(1)} %stack.24.place, f32[4]{0:T(128)S(1)} %copy-done.3, f32[72,64]{1,0:T(8,128)S(1)} %get-tuple-element.21.partial, f32[7,64,128]{2,1,0:T(8,128)S(1)} %get-tuple-element.18.weights.refs_10_, bf16[2,64,64,128]{3,2,1,0:T(8,128)(2,1)S(1)} %get-tuple-element.19.here, ...), custom_call_target="tpu_custom_call" | custom-call | flops 100000000 | bytes 1048576 | tf_op jit(solution)/shard_map/pallas_call | solution.py:584
  17.7 0.9 %collective-permute-start.4 = (f32[72,128]{1,0:T(8,128)S(1)}, f32[72,128]{1,0:T(8,128)S(1)}, u32[]{:S(2)}, u32[]{:S(2)}) collective-permute-start(f32[72,128]{1,0:T(8,128)S(1)} %get-tuple-element.24), channel_id=1, source_target_pairs={{0,1},{1,0},{2,3},{3,2},{4,5},{5,4},{6,7},{7,6},{8,9},{9,8},{10,11... | collective-permute-start | bytes 110600 | tf_op jit(solution)/shard_map/ppermute | solution.py:511
  18.6 0.9 %collective-permute-done.4 = f32[72,128]{1,0:T(8,128)S(1)} collective-permute-done((f32[72,128]{1,0:T(8,128)S(1)}, f32[72,128]{1,0:T(8,128)S(1)}, u32[]{:S(2)}, u32[]{:S(2)}) %collective-permute-start.4) | collective-permute-done | bytes 36896 | tf_op jit(solution)/shard_map/ppermute | solution.py:511
  19.5 2.3 %collective-permute-start.7 = (f32[72,128]{1,0:T(8,128)S(1)}, f32[72,128]{1,0:T(8,128)S(1)}, u32[]{:S(2)}, u32[]{:S(2)}) collective-permute-start(f32[72,128]{1,0:T(8,128)S(1)} %add.12.own.after), channel_id=1, source_target_pairs={{0,7},{1,6},{2,5},{3,4},{4,3},{5,2},{6,1},{7,0},{8,15},{9,14},{10,... | collective-permute-start | bytes 110600 | tf_op jit(solution)/shard_map/ppermute | solution.py:519
  21.8 0.0 collective-permute-start.6
  21.8 0.9 %collective-permute-start.5 = (f32[72,128]{1,0:T(8,128)S(1)}, f32[72,128]{1,0:T(8,128)S(1)}, u32[]{:S(2)}, u32[]{:S(2)}) collective-permute-start(f32[72,128]{1,0:T(8,128)S(1)} %add.12.own.after), channel_id=1, source_target_pairs={{0,3},{1,2},{2,1},{3,0},{4,7},{5,6},{6,5},{7,4},{8,11},{9,10},{10,... | collective-permute-start | bytes 110600 | tf_op jit(solution)/shard_map/ppermute | solution.py:519
  22.7 1.1 %collective-permute-done.7.oblique = f32[72,128]{1,0:T(8,128)S(1)} collective-permute-done((f32[72,128]{1,0:T(8,128)S(1)}, f32[72,128]{1,0:T(8,128)S(1)}, u32[]{:S(2)}, u32[]{:S(2)}) %collective-permute-start.7) | collective-permute-done | bytes 36896 | tf_op jit(solution)/shard_map/ppermute | solution.py:519
  23.8 1.4 %collective-permute-done.6.beside = f32[72,128]{1,0:T(8,128)S(1)} collective-permute-done((f32[72,128]{1,0:T(8,128)S(1)}, f32[72,128]{1,0:T(8,128)S(1)}, u32[]{:S(2)}, u32[]{:S(2)}) %collective-permute-start.6) | collective-permute-done | bytes 36896 | tf_op jit(solution)/shard_map/ppermute | solution.py:519
  25.2 1.3 %collective-permute-start.8 = (bf16[2,80,128]{2,1,0:T(8,128)(2,1)S(1)}, bf16[2,80,128]{2,1,0:T(8,128)(2,1)S(1)}, u32[]{:S(2)}, u32[]{:S(2)}) collective-permute-start(bf16[2,80,128]{2,1,0:T(8,128)(2,1)S(1)} %shard_map.64.pair.refs_0_), channel_id=1, source_target_pairs={{0,16},{1,25},{2,18},{3,27},{4,20},{5,29},{6,22},{7,31},{8,24},{9,... | collective-permute-start | bytes 122888 | tf_op jit(solution)/shard_map/ppermute | solution.py:528
  26.5 0.9 %collective-permute-start.11 = (bf16[64,32,128]{2,1,0:T(8,128)(2,1)S(1)}, bf16[64,32,128]{2,1,0:T(8,128)(2,1)S(1)}, u32[]{:S(2)}, u32[]{:S(2)}) collective-permute-start(bf16[64,32,128]{2,1,0:T(8,128)(2,1)S(1)} %shard_map.65), channel_id=1, source_target_pairs={{0,4},{1,2},{2,1},{3,7},{4,0},{5,6},{6,5},{7,3},{8,12},{9,10},{10,... | collective-permute-start | bytes 1572872 | tf_op jit(solution)/shard_map/ppermute | solution.py:507
  27.4 0.7 %collective-permute-start.9 = (bf16[2,80,128]{2,1,0:T(8,128)(2,1)S(1)}, bf16[2,80,128]{2,1,0:T(8,128)(2,1)S(1)}, u32[]{:S(2)}, u32[]{:S(2)}) collective-permute-start(bf16[2,80,128]{2,1,0:T(8,128)(2,1)S(1)} %shard_map.64.pair.refs_0_), channel_id=1, source_target_pairs={{0,9},{1,8},{2,11},{3,10},{4,13},{5,12},{6,15},{7,14},{8,1},{9,0},... | collective-permute-start | bytes 122888 | tf_op jit(solution)/shard_map/ppermute | solution.py:519
  28.1 2.6 %collective-permute-done.8.refs_1_ = bf16[2,80,128]{2,1,0:T(8,128)(2,1)S(1)} collective-permute-done((bf16[2,80,128]{2,1,0:T(8,128)(2,1)S(1)}, bf16[2,80,128]{2,1,0:T(8,128)(2,1)S(1)}, u32[]{:S(2)}, u32[]{:S(2)}) %collective-permute-start.8) | collective-permute-done | bytes 40992 | tf_op jit(solution)/shard_map/ppermute | solution.py:528
  30.7 0.8 %shard_map.66 = (f32[2,6,64,128]{3,2,1,0:T(8,128)S(1)}, f32[2,64,128]{2,1,0:T(8,128)S(1)}) custom-call(s32[7]{0:T(128)S(1)} %stack.24.place, f32[4]{0:T(128)S(1)} %copy-done.3, bf16[2,80,128]{2,1,0:T(8,128)(2,1)S(1)} %shard_map.64.pair.refs_0_, bf16[80,128]{1,0:T(8,128)(2,1)S(1)} %collective-permute-done.2.one_got, ...), custom_call_target="tpu_custom_call" | custom-call | flops 8589934592 | bytes 1048576 | tf_op jit(solution)/shard_map/pallas_call | solution.py:604
  31.5 0.0 collective-permute-done.9.refs_2_
  31.6 0.4 %collective-permute-done.10.refs_3_ = bf16[2,80,128]{2,1,0:T(8,128)(2,1)S(1)} collective-permute-done((bf16[2,80,128]{2,1,0:T(8,128)(2,1)S(1)}, bf16[2,80,128]{2,1,0:T(8,128)(2,1)S(1)}, u32[]{:S(2)}, u32[]{:S(2)}) %collective-permute-start.10) | collective-permute-done | bytes 40992 | tf_op jit(solution)/shard_map/ppermute | solution.py:511
  32.0 3.7 %collective-permute-done.11.refs_7_ = bf16[64,32,128]{2,1,0:T(8,128)(2,1)S(1)} collective-permute-done((bf16[64,32,128]{2,1,0:T(8,128)(2,1)S(1)}, bf16[64,32,128]{2,1,0:T(8,128)(2,1)S(1)}, u32[]{:S(2)}, u32[]{:S(2)}) %collective-permute-start.11) | collective-permute-done | bytes 524320 | tf_op jit(solution)/shard_map/ppermute | solution.py:507
  35.7 3.5 %shard_map.67 = (f32[1,64]{1,0:T(1,128)}, f32[2,64,128]{2,1,0:T(8,128)}) custom-call(s32[7]{0:T(128)S(1)} %stack.24.place, bf16[2,80,128]{2,1,0:T(8,128)(2,1)S(1)} %shard_map.64.pair.refs_0_, bf16[2,80,128]{2,1,0:T(8,128)(2,1)S(1)} %collective-permute-done.8.refs_1_, bf16[2,80,128]{2,1,0:T(8,128)(2,1)S(1)} %collective-permute-done.9.refs_2_, ...), custom_call_target="tpu_custom_call" | custom-call | flops 10000000 | bytes 5242880 | tf_op jit(solution)/shard_map/pallas_call | solution.py:614
  (11 shorter events, 0.1 us)
Async XLA Ops:
  0.6 5.3 %copy-start = (bf16[64,2,64,128]{3,2,1,0:T(8,128)(2,1)S(1)}, bf16[64,2,64,128]{3,2,1,0:T(8,128)(2,1)}, u32[]{:S(2)}) copy-start(bf16[64,2,64,128]{3,2,1,0:T(8,128)(2,1)} %refs_4_.1) | copy-start | bytes 6291460
  0.6 5.3 %copy-start.1 = (s32[2,64,128]{2,1,0:T(8,128)S(1)}, s32[2,64,128]{2,1,0:T(8,128)}, u32[]{:S(2)}) copy-start(s32[2,64,128]{2,1,0:T(8,128)} %labels_far.1) | copy-start | bytes 196612
  0.8 9.9 %copy-start.2 = (f32[2,64,128]{2,1,0:T(8,128)S(1)}, f32[2,64,128]{2,1,0:T(8,128)}, u32[]{:S(2)}) copy-start(f32[2,64,128]{2,1,0:T(8,128)} %refs_13_.1) | copy-start | bytes 196612
  0.8 9.9 %copy-start.3 = (f32[4]{0:T(128)S(1)}, f32[4]{0:T(128)}, u32[]{:S(2)}) copy-start(f32[4]{0:T(128)} %levels.7) | copy-start | bytes 52
  2.8 12.0 %collective-permute-start = (bf16[65,64,128]{2,1,0:T(8,128)(2,1)S(1)}, bf16[65,64,128]{2,1,0:T(8,128)(2,1)S(1)}, u32[]{:S(2)}, u32[]{:S(2)}) collective-permute-start(bf16[65,64,128]{2,1,0:T(8,128)(2,1)S(1)} %get-tuple-element.20), channel_id=1, source_target_pairs={{0,1},{1,0},{2,3},{3,2},{4,5},{5,4},{6,7},{7,6},{8,9},{9,8},{10,11... | collective-permute-start | bytes 3194888 | tf_op jit(solution)/shard_map/ppermute | solution.py:494
  3.3 12.8 %collective-permute-start.1 = (bf16[66,32,128]{2,1,0:T(8,128)(2,1)S(1)}, bf16[66,32,128]{2,1,0:T(8,128)(2,1)S(1)}, u32[]{:S(2)}, u32[]{:S(2)}) collective-permute-start(bf16[66,32,128]{2,1,0:T(8,128)(2,1)S(1)} %get-tuple-element.22), channel_id=1, source_target_pairs={{0,4},{1,2},{2,1},{3,7},{4,0},{5,6},{6,5},{7,3},{8,12},{9,10},{10,... | collective-permute-start | bytes 1622024 | tf_op jit(solution)/shard_map/ppermute | solution.py:507
  7.1 9.0 %collective-permute-start.3 = (bf16[80,128]{1,0:T(8,128)(2,1)S(1)}, bf16[80,128]{1,0:T(8,128)(2,1)S(1)}, u32[]{:S(2)}, u32[]{:S(2)}) collective-permute-start(bf16[80,128]{1,0:T(8,128)(2,1)S(1)} %get-tuple-element.23.two_pack), channel_id=1, source_target_pairs={{0,28},{4,8},{8,4},{12,16},{16,12},{20,24},{24,20},{28,0},{1,29},{... | collective-permute-start | bytes 61448 | tf_op jit(solution)/shard_map/ppermute | solution.py:494
  10.7 5.4 %collective-permute-start.2 = (bf16[80,128]{1,0:T(8,128)(2,1)S(1)}, bf16[80,128]{1,0:T(8,128)(2,1)S(1)}, u32[]{:S(2)}, u32[]{:S(2)}) collective-permute-start(bf16[80,128]{1,0:T(8,128)(2,1)S(1)} %get-tuple-element.16.after.one_pack), channel_id=1, source_target_pairs={{0,4},{4,0},{8,12},{12,8},{16,20},{20,16},{24,28},{28,24},{1,5},{5... | collective-permute-start | bytes 61448 | tf_op jit(solution)/shard_map/ppermute | solution.py:494
  17.7 1.8 %collective-permute-start.4 = (f32[72,128]{1,0:T(8,128)S(1)}, f32[72,128]{1,0:T(8,128)S(1)}, u32[]{:S(2)}, u32[]{:S(2)}) collective-permute-start(f32[72,128]{1,0:T(8,128)S(1)} %get-tuple-element.24), channel_id=1, source_target_pairs={{0,1},{1,0},{2,3},{3,2},{4,5},{5,4},{6,7},{7,6},{8,9},{9,8},{10,11... | collective-permute-start | bytes 110600 | tf_op jit(solution)/shard_map/ppermute | solution.py:511
  19.5 4.3 %collective-permute-start.7 = (f32[72,128]{1,0:T(8,128)S(1)}, f32[72,128]{1,0:T(8,128)S(1)}, u32[]{:S(2)}, u32[]{:S(2)}) collective-permute-start(f32[72,128]{1,0:T(8,128)S(1)} %add.12.own.after), channel_id=1, source_target_pairs={{0,7},{1,6},{2,5},{3,4},{4,3},{5,2},{6,1},{7,0},{8,15},{9,14},{10,... | collective-permute-start | bytes 110600 | tf_op jit(solution)/shard_map/ppermute | solution.py:519
  21.8 3.4 %collective-permute-start.6 = (f32[72,128]{1,0:T(8,128)S(1)}, f32[72,128]{1,0:T(8,128)S(1)}, u32[]{:S(2)}, u32[]{:S(2)}) collective-permute-start(f32[72,128]{1,0:T(8,128)S(1)} %add.12.own.after), channel_id=1, source_target_pairs={{0,5},{1,4},{2,7},{3,6},{4,1},{5,0},{6,3},{7,2},{8,13},{9,12},{10,... | collective-permute-start | bytes 110600 | tf_op jit(solution)/shard_map/ppermute | solution.py:519
  21.8 3.4 %collective-permute-start.5 = (f32[72,128]{1,0:T(8,128)S(1)}, f32[72,128]{1,0:T(8,128)S(1)}, u32[]{:S(2)}, u32[]{:S(2)}) collective-permute-start(f32[72,128]{1,0:T(8,128)S(1)} %add.12.own.after), channel_id=1, source_target_pairs={{0,3},{1,2},{2,1},{3,0},{4,7},{5,6},{6,5},{7,4},{8,11},{9,10},{10,... | collective-permute-start | bytes 110600 | tf_op jit(solution)/shard_map/ppermute | solution.py:519
  25.2 5.5 %collective-permute-start.8 = (bf16[2,80,128]{2,1,0:T(8,128)(2,1)S(1)}, bf16[2,80,128]{2,1,0:T(8,128)(2,1)S(1)}, u32[]{:S(2)}, u32[]{:S(2)}) collective-permute-start(bf16[2,80,128]{2,1,0:T(8,128)(2,1)S(1)} %shard_map.64.pair.refs_0_), channel_id=1, source_target_pairs={{0,16},{1,25},{2,18},{3,27},{4,20},{5,29},{6,22},{7,31},{8,24},{9,... | collective-permute-start | bytes 122888 | tf_op jit(solution)/shard_map/ppermute | solution.py:528
  26.5 9.2 %collective-permute-start.11 = (bf16[64,32,128]{2,1,0:T(8,128)(2,1)S(1)}, bf16[64,32,128]{2,1,0:T(8,128)(2,1)S(1)}, u32[]{:S(2)}, u32[]{:S(2)}) collective-permute-start(bf16[64,32,128]{2,1,0:T(8,128)(2,1)S(1)} %shard_map.65), channel_id=1, source_target_pairs={{0,4},{1,2},{2,1},{3,7},{4,0},{5,6},{6,5},{7,3},{8,12},{9,10},{10,... | collective-permute-start | bytes 1572872 | tf_op jit(solution)/shard_map/ppermute | solution.py:507
  27.4 4.2 %collective-permute-start.9 = (bf16[2,80,128]{2,1,0:T(8,128)(2,1)S(1)}, bf16[2,80,128]{2,1,0:T(8,128)(2,1)S(1)}, u32[]{:S(2)}, u32[]{:S(2)}) collective-permute-start(bf16[2,80,128]{2,1,0:T(8,128)(2,1)S(1)} %shard_map.64.pair.refs_0_), channel_id=1, source_target_pairs={{0,9},{1,8},{2,11},{3,10},{4,13},{5,12},{6,15},{7,14},{8,1},{9,0},... | collective-permute-start | bytes 122888 | tf_op jit(solution)/shard_map/ppermute | solution.py:519
  30.7 1.2 %collective-permute-start.10 = (bf16[2,80,128]{2,1,0:T(8,128)(2,1)S(1)}, bf16[2,80,128]{2,1,0:T(8,128)(2,1)S(1)}, u32[]{:S(2)}, u32[]{:S(2)}) collective-permute-start(bf16[2,80,128]{2,1,0:T(8,128)(2,1)S(1)} %collective-permute-done.8.refs_1_), channel_id=1, source_target_pairs={{0,1},{1,0},{2,3},{3,2},{4,5},{5,4},{6,7},{7,6},{8,9},{9,8},{10,11... | collective-permute-start | bytes 122888 | tf_op jit(solution)/shard_map/ppermute | solution.py:511

commit v10 on v9

--- a/solution.py
+++ b/solution.py
@@ -337,6 +337,21 @@
     for index, part in enumerate(parts):
         extra = jnp.where(rows == index, part, extra)
     out[modes:] = extra.astype(BF16)
+
+
+def widen_kernel(place, pair, zvec, inner_got, outer_got, own_wide, inner_wide, outer_wide):
+    modes, half = outer_wide.shape[:2]
+    side = lax.rem(place[1], 2)
+
+    def some(j, carry):
+        at = pl.ds(pl.multiple_of(j * MODES, MODES), MODES)
+        own_wide[at, 0] = zvec[at, 1 - side].astype(F32)
+        own_wide[at, 1] = zvec[at, side].astype(F32)
+        inner_wide[at] = inner_got[at].astype(F32)
+        outer_wide[at] = outer_got[at].astype(F32)
+        return carry
+
+    lax.fori_loop(0, modes // MODES, some, 0)
 
 
 def finish_kernel(place, *refs):
@@ -457,9 +472,9 @@
         for u in range(MODES):
             k = j * MODES + u
             scale = spread[pl.ds(k, 1), :]
-            for x, plane in enumerate((zvec[k, held[0]], zvec[k, held[1]], inner_got[k])):
-                fields[x] = fields[x] + scale * plane.astype(F32)
-            near = near + scale * outer_got[k].astype(F32)
+            for x, plane in enumerate((zvec[k, 0], zvec[k, 1], inner_got[k])):
+                fields[x] = fields[x] + scale * plane
+            near = near + scale * outer_got[k]
             last = last + scale * outer_last[k].astype(F32)
         return tuple(fields), near, last
 
@@ -593,7 +608,9 @@
     if parts == 4 and subs == 8:
         block = block + exchanged(block, "pln", 1)
         others = [partner(block, *masks) for masks in ((0, 3), (1, 1), (1, 3))]
-        [pair] = call(pair_kernel, [shape((2,) + packed, BF16)], [VMEM] * 4)(block, *others)
+        [pair] = call(
+            pair_kernel, [shape((2,) + packed, BF16)], [VMEM] * 4, flops=1 << 33
+        )(block, *others)
         far = far_partner(pair)
         blocks = [pair, far, partner(pair, 2, 1), exchanged(far, "pln", 1)]
     else:
@@ -607,9 +624,20 @@
         [SMEM, SMEM, ANY] + [VMEM] * 5,
         [pltpu.VMEM(field, F32)],
 
-        flops=1 << 33,
+        flops=1 << 31,
         moved=1 << 20,
     )(place, levels, blocks[0], one_got, two_got, weights, inner_face, outer_face)
+    wide = call(
+        widen_kernel,
+        [
+            shape((modes,) + field, F32),
+            shape((modes,) + plane, F32),
+            shape((modes, half, layers), F32),
+        ],
+        [SMEM, ANY] + [VMEM] * 3,
+        flops=1 << 30,
+        moved=1 << 20,
+    )(place, blocks[0], zvec, inner_got, outer_got)
     return tuple(
         call(
             finish_kernel,
@@ -623,7 +651,7 @@
             flops=10_000_000,
             moved=5 << 20,
         )(
-            place, *blocks, zvec, inner_got, outer_got, outer_last, picked, terms, weights, inner_face,
+            place, *blocks, *wide, outer_last, picked, terms, weights, inner_face,
             outer_face, resid,
         )
     )

time: 39.4 us -> 36.1 us (0.916)
  waiting for transfers between devices: 10.2 us -> 6.35 us
  Pallas kernels: 14.6 us -> 15.4 us
    ppermute x2, waiting for transfers between devices: 3.73 us -> 0.01 us  [swapped_all(): return lax.ppermute(value, ('sub', 'pln'), pairs)]
    ppermute x3, starting transfers between devices: 4.1 us -> 5.62 us  [swapped(): return lax.ppermute(value, axis, pairs)]
    pallas_call x1 -> x2, Pallas kernels: 0.04 us -> 1.09 us  [the longest x1 1.05 us: body(): call(widen_kernel, [shape((modes,) + field, F32), shape((modes,) + plane,...]
    ppermute x4, starting transfers between devices: 3.88 us -> 3.03 us  [partner(): return lax.ppermute(value, ('sub', 'pln'), pairs)]
    ppermute x2, starting transfers between devices: 0.89 us -> 0.07 us  [exchanged(): lax.ppermute(value, axis, [(i, i ^ mask) for i in range(lax.axis_size(axi...]
    ppermute x4, waiting for transfers between devices: 2.52 us -> 1.82 us  [partner(): return lax.ppermute(value, ('sub', 'pln'), pairs)]
    ppermute x2, starting transfers between devices: 3.48 us -> 2.83 us  [swapped_all(): return lax.ppermute(value, ('sub', 'pln'), pairs)]
    ppermute x1, waiting for transfers between devices: 2.63 us -> 3.18 us  [far_partner(): return lax.ppermute(value, ('sub', 'pln'), pairs)]
  transfers between devices with their start and end apart: 12 -> 12, of which waited for: 6 -> 6; matrix products, arithmetic and copies ran while one was open for 0% -> 0% of each run, Pallas kernels for 19% -> 24%
where the time goes in v10:
time: 36.1 us; the launch traced here: 36 us
  Pallas kernels  15.4 us (43%)
  starting transfers between devices  13.4 us (37%)
  waiting for transfers between devices  6.35 us (18%)
  between operations  0.76 us (2%)
    ppermute x3, starting transfers between devices, swapped(): return lax.ppermute(value, axis, pairs)  5.62 us
    pallas_call x1, Pallas kernels, body(): call(block_kernel, [shape((modes + 8, modes), F32), shape((7,) + plane, F...  4.02 us
    pallas_call x1, Pallas kernels, body(): call(finish_kernel, [shape((1, modes), F32), shape(field, F32)], [SMEM] +...  3.28 us
    ppermute x1, waiting for transfers between devices, far_partner(): return lax.ppermute(value, ('sub', 'pln'), pairs)  3.18 us
    ppermute x4, starting transfers between devices, partner(): return lax.ppermute(value, ('sub', 'pln'), pairs)  3.03 us
    ppermute x2, starting transfers between devices, swapped_all(): return lax.ppermute(value, ('sub', 'pln'), pairs)  2.83 us
    pallas_call x1, Pallas kernels, body(): call(stage_kernel, [shape((modes + 1, rows, layers), BF16), shape((modes...  2.02 us
    ppermute x1, starting transfers between devices, far_partner(): return lax.ppermute(value, ('sub', 'pln'), pairs)  1.82 us
  transfers between devices with their start and end apart: 12, of which 6 were waited for; matrix products, arithmetic and copies ran while one was open for 0% of the time, Pallas kernels for 24%

profile of v10, /device:TPU:0, one launch (start us, length us, event | category | flops | bytes accessed | tf_op | source)
XLA Modules:
  0.0 36.0 jit_solution(5748691948341727916)
XLA Ops:
  0.6 0.0 copy-start.1
  0.6 0.0 copy-start
  0.7 0.1 stack.24.place
  0.8 2.0 %shard_map.61 = (bf16[65,64,128]{2,1,0:T(8,128)(2,1)S(1)}, bf16[66,32,128]{2,1,0:T(8,128)(2,1)S(1)}) custom-call(s32[7]{0:T(128)S(1)} %stack.24.place, s32[2,64,128]{2,1,0:T(8,128)} %labels_far.1, bf16[64,2,64,128]{3,2,1,0:T(8,128)(2,1)} %zvec.5), custom_call_target="tpu_custom_call" | custom-call | bytes 2097152 | tf_op jit(solution)/shard_map/pallas_call | solution.py:557
  2.8 0.5 %collective-permute-start = (bf16[65,64,128]{2,1,0:T(8,128)(2,1)S(1)}, bf16[65,64,128]{2,1,0:T(8,128)(2,1)S(1)}, u32[]{:S(2)}, u32[]{:S(2)}) collective-permute-start(bf16[65,64,128]{2,1,0:T(8,128)(2,1)S(1)} %get-tuple-element.23), channel_id=1, source_target_pairs={{0,1},{1,0},{2,3},{3,2},{4,5},{5,4},{6,7},{7,6},{8,9},{9,8},{10,11... | collective-permute-start | bytes 3194888 | tf_op jit(solution)/shard_map/ppermute | solution.py:509
  3.3 2.6 %collective-permute-start.1 = (bf16[66,32,128]{2,1,0:T(8,128)(2,1)S(1)}, bf16[66,32,128]{2,1,0:T(8,128)(2,1)S(1)}, u32[]{:S(2)}, u32[]{:S(2)}) collective-permute-start(bf16[66,32,128]{2,1,0:T(8,128)(2,1)S(1)} %get-tuple-element.25), channel_id=1, source_target_pairs={{0,4},{1,2},{2,1},{3,7},{4,0},{5,6},{6,5},{7,3},{8,12},{9,10},{10,... | collective-permute-start | bytes 1622024 | tf_op jit(solution)/shard_map/ppermute | solution.py:522
  5.9 1.2 %shard_map.59 = (bf16[64,32,128]{2,1,0:T(8,128)(2,1)S(1)}, bf16[80,128]{1,0:T(8,128)(2,1)S(1)}, bf16[80,128]{1,0:T(8,128)(2,1)S(1)}) custom-call(s32[7]{0:T(128)S(1)} %stack.24.place, s32[2,64,128]{2,1,0:T(8,128)S(1)} %copy-done.1, bf16[64,2,64,128]{3,2,1,0:T(8,128)(2,1)S(1)} %copy-done), custom_call_target="tpu_custom_call" | custom-call | flops 10000000 | bytes 6291456 | tf_op jit(solution)/shard_map/pallas_call | solution.py:567
  7.1 0.1 collective-permute-start.2
  7.2 5.0 %collective-permute-start.3 = (bf16[80,128]{1,0:T(8,128)(2,1)S(1)}, bf16[80,128]{1,0:T(8,128)(2,1)S(1)}, u32[]{:S(2)}, u32[]{:S(2)}) collective-permute-start(bf16[80,128]{1,0:T(8,128)(2,1)S(1)} %get-tuple-element.26.two_pack), channel_id=1, source_target_pairs={{0,28},{4,8},{8,4},{12,16},{16,12},{20,24},{24,20},{28,0},{1,29},{... | collective-permute-start | bytes 61448 | tf_op jit(solution)/shard_map/ppermute | solution.py:509
  12.2 4.0 %shard_map.60 = (f32[72,64]{1,0:T(8,128)S(1)}, f32[7,64,128]{2,1,0:T(8,128)S(1)}, bf16[2,64,64,128]{3,2,1,0:T(8,128)(2,1)S(1)}) custom-call(s32[7]{0:T(128)S(1)} %stack.24.place, f32[4]{0:T(128)S(1)} %copy-done.3, s32[2,64,128]{2,1,0:T(8,128)S(1)} %copy-done.1, f32[2,64,128]{2,1,0:T(8,128)S(1)} %copy-done.2, bf16[64,2,64,128]{3,2,1,0:T(8,128)(2,1)S(1)} %copy-done, ...), custom_call_target="tpu_custom_call" | custom-call | flops 400000000 | bytes 3145728 | tf_op jit(solution)/shard_map/pallas_call | solution.py:578
  16.3 0.0 collective-permute-done.inner_got
  16.3 1.4 %shard_map.62 = (f32[72,64]{1,0:T(8,128)S(1)}, f32[64,128]{1,0:T(8,128)S(1)}) custom-call(s32[7]{0:T(128)S(1)} %stack.24.place, f32[4]{0:T(128)S(1)} %copy-done.3, f32[72,64]{1,0:T(8,128)S(1)} %get-tuple-element.20.partial, f32[7,64,128]{2,1,0:T(8,128)S(1)} %get-tuple-element.21.weights.refs_10_, bf16[2,64,64,128]{3,2,1,0:T(8,128)(2,1)S(1)} %get-tuple-element.22.here, ...), custom_call_target="tpu_custom_call" | custom-call | flops 100000000 | bytes 1048576 | tf_op jit(solution)/shard_map/pallas_call | solution.py:591
  17.7 0.0 collective-permute-done.3.two_got
  17.7 0.0 collective-permute-done.1.outer_got
  17.7 1.6 %shard_map.63 = (f32[72,128]{1,0:T(8,128)S(1)}, f32[64,128]{1,0:T(8,128)S(1)}) custom-call(s32[7]{0:T(128)S(1)} %stack.24.place, f32[4]{0:T(128)S(1)} %copy-done.3, f32[72,64]{1,0:T(8,128)S(1)} %get-tuple-element.24.partial, f32[7,64,128]{2,1,0:T(8,128)S(1)} %get-tuple-element.21.weights.refs_10_, bf16[2,64,64,128]{3,2,1,0:T(8,128)(2,1)S(1)} %get-tuple-element.22.here, ...), custom_call_target="tpu_custom_call" | custom-call | flops 100000000 | bytes 1048576 | tf_op jit(solution)/shard_map/pallas_call | solution.py:599
  19.3 0.1 collective-permute-start.4
  19.3 1.2 %collective-permute-done.4 = f32[72,128]{1,0:T(8,128)S(1)} collective-permute-done((f32[72,128]{1,0:T(8,128)S(1)}, f32[72,128]{1,0:T(8,128)S(1)}, u32[]{:S(2)}, u32[]{:S(2)}) %collective-permute-start.4) | collective-permute-done | bytes 36896 | tf_op jit(solution)/shard_map/ppermute | solution.py:526
  20.5 0.7 %collective-permute-start.5 = (f32[72,128]{1,0:T(8,128)S(1)}, f32[72,128]{1,0:T(8,128)S(1)}, u32[]{:S(2)}, u32[]{:S(2)}) collective-permute-start(f32[72,128]{1,0:T(8,128)S(1)} %add.12.own.after), channel_id=1, source_target_pairs={{0,3},{1,2},{2,1},{3,0},{4,7},{5,6},{6,5},{7,4},{8,11},{9,10},{10,... | collective-permute-start | bytes 110600 | tf_op jit(solution)/shard_map/ppermute | solution.py:534
  21.2 2.3 %collective-permute-start.7 = (f32[72,128]{1,0:T(8,128)S(1)}, f32[72,128]{1,0:T(8,128)S(1)}, u32[]{:S(2)}, u32[]{:S(2)}) collective-permute-start(f32[72,128]{1,0:T(8,128)S(1)} %add.12.own.after), channel_id=1, source_target_pairs={{0,7},{1,6},{2,5},{3,4},{4,3},{5,2},{6,1},{7,0},{8,15},{9,14},{10,... | collective-permute-start | bytes 110600 | tf_op jit(solution)/shard_map/ppermute | solution.py:534
  23.5 0.2 collective-permute-start.11
  23.8 0.2 collective-permute-done.5.across
  24.0 0.7 %collective-permute-done.6.beside = f32[72,128]{1,0:T(8,128)S(1)} collective-permute-done((f32[72,128]{1,0:T(8,128)S(1)}, f32[72,128]{1,0:T(8,128)S(1)}, u32[]{:S(2)}, u32[]{:S(2)}) %collective-permute-start.6) | collective-permute-done | bytes 36896 | tf_op jit(solution)/shard_map/ppermute | solution.py:534
  24.7 0.9 %collective-permute-done.7.oblique = f32[72,128]{1,0:T(8,128)S(1)} collective-permute-done((f32[72,128]{1,0:T(8,128)S(1)}, f32[72,128]{1,0:T(8,128)S(1)}, u32[]{:S(2)}, u32[]{:S(2)}) %collective-permute-start.7) | collective-permute-done | bytes 36896 | tf_op jit(solution)/shard_map/ppermute | solution.py:534
  25.6 1.8 %collective-permute-start.8 = (bf16[2,80,128]{2,1,0:T(8,128)(2,1)S(1)}, bf16[2,80,128]{2,1,0:T(8,128)(2,1)S(1)}, u32[]{:S(2)}, u32[]{:S(2)}) collective-permute-start(bf16[2,80,128]{2,1,0:T(8,128)(2,1)S(1)} %shard_map.64.pair.refs_0_), channel_id=1, source_target_pairs={{0,16},{1,25},{2,18},{3,27},{4,20},{5,29},{6,22},{7,31},{8,24},{9,... | collective-permute-start | bytes 122888 | tf_op jit(solution)/shard_map/ppermute | solution.py:543
  27.4 0.1 collective-permute-start.9
  27.5 0.8 %shard_map.67 = (f32[2,6,64,128]{3,2,1,0:T(8,128)S(1)}, f32[2,64,128]{2,1,0:T(8,128)S(1)}) custom-call(s32[7]{0:T(128)S(1)} %stack.24.place, f32[4]{0:T(128)S(1)} %copy-done.3, bf16[2,80,128]{2,1,0:T(8,128)(2,1)S(1)} %shard_map.64.pair.refs_0_, bf16[80,128]{1,0:T(8,128)(2,1)S(1)} %collective-permute-done.2.one_got, ...), custom_call_target="tpu_custom_call" | custom-call | flops 2147483648 | bytes 1048576 | tf_op jit(solution)/shard_map/pallas_call | solution.py:621
  28.3 3.2 %collective-permute-done.8.refs_1_ = bf16[2,80,128]{2,1,0:T(8,128)(2,1)S(1)} collective-permute-done((bf16[2,80,128]{2,1,0:T(8,128)(2,1)S(1)}, bf16[2,80,128]{2,1,0:T(8,128)(2,1)S(1)}, u32[]{:S(2)}, u32[]{:S(2)}) %collective-permute-start.8) | collective-permute-done | bytes 40992 | tf_op jit(solution)/shard_map/ppermute | solution.py:543
  31.5 0.0 collective-permute-start.10
  31.5 1.1 %shard_map.65 = (f32[64,2,64,128]{3,2,1,0:T(8,128)S(1)}, f32[64,64,128]{2,1,0:T(8,128)S(1)}, f32[64,32,128]{2,1,0:T(8,128)S(1)}) custom-call(s32[7]{0:T(128)S(1)} %stack.24.place, bf16[2,80,128]{2,1,0:T(8,128)(2,1)S(1)} %shard_map.64.pair.refs_0_, bf16[64,2,64,128]{3,2,1,0:T(8,128)(2,1)S(1)} %copy-done, ...), custom_call_target="tpu_custom_call" | custom-call | flops 1073741824 | bytes 1048576 | tf_op jit(solution)/shard_map/pallas_call | solution.py:630
  32.6 0.1 collective-permute-done.10.refs_3_
  32.7 0.0 collective-permute-done.11.refs_7_
  32.7 3.3 %shard_map.68 = (f32[1,64]{1,0:T(1,128)}, f32[2,64,128]{2,1,0:T(8,128)}) custom-call(s32[7]{0:T(128)S(1)} %stack.24.place, bf16[2,80,128]{2,1,0:T(8,128)(2,1)S(1)} %shard_map.64.pair.refs_0_, bf16[2,80,128]{2,1,0:T(8,128)(2,1)S(1)} %collective-permute-done.8.refs_1_, bf16[2,80,128]{2,1,0:T(8,128)(2,1)S(1)} %collective-permute-done.9.refs_2_, ...), custom_call_target="tpu_custom_call" | custom-call | flops 10000000 | bytes 5242880 | tf_op jit(solution)/shard_map/pallas_call | solution.py:642
  (12 shorter events, 0.1 us)
Async XLA Ops:
  0.6 5.3 %copy-start.1 = (s32[2,64,128]{2,1,0:T(8,128)S(1)}, s32[2,64,128]{2,1,0:T(8,128)}, u32[]{:S(2)}) copy-start(s32[2,64,128]{2,1,0:T(8,128)} %labels_far.1) | copy-start | bytes 196612
  0.6 5.3 %copy-start = (bf16[64,2,64,128]{3,2,1,0:T(8,128)(2,1)S(1)}, bf16[64,2,64,128]{3,2,1,0:T(8,128)(2,1)}, u32[]{:S(2)}) copy-start(bf16[64,2,64,128]{3,2,1,0:T(8,128)(2,1)} %zvec.5) | copy-start | bytes 6291460
  0.8 11.5 %copy-start.2 = (f32[2,64,128]{2,1,0:T(8,128)S(1)}, f32[2,64,128]{2,1,0:T(8,128)}, u32[]{:S(2)}) copy-start(f32[2,64,128]{2,1,0:T(8,128)} %refs_13_.1) | copy-start | bytes 196612
  0.8 11.5 %copy-start.3 = (f32[4]{0:T(128)S(1)}, f32[4]{0:T(128)}, u32[]{:S(2)}) copy-start(f32[4]{0:T(128)} %levels.7) | copy-start | bytes 52
  2.8 13.5 %collective-permute-start = (bf16[65,64,128]{2,1,0:T(8,128)(2,1)S(1)}, bf16[65,64,128]{2,1,0:T(8,128)(2,1)S(1)}, u32[]{:S(2)}, u32[]{:S(2)}) collective-permute-start(bf16[65,64,128]{2,1,0:T(8,128)(2,1)S(1)} %get-tuple-element.23), channel_id=1, source_target_pairs={{0,1},{1,0},{2,3},{3,2},{4,5},{5,4},{6,7},{7,6},{8,9},{9,8},{10,11... | collective-permute-start | bytes 3194888 | tf_op jit(solution)/shard_map/ppermute | solution.py:509
  3.3 14.4 %collective-permute-start.1 = (bf16[66,32,128]{2,1,0:T(8,128)(2,1)S(1)}, bf16[66,32,128]{2,1,0:T(8,128)(2,1)S(1)}, u32[]{:S(2)}, u32[]{:S(2)}) collective-permute-start(bf16[66,32,128]{2,1,0:T(8,128)(2,1)S(1)} %get-tuple-element.25), channel_id=1, source_target_pairs={{0,4},{1,2},{2,1},{3,7},{4,0},{5,6},{6,5},{7,3},{8,12},{9,10},{10,... | collective-permute-start | bytes 1622024 | tf_op jit(solution)/shard_map/ppermute | solution.py:522
  7.1 10.5 %collective-permute-start.2 = (bf16[80,128]{1,0:T(8,128)(2,1)S(1)}, bf16[80,128]{1,0:T(8,128)(2,1)S(1)}, u32[]{:S(2)}, u32[]{:S(2)}) collective-permute-start(bf16[80,128]{1,0:T(8,128)(2,1)S(1)} %get-tuple-element.19.after.one_pack), channel_id=1, source_target_pairs={{0,4},{4,0},{8,12},{12,8},{16,20},{20,16},{24,28},{28,24},{1,5},{5... | collective-permute-start | bytes 61448 | tf_op jit(solution)/shard_map/ppermute | solution.py:509
  7.2 10.5 %collective-permute-start.3 = (bf16[80,128]{1,0:T(8,128)(2,1)S(1)}, bf16[80,128]{1,0:T(8,128)(2,1)S(1)}, u32[]{:S(2)}, u32[]{:S(2)}) collective-permute-start(bf16[80,128]{1,0:T(8,128)(2,1)S(1)} %get-tuple-element.26.two_pack), channel_id=1, source_target_pairs={{0,28},{4,8},{8,4},{12,16},{16,12},{20,24},{24,20},{28,0},{1,29},{... | collective-permute-start | bytes 61448 | tf_op jit(solution)/shard_map/ppermute | solution.py:509
  19.3 1.3 %collective-permute-start.4 = (f32[72,128]{1,0:T(8,128)S(1)}, f32[72,128]{1,0:T(8,128)S(1)}, u32[]{:S(2)}, u32[]{:S(2)}) collective-permute-start(f32[72,128]{1,0:T(8,128)S(1)} %get-tuple-element.27), channel_id=1, source_target_pairs={{0,1},{1,0},{2,3},{3,2},{4,5},{5,4},{6,7},{7,6},{8,9},{9,8},{10,11... | collective-permute-start | bytes 110600 | tf_op jit(solution)/shard_map/ppermute | solution.py:526
  20.5 3.4 %collective-permute-start.5 = (f32[72,128]{1,0:T(8,128)S(1)}, f32[72,128]{1,0:T(8,128)S(1)}, u32[]{:S(2)}, u32[]{:S(2)}) collective-permute-start(f32[72,128]{1,0:T(8,128)S(1)} %add.12.own.after), channel_id=1, source_target_pairs={{0,3},{1,2},{2,1},{3,0},{4,7},{5,6},{6,5},{7,4},{8,11},{9,10},{10,... | collective-permute-start | bytes 110600 | tf_op jit(solution)/shard_map/ppermute | solution.py:534
  21.2 3.4 %collective-permute-start.6 = (f32[72,128]{1,0:T(8,128)S(1)}, f32[72,128]{1,0:T(8,128)S(1)}, u32[]{:S(2)}, u32[]{:S(2)}) collective-permute-start(f32[72,128]{1,0:T(8,128)S(1)} %add.12.own.after), channel_id=1, source_target_pairs={{0,5},{1,4},{2,7},{3,6},{4,1},{5,0},{6,3},{7,2},{8,13},{9,12},{10,... | collective-permute-start | bytes 110600 | tf_op jit(solution)/shard_map/ppermute | solution.py:534
  21.2 4.3 %collective-permute-start.7 = (f32[72,128]{1,0:T(8,128)S(1)}, f32[72,128]{1,0:T(8,128)S(1)}, u32[]{:S(2)}, u32[]{:S(2)}) collective-permute-start(f32[72,128]{1,0:T(8,128)S(1)} %add.12.own.after), channel_id=1, source_target_pairs={{0,7},{1,6},{2,5},{3,4},{4,3},{5,2},{6,1},{7,0},{8,15},{9,14},{10,... | collective-permute-start | bytes 110600 | tf_op jit(solution)/shard_map/ppermute | solution.py:534
  23.5 9.2 %collective-permute-start.11 = (bf16[64,32,128]{2,1,0:T(8,128)(2,1)S(1)}, bf16[64,32,128]{2,1,0:T(8,128)(2,1)S(1)}, u32[]{:S(2)}, u32[]{:S(2)}) collective-permute-start(bf16[64,32,128]{2,1,0:T(8,128)(2,1)S(1)} %shard_map.66), channel_id=1, source_target_pairs={{0,4},{1,2},{2,1},{3,7},{4,0},{5,6},{6,5},{7,3},{8,12},{9,10},{10,... | collective-permute-start | bytes 1572872 | tf_op jit(solution)/shard_map/ppermute | solution.py:522
  25.6 5.9 %collective-permute-start.8 = (bf16[2,80,128]{2,1,0:T(8,128)(2,1)S(1)}, bf16[2,80,128]{2,1,0:T(8,128)(2,1)S(1)}, u32[]{:S(2)}, u32[]{:S(2)}) collective-permute-start(bf16[2,80,128]{2,1,0:T(8,128)(2,1)S(1)} %shard_map.64.pair.refs_0_), channel_id=1, source_target_pairs={{0,16},{1,25},{2,18},{3,27},{4,20},{5,29},{6,22},{7,31},{8,24},{9,... | collective-permute-start | bytes 122888 | tf_op jit(solution)/shard_map/ppermute | solution.py:543
  27.4 5.1 %collective-permute-start.9 = (bf16[2,80,128]{2,1,0:T(8,128)(2,1)S(1)}, bf16[2,80,128]{2,1,0:T(8,128)(2,1)S(1)}, u32[]{:S(2)}, u32[]{:S(2)}) collective-permute-start(bf16[2,80,128]{2,1,0:T(8,128)(2,1)S(1)} %shard_map.64.pair.refs_0_), channel_id=1, source_target_pairs={{0,9},{1,8},{2,11},{3,10},{4,13},{5,12},{6,15},{7,14},{8,1},{9,0},... | collective-permute-start | bytes 122888 | tf_op jit(solution)/shard_map/ppermute | solution.py:534
  31.5 1.2 %collective-permute-start.10 = (bf16[2,80,128]{2,1,0:T(8,128)(2,1)S(1)}, bf16[2,80,128]{2,1,0:T(8,128)(2,1)S(1)}, u32[]{:S(2)}, u32[]{:S(2)}) collective-permute-start(bf16[2,80,128]{2,1,0:T(8,128)(2,1)S(1)} %collective-permute-done.8.refs_1_), channel_id=1, source_target_pairs={{0,1},{1,0},{2,3},{3,2},{4,5},{5,4},{6,7},{7,6},{8,9},{9,8},{10,11... | collective-permute-start | bytes 122888 | tf_op jit(solution)/shard_map/ppermute | solution.py:526

commit v11 on v10

--- a/solution.py
+++ b/solution.py
@@ -306,10 +306,9 @@
         terms[x, 5] = end_weight
 
 
-def pair_kernel(own, across, beside, oblique, out):
+def role_kernel(place, own, across, beside, out):
     modes = own.shape[1] // 2
-    encode(own[...] + across[...], modes, out.at[0])
-    encode(beside[...] + oblique[...], modes, out.at[1])
+    encode(jnp.where(place[3] == 0, own[...], beside[...]) + across[...], modes, out)
 
 
 def single_kernel(own, out):
@@ -378,7 +377,7 @@
             held_here = block.shape[0]
             if held_here <= 8:
                 for entry in range(held_here):
-                    s = jnp.bitwise_xor(place[3 + index], entry)
+                    s = jnp.bitwise_xor(place[4 + index], entry * len(blocks))
                     carry = body(block.at[entry], s, carry)
             else:
                 carry = lax.fori_loop(
@@ -534,12 +533,15 @@
     return lax.ppermute(value, ("sub", "pln"), pairs)
 
 
-FAR = (4, 6)
-
-
-def far_partner(value):
+def role_of(s, p):
+    return (p ^ (p >> 1) ^ (s >> 2)) & 1
+
+
+def across(value):
     subs, count = lax.axis_size("sub"), lax.axis_size("pln")
-    pairs = [(s * count + p, (s ^ FAR[p % 2]) * count + p) for s in range(subs) for p in range(count)]
+    pairs = [
+        (s * count + p, (s ^ role_of(s, p)) * count + (p ^ 3)) for s in range(subs) for p in range(count)
+    ]
     return lax.ppermute(value, ("sub", "pln"), pairs)
 
 
@@ -549,10 +551,10 @@
     subs, parts = lax.axis_size("sub"), lax.axis_size("pln")
     shape = jax.ShapeDtypeStruct
     at_sub, at_pln = lax.axis_index("sub"), lax.axis_index("pln")
-    core = at_pln % 2
-    masks = (0, FAR[0] + core * (FAR[1] - FAR[0]), 2, FAR[1] + core * (FAR[0] - FAR[1]))
-    orders = [at_sub ^ mask for mask in masks] if parts == 4 and subs == 8 else [0] * 4
-    place = jnp.stack([jnp.int32(v) for v in (at_sub, at_pln, parts, *orders)])
+    split = parts == 4 and subs == 8
+    role = role_of(at_sub, at_pln)
+    orders = [at_sub ^ role, at_sub ^ role ^ 1] if split else [0, 0]
+    place = jnp.stack([jnp.int32(v) for v in (at_sub, at_pln, parts, role, *orders)])
     pack = shape((modes + 16, planes * rows), BF16)
     inner_send, outer_near = call(
         stage_kernel,
@@ -605,17 +607,16 @@
         moved=1 << 20,
     )(place, levels, partial, weights, here, outer_got, one_pack, two_pack, one_got, two_got)
     packed = (modes + 16, 2 * modes)
-    if parts == 4 and subs == 8:
+    if split:
         block = block + exchanged(block, "pln", 1)
-        others = [partner(block, *masks) for masks in ((0, 3), (1, 1), (1, 3))]
-        [pair] = call(
-            pair_kernel, [shape((2,) + packed, BF16)], [VMEM] * 4, flops=1 << 33
-        )(block, *others)
-        far = far_partner(pair)
-        blocks = [pair, far, partner(pair, 2, 1), exchanged(far, "pln", 1)]
+        [packed_here] = call(
+            role_kernel, [shape(packed, BF16)], [SMEM] + [VMEM] * 3, flops=1 << 33
+        )(place, block, across(block), partner(block, 1, 1))
+        mine = jnp.stack([packed_here] + [partner(packed_here, *masks) for masks in ((2, 0), (4, 1), (6, 1))])
+        blocks = [mine, exchanged(mine, "pln", 1)]
     else:
-        [single] = call(single_kernel, [shape(packed, BF16)], [VMEM])(lax.psum(block, "pln"))
-        blocks = [lax.all_gather(single, "sub")]
+        [packed_here] = call(single_kernel, [shape(packed, BF16)], [VMEM])(lax.psum(block, "pln"))
+        blocks = [lax.all_gather(packed_here, "sub")]
     [outer_rest] = call(release_kernel, [rest], [ANY] * 2, aliases={1: 0})(block, outer_rest)
     outer_last = swapped_all(outer_rest)
     terms, picked = call(
@@ -626,7 +627,7 @@
 
         flops=1 << 31,
         moved=1 << 20,
-    )(place, levels, blocks[0], one_got, two_got, weights, inner_face, outer_face)
+    )(place, levels, packed_here, one_got, two_got, weights, inner_face, outer_face)
     wide = call(
         widen_kernel,
         [
@@ -637,7 +638,7 @@
         [SMEM, ANY] + [VMEM] * 3,
         flops=1 << 30,
         moved=1 << 20,
-    )(place, blocks[0], zvec, inner_got, outer_got)
+    )(place, packed_here, zvec, inner_got, outer_got)
     return tuple(
         call(
             finish_kernel,

time: 36.1 us -> 36.5 us (1.011)
  waiting for transfers between devices: 6.35 us -> 5.06 us
  starting transfers between devices: 13.4 us -> 14.5 us
  Pallas kernels: 15.4 us -> 15.9 us
    ppermute x4, starting transfers between devices: 3.03 us -> 5.4 us  [partner(): return lax.ppermute(value, ('sub', 'pln'), pairs)]
    ppermute x1, waiting for transfers between devices: 3.18 us -> 1.45 us  [across(): return lax.ppermute(value, ('sub', 'pln'), pairs)]
    ppermute x1, starting transfers between devices: 1.82 us -> 0.7 us  [across(): return lax.ppermute(value, ('sub', 'pln'), pairs)]
    pallas_call x1, Pallas kernels: 0.04 us -> 0.57 us  [body(): call(role_kernel, [shape(packed, BF16)], [SMEM] + [VMEM] * 3, flops=1 << 33)]
    ppermute x4, waiting for transfers between devices: 1.82 us -> 2.19 us  [partner(): return lax.ppermute(value, ('sub', 'pln'), pairs)]
  transfers between devices with their start and end apart: 12 -> 12, of which waited for: 6 -> 7; matrix products, arithmetic and copies ran while one was open for 0% -> 0% of each run, Pallas kernels for 24% -> 25%
where the time goes in v11:
time: 36.5 us; the launch traced here: 36.3 us
  Pallas kernels  15.9 us (44%)
  starting transfers between devices  14.5 us (40%)
  waiting for transfers between devices  5.06 us (14%)
  between operations  0.75 us (2%)
    ppermute x3, starting transfers between devices, swapped(): return lax.ppermute(value, axis, pairs)  5.62 us
    ppermute x4, starting transfers between devices, partner(): return lax.ppermute(value, ('sub', 'pln'), pairs)  5.4 us
    pallas_call x1, Pallas kernels, body(): call(block_kernel, [shape((modes + 8, modes), F32), shape((7,) + plane, F...  4.02 us
    pallas_call x1, Pallas kernels, body(): call(finish_kernel, [shape((1, modes), F32), shape(field, F32)], [SMEM] +...  3.28 us
    ppermute x2, starting transfers between devices, swapped_all(): return lax.ppermute(value, ('sub', 'pln'), pairs)  2.6 us
    ppermute x4, waiting for transfers between devices, partner(): return lax.ppermute(value, ('sub', 'pln'), pairs)  2.19 us
    pallas_call x1, Pallas kernels, body(): call(stage_kernel, [shape((modes + 1, rows, layers), BF16), shape((modes...  2.03 us
    pallas_call x1, Pallas kernels, body(): call(outer_kernel, [shape((modes + 8, 2 * modes), F32), shape(plane, F32)...  1.57 us
  transfers between devices with their start and end apart: 12, of which 7 were waited for; matrix products, arithmetic and copies ran while one was open for 0% of the time, Pallas kernels for 25%

profile of v11, /device:TPU:0, one launch (start us, length us, event | category | flops | bytes accessed | tf_op | source)
XLA Modules:
  0.0 36.3 jit_solution(17988800728122704139)
XLA Ops:
  0.6 0.0 copy-start.1
  0.6 0.0 copy-start
  0.7 0.1 stack.38.place
  0.8 2.0 %shard_map.61 = (bf16[65,64,128]{2,1,0:T(8,128)(2,1)S(1)}, bf16[66,32,128]{2,1,0:T(8,128)(2,1)S(1)}) custom-call(s32[6]{0:T(128)S(1)} %stack.38.place, s32[2,64,128]{2,1,0:T(8,128)} %labels_far.1, bf16[64,2,64,128]{3,2,1,0:T(8,128)(2,1)} %zvec.5), custom_call_target="tpu_custom_call" | custom-call | bytes 2097152 | tf_op jit(solution)/shard_map/pallas_call | solution.py:559
  2.8 0.5 %collective-permute-start = (bf16[65,64,128]{2,1,0:T(8,128)(2,1)S(1)}, bf16[65,64,128]{2,1,0:T(8,128)(2,1)S(1)}, u32[]{:S(2)}, u32[]{:S(2)}) collective-permute-start(bf16[65,64,128]{2,1,0:T(8,128)(2,1)S(1)} %get-tuple-element.23), channel_id=1, source_target_pairs={{0,1},{1,0},{2,3},{3,2},{4,5},{5,4},{6,7},{7,6},{8,9},{9,8},{10,11... | collective-permute-start | bytes 3194888 | tf_op jit(solution)/shard_map/ppermute | solution.py:508
  3.3 2.6 %collective-permute-start.1 = (bf16[66,32,128]{2,1,0:T(8,128)(2,1)S(1)}, bf16[66,32,128]{2,1,0:T(8,128)(2,1)S(1)}, u32[]{:S(2)}, u32[]{:S(2)}) collective-permute-start(bf16[66,32,128]{2,1,0:T(8,128)(2,1)S(1)} %get-tuple-element.25), channel_id=1, source_target_pairs={{0,4},{1,2},{2,1},{3,7},{4,0},{5,6},{6,5},{7,3},{8,12},{9,10},{10,... | collective-permute-start | bytes 1622024 | tf_op jit(solution)/shard_map/ppermute | solution.py:521
  5.9 1.2 %shard_map.59 = (bf16[64,32,128]{2,1,0:T(8,128)(2,1)S(1)}, bf16[80,128]{1,0:T(8,128)(2,1)S(1)}, bf16[80,128]{1,0:T(8,128)(2,1)S(1)}) custom-call(s32[6]{0:T(128)S(1)} %stack.38.place, s32[2,64,128]{2,1,0:T(8,128)S(1)} %copy-done.1, bf16[64,2,64,128]{3,2,1,0:T(8,128)(2,1)S(1)} %copy-done), custom_call_target="tpu_custom_call" | custom-call | flops 10000000 | bytes 6291456 | tf_op jit(solution)/shard_map/pallas_call | solution.py:569
  7.1 0.1 collective-permute-start.2
  7.2 5.0 %collective-permute-start.3 = (bf16[80,128]{1,0:T(8,128)(2,1)S(1)}, bf16[80,128]{1,0:T(8,128)(2,1)S(1)}, u32[]{:S(2)}, u32[]{:S(2)}) collective-permute-start(bf16[80,128]{1,0:T(8,128)(2,1)S(1)} %get-tuple-element.26.two_pack), channel_id=1, source_target_pairs={{0,28},{4,8},{8,4},{12,16},{16,12},{20,24},{24,20},{28,0},{1,29},{... | collective-permute-start | bytes 61448 | tf_op jit(solution)/shard_map/ppermute | solution.py:508
  12.2 4.0 %shard_map.60 = (f32[72,64]{1,0:T(8,128)S(1)}, f32[7,64,128]{2,1,0:T(8,128)S(1)}, bf16[2,64,64,128]{3,2,1,0:T(8,128)(2,1)S(1)}) custom-call(s32[6]{0:T(128)S(1)} %stack.38.place, f32[4]{0:T(128)S(1)} %copy-done.3, s32[2,64,128]{2,1,0:T(8,128)S(1)} %copy-done.1, f32[2,64,128]{2,1,0:T(8,128)S(1)} %copy-done.2, bf16[64,2,64,128]{3,2,1,0:T(8,128)(2,1)S(1)} %copy-done, ...), custom_call_target="tpu_custom_call" | custom-call | flops 400000000 | bytes 3145728 | tf_op jit(solution)/shard_map/pallas_call | solution.py:580
  16.3 0.0 collective-permute-done.inner_got
  16.3 1.4 %shard_map.62 = (f32[72,64]{1,0:T(8,128)S(1)}, f32[64,128]{1,0:T(8,128)S(1)}) custom-call(s32[6]{0:T(128)S(1)} %stack.38.place, f32[4]{0:T(128)S(1)} %copy-done.3, f32[72,64]{1,0:T(8,128)S(1)} %get-tuple-element.20.partial, f32[7,64,128]{2,1,0:T(8,128)S(1)} %get-tuple-element.21.weights.refs_8_, bf16[2,64,64,128]{3,2,1,0:T(8,128)(2,1)S(1)} %get-tuple-element.22.here, ...), custom_call_target="tpu_custom_call" | custom-call | flops 100000000 | bytes 1048576 | tf_op jit(solution)/shard_map/pallas_call | solution.py:593
  17.6 0.0 collective-permute-done.2.one_got
  17.6 0.0 collective-permute-done.3.two_got
  17.7 1.6 %shard_map.63 = (f32[72,128]{1,0:T(8,128)S(1)}, f32[64,128]{1,0:T(8,128)S(1)}) custom-call(s32[6]{0:T(128)S(1)} %stack.38.place, f32[4]{0:T(128)S(1)} %copy-done.3, f32[72,64]{1,0:T(8,128)S(1)} %get-tuple-element.24.partial, f32[7,64,128]{2,1,0:T(8,128)S(1)} %get-tuple-element.21.weights.refs_8_, bf16[2,64,64,128]{3,2,1,0:T(8,128)(2,1)S(1)} %get-tuple-element.22.here, ...), custom_call_target="tpu_custom_call" | custom-call | flops 100000000 | bytes 1048576 | tf_op jit(solution)/shard_map/pallas_call | solution.py:601
  19.2 0.1 collective-permute-start.4
  19.3 1.2 %collective-permute-done.4 = f32[72,128]{1,0:T(8,128)S(1)} collective-permute-done((f32[72,128]{1,0:T(8,128)S(1)}, f32[72,128]{1,0:T(8,128)S(1)}, u32[]{:S(2)}, u32[]{:S(2)}) %collective-permute-start.4) | collective-permute-done | bytes 36896 | tf_op jit(solution)/shard_map/ppermute | solution.py:525
  20.5 0.7 %collective-permute-start.5 = (f32[72,128]{1,0:T(8,128)S(1)}, f32[72,128]{1,0:T(8,128)S(1)}, u32[]{:S(2)}, u32[]{:S(2)}) collective-permute-start(f32[72,128]{1,0:T(8,128)S(1)} %add.3.own.after), channel_id=1, source_target_pairs={{0,3},{1,6},{2,5},{3,0},{4,7},{5,2},{6,1},{7,4},{8,11},{9,14},{10,... | collective-permute-start | bytes 110600 | tf_op jit(solution)/shard_map/ppermute | solution.py:545
  21.2 1.2 %collective-permute-start.6 = (f32[72,128]{1,0:T(8,128)S(1)}, f32[72,128]{1,0:T(8,128)S(1)}, u32[]{:S(2)}, u32[]{:S(2)}) collective-permute-start(f32[72,128]{1,0:T(8,128)S(1)} %add.3.own.after), channel_id=1, source_target_pairs={{0,5},{1,4},{2,7},{3,6},{4,1},{5,0},{6,3},{7,2},{8,13},{9,12},{10,... | collective-permute-start | bytes 110600 | tf_op jit(solution)/shard_map/ppermute | solution.py:533
  22.5 1.5 %collective-permute-done.5.across = f32[72,128]{1,0:T(8,128)S(1)} collective-permute-done((f32[72,128]{1,0:T(8,128)S(1)}, f32[72,128]{1,0:T(8,128)S(1)}, u32[]{:S(2)}, u32[]{:S(2)}) %collective-permute-start.5) | collective-permute-done | bytes 36896 | tf_op jit(solution)/shard_map/ppermute | solution.py:545
  23.9 0.8 %collective-permute-done.6.beside = f32[72,128]{1,0:T(8,128)S(1)} collective-permute-done((f32[72,128]{1,0:T(8,128)S(1)}, f32[72,128]{1,0:T(8,128)S(1)}, u32[]{:S(2)}, u32[]{:S(2)}) %collective-permute-start.6) | collective-permute-done | bytes 36896 | tf_op jit(solution)/shard_map/ppermute | solution.py:533
  24.7 0.6 %shard_map.64.pair = bf16[80,128]{1,0:T(8,128)(2,1)S(1)} custom-call(s32[6]{0:T(128)S(1)} %stack.38.place, f32[72,128]{1,0:T(8,128)S(1)} %add.3.own.after, f32[72,128]{1,0:T(8,128)S(1)} %collective-permute-done.5.across, f32[72,128]{1,0:T(8,128)S(1)} %collective-permute-done.6.beside), custom_call_target="tpu_custom_call" | custom-call | flops 8589934592 | tf_op jit(solution)/shard_map/pallas_call | solution.py:612
  25.3 1.2 %collective-permute-start.9 = (bf16[80,128]{1,0:T(8,128)(2,1)S(1)}, bf16[80,128]{1,0:T(8,128)(2,1)S(1)}, u32[]{:S(2)}, u32[]{:S(2)}) collective-permute-start(bf16[80,128]{1,0:T(8,128)(2,1)S(1)} %shard_map.64.pair), channel_id=1, source_target_pairs={{0,25},{1,24},{2,27},{3,26},{4,29},{5,28},{6,31},{7,30},{8,17},{9,... | collective-permute-start | bytes 61448 | tf_op jit(solution)/shard_map/ppermute | solution.py:533
  26.5 3.0 %collective-permute-start.7 = (bf16[80,128]{1,0:T(8,128)(2,1)S(1)}, bf16[80,128]{1,0:T(8,128)(2,1)S(1)}, u32[]{:S(2)}, u32[]{:S(2)}) collective-permute-start(bf16[80,128]{1,0:T(8,128)(2,1)S(1)} %shard_map.64.pair), channel_id=1, source_target_pairs={{0,8},{1,9},{2,10},{3,11},{4,12},{5,13},{6,14},{7,15},{8,0},{9,1},... | collective-permute-start | bytes 61448 | tf_op jit(solution)/shard_map/ppermute | solution.py:533
  29.5 0.8 %shard_map.67 = (f32[2,6,64,128]{3,2,1,0:T(8,128)S(1)}, f32[2,64,128]{2,1,0:T(8,128)S(1)}) custom-call(s32[6]{0:T(128)S(1)} %stack.38.place, f32[4]{0:T(128)S(1)} %copy-done.3, bf16[80,128]{1,0:T(8,128)(2,1)S(1)} %shard_map.64.pair, bf16[80,128]{1,0:T(8,128)(2,1)S(1)} %collective-permute-done.2.one_got, bf16[80,128]{1,0:T(8,128)(2,1)S(1)} %collective-permute-done.3.two_got, ...), custom_call_target="tpu_custom_call" | custom-call | flops 2147483648 | bytes 1048576 | tf_op jit(solution)/shard_map/pallas_call | solution.py:622
  30.3 0.1 collective-permute-done.9
  30.4 1.1 %collective-permute-done.8 = bf16[80,128]{1,0:T(8,128)(2,1)S(1)} collective-permute-done((bf16[80,128]{1,0:T(8,128)(2,1)S(1)}, bf16[80,128]{1,0:T(8,128)(2,1)S(1)}, u32[]{:S(2)}, u32[]{:S(2)}) %collective-permute-start.8) | collective-permute-done | bytes 20512 | tf_op jit(solution)/shard_map/ppermute | solution.py:533
  31.4 0.2 collective-permute-done.7
  31.7 0.1 collective-permute-start.10
  31.8 1.1 %shard_map.65 = (f32[64,2,64,128]{3,2,1,0:T(8,128)S(1)}, f32[64,64,128]{2,1,0:T(8,128)S(1)}, f32[64,32,128]{2,1,0:T(8,128)S(1)}) custom-call(s32[6]{0:T(128)S(1)} %stack.38.place, bf16[80,128]{1,0:T(8,128)(2,1)S(1)} %shard_map.64.pair, bf16[64,2,64,128]{3,2,1,0:T(8,128)(2,1)S(1)} %copy-done, bf16[65,64,128]{2,1,0:T(8,128)(2,1)S(1)} %collective-permute-done.inner_got, ...), custom_call_target="tpu_custom_call" | custom-call | flops 1073741824 | bytes 1048576 | tf_op jit(solution)/shard_map/pallas_call | solution.py:631
  32.8 0.2 collective-permute-done.10.refs_1_
  33.0 3.3 %shard_map.68 = (f32[1,64]{1,0:T(1,128)}, f32[2,64,128]{2,1,0:T(8,128)}) custom-call(s32[6]{0:T(128)S(1)} %stack.38.place, bf16[4,80,128]{2,1,0:T(8,128)(2,1)S(1)} %pad_maximum_fusion.refs_0_, bf16[4,80,128]{2,1,0:T(8,128)(2,1)S(1)} %collective-permute-done.10.refs_1_, f32[64,2,64,128]{3,2,1,0:T(8,128)S(1)} %get-tuple-element.28.refs_2_, ...), custom_call_target="tpu_custom_call" | custom-call | flops 10000000 | bytes 5242880 | tf_op jit(solution)/shard_map/pallas_call | solution.py:643
  (13 shorter events, 0.0 us)
Async XLA Ops:
  0.6 5.3 %copy-start.1 = (s32[2,64,128]{2,1,0:T(8,128)S(1)}, s32[2,64,128]{2,1,0:T(8,128)}, u32[]{:S(2)}) copy-start(s32[2,64,128]{2,1,0:T(8,128)} %labels_far.1) | copy-start | bytes 196612
  0.6 5.3 %copy-start = (bf16[64,2,64,128]{3,2,1,0:T(8,128)(2,1)S(1)}, bf16[64,2,64,128]{3,2,1,0:T(8,128)(2,1)}, u32[]{:S(2)}) copy-start(bf16[64,2,64,128]{3,2,1,0:T(8,128)(2,1)} %zvec.5) | copy-start | bytes 6291460
  0.7 11.5 %copy-start.2 = (f32[2,64,128]{2,1,0:T(8,128)S(1)}, f32[2,64,128]{2,1,0:T(8,128)}, u32[]{:S(2)}) copy-start(f32[2,64,128]{2,1,0:T(8,128)} %refs_11_.1) | copy-start | bytes 196612
  0.7 11.5 %copy-start.3 = (f32[4]{0:T(128)S(1)}, f32[4]{0:T(128)}, u32[]{:S(2)}) copy-start(f32[4]{0:T(128)} %levels.7) | copy-start | bytes 52
  2.8 13.5 %collective-permute-start = (bf16[65,64,128]{2,1,0:T(8,128)(2,1)S(1)}, bf16[65,64,128]{2,1,0:T(8,128)(2,1)S(1)}, u32[]{:S(2)}, u32[]{:S(2)}) collective-permute-start(bf16[65,64,128]{2,1,0:T(8,128)(2,1)S(1)} %get-tuple-element.23), channel_id=1, source_target_pairs={{0,1},{1,0},{2,3},{3,2},{4,5},{5,4},{6,7},{7,6},{8,9},{9,8},{10,11... | collective-permute-start | bytes 3194888 | tf_op jit(solution)/shard_map/ppermute | solution.py:508
  3.3 14.4 %collective-permute-start.1 = (bf16[66,32,128]{2,1,0:T(8,128)(2,1)S(1)}, bf16[66,32,128]{2,1,0:T(8,128)(2,1)S(1)}, u32[]{:S(2)}, u32[]{:S(2)}) collective-permute-start(bf16[66,32,128]{2,1,0:T(8,128)(2,1)S(1)} %get-tuple-element.25), channel_id=1, source_target_pairs={{0,4},{1,2},{2,1},{3,7},{4,0},{5,6},{6,5},{7,3},{8,12},{9,10},{10,... | collective-permute-start | bytes 1622024 | tf_op jit(solution)/shard_map/ppermute | solution.py:521
  7.1 10.5 %collective-permute-start.2 = (bf16[80,128]{1,0:T(8,128)(2,1)S(1)}, bf16[80,128]{1,0:T(8,128)(2,1)S(1)}, u32[]{:S(2)}, u32[]{:S(2)}) collective-permute-start(bf16[80,128]{1,0:T(8,128)(2,1)S(1)} %get-tuple-element.19.after.one_pack), channel_id=1, source_target_pairs={{0,4},{4,0},{8,12},{12,8},{16,20},{20,16},{24,28},{28,24},{1,5},{5... | collective-permute-start | bytes 61448 | tf_op jit(solution)/shard_map/ppermute | solution.py:508
  7.2 10.5 %collective-permute-start.3 = (bf16[80,128]{1,0:T(8,128)(2,1)S(1)}, bf16[80,128]{1,0:T(8,128)(2,1)S(1)}, u32[]{:S(2)}, u32[]{:S(2)}) collective-permute-start(bf16[80,128]{1,0:T(8,128)(2,1)S(1)} %get-tuple-element.26.two_pack), channel_id=1, source_target_pairs={{0,28},{4,8},{8,4},{12,16},{16,12},{20,24},{24,20},{28,0},{1,29},{... | collective-permute-start | bytes 61448 | tf_op jit(solution)/shard_map/ppermute | solution.py:508
  19.2 1.3 %collective-permute-start.4 = (f32[72,128]{1,0:T(8,128)S(1)}, f32[72,128]{1,0:T(8,128)S(1)}, u32[]{:S(2)}, u32[]{:S(2)}) collective-permute-start(f32[72,128]{1,0:T(8,128)S(1)} %get-tuple-element.27), channel_id=1, source_target_pairs={{0,1},{1,0},{2,3},{3,2},{4,5},{5,4},{6,7},{7,6},{8,9},{9,8},{10,11... | collective-permute-start | bytes 110600 | tf_op jit(solution)/shard_map/ppermute | solution.py:525
  20.5 3.4 %collective-permute-start.5 = (f32[72,128]{1,0:T(8,128)S(1)}, f32[72,128]{1,0:T(8,128)S(1)}, u32[]{:S(2)}, u32[]{:S(2)}) collective-permute-start(f32[72,128]{1,0:T(8,128)S(1)} %add.3.own.after), channel_id=1, source_target_pairs={{0,3},{1,6},{2,5},{3,0},{4,7},{5,2},{6,1},{7,4},{8,11},{9,14},{10,... | collective-permute-start | bytes 110600 | tf_op jit(solution)/shard_map/ppermute | solution.py:545
  21.2 3.5 %collective-permute-start.6 = (f32[72,128]{1,0:T(8,128)S(1)}, f32[72,128]{1,0:T(8,128)S(1)}, u32[]{:S(2)}, u32[]{:S(2)}) collective-permute-start(f32[72,128]{1,0:T(8,128)S(1)} %add.3.own.after), channel_id=1, source_target_pairs={{0,5},{1,4},{2,7},{3,6},{4,1},{5,0},{6,3},{7,2},{8,13},{9,12},{10,... | collective-permute-start | bytes 110600 | tf_op jit(solution)/shard_map/ppermute | solution.py:533
  22.5 10.6 %collective-permute-start.11 = (bf16[64,32,128]{2,1,0:T(8,128)(2,1)S(1)}, bf16[64,32,128]{2,1,0:T(8,128)(2,1)S(1)}, u32[]{:S(2)}, u32[]{:S(2)}) collective-permute-start(bf16[64,32,128]{2,1,0:T(8,128)(2,1)S(1)} %shard_map.66), channel_id=1, source_target_pairs={{0,4},{1,2},{2,1},{3,7},{4,0},{5,6},{6,5},{7,3},{8,12},{9,10},{10,... | collective-permute-start | bytes 1572872 | tf_op jit(solution)/shard_map/ppermute | solution.py:521
  25.3 5.1 %collective-permute-start.9 = (bf16[80,128]{1,0:T(8,128)(2,1)S(1)}, bf16[80,128]{1,0:T(8,128)(2,1)S(1)}, u32[]{:S(2)}, u32[]{:S(2)}) collective-permute-start(bf16[80,128]{1,0:T(8,128)(2,1)S(1)} %shard_map.64.pair), channel_id=1, source_target_pairs={{0,25},{1,24},{2,27},{3,26},{4,29},{5,28},{6,31},{7,30},{8,17},{9,... | collective-permute-start | bytes 61448 | tf_op jit(solution)/shard_map/ppermute | solution.py:533
  26.5 5.0 %collective-permute-start.8 = (bf16[80,128]{1,0:T(8,128)(2,1)S(1)}, bf16[80,128]{1,0:T(8,128)(2,1)S(1)}, u32[]{:S(2)}, u32[]{:S(2)}) collective-permute-start(bf16[80,128]{1,0:T(8,128)(2,1)S(1)} %shard_map.64.pair), channel_id=1, source_target_pairs={{0,17},{1,16},{2,19},{3,18},{4,21},{5,20},{6,23},{7,22},{8,25},{9,... | collective-permute-start | bytes 61448 | tf_op jit(solution)/shard_map/ppermute | solution.py:533
  26.5 5.2 %collective-permute-start.7 = (bf16[80,128]{1,0:T(8,128)(2,1)S(1)}, bf16[80,128]{1,0:T(8,128)(2,1)S(1)}, u32[]{:S(2)}, u32[]{:S(2)}) collective-permute-start(bf16[80,128]{1,0:T(8,128)(2,1)S(1)} %shard_map.64.pair), channel_id=1, source_target_pairs={{0,8},{1,9},{2,10},{3,11},{4,12},{5,13},{6,14},{7,15},{8,0},{9,1},... | collective-permute-start | bytes 61448 | tf_op jit(solution)/shard_map/ppermute | solution.py:533
  31.7 1.3 %collective-permute-start.10 = (bf16[4,80,128]{2,1,0:T(8,128)(2,1)S(1)}, bf16[4,80,128]{2,1,0:T(8,128)(2,1)S(1)}, u32[]{:S(2)}, u32[]{:S(2)}) collective-permute-start(bf16[4,80,128]{2,1,0:T(8,128)(2,1)S(1)} %pad_maximum_fusion.refs_0_), channel_id=1, source_target_pairs={{0,1},{1,0},{2,3},{3,2},{4,5},{5,4},{6,7},{7,6},{8,9},{9,8},{10,11... | collective-permute-start | bytes 245768 | tf_op jit(solution)/shard_map/ppermute | solution.py:525

commit v12 on v10

--- a/solution.py
+++ b/solution.py
@@ -15,7 +15,6 @@
 NT = (((1,), (1,)), ((), ()))
 TN = (((0,), (0,)), ((), ()))
 VMEM = pl.BlockSpec(memory_space=pltpu.VMEM)
-SMEM = pl.BlockSpec(memory_space=pltpu.SMEM)
 HBM = pl.BlockSpec(memory_space=pltpu.HBM)
 ANY = pl.BlockSpec(memory_space=pl.ANY)
 
@@ -33,14 +32,23 @@
     )
 
 
+def here_on(axis):
+    return lax.axis_index(axis).astype(jnp.int32)
+
+
+def ends_the_line():
+    p = here_on("pln")
+    return (p == 0) | (p == lax.axis_size("pln") - 1)
+
+
 def harmonic(left_value, right_value):
     return 2.0 * left_value * right_value / (left_value + right_value)
 
 
 def coefficients(labels, levels_ref):
     weighted = jnp.zeros(labels.shape, F32)
-    for level in range(levels_ref.shape[0]):
-        weighted = weighted + jnp.where(labels == level, levels_ref[level], 0.0)
+    for level in range(levels_ref.shape[1]):
+        weighted = weighted + jnp.where(labels == level, levels_ref[:, level:level + 1], 0.0)
     return weighted
 
 
@@ -53,10 +61,10 @@
     return ((row == 0) & lane_is((16, width), lane)).astype(BF16)
 
 
-def stage_kernel(place, labels_far, zvec, inner_send, outer_near, labels, label_sem, sems):
+def stage_kernel(labels_far, zvec, inner_send, outer_near, labels, label_sem, sems):
     modes, planes, rows, layers = zvec.shape
     half = rows // 2
-    side = lax.rem(place[1], 2)
+    side = lax.rem(here_on("pln"), 2)
     start = pl.multiple_of((1 - side) * half, half)
     label_copy = pltpu.make_async_copy(labels_far, labels, label_sem)
     copies = [
@@ -79,12 +87,12 @@
     pass
 
 
-def prepare_kernel(place, labels, held, outer_rest, one_pack, two_pack):
+def prepare_kernel(labels, held, outer_rest, one_pack, two_pack):
     modes, planes, rows, layers = held.shape
     half = rows // 2
     width = planes * rows
-    side = lax.rem(place[1], 2)
-    odd = lax.rem(place[0], 2) == 1
+    side = lax.rem(here_on("pln"), 2)
+    odd = lax.rem(here_on("sub"), 2) == 1
     one_lane = jnp.where(odd, 0, layers - 1)
     two_lane = jnp.where(odd, layers - 1, 0)
     row = lax.broadcasted_iota(jnp.int32, (16, layers), 0)
@@ -108,12 +116,12 @@
 
 
 def block_kernel(
-    place, levels, labels, resid, zvec, after, partial, weights, here, half_diag, link_y, link_z,
+    levels, labels, resid, zvec, after, partial, weights, here, half_diag, link_y, link_z,
 ):
     planes, rows, layers = labels.shape
     modes = here.shape[2]
-    side = lax.rem(place[1], 2)
-    at_edge = (place[1] == 0) | (place[1] == place[2] - 1)
+    side = lax.rem(here_on("pln"), 2)
+    at_edge = ends_the_line()
     held = (1 - side, side)
 
     def turn_rows(start):
@@ -214,10 +222,10 @@
     return total[:modes] - total[modes:]
 
 
-def inner_kernel(place, levels, partial, weights, here, inner_got, out, face, turned):
+def inner_kernel(levels, partial, weights, here, inner_got, out, face, turned):
     planes, rows, modes, layers = here.shape
     half = rows // 2
-    side = lax.rem(place[1], 2)
+    side = lax.rem(here_on("pln"), 2)
     base = pl.multiple_of(side * half, half)
     turn(inner_got, base, turned)
     face[...] = harmonic(weights[5], coefficients(inner_got[modes].astype(F32), levels))
@@ -226,13 +234,13 @@
 
 
 def outer_kernel(
-    place, levels, partial, weights, here, outer_got, one_pack, two_pack, one_got, two_got,
+    levels, partial, weights, here, outer_got, one_pack, two_pack, one_got, two_got,
     out, face, turned, face_here,
 ):
     planes, rows, modes, layers = here.shape
     half = rows // 2
-    side = lax.rem(place[1], 2)
-    at_edge = (place[1] == 0) | (place[1] == place[2] - 1)
+    side = lax.rem(here_on("pln"), 2)
+    at_edge = ends_the_line()
     base = pl.multiple_of(side * half, half)
     turn(outer_got, 0, turned)
     coef = coefficients(outer_got[modes:].astype(F32).reshape(rows, layers), levels)
@@ -240,7 +248,7 @@
     face[...] = jnp.where(at_edge, weights[6], between)
     face_here[...] = jnp.where(at_edge, 0.0, between)
     cross = face_product(face_here, base, here.at[1], turned)
-    odd = lax.rem(place[0], 2) == 1
+    odd = lax.rem(here_on("sub"), 2) == 1
 
     def coef_row(pack):
         return coefficients(pack[modes:modes + 16].astype(F32)[0:1], levels)
@@ -271,12 +279,12 @@
 
 
 def terms_kernel(
-    place, levels, pair, one_got, two_got, weights, inner_face, outer_face, terms, picked, coef_ref
+    levels, pair, one_got, two_got, weights, inner_face, outer_face, terms, picked, coef_ref
 ):
     modes, width = picked.shape[1:]
     rows, layers = inner_face.shape
-    side = lax.rem(place[1], 2)
-    odd = lax.rem(place[0], 2) == 1
+    side = lax.rem(here_on("pln"), 2)
+    odd = lax.rem(here_on("sub"), 2) == 1
     one_other, two_other = one_got[...].astype(F32), two_got[...].astype(F32)
     next_first = jnp.where(odd, two_other, one_other)
     prev_last = jnp.where(odd, one_other, two_other)
@@ -339,9 +347,9 @@
     out[modes:] = extra.astype(BF16)
 
 
-def widen_kernel(place, pair, zvec, inner_got, outer_got, own_wide, inner_wide, outer_wide):
+def widen_kernel(pair, zvec, inner_got, outer_got, own_wide, inner_wide, outer_wide):
     modes, half = outer_wide.shape[:2]
-    side = lax.rem(place[1], 2)
+    side = lax.rem(here_on("pln"), 2)
 
     def some(j, carry):
         at = pl.ds(pl.multiple_of(j * MODES, MODES), MODES)
@@ -354,7 +362,7 @@
     lax.fori_loop(0, modes // MODES, some, 0)
 
 
-def finish_kernel(place, *refs):
+def finish_kernel(*refs):
     count = len(refs) - 15
     blocks, refs = refs[:count], refs[count:]
     zvec, inner_got, outer_got, outer_last, picked, terms, middle, inner_face, outer_face, resid = refs[:10]
@@ -362,10 +370,10 @@
     subs = direction_ref.shape[0]
     modes, planes, rows, layers = zvec.shape
     half = rows // 2
-    me = place[0]
-    side = lax.rem(place[1], 2)
+    me = here_on("sub")
+    side = lax.rem(here_on("pln"), 2)
     odd = lax.rem(me, 2) == 1
-    at_edge = (place[1] == 0) | (place[1] == place[2] - 1)
+    at_edge = ends_the_line()
     held = (1 - side, side)
     square = (modes, modes)
     eye = lax.broadcasted_iota(jnp.int32, square, 0) == lax.broadcasted_iota(jnp.int32, square, 1)
@@ -378,7 +386,7 @@
             held_here = block.shape[0]
             if held_here <= 8:
                 for entry in range(held_here):
-                    s = jnp.bitwise_xor(place[3 + index], entry)
+                    s = jnp.bitwise_xor(jnp.bitwise_xor(me, mask_of(index, len(blocks))), entry)
                     carry = body(block.at[entry], s, carry)
             else:
                 carry = lax.fori_loop(
@@ -537,6 +545,13 @@
 FAR = (4, 6)
 
 
+def mask_of(index, count):
+    if count == 1:
+        return 0
+    swap = lax.rem(here_on("pln"), 2) * (FAR[1] - FAR[0])
+    return (0, FAR[0] + swap, 2, FAR[1] - swap)[index]
+
+
 def far_partner(value):
     subs, count = lax.axis_size("sub"), lax.axis_size("pln")
     pairs = [(s * count + p, (s ^ FAR[p % 2]) * count + p) for s in range(subs) for p in range(count)]
@@ -548,29 +563,25 @@
     half = rows // 2
     subs, parts = lax.axis_size("sub"), lax.axis_size("pln")
     shape = jax.ShapeDtypeStruct
-    at_sub, at_pln = lax.axis_index("sub"), lax.axis_index("pln")
-    core = at_pln % 2
-    masks = (0, FAR[0] + core * (FAR[1] - FAR[0]), 2, FAR[1] + core * (FAR[0] - FAR[1]))
-    orders = [at_sub ^ mask for mask in masks] if parts == 4 and subs == 8 else [0] * 4
-    place = jnp.stack([jnp.int32(v) for v in (at_sub, at_pln, parts, *orders)])
+    levels = levels.reshape(1, -1)
     pack = shape((modes + 16, planes * rows), BF16)
     inner_send, outer_near = call(
         stage_kernel,
         [shape((modes + 1, rows, layers), BF16), shape((modes + rows // half, half, layers), BF16)],
-        [SMEM, HBM, HBM],
+        [HBM, HBM],
         [pltpu.VMEM(labels.shape, jnp.int32), pltpu.SemaphoreType.DMA, pltpu.SemaphoreType.DMA((2,))],
         moved=2 << 20,
-    )(place, *(pltpu.with_memory_space_constraint(v, pltpu.HBM) for v in (labels, zvec)))
+    )(*(pltpu.with_memory_space_constraint(v, pltpu.HBM) for v in (labels, zvec)))
     outer_got = swapped_all(outer_near)
     inner_got = swapped(inner_send, "pln", 0)
     rest = shape((modes, half, layers), BF16)
     outer_rest, one_pack, two_pack = call(
         prepare_kernel,
         [rest, pack, pack],
-        [SMEM, VMEM, VMEM],
+        [VMEM, VMEM],
         flops=10_000_000,
         moved=6 << 20,
-    )(place, labels, zvec)
+    )(labels, zvec)
     one_got = swapped(one_pack, "sub", 0)
     two_got = swapped(two_pack, "sub", 1)
     field = (planes, rows, layers)
@@ -582,28 +593,28 @@
             shape((7,) + plane, F32),
             shape((planes, rows, modes, layers), BF16),
         ],
-        [SMEM, SMEM] + [VMEM] * 3 + [ANY],
+        [VMEM] * 4 + [ANY],
         [pltpu.VMEM(field, F32)] * 3,
         flops=400_000_000,
         moved=3 << 20,
-    )(place, levels, labels, resid, zvec, one_pack)
+    )(levels, labels, resid, zvec, one_pack)
     turned = pltpu.VMEM((half, modes, layers), BF16)
     partial, inner_face = call(
         inner_kernel,
         [shape((modes + 8, modes), F32), shape(plane, F32)],
-        [SMEM, SMEM] + [VMEM] * 4,
+        [VMEM] * 5,
         [turned],
         flops=100_000_000,
         moved=1 << 20,
-    )(place, levels, partial, weights, here, inner_got)
+    )(levels, partial, weights, here, inner_got)
     block, outer_face = call(
         outer_kernel,
         [shape((modes + 8, 2 * modes), F32), shape(plane, F32)],
-        [SMEM, SMEM] + [VMEM] * 8,
+        [VMEM] * 9,
         [turned, pltpu.VMEM(plane, F32)],
         flops=100_000_000,
         moved=1 << 20,
-    )(place, levels, partial, weights, here, outer_got, one_pack, two_pack, one_got, two_got)
+    )(levels, partial, weights, here, outer_got, one_pack, two_pack, one_got, two_got)
     packed = (modes + 16, 2 * modes)
     if parts == 4 and subs == 8:
         block = block + exchanged(block, "pln", 1)
@@ -621,12 +632,12 @@
     terms, picked = call(
         terms_kernel,
         [shape((planes, 6) + plane, F32), shape((2, modes, planes * rows), F32)],
-        [SMEM, SMEM, ANY] + [VMEM] * 5,
+        [VMEM, ANY] + [VMEM] * 5,
         [pltpu.VMEM(field, F32)],
 
         flops=1 << 31,
         moved=1 << 20,
-    )(place, levels, blocks[0], one_got, two_got, weights, inner_face, outer_face)
+    )(levels, blocks[0], one_got, two_got, weights, inner_face, outer_face)
     wide = call(
         widen_kernel,
         [
@@ -634,15 +645,15 @@
             shape((modes,) + plane, F32),
             shape((modes, half, layers), F32),
         ],
-        [SMEM, ANY] + [VMEM] * 3,
+        [ANY] + [VMEM] * 3,
         flops=1 << 30,
         moved=1 << 20,
-    )(place, blocks[0], zvec, inner_got, outer_got)
+    )(blocks[0], zvec, inner_got, outer_got)
     return tuple(
         call(
             finish_kernel,
             [shape((1, modes), F32), shape(field, F32)],
-            [SMEM] + [VMEM] * (10 + len(blocks)),
+            [VMEM] * (10 + len(blocks)),
             [
                 pltpu.VMEM((subs, modes), F32),
                 pltpu.VMEM((modes, layers), F32),
@@ -651,7 +662,7 @@
             flops=10_000_000,
             moved=5 << 20,
         )(
-            place, *blocks, *wide, outer_last, picked, terms, weights, inner_face,
+            *blocks, *wide, outer_last, picked, terms, weights, inner_face,
             outer_face, resid,
         )
     )

time: 36.1 us -> 33.2 us (0.920)
  Pallas kernels: 15.4 us -> 11.5 us
  waiting for transfers between devices: 6.35 us -> 7.1 us
    pallas_call x2, Pallas kernels: 4.51 us -> 3.44 us  [the longest x1 2.75 us: body(): call(finish_kernel, [shape((1, modes), F32), shape(field, F32)], [VMEM] *...]
    pallas_call x1, Pallas kernels: 1.05 us -> 0.5 us  [body(): call(widen_kernel, [shape((modes,) + field, F32), shape((modes,) + plane,...]
    ppermute x2, waiting for transfers between devices: 1.35 us -> 1.9 us  [exchanged(): lax.ppermute(value, axis, [(i, i ^ mask) for i in range(lax.axis_size(axi...]
    pallas_call x1, Pallas kernels: 0.8 us -> 0.26 us  [body(): call(terms_kernel, [shape((planes, 6) + plane, F32), shape((2, modes, pla...]
    pallas_call x1, Pallas kernels: 1.37 us -> 0.89 us  [body(): call(inner_kernel, [shape((modes + 8, modes), F32), shape(plane, F32)], [...]
    pallas_call x1, Pallas kernels: 4.02 us -> 3.57 us  [body(): call(block_kernel, [shape((modes + 8, modes), F32), shape((7,) + plane, F...]
    pallas_call x1, Pallas kernels: 2.02 us -> 1.6 us  [body(): call(stage_kernel, [shape((modes + 1, rows, layers), BF16), shape((modes...]
    pallas_call x1, Pallas kernels: 1.57 us -> 1.17 us  [body(): call(outer_kernel, [shape((modes + 8, 2 * modes), F32), shape(plane, F32)...]
  transfers between devices with their start and end apart: 12 -> 12, of which waited for: 6 -> 6; matrix products, arithmetic and copies ran while one was open for 0% -> 0% of each run, Pallas kernels for 24% -> 18%
where the time goes in v12:
time: 33.2 us; the launch traced here: 33.1 us
  starting transfers between devices  13.7 us (41%)
  Pallas kernels  11.5 us (35%)
  waiting for transfers between devices  7.1 us (21%)
  between operations  0.75 us (2%)
    ppermute x3, starting transfers between devices, swapped(): return lax.ppermute(value, axis, pairs)  5.62 us
    pallas_call x1, Pallas kernels, body(): call(block_kernel, [shape((modes + 8, modes), F32), shape((7,) + plane, F...  3.57 us
    ppermute x1, waiting for transfers between devices, far_partner(): return lax.ppermute(value, ('sub', 'pln'), pairs)  3.35 us
    ppermute x4, starting transfers between devices, partner(): return lax.ppermute(value, ('sub', 'pln'), pairs)  3.21 us
    ppermute x2, starting transfers between devices, swapped_all(): return lax.ppermute(value, ('sub', 'pln'), pairs)  2.83 us
    pallas_call x1, Pallas kernels, body(): call(finish_kernel, [shape((1, modes), F32), shape(field, F32)], [VMEM] *...  2.75 us
    ppermute x1, starting transfers between devices, far_partner(): return lax.ppermute(value, ('sub', 'pln'), pairs)  1.99 us
    ppermute x2, waiting for transfers between devices, exchanged(): lax.ppermute(value, axis, [(i, i ^ mask) for i in range(lax.axis_size(axi...  1.9 us
  transfers between devices with their start and end apart: 12, of which 6 were waited for; matrix products, arithmetic and copies ran while one was open for 0% of the time, Pallas kernels for 18%

profile of v12, /device:TPU:0, one launch (start us, length us, event | category | flops | bytes accessed | tf_op | source)
XLA Modules:
  0.0 33.1 jit_solution(10753351252939141277)
XLA Ops:
  0.7 1.6 %shard_map.61 = (bf16[65,64,128]{2,1,0:T(8,128)(2,1)S(1)}, bf16[66,32,128]{2,1,0:T(8,128)(2,1)S(1)}) custom-call(s32[2,64,128]{2,1,0:T(8,128)} %labels_far.1, bf16[64,2,64,128]{3,2,1,0:T(8,128)(2,1)} %zvec.5), custom_call_target="tpu_custom_call" | custom-call | bytes 2097152 | tf_op jit(solution)/shard_map/pallas_call | solution.py:568
  2.3 0.5 %collective-permute-start = (bf16[65,64,128]{2,1,0:T(8,128)(2,1)S(1)}, bf16[65,64,128]{2,1,0:T(8,128)(2,1)S(1)}, u32[]{:S(2)}, u32[]{:S(2)}) collective-permute-start(bf16[65,64,128]{2,1,0:T(8,128)(2,1)S(1)} %get-tuple-element.23), channel_id=1, source_target_pairs={{0,1},{1,0},{2,3},{3,2},{4,5},{5,4},{6,7},{7,6},{8,9},{9,8},{10,11... | collective-permute-start | bytes 3194888 | tf_op jit(solution)/shard_map/ppermute | solution.py:517
  2.8 2.6 %collective-permute-start.1 = (bf16[66,32,128]{2,1,0:T(8,128)(2,1)S(1)}, bf16[66,32,128]{2,1,0:T(8,128)(2,1)S(1)}, u32[]{:S(2)}, u32[]{:S(2)}) collective-permute-start(bf16[66,32,128]{2,1,0:T(8,128)(2,1)S(1)} %get-tuple-element.25), channel_id=1, source_target_pairs={{0,4},{1,2},{2,1},{3,7},{4,0},{5,6},{6,5},{7,3},{8,12},{9,10},{10,... | collective-permute-start | bytes 1622024 | tf_op jit(solution)/shard_map/ppermute | solution.py:530
  5.4 0.7 %shard_map.59 = (bf16[64,32,128]{2,1,0:T(8,128)(2,1)S(1)}, bf16[80,128]{1,0:T(8,128)(2,1)S(1)}, bf16[80,128]{1,0:T(8,128)(2,1)S(1)}) custom-call(s32[2,64,128]{2,1,0:T(8,128)S(1)} %copy-done.1, bf16[64,2,64,128]{3,2,1,0:T(8,128)(2,1)S(1)} %copy-done), custom_call_target="tpu_custom_call" | custom-call | flops 10000000 | bytes 6291456 | tf_op jit(solution)/shard_map/pallas_call | solution.py:578
  6.1 0.4 %collective-permute-start.2 = (bf16[80,128]{1,0:T(8,128)(2,1)S(1)}, bf16[80,128]{1,0:T(8,128)(2,1)S(1)}, u32[]{:S(2)}, u32[]{:S(2)}) collective-permute-start(bf16[80,128]{1,0:T(8,128)(2,1)S(1)} %get-tuple-element.19.after.one_pack), channel_id=1, source_target_pairs={{0,4},{4,0},{8,12},{12,8},{16,20},{20,16},{24,28},{28,24},{1,5},{5... | collective-permute-start | bytes 61448 | tf_op jit(solution)/shard_map/ppermute | solution.py:517
  6.5 4.7 %collective-permute-start.3 = (bf16[80,128]{1,0:T(8,128)(2,1)S(1)}, bf16[80,128]{1,0:T(8,128)(2,1)S(1)}, u32[]{:S(2)}, u32[]{:S(2)}) collective-permute-start(bf16[80,128]{1,0:T(8,128)(2,1)S(1)} %get-tuple-element.26.two_pack), channel_id=1, source_target_pairs={{0,28},{4,8},{8,4},{12,16},{16,12},{20,24},{24,20},{28,0},{1,29},{... | collective-permute-start | bytes 61448 | tf_op jit(solution)/shard_map/ppermute | solution.py:517
  11.2 3.6 %shard_map.60 = (f32[72,64]{1,0:T(8,128)S(1)}, f32[7,64,128]{2,1,0:T(8,128)S(1)}, bf16[2,64,64,128]{3,2,1,0:T(8,128)(2,1)S(1)}) custom-call(f32[1,4]{1,0:T(1,128)S(1)} %bitcast.1, s32[2,64,128]{2,1,0:T(8,128)S(1)} %copy-done.1, f32[2,64,128]{2,1,0:T(8,128)S(1)} %copy-done.2, bf16[64,2,64,128]{3,2,1,0:T(8,128)(2,1)S(1)} %copy-done, ...), custom_call_target="tpu_custom_call" | custom-call | flops 400000000 | bytes 3145728 | tf_op jit(solution)/shard_map/pallas_call | solution.py:589
  14.8 0.0 collective-permute-done.inner_got
  14.8 0.9 %shard_map.62 = (f32[72,64]{1,0:T(8,128)S(1)}, f32[64,128]{1,0:T(8,128)S(1)}) custom-call(f32[1,4]{1,0:T(1,128)S(1)} %bitcast.2, f32[72,64]{1,0:T(8,128)S(1)} %get-tuple-element.20.partial, f32[7,64,128]{2,1,0:T(8,128)S(1)} %get-tuple-element.21.weights.refs_10_, bf16[2,64,64,128]{3,2,1,0:T(8,128)(2,1)S(1)} %get-tuple-element.22.here, ...), custom_call_target="tpu_custom_call" | custom-call | flops 100000000 | bytes 1048576 | tf_op jit(solution)/shard_map/pallas_call | solution.py:602
  15.7 0.0 collective-permute-done.2.one_got
  15.7 0.0 collective-permute-done.3.two_got
  15.7 0.0 collective-permute-done.1.outer_got
  15.7 1.2 %shard_map.63 = (f32[72,128]{1,0:T(8,128)S(1)}, f32[64,128]{1,0:T(8,128)S(1)}) custom-call(f32[1,4]{1,0:T(1,128)S(1)} %bitcast.3, f32[72,64]{1,0:T(8,128)S(1)} %get-tuple-element.24.partial, f32[7,64,128]{2,1,0:T(8,128)S(1)} %get-tuple-element.21.weights.refs_10_, bf16[2,64,64,128]{3,2,1,0:T(8,128)(2,1)S(1)} %get-tuple-element.22.here, ...), custom_call_target="tpu_custom_call" | custom-call | flops 100000000 | bytes 1048576 | tf_op jit(solution)/shard_map/pallas_call | solution.py:610
  16.9 0.1 collective-permute-start.4
  17.0 1.2 %collective-permute-done.4 = f32[72,128]{1,0:T(8,128)S(1)} collective-permute-done((f32[72,128]{1,0:T(8,128)S(1)}, f32[72,128]{1,0:T(8,128)S(1)}, u32[]{:S(2)}, u32[]{:S(2)}) %collective-permute-start.4) | collective-permute-done | bytes 36896 | tf_op jit(solution)/shard_map/ppermute | solution.py:534
  18.2 0.7 %collective-permute-start.5 = (f32[72,128]{1,0:T(8,128)S(1)}, f32[72,128]{1,0:T(8,128)S(1)}, u32[]{:S(2)}, u32[]{:S(2)}) collective-permute-start(f32[72,128]{1,0:T(8,128)S(1)} %add.3.own.after), channel_id=1, source_target_pairs={{0,3},{1,2},{2,1},{3,0},{4,7},{5,6},{6,5},{7,4},{8,11},{9,10},{10,... | collective-permute-start | bytes 110600 | tf_op jit(solution)/shard_map/ppermute | solution.py:542
  18.8 0.0 collective-permute-start.6
  18.9 2.3 %collective-permute-start.7 = (f32[72,128]{1,0:T(8,128)S(1)}, f32[72,128]{1,0:T(8,128)S(1)}, u32[]{:S(2)}, u32[]{:S(2)}) collective-permute-start(f32[72,128]{1,0:T(8,128)S(1)} %add.3.own.after), channel_id=1, source_target_pairs={{0,7},{1,6},{2,5},{3,4},{4,3},{5,2},{6,1},{7,0},{8,15},{9,14},{10,... | collective-permute-start | bytes 110600 | tf_op jit(solution)/shard_map/ppermute | solution.py:542
  21.1 0.2 collective-permute-start.11
  21.4 0.2 collective-permute-done.5.across
  21.6 0.7 %collective-permute-done.6.beside = f32[72,128]{1,0:T(8,128)S(1)} collective-permute-done((f32[72,128]{1,0:T(8,128)S(1)}, f32[72,128]{1,0:T(8,128)S(1)}, u32[]{:S(2)}, u32[]{:S(2)}) %collective-permute-start.6) | collective-permute-done | bytes 36896 | tf_op jit(solution)/shard_map/ppermute | solution.py:542
  22.3 0.9 %collective-permute-done.7.oblique = f32[72,128]{1,0:T(8,128)S(1)} collective-permute-done((f32[72,128]{1,0:T(8,128)S(1)}, f32[72,128]{1,0:T(8,128)S(1)}, u32[]{:S(2)}, u32[]{:S(2)}) %collective-permute-start.7) | collective-permute-done | bytes 36896 | tf_op jit(solution)/shard_map/ppermute | solution.py:542
  23.2 2.0 %collective-permute-start.8 = (bf16[2,80,128]{2,1,0:T(8,128)(2,1)S(1)}, bf16[2,80,128]{2,1,0:T(8,128)(2,1)S(1)}, u32[]{:S(2)}, u32[]{:S(2)}) collective-permute-start(bf16[2,80,128]{2,1,0:T(8,128)(2,1)S(1)} %shard_map.64.pair.refs_0_), channel_id=1, source_target_pairs={{0,16},{1,25},{2,18},{3,27},{4,20},{5,29},{6,22},{7,31},{8,24},{9,... | collective-permute-start | bytes 122888 | tf_op jit(solution)/shard_map/ppermute | solution.py:558
  25.2 0.2 collective-permute-start.9
  25.5 0.3 shard_map.67
  25.7 3.4 %collective-permute-done.8.refs_1_ = bf16[2,80,128]{2,1,0:T(8,128)(2,1)S(1)} collective-permute-done((bf16[2,80,128]{2,1,0:T(8,128)(2,1)S(1)}, bf16[2,80,128]{2,1,0:T(8,128)(2,1)S(1)}, u32[]{:S(2)}, u32[]{:S(2)}) %collective-permute-start.8) | collective-permute-done | bytes 40992 | tf_op jit(solution)/shard_map/ppermute | solution.py:558
  29.1 0.0 collective-permute-start.10
  29.1 0.5 %shard_map.65 = (f32[64,2,64,128]{3,2,1,0:T(8,128)S(1)}, f32[64,64,128]{2,1,0:T(8,128)S(1)}, f32[64,32,128]{2,1,0:T(8,128)S(1)}) custom-call(bf16[2,80,128]{2,1,0:T(8,128)(2,1)S(1)} %shard_map.64.pair.refs_0_, bf16[64,2,64,128]{3,2,1,0:T(8,128)(2,1)S(1)} %copy-done, bf16[65,64,128]{2,1,0:T(8,128)(2,1)S(1)} %collective-permute-done.inner_got, ...), custom_call_target="tpu_custom_call" | custom-call | flops 1073741824 | bytes 1048576 | tf_op jit(solution)/shard_map/pallas_call | solution.py:641
  29.6 0.0 collective-permute-done.9.refs_2_
  29.6 0.7 %collective-permute-done.10.refs_3_ = bf16[2,80,128]{2,1,0:T(8,128)(2,1)S(1)} collective-permute-done((bf16[2,80,128]{2,1,0:T(8,128)(2,1)S(1)}, bf16[2,80,128]{2,1,0:T(8,128)(2,1)S(1)}, u32[]{:S(2)}, u32[]{:S(2)}) %collective-permute-start.10) | collective-permute-done | bytes 40992 | tf_op jit(solution)/shard_map/ppermute | solution.py:534
  30.3 0.0 collective-permute-done.11.refs_7_
  30.3 2.7 %shard_map.68 = (f32[1,64]{1,0:T(1,128)}, f32[2,64,128]{2,1,0:T(8,128)}) custom-call(bf16[2,80,128]{2,1,0:T(8,128)(2,1)S(1)} %shard_map.64.pair.refs_0_, bf16[2,80,128]{2,1,0:T(8,128)(2,1)S(1)} %collective-permute-done.8.refs_1_, bf16[2,80,128]{2,1,0:T(8,128)(2,1)S(1)} %collective-permute-done.9.refs_2_, ...), custom_call_target="tpu_custom_call" | custom-call | flops 10000000 | bytes 5242880 | tf_op jit(solution)/shard_map/pallas_call | solution.py:653
  (11 shorter events, 0.1 us)
Async XLA Ops:
  0.6 4.8 %copy-start.1 = (s32[2,64,128]{2,1,0:T(8,128)S(1)}, s32[2,64,128]{2,1,0:T(8,128)}, u32[]{:S(2)}) copy-start(s32[2,64,128]{2,1,0:T(8,128)} %labels_far.1) | copy-start | bytes 196612
  0.6 4.7 %copy-start = (bf16[64,2,64,128]{3,2,1,0:T(8,128)(2,1)S(1)}, bf16[64,2,64,128]{3,2,1,0:T(8,128)(2,1)}, u32[]{:S(2)}) copy-start(bf16[64,2,64,128]{3,2,1,0:T(8,128)(2,1)} %zvec.5) | copy-start | bytes 6291460
  0.7 10.5 %copy-start.3 = (f32[4]{0:T(128)S(1)}, f32[4]{0:T(128)}, u32[]{:S(2)}) copy-start(f32[4]{0:T(128)} %param.5) | copy-start | bytes 52
  0.7 10.5 %copy-start.2 = (f32[2,64,128]{2,1,0:T(8,128)S(1)}, f32[2,64,128]{2,1,0:T(8,128)}, u32[]{:S(2)}) copy-start(f32[2,64,128]{2,1,0:T(8,128)} %refs_13_.1) | copy-start | bytes 196612
  2.3 12.5 %collective-permute-start = (bf16[65,64,128]{2,1,0:T(8,128)(2,1)S(1)}, bf16[65,64,128]{2,1,0:T(8,128)(2,1)S(1)}, u32[]{:S(2)}, u32[]{:S(2)}) collective-permute-start(bf16[65,64,128]{2,1,0:T(8,128)(2,1)S(1)} %get-tuple-element.23), channel_id=1, source_target_pairs={{0,1},{1,0},{2,3},{3,2},{4,5},{5,4},{6,7},{7,6},{8,9},{9,8},{10,11... | collective-permute-start | bytes 3194888 | tf_op jit(solution)/shard_map/ppermute | solution.py:517
  2.8 12.9 %collective-permute-start.1 = (bf16[66,32,128]{2,1,0:T(8,128)(2,1)S(1)}, bf16[66,32,128]{2,1,0:T(8,128)(2,1)S(1)}, u32[]{:S(2)}, u32[]{:S(2)}) collective-permute-start(bf16[66,32,128]{2,1,0:T(8,128)(2,1)S(1)} %get-tuple-element.25), channel_id=1, source_target_pairs={{0,4},{1,2},{2,1},{3,7},{4,0},{5,6},{6,5},{7,3},{8,12},{9,10},{10,... | collective-permute-start | bytes 1622024 | tf_op jit(solution)/shard_map/ppermute | solution.py:530
  6.1 9.6 %collective-permute-start.2 = (bf16[80,128]{1,0:T(8,128)(2,1)S(1)}, bf16[80,128]{1,0:T(8,128)(2,1)S(1)}, u32[]{:S(2)}, u32[]{:S(2)}) collective-permute-start(bf16[80,128]{1,0:T(8,128)(2,1)S(1)} %get-tuple-element.19.after.one_pack), channel_id=1, source_target_pairs={{0,4},{4,0},{8,12},{12,8},{16,20},{20,16},{24,28},{28,24},{1,5},{5... | collective-permute-start | bytes 61448 | tf_op jit(solution)/shard_map/ppermute | solution.py:517
  6.5 9.2 %collective-permute-start.3 = (bf16[80,128]{1,0:T(8,128)(2,1)S(1)}, bf16[80,128]{1,0:T(8,128)(2,1)S(1)}, u32[]{:S(2)}, u32[]{:S(2)}) collective-permute-start(bf16[80,128]{1,0:T(8,128)(2,1)S(1)} %get-tuple-element.26.two_pack), channel_id=1, source_target_pairs={{0,28},{4,8},{8,4},{12,16},{16,12},{20,24},{24,20},{28,0},{1,29},{... | collective-permute-start | bytes 61448 | tf_op jit(solution)/shard_map/ppermute | solution.py:517
  16.9 1.3 %collective-permute-start.4 = (f32[72,128]{1,0:T(8,128)S(1)}, f32[72,128]{1,0:T(8,128)S(1)}, u32[]{:S(2)}, u32[]{:S(2)}) collective-permute-start(f32[72,128]{1,0:T(8,128)S(1)} %get-tuple-element.27), channel_id=1, source_target_pairs={{0,1},{1,0},{2,3},{3,2},{4,5},{5,4},{6,7},{7,6},{8,9},{9,8},{10,11... | collective-permute-start | bytes 110600 | tf_op jit(solution)/shard_map/ppermute | solution.py:534
  18.2 3.4 %collective-permute-start.5 = (f32[72,128]{1,0:T(8,128)S(1)}, f32[72,128]{1,0:T(8,128)S(1)}, u32[]{:S(2)}, u32[]{:S(2)}) collective-permute-start(f32[72,128]{1,0:T(8,128)S(1)} %add.3.own.after), channel_id=1, source_target_pairs={{0,3},{1,2},{2,1},{3,0},{4,7},{5,6},{6,5},{7,4},{8,11},{9,10},{10,... | collective-permute-start | bytes 110600 | tf_op jit(solution)/shard_map/ppermute | solution.py:542
  18.8 3.4 %collective-permute-start.6 = (f32[72,128]{1,0:T(8,128)S(1)}, f32[72,128]{1,0:T(8,128)S(1)}, u32[]{:S(2)}, u32[]{:S(2)}) collective-permute-start(f32[72,128]{1,0:T(8,128)S(1)} %add.3.own.after), channel_id=1, source_target_pairs={{0,5},{1,4},{2,7},{3,6},{4,1},{5,0},{6,3},{7,2},{8,13},{9,12},{10,... | collective-permute-start | bytes 110600 | tf_op jit(solution)/shard_map/ppermute | solution.py:542
  18.9 4.3 %collective-permute-start.7 = (f32[72,128]{1,0:T(8,128)S(1)}, f32[72,128]{1,0:T(8,128)S(1)}, u32[]{:S(2)}, u32[]{:S(2)}) collective-permute-start(f32[72,128]{1,0:T(8,128)S(1)} %add.3.own.after), channel_id=1, source_target_pairs={{0,7},{1,6},{2,5},{3,4},{4,3},{5,2},{6,1},{7,0},{8,15},{9,14},{10,... | collective-permute-start | bytes 110600 | tf_op jit(solution)/shard_map/ppermute | solution.py:542
  21.1 9.2 %collective-permute-start.11 = (bf16[64,32,128]{2,1,0:T(8,128)(2,1)S(1)}, bf16[64,32,128]{2,1,0:T(8,128)(2,1)S(1)}, u32[]{:S(2)}, u32[]{:S(2)}) collective-permute-start(bf16[64,32,128]{2,1,0:T(8,128)(2,1)S(1)} %shard_map.66), channel_id=1, source_target_pairs={{0,4},{1,2},{2,1},{3,7},{4,0},{5,6},{6,5},{7,3},{8,12},{9,10},{10,... | collective-permute-start | bytes 1572872 | tf_op jit(solution)/shard_map/ppermute | solution.py:530
  23.2 5.8 %collective-permute-start.8 = (bf16[2,80,128]{2,1,0:T(8,128)(2,1)S(1)}, bf16[2,80,128]{2,1,0:T(8,128)(2,1)S(1)}, u32[]{:S(2)}, u32[]{:S(2)}) collective-permute-start(bf16[2,80,128]{2,1,0:T(8,128)(2,1)S(1)} %shard_map.64.pair.refs_0_), channel_id=1, source_target_pairs={{0,16},{1,25},{2,18},{3,27},{4,20},{5,29},{6,22},{7,31},{8,24},{9,... | collective-permute-start | bytes 122888 | tf_op jit(solution)/shard_map/ppermute | solution.py:558
  25.2 4.4 %collective-permute-start.9 = (bf16[2,80,128]{2,1,0:T(8,128)(2,1)S(1)}, bf16[2,80,128]{2,1,0:T(8,128)(2,1)S(1)}, u32[]{:S(2)}, u32[]{:S(2)}) collective-permute-start(bf16[2,80,128]{2,1,0:T(8,128)(2,1)S(1)} %shard_map.64.pair.refs_0_), channel_id=1, source_target_pairs={{0,9},{1,8},{2,11},{3,10},{4,13},{5,12},{6,15},{7,14},{8,1},{9,0},... | collective-permute-start | bytes 122888 | tf_op jit(solution)/shard_map/ppermute | solution.py:542
  29.1 1.2 %collective-permute-start.10 = (bf16[2,80,128]{2,1,0:T(8,128)(2,1)S(1)}, bf16[2,80,128]{2,1,0:T(8,128)(2,1)S(1)}, u32[]{:S(2)}, u32[]{:S(2)}) collective-permute-start(bf16[2,80,128]{2,1,0:T(8,128)(2,1)S(1)} %collective-permute-done.8.refs_1_), channel_id=1, source_target_pairs={{0,1},{1,0},{2,3},{3,2},{4,5},{5,4},{6,7},{7,6},{8,9},{9,8},{10,11... | collective-permute-start | bytes 122888 | tf_op jit(solution)/shard_map/ppermute | solution.py:534

commit v13 on v12

--- a/solution.py
+++ b/solution.py
@@ -61,30 +61,30 @@
     return ((row == 0) & lane_is((16, width), lane)).astype(BF16)
 
 
-def stage_kernel(labels_far, zvec, inner_send, outer_near, labels, label_sem, sems):
+def stage_kernel(labels_far, zvec, inner_send, first_part, second_part, labels, label_sem, sems):
     modes, planes, rows, layers = zvec.shape
-    half = rows // 2
+    quarter = second_part.shape[1]
     side = lax.rem(here_on("pln"), 2)
-    start = pl.multiple_of((1 - side) * half, half)
+    start = pl.multiple_of((1 - side) * (rows // 2), quarter)
     label_copy = pltpu.make_async_copy(labels_far, labels, label_sem)
     copies = [
         pltpu.make_async_copy(
-            zvec.at[:, side, pl.ds(start, half), :], outer_near.at[pl.ds(0, modes)], sems.at[0]
-        ),
-        pltpu.make_async_copy(zvec.at[:, 1 - side], inner_send.at[pl.ds(0, modes)], sems.at[1]),
+            zvec.at[:, side, pl.ds(start + index * quarter, quarter), :], out.at[pl.ds(0, modes)],
+            sems.at[index],
+        )
+        for index, out in enumerate((first_part, second_part))
     ]
+    copies.append(
+        pltpu.make_async_copy(zvec.at[:, 1 - side], inner_send.at[pl.ds(0, modes)], sems.at[2])
+    )
     label_copy.start()
     for copy in copies:
         copy.start()
     label_copy.wait()
-    outer_near[modes:] = labels[side].astype(F32).astype(BF16).reshape(rows // half, half, layers)
+    first_part[modes:] = labels[side].astype(F32).astype(BF16).reshape(rows // quarter, quarter, layers)
     inner_send[modes] = labels[1 - side].astype(F32).astype(BF16)
     for copy in copies:
         copy.wait()
-
-
-def release_kernel(after, outer_rest, outer_out):
-    pass
 
 
 def prepare_kernel(labels, held, outer_rest, one_pack, two_pack):
@@ -113,6 +113,10 @@
                 [ends[index:index + 1, j * width:(j + 1) * width] for j in range(CHUNK)], axis=0
             ).astype(BF16)
         outer_rest[at] = held[at, side, pl.ds(pl.multiple_of(side * half, half), half), :]
+
+
+def release_kernel(after, outer_rest, outer_out):
+    pass
 
 
 def block_kernel(
@@ -233,20 +237,27 @@
     out[modes:, :] = partial[modes:, :]
 
 
-def outer_kernel(
-    levels, partial, weights, here, outer_got, one_pack, two_pack, one_got, two_got,
-    out, face, turned, face_here,
-):
+def outer_kernel(levels, partial, weights, here, outer_got, out, face, face_here, turned):
     planes, rows, modes, layers = here.shape
-    half = rows // 2
-    side = lax.rem(here_on("pln"), 2)
+    quarter = turned.shape[0]
     at_edge = ends_the_line()
-    base = pl.multiple_of(side * half, half)
+    base = pl.multiple_of(lax.rem(here_on("pln"), 2) * (rows // 2), quarter)
     turn(outer_got, 0, turned)
     coef = coefficients(outer_got[modes:].astype(F32).reshape(rows, layers), levels)
     between = harmonic(weights[6], coef)
     face[...] = jnp.where(at_edge, weights[6], between)
     face_here[...] = jnp.where(at_edge, 0.0, between)
+    out[:modes, :] = partial[:modes, :] + 0.5 * face_product(face_here, base, here.at[1], turned)
+    out[modes:, :] = partial[modes:, :]
+
+
+def last_kernel(
+    levels, partial, face_here, here, outer_got, one_pack, two_pack, one_got, two_got, out, turned
+):
+    planes, rows, modes, layers = here.shape
+    quarter = turned.shape[0]
+    base = pl.multiple_of(lax.rem(here_on("pln"), 2) * (rows // 2) + quarter, quarter)
+    turn(outer_got, 0, turned)
     cross = face_product(face_here, base, here.at[1], turned)
     odd = lax.rem(here_on("sub"), 2) == 1
 
@@ -347,8 +358,11 @@
     out[modes:] = extra.astype(BF16)
 
 
-def widen_kernel(pair, zvec, inner_got, outer_got, own_wide, inner_wide, outer_wide):
+def widen_kernel(
+    packed, zvec, inner_got, outer_got, outer_next, own_wide, inner_wide, outer_wide
+):
     modes, half = outer_wide.shape[:2]
+    quarter = half // 2
     side = lax.rem(here_on("pln"), 2)
 
     def some(j, carry):
@@ -356,7 +370,8 @@
         own_wide[at, 0] = zvec[at, 1 - side].astype(F32)
         own_wide[at, 1] = zvec[at, side].astype(F32)
         inner_wide[at] = inner_got[at].astype(F32)
-        outer_wide[at] = outer_got[at].astype(F32)
+        outer_wide[at, :quarter, :] = outer_got[at].astype(F32)
+        outer_wide[at, quarter:, :] = outer_next[at].astype(F32)
         return carry
 
     lax.fori_loop(0, modes // MODES, some, 0)
@@ -517,7 +532,7 @@
     return lax.ppermute(value, axis, pairs)
 
 
-def swapped_all(value):
+def swapped_all(value, mask=1):
     subs, count = lax.axis_size("sub"), lax.axis_size("pln")
     pairs = []
     for s in range(subs):
@@ -525,7 +540,7 @@
             if 0 < i < count - 1:
                 to = (s, i + 1 if i % 2 else i - 1)
             else:
-                to = (s ^ 1, i)
+                to = (s ^ mask, i)
             pairs.append((s * count + i, to[0] * count + to[1]))
     return lax.ppermute(value, ("sub", "pln"), pairs)
 
@@ -565,14 +580,20 @@
     shape = jax.ShapeDtypeStruct
     levels = levels.reshape(1, -1)
     pack = shape((modes + 16, planes * rows), BF16)
-    inner_send, outer_near = call(
+    quarter = half // 2
+    inner_send, first_part, second_part = call(
         stage_kernel,
-        [shape((modes + 1, rows, layers), BF16), shape((modes + rows // half, half, layers), BF16)],
+        [
+            shape((modes + 1, rows, layers), BF16),
+            shape((modes + rows // quarter, quarter, layers), BF16),
+            shape((modes, quarter, layers), BF16),
+        ],
         [HBM, HBM],
-        [pltpu.VMEM(labels.shape, jnp.int32), pltpu.SemaphoreType.DMA, pltpu.SemaphoreType.DMA((2,))],
+        [pltpu.VMEM(labels.shape, jnp.int32), pltpu.SemaphoreType.DMA, pltpu.SemaphoreType.DMA((3,))],
         moved=2 << 20,
     )(*(pltpu.with_memory_space_constraint(v, pltpu.HBM) for v in (labels, zvec)))
-    outer_got = swapped_all(outer_near)
+    outer_got = swapped_all(first_part)
+    outer_next = swapped_all(second_part, 2 if subs % 4 == 0 else 1)
     inner_got = swapped(inner_send, "pln", 0)
     rest = shape((modes, half, layers), BF16)
     outer_rest, one_pack, two_pack = call(
@@ -607,14 +628,23 @@
         flops=100_000_000,
         moved=1 << 20,
     )(levels, partial, weights, here, inner_got)
-    block, outer_face = call(
+    turned = pltpu.VMEM((quarter, modes, layers), BF16)
+    partial, outer_face, face_here = call(
         outer_kernel,
-        [shape((modes + 8, 2 * modes), F32), shape(plane, F32)],
-        [VMEM] * 9,
-        [turned, pltpu.VMEM(plane, F32)],
+        [shape((modes + 8, modes), F32), shape(plane, F32), shape(plane, F32)],
+        [VMEM] * 5,
+        [turned],
         flops=100_000_000,
         moved=1 << 20,
-    )(levels, partial, weights, here, outer_got, one_pack, two_pack, one_got, two_got)
+    )(levels, partial, weights, here, outer_got)
+    [block] = call(
+        last_kernel,
+        [shape((modes + 8, 2 * modes), F32)],
+        [VMEM] * 9,
+        [turned],
+        flops=100_000_000,
+        moved=1 << 20,
+    )(levels, partial, face_here, here, outer_next, one_pack, two_pack, one_got, two_got)
     packed = (modes + 16, 2 * modes)
     if parts == 4 and subs == 8:
         block = block + exchanged(block, "pln", 1)
@@ -645,10 +675,10 @@
             shape((modes,) + plane, F32),
             shape((modes, half, layers), F32),
         ],
-        [ANY] + [VMEM] * 3,
+        [ANY] + [VMEM] * 4,
         flops=1 << 30,
         moved=1 << 20,
-    )(blocks[0], zvec, inner_got, outer_got)
+    )(blocks[0], zvec, inner_got, outer_got, outer_next)
     return tuple(
         call(
             finish_kernel,

time: 33.2 us -> 33.7 us (1.015)
  starting transfers between devices: 13.7 us -> 14.2 us
    ppermute x2 -> x3, starting transfers between devices: 2.83 us -> 4.4 us  [swapped_all(): return lax.ppermute(value, ('sub', 'pln'), pairs)]
    ppermute x3, starting transfers between devices: 5.62 us -> 4.49 us  [swapped(): return lax.ppermute(value, axis, pairs)]
    pallas_call x1 -> x2, Pallas kernels: 1.17 us -> 0.92 us  [the longest x1 0.49 us: body(): call(last_kernel, [shape((modes + 8, 2 * modes), F32)], [VMEM] * 9, [turn...]
  transfers between devices with their start and end apart: 12 -> 13, of which waited for: 6 -> 6; matrix products, arithmetic and copies ran while one was open for 0% -> 0% of each run, Pallas kernels for 18% -> 19%
where the time goes in v13:
time: 33.7 us; the launch traced here: 33.5 us
  starting transfers between devices  14.2 us (42%)
  Pallas kernels  11.2 us (33%)
  waiting for transfers between devices  7.26 us (22%)
  between operations  0.76 us (2%)
    ppermute x3, starting transfers between devices, swapped(): return lax.ppermute(value, axis, pairs)  4.49 us
    ppermute x3, starting transfers between devices, swapped_all(): return lax.ppermute(value, ('sub', 'pln'), pairs)  4.4 us
    pallas_call x1, Pallas kernels, body(): call(block_kernel, [shape((modes + 8, modes), F32), shape((7,) + plane, F...  3.57 us
    ppermute x1, waiting for transfers between devices, far_partner(): return lax.ppermute(value, ('sub', 'pln'), pairs)  3.22 us
    ppermute x4, starting transfers between devices, partner(): return lax.ppermute(value, ('sub', 'pln'), pairs)  3.04 us
    pallas_call x1, Pallas kernels, body(): call(finish_kernel, [shape((1, modes), F32), shape(field, F32)], [VMEM] *...  2.73 us
    ppermute x1, starting transfers between devices, far_partner(): return lax.ppermute(value, ('sub', 'pln'), pairs)  2.23 us
    ppermute x4, waiting for transfers between devices, partner(): return lax.ppermute(value, ('sub', 'pln'), pairs)  2.13 us
  transfers between devices with their start and end apart: 13, of which 6 were waited for; matrix products, arithmetic and copies ran while one was open for 0% of the time, Pallas kernels for 19%

profile of v13, /device:TPU:0, one launch (start us, length us, event | category | flops | bytes accessed | tf_op | source)
XLA Modules:
  0.0 33.5 jit_solution(5707697484593058422)
XLA Ops:
  0.7 1.6 %shard_map.61 = (bf16[65,64,128]{2,1,0:T(8,128)(2,1)S(1)}, bf16[68,16,128]{2,1,0:T(8,128)(2,1)S(1)}, bf16[64,16,128]{2,1,0:T(8,128)(2,1)S(1)}) custom-call(s32[2,64,128]{2,1,0:T(8,128)} %labels_far.1, bf16[64,2,64,128]{3,2,1,0:T(8,128)(2,1)} %zvec.5), custom_call_target="tpu_custom_call" | custom-call | bytes 2097152 | tf_op jit(solution)/shard_map/pallas_call | solution.py:584
  2.3 0.5 %collective-permute-start = (bf16[65,64,128]{2,1,0:T(8,128)(2,1)S(1)}, bf16[65,64,128]{2,1,0:T(8,128)(2,1)S(1)}, u32[]{:S(2)}, u32[]{:S(2)}) collective-permute-start(bf16[65,64,128]{2,1,0:T(8,128)(2,1)S(1)} %get-tuple-element.25), channel_id=1, source_target_pairs={{0,1},{1,0},{2,3},{3,2},{4,5},{5,4},{6,7},{7,6},{8,9},{9,8},{10,11... | collective-permute-start | bytes 3194888 | tf_op jit(solution)/shard_map/ppermute | solution.py:532
  2.8 2.6 %collective-permute-start.1 = (bf16[68,16,128]{2,1,0:T(8,128)(2,1)S(1)}, bf16[68,16,128]{2,1,0:T(8,128)(2,1)S(1)}, u32[]{:S(2)}, u32[]{:S(2)}) collective-permute-start(bf16[68,16,128]{2,1,0:T(8,128)(2,1)S(1)} %get-tuple-element.27), channel_id=1, source_target_pairs={{0,4},{1,2},{2,1},{3,7},{4,0},{5,6},{6,5},{7,3},{8,12},{9,10},{10,... | collective-permute-start | bytes 835592 | tf_op jit(solution)/shard_map/ppermute | solution.py:545
  5.4 1.6 %collective-permute-start.2 = (bf16[64,16,128]{2,1,0:T(8,128)(2,1)S(1)}, bf16[64,16,128]{2,1,0:T(8,128)(2,1)S(1)}, u32[]{:S(2)}, u32[]{:S(2)}) collective-permute-start(bf16[64,16,128]{2,1,0:T(8,128)(2,1)S(1)} %get-tuple-element.30), channel_id=1, source_target_pairs={{0,8},{1,2},{2,1},{3,11},{4,12},{5,6},{6,5},{7,15},{8,0},{9,10},{1... | collective-permute-start | bytes 786440 | tf_op jit(solution)/shard_map/ppermute | solution.py:545
  7.0 0.7 %shard_map.59 = (bf16[64,32,128]{2,1,0:T(8,128)(2,1)S(1)}, bf16[80,128]{1,0:T(8,128)(2,1)S(1)}, bf16[80,128]{1,0:T(8,128)(2,1)S(1)}) custom-call(s32[2,64,128]{2,1,0:T(8,128)S(1)} %copy-done.1, bf16[64,2,64,128]{3,2,1,0:T(8,128)(2,1)S(1)} %copy-done), custom_call_target="tpu_custom_call" | custom-call | flops 10000000 | bytes 6291456 | tf_op jit(solution)/shard_map/pallas_call | solution.py:599
  7.7 0.5 %collective-permute-start.3 = (bf16[80,128]{1,0:T(8,128)(2,1)S(1)}, bf16[80,128]{1,0:T(8,128)(2,1)S(1)}, u32[]{:S(2)}, u32[]{:S(2)}) collective-permute-start(bf16[80,128]{1,0:T(8,128)(2,1)S(1)} %get-tuple-element.21.after.one_pack), channel_id=1, source_target_pairs={{0,4},{4,0},{8,12},{12,8},{16,20},{20,16},{24,28},{28,24},{1,5},{5... | collective-permute-start | bytes 61448 | tf_op jit(solution)/shard_map/ppermute | solution.py:532
  8.2 3.4 %collective-permute-start.4 = (bf16[80,128]{1,0:T(8,128)(2,1)S(1)}, bf16[80,128]{1,0:T(8,128)(2,1)S(1)}, u32[]{:S(2)}, u32[]{:S(2)}) collective-permute-start(bf16[80,128]{1,0:T(8,128)(2,1)S(1)} %get-tuple-element.31.two_pack), channel_id=1, source_target_pairs={{0,28},{4,8},{8,4},{12,16},{16,12},{20,24},{24,20},{28,0},{1,29},{... | collective-permute-start | bytes 61448 | tf_op jit(solution)/shard_map/ppermute | solution.py:532
  11.7 3.6 %shard_map.60 = (f32[72,64]{1,0:T(8,128)S(1)}, f32[7,64,128]{2,1,0:T(8,128)S(1)}, bf16[2,64,64,128]{3,2,1,0:T(8,128)(2,1)S(1)}) custom-call(f32[1,4]{1,0:T(1,128)S(1)} %bitcast.1, s32[2,64,128]{2,1,0:T(8,128)S(1)} %copy-done.1, f32[2,64,128]{2,1,0:T(8,128)S(1)} %copy-done.2, bf16[64,2,64,128]{3,2,1,0:T(8,128)(2,1)S(1)} %copy-done, ...), custom_call_target="tpu_custom_call" | custom-call | flops 400000000 | bytes 3145728 | tf_op jit(solution)/shard_map/pallas_call | solution.py:610
  15.2 0.9 %shard_map.62 = (f32[72,64]{1,0:T(8,128)S(1)}, f32[64,128]{1,0:T(8,128)S(1)}) custom-call(f32[1,4]{1,0:T(1,128)S(1)} %bitcast.2, f32[72,64]{1,0:T(8,128)S(1)} %get-tuple-element.22.partial, f32[7,64,128]{2,1,0:T(8,128)S(1)} %get-tuple-element.23.weights.refs_10_, bf16[2,64,64,128]{3,2,1,0:T(8,128)(2,1)S(1)} %get-tuple-element.24.here, ...), custom_call_target="tpu_custom_call" | custom-call | flops 100000000 | bytes 1048576 | tf_op jit(solution)/shard_map/pallas_call | solution.py:623
  16.1 0.4 %shard_map.63 = (f32[72,64]{1,0:T(8,128)S(1)}, f32[64,128]{1,0:T(8,128)S(1)}, f32[64,128]{1,0:T(8,128)S(1)}) custom-call(f32[1,4]{1,0:T(1,128)S(1)} %bitcast.3, f32[72,64]{1,0:T(8,128)S(1)} %get-tuple-element.26.partial, f32[7,64,128]{2,1,0:T(8,128)S(1)} %get-tuple-element.23.weights.refs_10_, bf16[2,64,64,128]{3,2,1,0:T(8,128)(2,1)S(1)} %get-tuple-element.24.here, ...), custom_call_target="tpu_custom_call" | custom-call | flops 100000000 | bytes 1048576 | tf_op jit(solution)/shard_map/pallas_call | solution.py:632
  16.6 0.0 collective-permute-done.3.one_got
  16.6 0.0 collective-permute-done.4.two_got
  16.6 0.5 %shard_map.64 = f32[72,128]{1,0:T(8,128)S(1)} custom-call(f32[1,4]{1,0:T(1,128)S(1)} %bitcast.4, f32[72,64]{1,0:T(8,128)S(1)} %get-tuple-element.28.partial, f32[64,128]{1,0:T(8,128)S(1)} %get-tuple-element.29.face_here, bf16[2,64,64,128]{3,2,1,0:T(8,128)(2,1)S(1)} %get-tuple-element.24.here, ...), custom_call_target="tpu_custom_call" | custom-call | flops 100000000 | bytes 1048576 | tf_op jit(solution)/shard_map/pallas_call | solution.py:640
  17.1 0.1 collective-permute-start.5
  17.2 1.2 %collective-permute-done.5 = f32[72,128]{1,0:T(8,128)S(1)} collective-permute-done((f32[72,128]{1,0:T(8,128)S(1)}, f32[72,128]{1,0:T(8,128)S(1)}, u32[]{:S(2)}, u32[]{:S(2)}) %collective-permute-start.5) | collective-permute-done | bytes 36896 | tf_op jit(solution)/shard_map/ppermute | solution.py:549
  18.4 1.0 %collective-permute-start.6 = (f32[72,128]{1,0:T(8,128)S(1)}, f32[72,128]{1,0:T(8,128)S(1)}, u32[]{:S(2)}, u32[]{:S(2)}) collective-permute-start(f32[72,128]{1,0:T(8,128)S(1)} %add.3.own.after), channel_id=1, source_target_pairs={{0,3},{1,2},{2,1},{3,0},{4,7},{5,6},{6,5},{7,4},{8,11},{9,10},{10,... | collective-permute-start | bytes 110600 | tf_op jit(solution)/shard_map/ppermute | solution.py:557
  19.4 0.0 collective-permute-start.7
  19.4 1.9 %collective-permute-start.8 = (f32[72,128]{1,0:T(8,128)S(1)}, f32[72,128]{1,0:T(8,128)S(1)}, u32[]{:S(2)}, u32[]{:S(2)}) collective-permute-start(f32[72,128]{1,0:T(8,128)S(1)} %add.3.own.after), channel_id=1, source_target_pairs={{0,7},{1,6},{2,5},{3,4},{4,3},{5,2},{6,1},{7,0},{8,15},{9,14},{10,... | collective-permute-start | bytes 110600 | tf_op jit(solution)/shard_map/ppermute | solution.py:557
  21.4 0.2 collective-permute-start.12
  21.6 0.2 collective-permute-done.6.across
  21.8 1.0 %collective-permute-done.7.beside = f32[72,128]{1,0:T(8,128)S(1)} collective-permute-done((f32[72,128]{1,0:T(8,128)S(1)}, f32[72,128]{1,0:T(8,128)S(1)}, u32[]{:S(2)}, u32[]{:S(2)}) %collective-permute-start.7) | collective-permute-done | bytes 36896 | tf_op jit(solution)/shard_map/ppermute | solution.py:557
  22.8 0.9 %collective-permute-done.8.oblique = f32[72,128]{1,0:T(8,128)S(1)} collective-permute-done((f32[72,128]{1,0:T(8,128)S(1)}, f32[72,128]{1,0:T(8,128)S(1)}, u32[]{:S(2)}, u32[]{:S(2)}) %collective-permute-start.8) | collective-permute-done | bytes 36896 | tf_op jit(solution)/shard_map/ppermute | solution.py:557
  23.8 2.2 %collective-permute-start.9 = (bf16[2,80,128]{2,1,0:T(8,128)(2,1)S(1)}, bf16[2,80,128]{2,1,0:T(8,128)(2,1)S(1)}, u32[]{:S(2)}, u32[]{:S(2)}) collective-permute-start(bf16[2,80,128]{2,1,0:T(8,128)(2,1)S(1)} %shard_map.65.packed.pair.refs_0_), channel_id=1, source_target_pairs={{0,16},{1,25},{2,18},{3,27},{4,20},{5,29},{6,22},{7,31},{8,24},{9,... | collective-permute-start | bytes 122888 | tf_op jit(solution)/shard_map/ppermute | solution.py:573
  26.0 0.1 collective-permute-start.10
  26.1 0.3 shard_map.68
  26.3 3.2 %collective-permute-done.9.refs_1_ = bf16[2,80,128]{2,1,0:T(8,128)(2,1)S(1)} collective-permute-done((bf16[2,80,128]{2,1,0:T(8,128)(2,1)S(1)}, bf16[2,80,128]{2,1,0:T(8,128)(2,1)S(1)}, u32[]{:S(2)}, u32[]{:S(2)}) %collective-permute-start.9) | collective-permute-done | bytes 40992 | tf_op jit(solution)/shard_map/ppermute | solution.py:573
  29.5 0.0 collective-permute-start.11
  29.6 0.5 %shard_map.66 = (f32[64,2,64,128]{3,2,1,0:T(8,128)S(1)}, f32[64,64,128]{2,1,0:T(8,128)S(1)}, f32[64,32,128]{2,1,0:T(8,128)S(1)}) custom-call(bf16[2,80,128]{2,1,0:T(8,128)(2,1)S(1)} %shard_map.65.packed.pair.refs_0_, bf16[64,2,64,128]{3,2,1,0:T(8,128)(2,1)S(1)} %copy-done, bf16[65,64,128]{2,1,0:T(8,128)(2,1)S(1)} %collective-permute-done.inner_got, ...), custom_call_target="tpu_custom_call" | custom-call | flops 1073741824 | bytes 1048576 | tf_op jit(solution)/shard_map/pallas_call | solution.py:671
  30.1 0.0 collective-permute-done.10.refs_2_
  30.1 0.7 %collective-permute-done.11.refs_3_ = bf16[2,80,128]{2,1,0:T(8,128)(2,1)S(1)} collective-permute-done((bf16[2,80,128]{2,1,0:T(8,128)(2,1)S(1)}, bf16[2,80,128]{2,1,0:T(8,128)(2,1)S(1)}, u32[]{:S(2)}, u32[]{:S(2)}) %collective-permute-start.11) | collective-permute-done | bytes 40992 | tf_op jit(solution)/shard_map/ppermute | solution.py:549
  30.8 0.0 collective-permute-done.12.refs_7_
  30.8 2.7 %shard_map.69 = (f32[1,64]{1,0:T(1,128)}, f32[2,64,128]{2,1,0:T(8,128)}) custom-call(bf16[2,80,128]{2,1,0:T(8,128)(2,1)S(1)} %shard_map.65.packed.pair.refs_0_, bf16[2,80,128]{2,1,0:T(8,128)(2,1)S(1)} %collective-permute-done.9.refs_1_, bf16[2,80,128]{2,1,0:T(8,128)(2,1)S(1)} %collective-permute-done.10.refs_2_, ...), custom_call_target="tpu_custom_call" | custom-call | flops 10000000 | bytes 5242880 | tf_op jit(solution)/shard_map/pallas_call | solution.py:683
  (14 shorter events, 0.1 us)
Async XLA Ops:
  0.6 6.3 %copy-start.1 = (s32[2,64,128]{2,1,0:T(8,128)S(1)}, s32[2,64,128]{2,1,0:T(8,128)}, u32[]{:S(2)}) copy-start(s32[2,64,128]{2,1,0:T(8,128)} %labels_far.1) | copy-start | bytes 196612
  0.6 6.3 %copy-start = (bf16[64,2,64,128]{3,2,1,0:T(8,128)(2,1)S(1)}, bf16[64,2,64,128]{3,2,1,0:T(8,128)(2,1)}, u32[]{:S(2)}) copy-start(bf16[64,2,64,128]{3,2,1,0:T(8,128)(2,1)} %zvec.5) | copy-start | bytes 6291460
  0.7 11.0 %copy-start.3 = (f32[4]{0:T(128)S(1)}, f32[4]{0:T(128)}, u32[]{:S(2)}) copy-start(f32[4]{0:T(128)} %param.5) | copy-start | bytes 52
  0.7 11.0 %copy-start.2 = (f32[2,64,128]{2,1,0:T(8,128)S(1)}, f32[2,64,128]{2,1,0:T(8,128)}, u32[]{:S(2)}) copy-start(f32[2,64,128]{2,1,0:T(8,128)} %refs_13_.1) | copy-start | bytes 196612
  2.3 12.9 %collective-permute-start = (bf16[65,64,128]{2,1,0:T(8,128)(2,1)S(1)}, bf16[65,64,128]{2,1,0:T(8,128)(2,1)S(1)}, u32[]{:S(2)}, u32[]{:S(2)}) collective-permute-start(bf16[65,64,128]{2,1,0:T(8,128)(2,1)S(1)} %get-tuple-element.25), channel_id=1, source_target_pairs={{0,1},{1,0},{2,3},{3,2},{4,5},{5,4},{6,7},{7,6},{8,9},{9,8},{10,11... | collective-permute-start | bytes 3194888 | tf_op jit(solution)/shard_map/ppermute | solution.py:532
  2.8 13.3 %collective-permute-start.1 = (bf16[68,16,128]{2,1,0:T(8,128)(2,1)S(1)}, bf16[68,16,128]{2,1,0:T(8,128)(2,1)S(1)}, u32[]{:S(2)}, u32[]{:S(2)}) collective-permute-start(bf16[68,16,128]{2,1,0:T(8,128)(2,1)S(1)} %get-tuple-element.27), channel_id=1, source_target_pairs={{0,4},{1,2},{2,1},{3,7},{4,0},{5,6},{6,5},{7,3},{8,12},{9,10},{10,... | collective-permute-start | bytes 835592 | tf_op jit(solution)/shard_map/ppermute | solution.py:545
  5.4 11.2 %collective-permute-start.2 = (bf16[64,16,128]{2,1,0:T(8,128)(2,1)S(1)}, bf16[64,16,128]{2,1,0:T(8,128)(2,1)S(1)}, u32[]{:S(2)}, u32[]{:S(2)}) collective-permute-start(bf16[64,16,128]{2,1,0:T(8,128)(2,1)S(1)} %get-tuple-element.30), channel_id=1, source_target_pairs={{0,8},{1,2},{2,1},{3,11},{4,12},{5,6},{6,5},{7,15},{8,0},{9,10},{1... | collective-permute-start | bytes 786440 | tf_op jit(solution)/shard_map/ppermute | solution.py:545
  7.7 8.9 %collective-permute-start.3 = (bf16[80,128]{1,0:T(8,128)(2,1)S(1)}, bf16[80,128]{1,0:T(8,128)(2,1)S(1)}, u32[]{:S(2)}, u32[]{:S(2)}) collective-permute-start(bf16[80,128]{1,0:T(8,128)(2,1)S(1)} %get-tuple-element.21.after.one_pack), channel_id=1, source_target_pairs={{0,4},{4,0},{8,12},{12,8},{16,20},{20,16},{24,28},{28,24},{1,5},{5... | collective-permute-start | bytes 61448 | tf_op jit(solution)/shard_map/ppermute | solution.py:532
  8.2 8.4 %collective-permute-start.4 = (bf16[80,128]{1,0:T(8,128)(2,1)S(1)}, bf16[80,128]{1,0:T(8,128)(2,1)S(1)}, u32[]{:S(2)}, u32[]{:S(2)}) collective-permute-start(bf16[80,128]{1,0:T(8,128)(2,1)S(1)} %get-tuple-element.31.two_pack), channel_id=1, source_target_pairs={{0,28},{4,8},{8,4},{12,16},{16,12},{20,24},{24,20},{28,0},{1,29},{... | collective-permute-start | bytes 61448 | tf_op jit(solution)/shard_map/ppermute | solution.py:532
  17.1 1.3 %collective-permute-start.5 = (f32[72,128]{1,0:T(8,128)S(1)}, f32[72,128]{1,0:T(8,128)S(1)}, u32[]{:S(2)}, u32[]{:S(2)}) collective-permute-start(f32[72,128]{1,0:T(8,128)S(1)} %shard_map.64), channel_id=1, source_target_pairs={{0,1},{1,0},{2,3},{3,2},{4,5},{5,4},{6,7},{7,6},{8,9},{9,8},{10,11... | collective-permute-start | bytes 110600 | tf_op jit(solution)/shard_map/ppermute | solution.py:549
  18.4 3.4 %collective-permute-start.6 = (f32[72,128]{1,0:T(8,128)S(1)}, f32[72,128]{1,0:T(8,128)S(1)}, u32[]{:S(2)}, u32[]{:S(2)}) collective-permute-start(f32[72,128]{1,0:T(8,128)S(1)} %add.3.own.after), channel_id=1, source_target_pairs={{0,3},{1,2},{2,1},{3,0},{4,7},{5,6},{6,5},{7,4},{8,11},{9,10},{10,... | collective-permute-start | bytes 110600 | tf_op jit(solution)/shard_map/ppermute | solution.py:557
  19.4 3.4 %collective-permute-start.7 = (f32[72,128]{1,0:T(8,128)S(1)}, f32[72,128]{1,0:T(8,128)S(1)}, u32[]{:S(2)}, u32[]{:S(2)}) collective-permute-start(f32[72,128]{1,0:T(8,128)S(1)} %add.3.own.after), channel_id=1, source_target_pairs={{0,5},{1,4},{2,7},{3,6},{4,1},{5,0},{6,3},{7,2},{8,13},{9,12},{10,... | collective-permute-start | bytes 110600 | tf_op jit(solution)/shard_map/ppermute | solution.py:557
  19.4 4.3 %collective-permute-start.8 = (f32[72,128]{1,0:T(8,128)S(1)}, f32[72,128]{1,0:T(8,128)S(1)}, u32[]{:S(2)}, u32[]{:S(2)}) collective-permute-start(f32[72,128]{1,0:T(8,128)S(1)} %add.3.own.after), channel_id=1, source_target_pairs={{0,7},{1,6},{2,5},{3,4},{4,3},{5,2},{6,1},{7,0},{8,15},{9,14},{10,... | collective-permute-start | bytes 110600 | tf_op jit(solution)/shard_map/ppermute | solution.py:557
  21.4 9.4 %collective-permute-start.12 = (bf16[64,32,128]{2,1,0:T(8,128)(2,1)S(1)}, bf16[64,32,128]{2,1,0:T(8,128)(2,1)S(1)}, u32[]{:S(2)}, u32[]{:S(2)}) collective-permute-start(bf16[64,32,128]{2,1,0:T(8,128)(2,1)S(1)} %shard_map.67), channel_id=1, source_target_pairs={{0,4},{1,2},{2,1},{3,7},{4,0},{5,6},{6,5},{7,3},{8,12},{9,10},{10,... | collective-permute-start | bytes 1572872 | tf_op jit(solution)/shard_map/ppermute | solution.py:545
  23.8 5.8 %collective-permute-start.9 = (bf16[2,80,128]{2,1,0:T(8,128)(2,1)S(1)}, bf16[2,80,128]{2,1,0:T(8,128)(2,1)S(1)}, u32[]{:S(2)}, u32[]{:S(2)}) collective-permute-start(bf16[2,80,128]{2,1,0:T(8,128)(2,1)S(1)} %shard_map.65.packed.pair.refs_0_), channel_id=1, source_target_pairs={{0,16},{1,25},{2,18},{3,27},{4,20},{5,29},{6,22},{7,31},{8,24},{9,... | collective-permute-start | bytes 122888 | tf_op jit(solution)/shard_map/ppermute | solution.py:573
  26.0 4.1 %collective-permute-start.10 = (bf16[2,80,128]{2,1,0:T(8,128)(2,1)S(1)}, bf16[2,80,128]{2,1,0:T(8,128)(2,1)S(1)}, u32[]{:S(2)}, u32[]{:S(2)}) collective-permute-start(bf16[2,80,128]{2,1,0:T(8,128)(2,1)S(1)} %shard_map.65.packed.pair.refs_0_), channel_id=1, source_target_pairs={{0,9},{1,8},{2,11},{3,10},{4,13},{5,12},{6,15},{7,14},{8,1},{9,0},... | collective-permute-start | bytes 122888 | tf_op jit(solution)/shard_map/ppermute | solution.py:557
  29.5 1.2 %collective-permute-start.11 = (bf16[2,80,128]{2,1,0:T(8,128)(2,1)S(1)}, bf16[2,80,128]{2,1,0:T(8,128)(2,1)S(1)}, u32[]{:S(2)}, u32[]{:S(2)}) collective-permute-start(bf16[2,80,128]{2,1,0:T(8,128)(2,1)S(1)} %collective-permute-done.9.refs_1_), channel_id=1, source_target_pairs={{0,1},{1,0},{2,3},{3,2},{4,5},{5,4},{6,7},{7,6},{8,9},{9,8},{10,11... | collective-permute-start | bytes 122888 | tf_op jit(solution)/shard_map/ppermute | solution.py:549

commit v14 on v13

--- a/solution.py
+++ b/solution.py
@@ -100,9 +100,10 @@
     both = both.astype(BF16)
     flat = labels[...].astype(F32).astype(BF16).reshape(width, layers)
     for out, lane in ((one_pack, one_lane), (two_pack, two_lane)):
-        out[modes:] = lax.dot_general(
+        out[modes:modes + 16] = lax.dot_general(
             pick_row(lane, layers), flat, NT, preferred_element_type=F32
         ).astype(BF16)
+    two_pack[modes + 16:] = jnp.zeros((16, width), BF16)
     for k in range(0, modes, CHUNK):
         at = slice(k, k + CHUNK)
         ends = lax.dot_general(
@@ -252,7 +253,7 @@
 
 
 def last_kernel(
-    levels, partial, face_here, here, outer_got, one_pack, two_pack, one_got, two_got, out, turned
+    levels, partial, face_here, here, outer_got, two_pack, one_pack, two_got, one_got, out, turned
 ):
     planes, rows, modes, layers = here.shape
     quarter = turned.shape[0]
@@ -264,8 +265,9 @@
     def coef_row(pack):
         return coefficients(pack[modes:modes + 16].astype(F32)[0:1], levels)
 
-    one, two = one_pack[...].astype(F32), two_pack[...].astype(F32)
-    one_other, two_other = one_got[...].astype(F32), two_got[...].astype(F32)
+    one, two, one_other, two_other = (
+        ref[:modes + 16].astype(F32) for ref in (one_pack, two_pack, one_got, two_got)
+    )
     first, last = jnp.where(odd, one, two), jnp.where(odd, two, one)
     next_first = jnp.where(odd, two_other, one_other)
     prev_last = jnp.where(odd, one_other, two_other)
@@ -296,7 +298,7 @@
     rows, layers = inner_face.shape
     side = lax.rem(here_on("pln"), 2)
     odd = lax.rem(here_on("sub"), 2) == 1
-    one_other, two_other = one_got[...].astype(F32), two_got[...].astype(F32)
+    one_other, two_other = (ref[:modes + 16].astype(F32) for ref in (one_got, two_got))
     next_first = jnp.where(odd, two_other, one_other)
     prev_last = jnp.where(odd, one_other, two_other)
     picked[0] = next_first[:modes]
@@ -598,7 +600,7 @@
     rest = shape((modes, half, layers), BF16)
     outer_rest, one_pack, two_pack = call(
         prepare_kernel,
-        [rest, pack, pack],
+        [rest, pack, shape((modes + 32, planes * rows), BF16)],
         [VMEM, VMEM],
         flops=10_000_000,
         moved=6 << 20,
@@ -644,7 +646,7 @@
         [turned],
         flops=100_000_000,
         moved=1 << 20,
-    )(levels, partial, face_here, here, outer_next, one_pack, two_pack, one_got, two_got)
+    )(levels, partial, face_here, here, outer_next, two_pack, one_pack, two_got, one_got)
     packed = (modes + 16, 2 * modes)
     if parts == 4 and subs == 8:
         block = block + exchanged(block, "pln", 1)

time: 33.7 us -> 34.9 us (1.036)
  waiting for transfers between devices: 7.26 us -> 9.45 us
  starting transfers between devices: 14.2 us -> 13.2 us
    ppermute x1, starting transfers between devices: 2.23 us -> 0.07 us  [far_partner(): return lax.ppermute(value, ('sub', 'pln'), pairs)]
    ppermute x1, waiting for transfers between devices: 3.22 us -> 4.97 us  [far_partner(): return lax.ppermute(value, ('sub', 'pln'), pairs)]
    ppermute x3, starting transfers between devices: 4.49 us -> 2.97 us  [swapped(): return lax.ppermute(value, axis, pairs)]
    ppermute x3, starting transfers between devices: 4.4 us -> 5.7 us  [swapped_all(): return lax.ppermute(value, ('sub', 'pln'), pairs)]
    ppermute x2, starting transfers between devices: 0.07 us -> 1.02 us  [exchanged(): lax.ppermute(value, axis, [(i, i ^ mask) for i in range(lax.axis_size(axi...]
    ppermute x4, waiting for transfers between devices: 2.13 us -> 2.9 us  [partner(): return lax.ppermute(value, ('sub', 'pln'), pairs)]
    ppermute x4, starting transfers between devices: 3.04 us -> 3.49 us  [partner(): return lax.ppermute(value, ('sub', 'pln'), pairs)]
  transfers between devices with their start and end apart: 13 -> 13, of which waited for: 6 -> 5; matrix products, arithmetic and copies ran while one was open for 0% -> 0% of each run, Pallas kernels for 19% -> 18%
where the time goes in v14:
time: 34.9 us; the launch traced here: 34.7 us
  starting transfers between devices  13.2 us (38%)
  Pallas kernels  11.2 us (32%)
  waiting for transfers between devices  9.45 us (27%)
  between operations  0.78 us (2%)
    ppermute x3, starting transfers between devices, swapped_all(): return lax.ppermute(value, ('sub', 'pln'), pairs)  5.7 us
    ppermute x1, waiting for transfers between devices, far_partner(): return lax.ppermute(value, ('sub', 'pln'), pairs)  4.97 us
    pallas_call x1, Pallas kernels, body(): call(block_kernel, [shape((modes + 8, modes), F32), shape((7,) + plane, F...  3.58 us
    ppermute x4, starting transfers between devices, partner(): return lax.ppermute(value, ('sub', 'pln'), pairs)  3.49 us
    ppermute x3, starting transfers between devices, swapped(): return lax.ppermute(value, axis, pairs)  2.97 us
    ppermute x4, waiting for transfers between devices, partner(): return lax.ppermute(value, ('sub', 'pln'), pairs)  2.9 us
    pallas_call x1, Pallas kernels, body(): call(finish_kernel, [shape((1, modes), F32), shape(field, F32)], [VMEM] *...  2.73 us
    pallas_call x1, Pallas kernels, body(): call(stage_kernel, [shape((modes + 1, rows, layers), BF16), shape((modes...  1.61 us
  transfers between devices with their start and end apart: 13, of which 5 were waited for; matrix products, arithmetic and copies ran while one was open for 0% of the time, Pallas kernels for 18%

profile of v14, /device:TPU:0, one launch (start us, length us, event | category | flops | bytes accessed | tf_op | source)
XLA Modules:
  0.0 34.7 jit_solution(15828046382239537593)
XLA Ops:
  0.7 1.6 %shard_map.61 = (bf16[65,64,128]{2,1,0:T(8,128)(2,1)S(1)}, bf16[68,16,128]{2,1,0:T(8,128)(2,1)S(1)}, bf16[64,16,128]{2,1,0:T(8,128)(2,1)S(1)}) custom-call(s32[2,64,128]{2,1,0:T(8,128)} %labels_far.1, bf16[64,2,64,128]{3,2,1,0:T(8,128)(2,1)} %zvec.5), custom_call_target="tpu_custom_call" | custom-call | bytes 2097152 | tf_op jit(solution)/shard_map/pallas_call | solution.py:586
  2.3 0.5 %collective-permute-start = (bf16[65,64,128]{2,1,0:T(8,128)(2,1)S(1)}, bf16[65,64,128]{2,1,0:T(8,128)(2,1)S(1)}, u32[]{:S(2)}, u32[]{:S(2)}) collective-permute-start(bf16[65,64,128]{2,1,0:T(8,128)(2,1)S(1)} %get-tuple-element.25), channel_id=1, source_target_pairs={{0,1},{1,0},{2,3},{3,2},{4,5},{5,4},{6,7},{7,6},{8,9},{9,8},{10,11... | collective-permute-start | bytes 3194888 | tf_op jit(solution)/shard_map/ppermute | solution.py:534
  2.8 2.6 %collective-permute-start.1 = (bf16[68,16,128]{2,1,0:T(8,128)(2,1)S(1)}, bf16[68,16,128]{2,1,0:T(8,128)(2,1)S(1)}, u32[]{:S(2)}, u32[]{:S(2)}) collective-permute-start(bf16[68,16,128]{2,1,0:T(8,128)(2,1)S(1)} %get-tuple-element.27), channel_id=1, source_target_pairs={{0,4},{1,2},{2,1},{3,7},{4,0},{5,6},{6,5},{7,3},{8,12},{9,10},{10,... | collective-permute-start | bytes 835592 | tf_op jit(solution)/shard_map/ppermute | solution.py:547
  5.4 1.6 %collective-permute-start.2 = (bf16[64,16,128]{2,1,0:T(8,128)(2,1)S(1)}, bf16[64,16,128]{2,1,0:T(8,128)(2,1)S(1)}, u32[]{:S(2)}, u32[]{:S(2)}) collective-permute-start(bf16[64,16,128]{2,1,0:T(8,128)(2,1)S(1)} %get-tuple-element.30), channel_id=1, source_target_pairs={{0,8},{1,2},{2,1},{3,11},{4,12},{5,6},{6,5},{7,15},{8,0},{9,10},{1... | collective-permute-start | bytes 786440 | tf_op jit(solution)/shard_map/ppermute | solution.py:547
  7.0 0.7 %shard_map.59 = (bf16[64,32,128]{2,1,0:T(8,128)(2,1)S(1)}, bf16[80,128]{1,0:T(8,128)(2,1)S(1)}, bf16[96,128]{1,0:T(8,128)(2,1)S(1)}) custom-call(s32[2,64,128]{2,1,0:T(8,128)S(1)} %copy-done.1, bf16[64,2,64,128]{3,2,1,0:T(8,128)(2,1)S(1)} %copy-done), custom_call_target="tpu_custom_call" | custom-call | flops 10000000 | bytes 6291456 | tf_op jit(solution)/shard_map/pallas_call | solution.py:601
  7.7 2.5 %collective-permute-start.3 = (bf16[96,128]{1,0:T(8,128)(2,1)S(1)}, bf16[96,128]{1,0:T(8,128)(2,1)S(1)}, u32[]{:S(2)}, u32[]{:S(2)}) collective-permute-start(bf16[96,128]{1,0:T(8,128)(2,1)S(1)} %get-tuple-element.31.two_pack), channel_id=1, source_target_pairs={{0,28},{4,8},{8,4},{12,16},{16,12},{20,24},{24,20},{28,0},{1,29},{... | collective-permute-start | bytes 73736 | tf_op jit(solution)/shard_map/ppermute | solution.py:534
  10.1 0.0 collective-permute-start.4
  10.1 3.6 %shard_map.60 = (f32[72,64]{1,0:T(8,128)S(1)}, f32[7,64,128]{2,1,0:T(8,128)S(1)}, bf16[2,64,64,128]{3,2,1,0:T(8,128)(2,1)S(1)}) custom-call(f32[1,4]{1,0:T(1,128)S(1)} %bitcast.1, s32[2,64,128]{2,1,0:T(8,128)S(1)} %copy-done.1, f32[2,64,128]{2,1,0:T(8,128)S(1)} %copy-done.2, bf16[64,2,64,128]{3,2,1,0:T(8,128)(2,1)S(1)} %copy-done, ...), custom_call_target="tpu_custom_call" | custom-call | flops 400000000 | bytes 3145728 | tf_op jit(solution)/shard_map/pallas_call | solution.py:612
  13.7 0.9 %shard_map.62 = (f32[72,64]{1,0:T(8,128)S(1)}, f32[64,128]{1,0:T(8,128)S(1)}) custom-call(f32[1,4]{1,0:T(1,128)S(1)} %bitcast.2, f32[72,64]{1,0:T(8,128)S(1)} %get-tuple-element.22.partial, f32[7,64,128]{2,1,0:T(8,128)S(1)} %get-tuple-element.23.weights.refs_10_, bf16[2,64,64,128]{3,2,1,0:T(8,128)(2,1)S(1)} %get-tuple-element.24.here, ...), custom_call_target="tpu_custom_call" | custom-call | flops 100000000 | bytes 1048576 | tf_op jit(solution)/shard_map/pallas_call | solution.py:625
  14.6 0.0 collective-permute-done.1.outer_got
  14.6 0.4 %shard_map.63 = (f32[72,64]{1,0:T(8,128)S(1)}, f32[64,128]{1,0:T(8,128)S(1)}, f32[64,128]{1,0:T(8,128)S(1)}) custom-call(f32[1,4]{1,0:T(1,128)S(1)} %bitcast.3, f32[72,64]{1,0:T(8,128)S(1)} %get-tuple-element.26.partial, f32[7,64,128]{2,1,0:T(8,128)S(1)} %get-tuple-element.23.weights.refs_10_, bf16[2,64,64,128]{3,2,1,0:T(8,128)(2,1)S(1)} %get-tuple-element.24.here, ...), custom_call_target="tpu_custom_call" | custom-call | flops 100000000 | bytes 1048576 | tf_op jit(solution)/shard_map/pallas_call | solution.py:634
  15.1 0.0 collective-permute-done.4.one_got
  15.1 0.0 collective-permute-done.3.two_got
  15.1 0.5 %shard_map.64 = f32[72,128]{1,0:T(8,128)S(1)} custom-call(f32[1,4]{1,0:T(1,128)S(1)} %bitcast.4, f32[72,64]{1,0:T(8,128)S(1)} %get-tuple-element.28.partial, f32[64,128]{1,0:T(8,128)S(1)} %get-tuple-element.29.face_here, bf16[2,64,64,128]{3,2,1,0:T(8,128)(2,1)S(1)} %get-tuple-element.24.here, ...), custom_call_target="tpu_custom_call" | custom-call | flops 100000000 | bytes 1048576 | tf_op jit(solution)/shard_map/pallas_call | solution.py:642
  15.6 1.0 %collective-permute-start.5 = (f32[72,128]{1,0:T(8,128)S(1)}, f32[72,128]{1,0:T(8,128)S(1)}, u32[]{:S(2)}, u32[]{:S(2)}) collective-permute-start(f32[72,128]{1,0:T(8,128)S(1)} %shard_map.64), channel_id=1, source_target_pairs={{0,1},{1,0},{2,3},{3,2},{4,5},{5,4},{6,7},{7,6},{8,9},{9,8},{10,11... | collective-permute-start | bytes 110600 | tf_op jit(solution)/shard_map/ppermute | solution.py:551
  16.6 0.9 %collective-permute-done.5 = f32[72,128]{1,0:T(8,128)S(1)} collective-permute-done((f32[72,128]{1,0:T(8,128)S(1)}, f32[72,128]{1,0:T(8,128)S(1)}, u32[]{:S(2)}, u32[]{:S(2)}) %collective-permute-start.5) | collective-permute-done | bytes 36896 | tf_op jit(solution)/shard_map/ppermute | solution.py:551
  17.5 1.5 %collective-permute-start.6 = (f32[72,128]{1,0:T(8,128)S(1)}, f32[72,128]{1,0:T(8,128)S(1)}, u32[]{:S(2)}, u32[]{:S(2)}) collective-permute-start(f32[72,128]{1,0:T(8,128)S(1)} %add.3.own.after), channel_id=1, source_target_pairs={{0,3},{1,2},{2,1},{3,0},{4,7},{5,6},{6,5},{7,4},{8,11},{9,10},{10,... | collective-permute-start | bytes 110600 | tf_op jit(solution)/shard_map/ppermute | solution.py:559
  18.9 2.0 %collective-permute-start.7 = (f32[72,128]{1,0:T(8,128)S(1)}, f32[72,128]{1,0:T(8,128)S(1)}, u32[]{:S(2)}, u32[]{:S(2)}) collective-permute-start(f32[72,128]{1,0:T(8,128)S(1)} %add.3.own.after), channel_id=1, source_target_pairs={{0,5},{1,4},{2,7},{3,6},{4,1},{5,0},{6,3},{7,2},{8,13},{9,12},{10,... | collective-permute-start | bytes 110600 | tf_op jit(solution)/shard_map/ppermute | solution.py:559
  20.9 0.0 collective-permute-start.8
  20.9 1.5 %collective-permute-start.12 = (bf16[64,32,128]{2,1,0:T(8,128)(2,1)S(1)}, bf16[64,32,128]{2,1,0:T(8,128)(2,1)S(1)}, u32[]{:S(2)}, u32[]{:S(2)}) collective-permute-start(bf16[64,32,128]{2,1,0:T(8,128)(2,1)S(1)} %shard_map.67), channel_id=1, source_target_pairs={{0,4},{1,2},{2,1},{3,7},{4,0},{5,6},{6,5},{7,3},{8,12},{9,10},{10,... | collective-permute-start | bytes 1572872 | tf_op jit(solution)/shard_map/ppermute | solution.py:547
  22.4 0.0 collective-permute-done.6.across
  22.4 0.1 collective-permute-done.7.beside
  22.6 2.7 %collective-permute-done.8.oblique = f32[72,128]{1,0:T(8,128)S(1)} collective-permute-done((f32[72,128]{1,0:T(8,128)S(1)}, f32[72,128]{1,0:T(8,128)S(1)}, u32[]{:S(2)}, u32[]{:S(2)}) %collective-permute-start.8) | collective-permute-done | bytes 36896 | tf_op jit(solution)/shard_map/ppermute | solution.py:559
  25.4 0.1 collective-permute-start.9
  25.4 0.1 collective-permute-start.10
  25.5 0.3 shard_map.68
  25.8 5.0 %collective-permute-done.9.refs_1_ = bf16[2,80,128]{2,1,0:T(8,128)(2,1)S(1)} collective-permute-done((bf16[2,80,128]{2,1,0:T(8,128)(2,1)S(1)}, bf16[2,80,128]{2,1,0:T(8,128)(2,1)S(1)}, u32[]{:S(2)}, u32[]{:S(2)}) %collective-permute-start.9) | collective-permute-done | bytes 40992 | tf_op jit(solution)/shard_map/ppermute | solution.py:575
  30.8 0.0 collective-permute-start.11
  30.8 0.5 %shard_map.66 = (f32[64,2,64,128]{3,2,1,0:T(8,128)S(1)}, f32[64,64,128]{2,1,0:T(8,128)S(1)}, f32[64,32,128]{2,1,0:T(8,128)S(1)}) custom-call(bf16[2,80,128]{2,1,0:T(8,128)(2,1)S(1)} %shard_map.65.packed.pair.refs_0_, bf16[64,2,64,128]{3,2,1,0:T(8,128)(2,1)S(1)} %copy-done, bf16[65,64,128]{2,1,0:T(8,128)(2,1)S(1)} %collective-permute-done.inner_got, ...), custom_call_target="tpu_custom_call" | custom-call | flops 1073741824 | bytes 1048576 | tf_op jit(solution)/shard_map/pallas_call | solution.py:673
  31.3 0.7 %collective-permute-done.11.refs_3_ = bf16[2,80,128]{2,1,0:T(8,128)(2,1)S(1)} collective-permute-done((bf16[2,80,128]{2,1,0:T(8,128)(2,1)S(1)}, bf16[2,80,128]{2,1,0:T(8,128)(2,1)S(1)}, u32[]{:S(2)}, u32[]{:S(2)}) %collective-permute-start.11) | collective-permute-done | bytes 40992 | tf_op jit(solution)/shard_map/ppermute | solution.py:551
  32.0 0.0 collective-permute-done.12.refs_7_
  32.0 2.7 %shard_map.69 = (f32[1,64]{1,0:T(1,128)}, f32[2,64,128]{2,1,0:T(8,128)}) custom-call(bf16[2,80,128]{2,1,0:T(8,128)(2,1)S(1)} %shard_map.65.packed.pair.refs_0_, bf16[2,80,128]{2,1,0:T(8,128)(2,1)S(1)} %collective-permute-done.9.refs_1_, bf16[2,80,128]{2,1,0:T(8,128)(2,1)S(1)} %collective-permute-done.10.refs_2_, ...), custom_call_target="tpu_custom_call" | custom-call | flops 10000000 | bytes 5242880 | tf_op jit(solution)/shard_map/pallas_call | solution.py:685
  (14 shorter events, 0.1 us)
Async XLA Ops:
  0.6 6.3 %copy-start.1 = (s32[2,64,128]{2,1,0:T(8,128)S(1)}, s32[2,64,128]{2,1,0:T(8,128)}, u32[]{:S(2)}) copy-start(s32[2,64,128]{2,1,0:T(8,128)} %labels_far.1) | copy-start | bytes 196612
  0.6 6.3 %copy-start = (bf16[64,2,64,128]{3,2,1,0:T(8,128)(2,1)S(1)}, bf16[64,2,64,128]{3,2,1,0:T(8,128)(2,1)}, u32[]{:S(2)}) copy-start(bf16[64,2,64,128]{3,2,1,0:T(8,128)(2,1)} %zvec.5) | copy-start | bytes 6291460
  0.7 9.5 %copy-start.3 = (f32[4]{0:T(128)S(1)}, f32[4]{0:T(128)}, u32[]{:S(2)}) copy-start(f32[4]{0:T(128)} %param.5) | copy-start | bytes 52
  0.7 9.5 %copy-start.2 = (f32[2,64,128]{2,1,0:T(8,128)S(1)}, f32[2,64,128]{2,1,0:T(8,128)}, u32[]{:S(2)}) copy-start(f32[2,64,128]{2,1,0:T(8,128)} %refs_13_.1) | copy-start | bytes 196612
  2.3 11.4 %collective-permute-start = (bf16[65,64,128]{2,1,0:T(8,128)(2,1)S(1)}, bf16[65,64,128]{2,1,0:T(8,128)(2,1)S(1)}, u32[]{:S(2)}, u32[]{:S(2)}) collective-permute-start(bf16[65,64,128]{2,1,0:T(8,128)(2,1)S(1)} %get-tuple-element.25), channel_id=1, source_target_pairs={{0,1},{1,0},{2,3},{3,2},{4,5},{5,4},{6,7},{7,6},{8,9},{9,8},{10,11... | collective-permute-start | bytes 3194888 | tf_op jit(solution)/shard_map/ppermute | solution.py:534
  2.8 11.8 %collective-permute-start.1 = (bf16[68,16,128]{2,1,0:T(8,128)(2,1)S(1)}, bf16[68,16,128]{2,1,0:T(8,128)(2,1)S(1)}, u32[]{:S(2)}, u32[]{:S(2)}) collective-permute-start(bf16[68,16,128]{2,1,0:T(8,128)(2,1)S(1)} %get-tuple-element.27), channel_id=1, source_target_pairs={{0,4},{1,2},{2,1},{3,7},{4,0},{5,6},{6,5},{7,3},{8,12},{9,10},{10,... | collective-permute-start | bytes 835592 | tf_op jit(solution)/shard_map/ppermute | solution.py:547
  5.4 9.7 %collective-permute-start.2 = (bf16[64,16,128]{2,1,0:T(8,128)(2,1)S(1)}, bf16[64,16,128]{2,1,0:T(8,128)(2,1)S(1)}, u32[]{:S(2)}, u32[]{:S(2)}) collective-permute-start(bf16[64,16,128]{2,1,0:T(8,128)(2,1)S(1)} %get-tuple-element.30), channel_id=1, source_target_pairs={{0,8},{1,2},{2,1},{3,11},{4,12},{5,6},{6,5},{7,15},{8,0},{9,10},{1... | collective-permute-start | bytes 786440 | tf_op jit(solution)/shard_map/ppermute | solution.py:547
  7.7 7.4 %collective-permute-start.3 = (bf16[96,128]{1,0:T(8,128)(2,1)S(1)}, bf16[96,128]{1,0:T(8,128)(2,1)S(1)}, u32[]{:S(2)}, u32[]{:S(2)}) collective-permute-start(bf16[96,128]{1,0:T(8,128)(2,1)S(1)} %get-tuple-element.31.two_pack), channel_id=1, source_target_pairs={{0,28},{4,8},{8,4},{12,16},{16,12},{20,24},{24,20},{28,0},{1,29},{... | collective-permute-start | bytes 73736 | tf_op jit(solution)/shard_map/ppermute | solution.py:534
  10.1 4.9 %collective-permute-start.4 = (bf16[80,128]{1,0:T(8,128)(2,1)S(1)}, bf16[80,128]{1,0:T(8,128)(2,1)S(1)}, u32[]{:S(2)}, u32[]{:S(2)}) collective-permute-start(bf16[80,128]{1,0:T(8,128)(2,1)S(1)} %get-tuple-element.21.after.one_pack), channel_id=1, source_target_pairs={{0,4},{4,0},{8,12},{12,8},{16,20},{20,16},{24,28},{28,24},{1,5},{5... | collective-permute-start | bytes 61448 | tf_op jit(solution)/shard_map/ppermute | solution.py:534
  15.6 1.9 %collective-permute-start.5 = (f32[72,128]{1,0:T(8,128)S(1)}, f32[72,128]{1,0:T(8,128)S(1)}, u32[]{:S(2)}, u32[]{:S(2)}) collective-permute-start(f32[72,128]{1,0:T(8,128)S(1)} %shard_map.64), channel_id=1, source_target_pairs={{0,1},{1,0},{2,3},{3,2},{4,5},{5,4},{6,7},{7,6},{8,9},{9,8},{10,11... | collective-permute-start | bytes 110600 | tf_op jit(solution)/shard_map/ppermute | solution.py:551
  17.5 5.0 %collective-permute-start.6 = (f32[72,128]{1,0:T(8,128)S(1)}, f32[72,128]{1,0:T(8,128)S(1)}, u32[]{:S(2)}, u32[]{:S(2)}) collective-permute-start(f32[72,128]{1,0:T(8,128)S(1)} %add.3.own.after), channel_id=1, source_target_pairs={{0,3},{1,2},{2,1},{3,0},{4,7},{5,6},{6,5},{7,4},{8,11},{9,10},{10,... | collective-permute-start | bytes 110600 | tf_op jit(solution)/shard_map/ppermute | solution.py:559
  18.9 3.6 %collective-permute-start.7 = (f32[72,128]{1,0:T(8,128)S(1)}, f32[72,128]{1,0:T(8,128)S(1)}, u32[]{:S(2)}, u32[]{:S(2)}) collective-permute-start(f32[72,128]{1,0:T(8,128)S(1)} %add.3.own.after), channel_id=1, source_target_pairs={{0,5},{1,4},{2,7},{3,6},{4,1},{5,0},{6,3},{7,2},{8,13},{9,12},{10,... | collective-permute-start | bytes 110600 | tf_op jit(solution)/shard_map/ppermute | solution.py:559
  20.9 4.4 %collective-permute-start.8 = (f32[72,128]{1,0:T(8,128)S(1)}, f32[72,128]{1,0:T(8,128)S(1)}, u32[]{:S(2)}, u32[]{:S(2)}) collective-permute-start(f32[72,128]{1,0:T(8,128)S(1)} %add.3.own.after), channel_id=1, source_target_pairs={{0,7},{1,6},{2,5},{3,4},{4,3},{5,2},{6,1},{7,0},{8,15},{9,14},{10,... | collective-permute-start | bytes 110600 | tf_op jit(solution)/shard_map/ppermute | solution.py:559
  20.9 11.1 %collective-permute-start.12 = (bf16[64,32,128]{2,1,0:T(8,128)(2,1)S(1)}, bf16[64,32,128]{2,1,0:T(8,128)(2,1)S(1)}, u32[]{:S(2)}, u32[]{:S(2)}) collective-permute-start(bf16[64,32,128]{2,1,0:T(8,128)(2,1)S(1)} %shard_map.67), channel_id=1, source_target_pairs={{0,4},{1,2},{2,1},{3,7},{4,0},{5,6},{6,5},{7,3},{8,12},{9,10},{10,... | collective-permute-start | bytes 1572872 | tf_op jit(solution)/shard_map/ppermute | solution.py:547
  25.4 5.4 %collective-permute-start.9 = (bf16[2,80,128]{2,1,0:T(8,128)(2,1)S(1)}, bf16[2,80,128]{2,1,0:T(8,128)(2,1)S(1)}, u32[]{:S(2)}, u32[]{:S(2)}) collective-permute-start(bf16[2,80,128]{2,1,0:T(8,128)(2,1)S(1)} %shard_map.65.packed.pair.refs_0_), channel_id=1, source_target_pairs={{0,16},{1,25},{2,18},{3,27},{4,20},{5,29},{6,22},{7,31},{8,24},{9,... | collective-permute-start | bytes 122888 | tf_op jit(solution)/shard_map/ppermute | solution.py:575
  25.4 5.8 %collective-permute-start.10 = (bf16[2,80,128]{2,1,0:T(8,128)(2,1)S(1)}, bf16[2,80,128]{2,1,0:T(8,128)(2,1)S(1)}, u32[]{:S(2)}, u32[]{:S(2)}) collective-permute-start(bf16[2,80,128]{2,1,0:T(8,128)(2,1)S(1)} %shard_map.65.packed.pair.refs_0_), channel_id=1, source_target_pairs={{0,9},{1,8},{2,11},{3,10},{4,13},{5,12},{6,15},{7,14},{8,1},{9,0},... | collective-permute-start | bytes 122888 | tf_op jit(solution)/shard_map/ppermute | solution.py:559
  30.8 1.2 %collective-permute-start.11 = (bf16[2,80,128]{2,1,0:T(8,128)(2,1)S(1)}, bf16[2,80,128]{2,1,0:T(8,128)(2,1)S(1)}, u32[]{:S(2)}, u32[]{:S(2)}) collective-permute-start(bf16[2,80,128]{2,1,0:T(8,128)(2,1)S(1)} %collective-permute-done.9.refs_1_), channel_id=1, source_target_pairs={{0,1},{1,0},{2,3},{3,2},{4,5},{5,4},{6,7},{7,6},{8,9},{9,8},{10,11... | collective-permute-start | bytes 122888 | tf_op jit(solution)/shard_map/ppermute | solution.py:551

commit v15 on v12

--- a/solution.py
+++ b/solution.py
@@ -153,14 +153,14 @@
         link_z[x] = inner_z
 
     def step(j, carry):
-        total, rhs, wide = carry
+        total, wide = carry
         turn_rows(pl.multiple_of(jnp.minimum((j + 1) * STEP, rows - STEP), STEP))
         for u in range(STEP):
             y = j * STEP + u
             at = pl.ds(y, 1)
             ahead = jnp.minimum(y + 1, rows - 1)
             up = [here[x, ahead].astype(F32) for x in range(2)]
-            images = []
+            images, parts = [], []
             for x in range(2):
                 image = (
                     half_diag[x, at, :] * wide[x]
@@ -169,31 +169,34 @@
                 )
                 if x == 0:
                     image = image - weights[0, at, :] * wide[1]
-                rhs = rhs + resid[held[x], at, :] * wide[x]
                 images.append(image.astype(BF16))
+                value = resid[held[x], at, :]
+                high = value.astype(BF16).astype(F32)
+                part = jnp.where(part_row == 0, high, jnp.where(part_row == 1, value - high, 0.0))
+                parts.append(part.astype(BF16))
             total = total + lax.dot_general(
-                jnp.concatenate(images, axis=1),
+                jnp.concatenate(
+                    [jnp.concatenate(images, axis=1), jnp.concatenate(parts, axis=1)], axis=0
+                ),
                 jnp.concatenate([here[0, y], here[1, y]], axis=1),
                 NT,
                 preferred_element_type=F32,
             )
             wide = up
-        return total, rhs, wide
-
-    total, rhs, _ = lax.fori_loop(
+        return total, wide
+
+    part_row = lax.broadcasted_iota(jnp.int32, (16, layers), 0)
+    total, _ = lax.fori_loop(
         0,
         rows // STEP,
         step,
         (
-            jnp.zeros((modes, modes), F32),
-            jnp.zeros((modes, layers), F32),
+            jnp.zeros((modes + 16, modes), F32),
             [here[x, 0].astype(F32) for x in range(2)],
         ),
     )
-    partial[:modes, :] = total
-    partial[modes:, :] = lax.dot_general(
-        jnp.ones((8, layers), F32), rhs, NT, precision=PRECISE, preferred_element_type=F32
-    )
+    partial[:modes, :] = total[:modes]
+    partial[modes:, :] = jnp.broadcast_to(total[modes:modes + 1] + total[modes + 1:modes + 2], (8, modes))
 
 
 def turn(got, start, out):
@@ -548,13 +551,19 @@
 def mask_of(index, count):
     if count == 1:
         return 0
-    swap = lax.rem(here_on("pln"), 2) * (FAR[1] - FAR[0])
+    swap = far_role(here_on("sub"), here_on("pln")) * (FAR[1] - FAR[0])
     return (0, FAR[0] + swap, 2, FAR[1] - swap)[index]
+
+
+def far_role(s, p):
+    return (p ^ (s >> 2)) & 1
 
 
 def far_partner(value):
     subs, count = lax.axis_size("sub"), lax.axis_size("pln")
-    pairs = [(s * count + p, (s ^ FAR[p % 2]) * count + p) for s in range(subs) for p in range(count)]
+    pairs = [
+        (s * count + p, (s ^ FAR[far_role(s, p)]) * count + (p ^ 1)) for s in range(subs) for p in range(count)
+    ]
     return lax.ppermute(value, ("sub", "pln"), pairs)
 
 

time: 33.2 us -> 33 us (level)
  starting transfers between devices: 13.7 us -> 14.7 us
  waiting for transfers between devices: 7.1 us -> 6.1 us
    ppermute x1, waiting for transfers between devices: 3.35 us -> 2.33 us  [far_partner(): return lax.ppermute(value, ('sub', 'pln'), pairs)]
    ppermute x2, starting transfers between devices: 0.07 us -> 0.82 us  [exchanged(): lax.ppermute(value, axis, [(i, i ^ mask) for i in range(lax.axis_size(axi...]
    ppermute x2, waiting for transfers between devices: 0.03 us -> 0.38 us  [swapped_all(): return lax.ppermute(value, ('sub', 'pln'), pairs)]
    ppermute x2, waiting for transfers between devices: 1.9 us -> 1.55 us  [exchanged(): lax.ppermute(value, axis, [(i, i ^ mask) for i in range(lax.axis_size(axi...]
  transfers between devices with their start and end apart: 12 -> 12, of which waited for: 6 -> 7; matrix products, arithmetic and copies ran while one was open for 0% -> 0% of each run, Pallas kernels for 18% -> 17%
where the time goes in v15:
time: 33 us; the launch traced here: 32.9 us
  starting transfers between devices  14.7 us (45%)
  Pallas kernels  11.2 us (34%)
  waiting for transfers between devices  6.1 us (18%)
  between operations  0.77 us (2%)
    ppermute x3, starting transfers between devices, swapped(): return lax.ppermute(value, axis, pairs)  5.62 us
    pallas_call x1, Pallas kernels, body(): call(block_kernel, [shape((modes + 8, modes), F32), shape((7,) + plane, F...  3.37 us
    ppermute x4, starting transfers between devices, partner(): return lax.ppermute(value, ('sub', 'pln'), pairs)  3.31 us
    ppermute x2, starting transfers between devices, swapped_all(): return lax.ppermute(value, ('sub', 'pln'), pairs)  2.83 us
    pallas_call x1, Pallas kernels, body(): call(finish_kernel, [shape((1, modes), F32), shape(field, F32)], [VMEM] *...  2.75 us
    ppermute x1, waiting for transfers between devices, far_partner(): return lax.ppermute(value, ('sub', 'pln'), pairs)  2.33 us
    ppermute x1, starting transfers between devices, far_partner(): return lax.ppermute(value, ('sub', 'pln'), pairs)  2.15 us
    ppermute x4, waiting for transfers between devices, partner(): return lax.ppermute(value, ('sub', 'pln'), pairs)  1.82 us
  transfers between devices with their start and end apart: 12, of which 7 were waited for; matrix products, arithmetic and copies ran while one was open for 0% of the time, Pallas kernels for 17%

profile of v15, /device:TPU:0, one launch (start us, length us, event | category | flops | bytes accessed | tf_op | source)
XLA Modules:
  0.0 32.9 jit_solution(1147766155992990829)
XLA Ops:
  0.7 1.6 %shard_map.61 = (bf16[65,64,128]{2,1,0:T(8,128)(2,1)S(1)}, bf16[66,32,128]{2,1,0:T(8,128)(2,1)S(1)}) custom-call(s32[2,64,128]{2,1,0:T(8,128)} %labels_far.1, bf16[64,2,64,128]{3,2,1,0:T(8,128)(2,1)} %zvec.5), custom_call_target="tpu_custom_call" | custom-call | bytes 2097152 | tf_op jit(solution)/shard_map/pallas_call | solution.py:577
  2.3 0.5 %collective-permute-start = (bf16[65,64,128]{2,1,0:T(8,128)(2,1)S(1)}, bf16[65,64,128]{2,1,0:T(8,128)(2,1)S(1)}, u32[]{:S(2)}, u32[]{:S(2)}) collective-permute-start(bf16[65,64,128]{2,1,0:T(8,128)(2,1)S(1)} %get-tuple-element.23), channel_id=1, source_target_pairs={{0,1},{1,0},{2,3},{3,2},{4,5},{5,4},{6,7},{7,6},{8,9},{9,8},{10,11... | collective-permute-start | bytes 3194888 | tf_op jit(solution)/shard_map/ppermute | solution.py:520
  2.8 2.6 %collective-permute-start.1 = (bf16[66,32,128]{2,1,0:T(8,128)(2,1)S(1)}, bf16[66,32,128]{2,1,0:T(8,128)(2,1)S(1)}, u32[]{:S(2)}, u32[]{:S(2)}) collective-permute-start(bf16[66,32,128]{2,1,0:T(8,128)(2,1)S(1)} %get-tuple-element.25), channel_id=1, source_target_pairs={{0,4},{1,2},{2,1},{3,7},{4,0},{5,6},{6,5},{7,3},{8,12},{9,10},{10,... | collective-permute-start | bytes 1622024 | tf_op jit(solution)/shard_map/ppermute | solution.py:533
  5.4 0.7 %shard_map.59 = (bf16[64,32,128]{2,1,0:T(8,128)(2,1)S(1)}, bf16[80,128]{1,0:T(8,128)(2,1)S(1)}, bf16[80,128]{1,0:T(8,128)(2,1)S(1)}) custom-call(s32[2,64,128]{2,1,0:T(8,128)S(1)} %copy-done.1, bf16[64,2,64,128]{3,2,1,0:T(8,128)(2,1)S(1)} %copy-done), custom_call_target="tpu_custom_call" | custom-call | flops 10000000 | bytes 6291456 | tf_op jit(solution)/shard_map/pallas_call | solution.py:587
  6.1 0.4 %collective-permute-start.2 = (bf16[80,128]{1,0:T(8,128)(2,1)S(1)}, bf16[80,128]{1,0:T(8,128)(2,1)S(1)}, u32[]{:S(2)}, u32[]{:S(2)}) collective-permute-start(bf16[80,128]{1,0:T(8,128)(2,1)S(1)} %get-tuple-element.19.after.one_pack), channel_id=1, source_target_pairs={{0,4},{4,0},{8,12},{12,8},{16,20},{20,16},{24,28},{28,24},{1,5},{5... | collective-permute-start | bytes 61448 | tf_op jit(solution)/shard_map/ppermute | solution.py:520
  6.5 4.7 %collective-permute-start.3 = (bf16[80,128]{1,0:T(8,128)(2,1)S(1)}, bf16[80,128]{1,0:T(8,128)(2,1)S(1)}, u32[]{:S(2)}, u32[]{:S(2)}) collective-permute-start(bf16[80,128]{1,0:T(8,128)(2,1)S(1)} %get-tuple-element.26.two_pack), channel_id=1, source_target_pairs={{0,28},{4,8},{8,4},{12,16},{16,12},{20,24},{24,20},{28,0},{1,29},{... | collective-permute-start | bytes 61448 | tf_op jit(solution)/shard_map/ppermute | solution.py:520
  11.2 3.4 %shard_map.60 = (f32[72,64]{1,0:T(8,128)S(1)}, f32[7,64,128]{2,1,0:T(8,128)S(1)}, bf16[2,64,64,128]{3,2,1,0:T(8,128)(2,1)S(1)}) custom-call(f32[1,4]{1,0:T(1,128)S(1)} %bitcast.1, s32[2,64,128]{2,1,0:T(8,128)S(1)} %copy-done.1, f32[2,64,128]{2,1,0:T(8,128)S(1)} %copy-done.2, bf16[64,2,64,128]{3,2,1,0:T(8,128)(2,1)S(1)} %copy-done, ...), custom_call_target="tpu_custom_call" | custom-call | flops 400000000 | bytes 3145728 | tf_op jit(solution)/shard_map/pallas_call | solution.py:598
  14.6 0.0 collective-permute-done.inner_got
  14.6 0.9 %shard_map.62 = (f32[72,64]{1,0:T(8,128)S(1)}, f32[64,128]{1,0:T(8,128)S(1)}) custom-call(f32[1,4]{1,0:T(1,128)S(1)} %bitcast.2, f32[72,64]{1,0:T(8,128)S(1)} %get-tuple-element.20.partial, f32[7,64,128]{2,1,0:T(8,128)S(1)} %get-tuple-element.21.weights.refs_10_, bf16[2,64,64,128]{3,2,1,0:T(8,128)(2,1)S(1)} %get-tuple-element.22.here, ...), custom_call_target="tpu_custom_call" | custom-call | flops 100000000 | bytes 1048576 | tf_op jit(solution)/shard_map/pallas_call | solution.py:611
  15.5 0.0 collective-permute-done.2.one_got
  15.5 0.0 collective-permute-done.3.two_got
  15.5 0.0 collective-permute-done.1.outer_got
  15.5 1.2 %shard_map.63 = (f32[72,128]{1,0:T(8,128)S(1)}, f32[64,128]{1,0:T(8,128)S(1)}) custom-call(f32[1,4]{1,0:T(1,128)S(1)} %bitcast.3, f32[72,64]{1,0:T(8,128)S(1)} %get-tuple-element.24.partial, f32[7,64,128]{2,1,0:T(8,128)S(1)} %get-tuple-element.21.weights.refs_10_, bf16[2,64,64,128]{3,2,1,0:T(8,128)(2,1)S(1)} %get-tuple-element.22.here, ...), custom_call_target="tpu_custom_call" | custom-call | flops 100000000 | bytes 1048576 | tf_op jit(solution)/shard_map/pallas_call | solution.py:619
  16.7 0.1 collective-permute-start.4
  16.7 1.2 %collective-permute-done.4 = f32[72,128]{1,0:T(8,128)S(1)} collective-permute-done((f32[72,128]{1,0:T(8,128)S(1)}, f32[72,128]{1,0:T(8,128)S(1)}, u32[]{:S(2)}, u32[]{:S(2)}) %collective-permute-start.4) | collective-permute-done | bytes 36896 | tf_op jit(solution)/shard_map/ppermute | solution.py:537
  17.9 0.7 %collective-permute-start.5 = (f32[72,128]{1,0:T(8,128)S(1)}, f32[72,128]{1,0:T(8,128)S(1)}, u32[]{:S(2)}, u32[]{:S(2)}) collective-permute-start(f32[72,128]{1,0:T(8,128)S(1)} %add.3.own.after), channel_id=1, source_target_pairs={{0,3},{1,2},{2,1},{3,0},{4,7},{5,6},{6,5},{7,4},{8,11},{9,10},{10,... | collective-permute-start | bytes 110600 | tf_op jit(solution)/shard_map/ppermute | solution.py:545
  18.6 0.0 collective-permute-start.6
  18.6 2.3 %collective-permute-start.7 = (f32[72,128]{1,0:T(8,128)S(1)}, f32[72,128]{1,0:T(8,128)S(1)}, u32[]{:S(2)}, u32[]{:S(2)}) collective-permute-start(f32[72,128]{1,0:T(8,128)S(1)} %add.3.own.after), channel_id=1, source_target_pairs={{0,7},{1,6},{2,5},{3,4},{4,3},{5,2},{6,1},{7,0},{8,15},{9,14},{10,... | collective-permute-start | bytes 110600 | tf_op jit(solution)/shard_map/ppermute | solution.py:545
  20.9 0.2 collective-permute-start.11
  21.2 0.2 collective-permute-done.5.across
  21.4 0.7 %collective-permute-done.6.beside = f32[72,128]{1,0:T(8,128)S(1)} collective-permute-done((f32[72,128]{1,0:T(8,128)S(1)}, f32[72,128]{1,0:T(8,128)S(1)}, u32[]{:S(2)}, u32[]{:S(2)}) %collective-permute-start.6) | collective-permute-done | bytes 36896 | tf_op jit(solution)/shard_map/ppermute | solution.py:545
  22.1 0.9 %collective-permute-done.7.oblique = f32[72,128]{1,0:T(8,128)S(1)} collective-permute-done((f32[72,128]{1,0:T(8,128)S(1)}, f32[72,128]{1,0:T(8,128)S(1)}, u32[]{:S(2)}, u32[]{:S(2)}) %collective-permute-start.7) | collective-permute-done | bytes 36896 | tf_op jit(solution)/shard_map/ppermute | solution.py:545
  23.0 2.1 %collective-permute-start.8 = (bf16[2,80,128]{2,1,0:T(8,128)(2,1)S(1)}, bf16[2,80,128]{2,1,0:T(8,128)(2,1)S(1)}, u32[]{:S(2)}, u32[]{:S(2)}) collective-permute-start(bf16[2,80,128]{2,1,0:T(8,128)(2,1)S(1)} %shard_map.64.pair.refs_0_), channel_id=1, source_target_pairs={{0,17},{1,24},{2,19},{3,26},{4,21},{5,28},{6,23},{7,30},{8,25},{9,... | collective-permute-start | bytes 122888 | tf_op jit(solution)/shard_map/ppermute | solution.py:567
  25.2 0.3 %collective-permute-start.9 = (bf16[2,80,128]{2,1,0:T(8,128)(2,1)S(1)}, bf16[2,80,128]{2,1,0:T(8,128)(2,1)S(1)}, u32[]{:S(2)}, u32[]{:S(2)}) collective-permute-start(bf16[2,80,128]{2,1,0:T(8,128)(2,1)S(1)} %shard_map.64.pair.refs_0_), channel_id=1, source_target_pairs={{0,9},{1,8},{2,11},{3,10},{4,13},{5,12},{6,15},{7,14},{8,1},{9,0},... | collective-permute-start | bytes 122888 | tf_op jit(solution)/shard_map/ppermute | solution.py:545
  25.5 0.3 shard_map.67
  25.8 2.3 %collective-permute-done.8.refs_1_ = bf16[2,80,128]{2,1,0:T(8,128)(2,1)S(1)} collective-permute-done((bf16[2,80,128]{2,1,0:T(8,128)(2,1)S(1)}, bf16[2,80,128]{2,1,0:T(8,128)(2,1)S(1)}, u32[]{:S(2)}, u32[]{:S(2)}) %collective-permute-start.8) | collective-permute-done | bytes 40992 | tf_op jit(solution)/shard_map/ppermute | solution.py:567
  28.1 0.7 %collective-permute-start.10 = (bf16[2,80,128]{2,1,0:T(8,128)(2,1)S(1)}, bf16[2,80,128]{2,1,0:T(8,128)(2,1)S(1)}, u32[]{:S(2)}, u32[]{:S(2)}) collective-permute-start(bf16[2,80,128]{2,1,0:T(8,128)(2,1)S(1)} %collective-permute-done.8.refs_1_), channel_id=1, source_target_pairs={{0,1},{1,0},{2,3},{3,2},{4,5},{5,4},{6,7},{7,6},{8,9},{9,8},{10,11... | collective-permute-start | bytes 122888 | tf_op jit(solution)/shard_map/ppermute | solution.py:537
  28.8 0.5 %shard_map.65 = (f32[64,2,64,128]{3,2,1,0:T(8,128)S(1)}, f32[64,64,128]{2,1,0:T(8,128)S(1)}, f32[64,32,128]{2,1,0:T(8,128)S(1)}) custom-call(bf16[2,80,128]{2,1,0:T(8,128)(2,1)S(1)} %shard_map.64.pair.refs_0_, bf16[64,2,64,128]{3,2,1,0:T(8,128)(2,1)S(1)} %copy-done, bf16[65,64,128]{2,1,0:T(8,128)(2,1)S(1)} %collective-permute-done.inner_got, ...), custom_call_target="tpu_custom_call" | custom-call | flops 1073741824 | bytes 1048576 | tf_op jit(solution)/shard_map/pallas_call | solution.py:650
  29.4 0.0 collective-permute-done.9.refs_2_
  29.4 0.4 %collective-permute-done.10.refs_3_ = bf16[2,80,128]{2,1,0:T(8,128)(2,1)S(1)} collective-permute-done((bf16[2,80,128]{2,1,0:T(8,128)(2,1)S(1)}, bf16[2,80,128]{2,1,0:T(8,128)(2,1)S(1)}, u32[]{:S(2)}, u32[]{:S(2)}) %collective-permute-start.10) | collective-permute-done | bytes 40992 | tf_op jit(solution)/shard_map/ppermute | solution.py:537
  29.7 0.4 %collective-permute-done.11.refs_7_ = bf16[64,32,128]{2,1,0:T(8,128)(2,1)S(1)} collective-permute-done((bf16[64,32,128]{2,1,0:T(8,128)(2,1)S(1)}, bf16[64,32,128]{2,1,0:T(8,128)(2,1)S(1)}, u32[]{:S(2)}, u32[]{:S(2)}) %collective-permute-start.11) | collective-permute-done | bytes 524320 | tf_op jit(solution)/shard_map/ppermute | solution.py:533
  30.1 2.7 %shard_map.68 = (f32[1,64]{1,0:T(1,128)}, f32[2,64,128]{2,1,0:T(8,128)}) custom-call(bf16[2,80,128]{2,1,0:T(8,128)(2,1)S(1)} %shard_map.64.pair.refs_0_, bf16[2,80,128]{2,1,0:T(8,128)(2,1)S(1)} %collective-permute-done.8.refs_1_, bf16[2,80,128]{2,1,0:T(8,128)(2,1)S(1)} %collective-permute-done.9.refs_2_, ...), custom_call_target="tpu_custom_call" | custom-call | flops 10000000 | bytes 5242880 | tf_op jit(solution)/shard_map/pallas_call | solution.py:662
  (11 shorter events, 0.1 us)
Async XLA Ops:
  0.6 4.8 %copy-start.1 = (s32[2,64,128]{2,1,0:T(8,128)S(1)}, s32[2,64,128]{2,1,0:T(8,128)}, u32[]{:S(2)}) copy-start(s32[2,64,128]{2,1,0:T(8,128)} %labels_far.1) | copy-start | bytes 196612
  0.6 4.7 %copy-start = (bf16[64,2,64,128]{3,2,1,0:T(8,128)(2,1)S(1)}, bf16[64,2,64,128]{3,2,1,0:T(8,128)(2,1)}, u32[]{:S(2)}) copy-start(bf16[64,2,64,128]{3,2,1,0:T(8,128)(2,1)} %zvec.5) | copy-start | bytes 6291460
  0.7 10.5 %copy-start.3 = (f32[4]{0:T(128)S(1)}, f32[4]{0:T(128)}, u32[]{:S(2)}) copy-start(f32[4]{0:T(128)} %param.5) | copy-start | bytes 52
  0.7 10.5 %copy-start.2 = (f32[2,64,128]{2,1,0:T(8,128)S(1)}, f32[2,64,128]{2,1,0:T(8,128)}, u32[]{:S(2)}) copy-start(f32[2,64,128]{2,1,0:T(8,128)} %refs_13_.1) | copy-start | bytes 196612
  2.3 12.3 %collective-permute-start = (bf16[65,64,128]{2,1,0:T(8,128)(2,1)S(1)}, bf16[65,64,128]{2,1,0:T(8,128)(2,1)S(1)}, u32[]{:S(2)}, u32[]{:S(2)}) collective-permute-start(bf16[65,64,128]{2,1,0:T(8,128)(2,1)S(1)} %get-tuple-element.23), channel_id=1, source_target_pairs={{0,1},{1,0},{2,3},{3,2},{4,5},{5,4},{6,7},{7,6},{8,9},{9,8},{10,11... | collective-permute-start | bytes 3194888 | tf_op jit(solution)/shard_map/ppermute | solution.py:520
  2.8 12.7 %collective-permute-start.1 = (bf16[66,32,128]{2,1,0:T(8,128)(2,1)S(1)}, bf16[66,32,128]{2,1,0:T(8,128)(2,1)S(1)}, u32[]{:S(2)}, u32[]{:S(2)}) collective-permute-start(bf16[66,32,128]{2,1,0:T(8,128)(2,1)S(1)} %get-tuple-element.25), channel_id=1, source_target_pairs={{0,4},{1,2},{2,1},{3,7},{4,0},{5,6},{6,5},{7,3},{8,12},{9,10},{10,... | collective-permute-start | bytes 1622024 | tf_op jit(solution)/shard_map/ppermute | solution.py:533
  6.1 9.4 %collective-permute-start.2 = (bf16[80,128]{1,0:T(8,128)(2,1)S(1)}, bf16[80,128]{1,0:T(8,128)(2,1)S(1)}, u32[]{:S(2)}, u32[]{:S(2)}) collective-permute-start(bf16[80,128]{1,0:T(8,128)(2,1)S(1)} %get-tuple-element.19.after.one_pack), channel_id=1, source_target_pairs={{0,4},{4,0},{8,12},{12,8},{16,20},{20,16},{24,28},{28,24},{1,5},{5... | collective-permute-start | bytes 61448 | tf_op jit(solution)/shard_map/ppermute | solution.py:520
  6.5 9.0 %collective-permute-start.3 = (bf16[80,128]{1,0:T(8,128)(2,1)S(1)}, bf16[80,128]{1,0:T(8,128)(2,1)S(1)}, u32[]{:S(2)}, u32[]{:S(2)}) collective-permute-start(bf16[80,128]{1,0:T(8,128)(2,1)S(1)} %get-tuple-element.26.two_pack), channel_id=1, source_target_pairs={{0,28},{4,8},{8,4},{12,16},{16,12},{20,24},{24,20},{28,0},{1,29},{... | collective-permute-start | bytes 61448 | tf_op jit(solution)/shard_map/ppermute | solution.py:520
  16.7 1.3 %collective-permute-start.4 = (f32[72,128]{1,0:T(8,128)S(1)}, f32[72,128]{1,0:T(8,128)S(1)}, u32[]{:S(2)}, u32[]{:S(2)}) collective-permute-start(f32[72,128]{1,0:T(8,128)S(1)} %get-tuple-element.27), channel_id=1, source_target_pairs={{0,1},{1,0},{2,3},{3,2},{4,5},{5,4},{6,7},{7,6},{8,9},{9,8},{10,11... | collective-permute-start | bytes 110600 | tf_op jit(solution)/shard_map/ppermute | solution.py:537
  17.9 3.4 %collective-permute-start.5 = (f32[72,128]{1,0:T(8,128)S(1)}, f32[72,128]{1,0:T(8,128)S(1)}, u32[]{:S(2)}, u32[]{:S(2)}) collective-permute-start(f32[72,128]{1,0:T(8,128)S(1)} %add.3.own.after), channel_id=1, source_target_pairs={{0,3},{1,2},{2,1},{3,0},{4,7},{5,6},{6,5},{7,4},{8,11},{9,10},{10,... | collective-permute-start | bytes 110600 | tf_op jit(solution)/shard_map/ppermute | solution.py:545
  18.6 3.4 %collective-permute-start.6 = (f32[72,128]{1,0:T(8,128)S(1)}, f32[72,128]{1,0:T(8,128)S(1)}, u32[]{:S(2)}, u32[]{:S(2)}) collective-permute-start(f32[72,128]{1,0:T(8,128)S(1)} %add.3.own.after), channel_id=1, source_target_pairs={{0,5},{1,4},{2,7},{3,6},{4,1},{5,0},{6,3},{7,2},{8,13},{9,12},{10,... | collective-permute-start | bytes 110600 | tf_op jit(solution)/shard_map/ppermute | solution.py:545
  18.6 4.3 %collective-permute-start.7 = (f32[72,128]{1,0:T(8,128)S(1)}, f32[72,128]{1,0:T(8,128)S(1)}, u32[]{:S(2)}, u32[]{:S(2)}) collective-permute-start(f32[72,128]{1,0:T(8,128)S(1)} %add.3.own.after), channel_id=1, source_target_pairs={{0,7},{1,6},{2,5},{3,4},{4,3},{5,2},{6,1},{7,0},{8,15},{9,14},{10,... | collective-permute-start | bytes 110600 | tf_op jit(solution)/shard_map/ppermute | solution.py:545
  20.9 9.2 %collective-permute-start.11 = (bf16[64,32,128]{2,1,0:T(8,128)(2,1)S(1)}, bf16[64,32,128]{2,1,0:T(8,128)(2,1)S(1)}, u32[]{:S(2)}, u32[]{:S(2)}) collective-permute-start(bf16[64,32,128]{2,1,0:T(8,128)(2,1)S(1)} %shard_map.66), channel_id=1, source_target_pairs={{0,4},{1,2},{2,1},{3,7},{4,0},{5,6},{6,5},{7,3},{8,12},{9,10},{10,... | collective-permute-start | bytes 1572872 | tf_op jit(solution)/shard_map/ppermute | solution.py:533
  23.0 5.1 %collective-permute-start.8 = (bf16[2,80,128]{2,1,0:T(8,128)(2,1)S(1)}, bf16[2,80,128]{2,1,0:T(8,128)(2,1)S(1)}, u32[]{:S(2)}, u32[]{:S(2)}) collective-permute-start(bf16[2,80,128]{2,1,0:T(8,128)(2,1)S(1)} %shard_map.64.pair.refs_0_), channel_id=1, source_target_pairs={{0,17},{1,24},{2,19},{3,26},{4,21},{5,28},{6,23},{7,30},{8,25},{9,... | collective-permute-start | bytes 122888 | tf_op jit(solution)/shard_map/ppermute | solution.py:567
  25.2 4.2 %collective-permute-start.9 = (bf16[2,80,128]{2,1,0:T(8,128)(2,1)S(1)}, bf16[2,80,128]{2,1,0:T(8,128)(2,1)S(1)}, u32[]{:S(2)}, u32[]{:S(2)}) collective-permute-start(bf16[2,80,128]{2,1,0:T(8,128)(2,1)S(1)} %shard_map.64.pair.refs_0_), channel_id=1, source_target_pairs={{0,9},{1,8},{2,11},{3,10},{4,13},{5,12},{6,15},{7,14},{8,1},{9,0},... | collective-permute-start | bytes 122888 | tf_op jit(solution)/shard_map/ppermute | solution.py:545
  28.1 1.6 %collective-permute-start.10 = (bf16[2,80,128]{2,1,0:T(8,128)(2,1)S(1)}, bf16[2,80,128]{2,1,0:T(8,128)(2,1)S(1)}, u32[]{:S(2)}, u32[]{:S(2)}) collective-permute-start(bf16[2,80,128]{2,1,0:T(8,128)(2,1)S(1)} %collective-permute-done.8.refs_1_), channel_id=1, source_target_pairs={{0,1},{1,0},{2,3},{3,2},{4,5},{5,4},{6,7},{7,6},{8,9},{9,8},{10,11... | collective-permute-start | bytes 122888 | tf_op jit(solution)/shard_map/ppermute | solution.py:537

commit v16 on v15

--- a/solution.py
+++ b/solution.py
@@ -520,7 +520,7 @@
     return lax.ppermute(value, axis, pairs)
 
 
-def swapped_all(value):
+def swapped_all(value, mask=1):
     subs, count = lax.axis_size("sub"), lax.axis_size("pln")
     pairs = []
     for s in range(subs):
@@ -528,7 +528,7 @@
             if 0 < i < count - 1:
                 to = (s, i + 1 if i % 2 else i - 1)
             else:
-                to = (s ^ 1, i)
+                to = (s ^ mask, i)
             pairs.append((s * count + i, to[0] * count + to[1]))
     return lax.ppermute(value, ("sub", "pln"), pairs)
 
@@ -581,7 +581,7 @@
         [pltpu.VMEM(labels.shape, jnp.int32), pltpu.SemaphoreType.DMA, pltpu.SemaphoreType.DMA((2,))],
         moved=2 << 20,
     )(*(pltpu.with_memory_space_constraint(v, pltpu.HBM) for v in (labels, zvec)))
-    outer_got = swapped_all(outer_near)
+    outer_got = swapped_all(outer_near, 2 if subs % 4 == 0 else 1)
     inner_got = swapped(inner_send, "pln", 0)
     rest = shape((modes, half, layers), BF16)
     outer_rest, one_pack, two_pack = call(

time: 33 us -> 34.2 us (1.036)
  waiting for transfers between devices: 6.1 us -> 9.51 us
  starting transfers between devices: 14.7 us -> 12.5 us
    ppermute x3, waiting for transfers between devices: 0.01 us -> 2.25 us  [swapped(): return lax.ppermute(value, axis, pairs)]
    ppermute x1, starting transfers between devices: 2.15 us -> 0.68 us  [far_partner(): return lax.ppermute(value, ('sub', 'pln'), pairs)]
    ppermute x3, starting transfers between devices: 5.62 us -> 4.49 us  [swapped(): return lax.ppermute(value, axis, pairs)]
    ppermute x1, waiting for transfers between devices: 2.33 us -> 3.12 us  [far_partner(): return lax.ppermute(value, ('sub', 'pln'), pairs)]
    ppermute x2, waiting for transfers between devices: 0.38 us -> 0.95 us  [swapped_all(): return lax.ppermute(value, ('sub', 'pln'), pairs)]
  transfers between devices with their start and end apart: 12 -> 12, of which waited for: 7 -> 8; matrix products, arithmetic and copies ran while one was open for 0% -> 0% of each run, Pallas kernels for 17% -> 17%
where the time goes in v16:
time: 34.2 us; the launch traced here: 34 us
  starting transfers between devices  12.5 us (37%)
  Pallas kernels  11.2 us (33%)
  waiting for transfers between devices  9.51 us (28%)
  between operations  0.75 us (2%)
    ppermute x3, starting transfers between devices, swapped(): return lax.ppermute(value, axis, pairs)  4.49 us
    ppermute x4, starting transfers between devices, partner(): return lax.ppermute(value, ('sub', 'pln'), pairs)  3.4 us
    pallas_call x1, Pallas kernels, body(): call(block_kernel, [shape((modes + 8, modes), F32), shape((7,) + plane, F...  3.37 us
    ppermute x1, waiting for transfers between devices, far_partner(): return lax.ppermute(value, ('sub', 'pln'), pairs)  3.12 us
    ppermute x2, starting transfers between devices, swapped_all(): return lax.ppermute(value, ('sub', 'pln'), pairs)  2.89 us
    pallas_call x1, Pallas kernels, body(): call(finish_kernel, [shape((1, modes), F32), shape(field, F32)], [VMEM] *...  2.75 us
    ppermute x3, waiting for transfers between devices, swapped(): return lax.ppermute(value, axis, pairs)  2.25 us
    ppermute x4, waiting for transfers between devices, partner(): return lax.ppermute(value, ('sub', 'pln'), pairs)  1.63 us
  transfers between devices with their start and end apart: 12, of which 8 were waited for; matrix products, arithmetic and copies ran while one was open for 0% of the time, Pallas kernels for 17%

profile of v16, /device:TPU:0, one launch (start us, length us, event | category | flops | bytes accessed | tf_op | source)
XLA Modules:
  0.0 34.0 jit_solution(10476051844818230448)
XLA Ops:
  0.7 1.6 %shard_map.61 = (bf16[65,64,128]{2,1,0:T(8,128)(2,1)S(1)}, bf16[66,32,128]{2,1,0:T(8,128)(2,1)S(1)}) custom-call(s32[2,64,128]{2,1,0:T(8,128)} %labels_far.1, bf16[64,2,64,128]{3,2,1,0:T(8,128)(2,1)} %zvec.5), custom_call_target="tpu_custom_call" | custom-call | bytes 2097152 | tf_op jit(solution)/shard_map/pallas_call | solution.py:577
  2.3 0.5 %collective-permute-start = (bf16[65,64,128]{2,1,0:T(8,128)(2,1)S(1)}, bf16[65,64,128]{2,1,0:T(8,128)(2,1)S(1)}, u32[]{:S(2)}, u32[]{:S(2)}) collective-permute-start(bf16[65,64,128]{2,1,0:T(8,128)(2,1)S(1)} %get-tuple-element.23), channel_id=1, source_target_pairs={{0,1},{1,0},{2,3},{3,2},{4,5},{5,4},{6,7},{7,6},{8,9},{9,8},{10,11... | collective-permute-start | bytes 3194888 | tf_op jit(solution)/shard_map/ppermute | solution.py:520
  2.8 2.6 %collective-permute-start.1 = (bf16[66,32,128]{2,1,0:T(8,128)(2,1)S(1)}, bf16[66,32,128]{2,1,0:T(8,128)(2,1)S(1)}, u32[]{:S(2)}, u32[]{:S(2)}) collective-permute-start(bf16[66,32,128]{2,1,0:T(8,128)(2,1)S(1)} %get-tuple-element.25), channel_id=1, source_target_pairs={{0,8},{1,2},{2,1},{3,11},{4,12},{5,6},{6,5},{7,15},{8,0},{9,10},{1... | collective-permute-start | bytes 1622024 | tf_op jit(solution)/shard_map/ppermute | solution.py:533
  5.4 0.7 %shard_map.59 = (bf16[64,32,128]{2,1,0:T(8,128)(2,1)S(1)}, bf16[80,128]{1,0:T(8,128)(2,1)S(1)}, bf16[80,128]{1,0:T(8,128)(2,1)S(1)}) custom-call(s32[2,64,128]{2,1,0:T(8,128)S(1)} %copy-done.1, bf16[64,2,64,128]{3,2,1,0:T(8,128)(2,1)S(1)} %copy-done), custom_call_target="tpu_custom_call" | custom-call | flops 10000000 | bytes 6291456 | tf_op jit(solution)/shard_map/pallas_call | solution.py:587
  6.1 1.6 %collective-permute-start.2 = (bf16[80,128]{1,0:T(8,128)(2,1)S(1)}, bf16[80,128]{1,0:T(8,128)(2,1)S(1)}, u32[]{:S(2)}, u32[]{:S(2)}) collective-permute-start(bf16[80,128]{1,0:T(8,128)(2,1)S(1)} %get-tuple-element.19.after.one_pack), channel_id=1, source_target_pairs={{0,4},{4,0},{8,12},{12,8},{16,20},{20,16},{24,28},{28,24},{1,5},{5... | collective-permute-start | bytes 61448 | tf_op jit(solution)/shard_map/ppermute | solution.py:520
  7.7 2.4 %collective-permute-start.3 = (bf16[80,128]{1,0:T(8,128)(2,1)S(1)}, bf16[80,128]{1,0:T(8,128)(2,1)S(1)}, u32[]{:S(2)}, u32[]{:S(2)}) collective-permute-start(bf16[80,128]{1,0:T(8,128)(2,1)S(1)} %get-tuple-element.26.two_pack), channel_id=1, source_target_pairs={{0,28},{4,8},{8,4},{12,16},{16,12},{20,24},{24,20},{28,0},{1,29},{... | collective-permute-start | bytes 61448 | tf_op jit(solution)/shard_map/ppermute | solution.py:520
  10.1 3.4 %shard_map.60 = (f32[72,64]{1,0:T(8,128)S(1)}, f32[7,64,128]{2,1,0:T(8,128)S(1)}, bf16[2,64,64,128]{3,2,1,0:T(8,128)(2,1)S(1)}) custom-call(f32[1,4]{1,0:T(1,128)S(1)} %bitcast.1, s32[2,64,128]{2,1,0:T(8,128)S(1)} %copy-done.1, f32[2,64,128]{2,1,0:T(8,128)S(1)} %copy-done.2, bf16[64,2,64,128]{3,2,1,0:T(8,128)(2,1)S(1)} %copy-done, ...), custom_call_target="tpu_custom_call" | custom-call | flops 400000000 | bytes 3145728 | tf_op jit(solution)/shard_map/pallas_call | solution.py:598
  13.5 0.0 collective-permute-done.inner_got
  13.5 0.9 %shard_map.62 = (f32[72,64]{1,0:T(8,128)S(1)}, f32[64,128]{1,0:T(8,128)S(1)}) custom-call(f32[1,4]{1,0:T(1,128)S(1)} %bitcast.2, f32[72,64]{1,0:T(8,128)S(1)} %get-tuple-element.20.partial, f32[7,64,128]{2,1,0:T(8,128)S(1)} %get-tuple-element.21.weights.refs_10_, bf16[2,64,64,128]{3,2,1,0:T(8,128)(2,1)S(1)} %get-tuple-element.22.here, ...), custom_call_target="tpu_custom_call" | custom-call | flops 100000000 | bytes 1048576 | tf_op jit(solution)/shard_map/pallas_call | solution.py:611
  14.4 0.0 collective-permute-done.2.one_got
  14.4 2.2 %collective-permute-done.3.two_got = bf16[80,128]{1,0:T(8,128)(2,1)S(1)} collective-permute-done((bf16[80,128]{1,0:T(8,128)(2,1)S(1)}, bf16[80,128]{1,0:T(8,128)(2,1)S(1)}, u32[]{:S(2)}, u32[]{:S(2)}) %collective-permute-start.3) | collective-permute-done | bytes 20512 | tf_op jit(solution)/shard_map/ppermute | solution.py:520
  16.6 0.0 collective-permute-done.1.outer_got
  16.6 1.2 %shard_map.63 = (f32[72,128]{1,0:T(8,128)S(1)}, f32[64,128]{1,0:T(8,128)S(1)}) custom-call(f32[1,4]{1,0:T(1,128)S(1)} %bitcast.3, f32[72,64]{1,0:T(8,128)S(1)} %get-tuple-element.24.partial, f32[7,64,128]{2,1,0:T(8,128)S(1)} %get-tuple-element.21.weights.refs_10_, bf16[2,64,64,128]{3,2,1,0:T(8,128)(2,1)S(1)} %get-tuple-element.22.here, ...), custom_call_target="tpu_custom_call" | custom-call | flops 100000000 | bytes 1048576 | tf_op jit(solution)/shard_map/pallas_call | solution.py:619
  17.8 0.1 collective-permute-start.4
  17.9 1.2 %collective-permute-done.4 = f32[72,128]{1,0:T(8,128)S(1)} collective-permute-done((f32[72,128]{1,0:T(8,128)S(1)}, f32[72,128]{1,0:T(8,128)S(1)}, u32[]{:S(2)}, u32[]{:S(2)}) %collective-permute-start.4) | collective-permute-done | bytes 36896 | tf_op jit(solution)/shard_map/ppermute | solution.py:537
  19.1 0.4 %collective-permute-start.5 = (f32[72,128]{1,0:T(8,128)S(1)}, f32[72,128]{1,0:T(8,128)S(1)}, u32[]{:S(2)}, u32[]{:S(2)}) collective-permute-start(f32[72,128]{1,0:T(8,128)S(1)} %add.3.own.after), channel_id=1, source_target_pairs={{0,3},{1,2},{2,1},{3,0},{4,7},{5,6},{6,5},{7,4},{8,11},{9,10},{10,... | collective-permute-start | bytes 110600 | tf_op jit(solution)/shard_map/ppermute | solution.py:545
  19.5 0.0 collective-permute-start.6
  19.5 2.6 %collective-permute-start.7 = (f32[72,128]{1,0:T(8,128)S(1)}, f32[72,128]{1,0:T(8,128)S(1)}, u32[]{:S(2)}, u32[]{:S(2)}) collective-permute-start(f32[72,128]{1,0:T(8,128)S(1)} %add.3.own.after), channel_id=1, source_target_pairs={{0,7},{1,6},{2,5},{3,4},{4,3},{5,2},{6,1},{7,0},{8,15},{9,14},{10,... | collective-permute-start | bytes 110600 | tf_op jit(solution)/shard_map/ppermute | solution.py:545
  22.1 0.2 collective-permute-start.11
  22.3 0.2 collective-permute-done.5.across
  22.5 0.4 %collective-permute-done.6.beside = f32[72,128]{1,0:T(8,128)S(1)} collective-permute-done((f32[72,128]{1,0:T(8,128)S(1)}, f32[72,128]{1,0:T(8,128)S(1)}, u32[]{:S(2)}, u32[]{:S(2)}) %collective-permute-start.6) | collective-permute-done | bytes 36896 | tf_op jit(solution)/shard_map/ppermute | solution.py:545
  22.9 1.0 %collective-permute-done.7.oblique = f32[72,128]{1,0:T(8,128)S(1)} collective-permute-done((f32[72,128]{1,0:T(8,128)S(1)}, f32[72,128]{1,0:T(8,128)S(1)}, u32[]{:S(2)}, u32[]{:S(2)}) %collective-permute-start.7) | collective-permute-done | bytes 36896 | tf_op jit(solution)/shard_map/ppermute | solution.py:545
  24.0 0.7 %collective-permute-start.8 = (bf16[2,80,128]{2,1,0:T(8,128)(2,1)S(1)}, bf16[2,80,128]{2,1,0:T(8,128)(2,1)S(1)}, u32[]{:S(2)}, u32[]{:S(2)}) collective-permute-start(bf16[2,80,128]{2,1,0:T(8,128)(2,1)S(1)} %shard_map.64.pair.refs_0_), channel_id=1, source_target_pairs={{0,17},{1,24},{2,19},{3,26},{4,21},{5,28},{6,23},{7,30},{8,25},{9,... | collective-permute-start | bytes 122888 | tf_op jit(solution)/shard_map/ppermute | solution.py:567
  24.7 0.4 %collective-permute-start.9 = (bf16[2,80,128]{2,1,0:T(8,128)(2,1)S(1)}, bf16[2,80,128]{2,1,0:T(8,128)(2,1)S(1)}, u32[]{:S(2)}, u32[]{:S(2)}) collective-permute-start(bf16[2,80,128]{2,1,0:T(8,128)(2,1)S(1)} %shard_map.64.pair.refs_0_), channel_id=1, source_target_pairs={{0,9},{1,8},{2,11},{3,10},{4,13},{5,12},{6,15},{7,14},{8,1},{9,0},... | collective-permute-start | bytes 122888 | tf_op jit(solution)/shard_map/ppermute | solution.py:545
  25.1 0.3 shard_map.67
  25.4 3.1 %collective-permute-done.8.refs_1_ = bf16[2,80,128]{2,1,0:T(8,128)(2,1)S(1)} collective-permute-done((bf16[2,80,128]{2,1,0:T(8,128)(2,1)S(1)}, bf16[2,80,128]{2,1,0:T(8,128)(2,1)S(1)}, u32[]{:S(2)}, u32[]{:S(2)}) %collective-permute-start.8) | collective-permute-done | bytes 40992 | tf_op jit(solution)/shard_map/ppermute | solution.py:567
  28.5 1.0 %collective-permute-start.10 = (bf16[2,80,128]{2,1,0:T(8,128)(2,1)S(1)}, bf16[2,80,128]{2,1,0:T(8,128)(2,1)S(1)}, u32[]{:S(2)}, u32[]{:S(2)}) collective-permute-start(bf16[2,80,128]{2,1,0:T(8,128)(2,1)S(1)} %collective-permute-done.8.refs_1_), channel_id=1, source_target_pairs={{0,1},{1,0},{2,3},{3,2},{4,5},{5,4},{6,7},{7,6},{8,9},{9,8},{10,11... | collective-permute-start | bytes 122888 | tf_op jit(solution)/shard_map/ppermute | solution.py:537
  29.4 0.5 %shard_map.65 = (f32[64,2,64,128]{3,2,1,0:T(8,128)S(1)}, f32[64,64,128]{2,1,0:T(8,128)S(1)}, f32[64,32,128]{2,1,0:T(8,128)S(1)}) custom-call(bf16[2,80,128]{2,1,0:T(8,128)(2,1)S(1)} %shard_map.64.pair.refs_0_, bf16[64,2,64,128]{3,2,1,0:T(8,128)(2,1)S(1)} %copy-done, bf16[65,64,128]{2,1,0:T(8,128)(2,1)S(1)} %collective-permute-done.inner_got, ...), custom_call_target="tpu_custom_call" | custom-call | flops 1073741824 | bytes 1048576 | tf_op jit(solution)/shard_map/pallas_call | solution.py:650
  30.0 0.0 collective-permute-done.9.refs_2_
  30.0 0.4 %collective-permute-done.10.refs_3_ = bf16[2,80,128]{2,1,0:T(8,128)(2,1)S(1)} collective-permute-done((bf16[2,80,128]{2,1,0:T(8,128)(2,1)S(1)}, bf16[2,80,128]{2,1,0:T(8,128)(2,1)S(1)}, u32[]{:S(2)}, u32[]{:S(2)}) %collective-permute-start.10) | collective-permute-done | bytes 40992 | tf_op jit(solution)/shard_map/ppermute | solution.py:537
  30.3 0.9 %collective-permute-done.11.refs_7_ = bf16[64,32,128]{2,1,0:T(8,128)(2,1)S(1)} collective-permute-done((bf16[64,32,128]{2,1,0:T(8,128)(2,1)S(1)}, bf16[64,32,128]{2,1,0:T(8,128)(2,1)S(1)}, u32[]{:S(2)}, u32[]{:S(2)}) %collective-permute-start.11) | collective-permute-done | bytes 524320 | tf_op jit(solution)/shard_map/ppermute | solution.py:533
  31.3 2.7 %shard_map.68 = (f32[1,64]{1,0:T(1,128)}, f32[2,64,128]{2,1,0:T(8,128)}) custom-call(bf16[2,80,128]{2,1,0:T(8,128)(2,1)S(1)} %shard_map.64.pair.refs_0_, bf16[2,80,128]{2,1,0:T(8,128)(2,1)S(1)} %collective-permute-done.8.refs_1_, bf16[2,80,128]{2,1,0:T(8,128)(2,1)S(1)} %collective-permute-done.9.refs_2_, ...), custom_call_target="tpu_custom_call" | custom-call | flops 10000000 | bytes 5242880 | tf_op jit(solution)/shard_map/pallas_call | solution.py:662
  (11 shorter events, 0.1 us)
Async XLA Ops:
  0.6 4.8 %copy-start.1 = (s32[2,64,128]{2,1,0:T(8,128)S(1)}, s32[2,64,128]{2,1,0:T(8,128)}, u32[]{:S(2)}) copy-start(s32[2,64,128]{2,1,0:T(8,128)} %labels_far.1) | copy-start | bytes 196612
  0.6 4.8 %copy-start = (bf16[64,2,64,128]{3,2,1,0:T(8,128)(2,1)S(1)}, bf16[64,2,64,128]{3,2,1,0:T(8,128)(2,1)}, u32[]{:S(2)}) copy-start(bf16[64,2,64,128]{3,2,1,0:T(8,128)(2,1)} %zvec.5) | copy-start | bytes 6291460
  0.7 9.5 %copy-start.3 = (f32[4]{0:T(128)S(1)}, f32[4]{0:T(128)}, u32[]{:S(2)}) copy-start(f32[4]{0:T(128)} %param.5) | copy-start | bytes 52
  0.7 9.5 %copy-start.2 = (f32[2,64,128]{2,1,0:T(8,128)S(1)}, f32[2,64,128]{2,1,0:T(8,128)}, u32[]{:S(2)}) copy-start(f32[2,64,128]{2,1,0:T(8,128)} %refs_13_.1) | copy-start | bytes 196612
  2.3 11.2 %collective-permute-start = (bf16[65,64,128]{2,1,0:T(8,128)(2,1)S(1)}, bf16[65,64,128]{2,1,0:T(8,128)(2,1)S(1)}, u32[]{:S(2)}, u32[]{:S(2)}) collective-permute-start(bf16[65,64,128]{2,1,0:T(8,128)(2,1)S(1)} %get-tuple-element.23), channel_id=1, source_target_pairs={{0,1},{1,0},{2,3},{3,2},{4,5},{5,4},{6,7},{7,6},{8,9},{9,8},{10,11... | collective-permute-start | bytes 3194888 | tf_op jit(solution)/shard_map/ppermute | solution.py:520
  2.8 13.9 %collective-permute-start.1 = (bf16[66,32,128]{2,1,0:T(8,128)(2,1)S(1)}, bf16[66,32,128]{2,1,0:T(8,128)(2,1)S(1)}, u32[]{:S(2)}, u32[]{:S(2)}) collective-permute-start(bf16[66,32,128]{2,1,0:T(8,128)(2,1)S(1)} %get-tuple-element.25), channel_id=1, source_target_pairs={{0,8},{1,2},{2,1},{3,11},{4,12},{5,6},{6,5},{7,15},{8,0},{9,10},{1... | collective-permute-start | bytes 1622024 | tf_op jit(solution)/shard_map/ppermute | solution.py:533
  6.1 8.2 %collective-permute-start.2 = (bf16[80,128]{1,0:T(8,128)(2,1)S(1)}, bf16[80,128]{1,0:T(8,128)(2,1)S(1)}, u32[]{:S(2)}, u32[]{:S(2)}) collective-permute-start(bf16[80,128]{1,0:T(8,128)(2,1)S(1)} %get-tuple-element.19.after.one_pack), channel_id=1, source_target_pairs={{0,4},{4,0},{8,12},{12,8},{16,20},{20,16},{24,28},{28,24},{1,5},{5... | collective-permute-start | bytes 61448 | tf_op jit(solution)/shard_map/ppermute | solution.py:520
  7.7 8.9 %collective-permute-start.3 = (bf16[80,128]{1,0:T(8,128)(2,1)S(1)}, bf16[80,128]{1,0:T(8,128)(2,1)S(1)}, u32[]{:S(2)}, u32[]{:S(2)}) collective-permute-start(bf16[80,128]{1,0:T(8,128)(2,1)S(1)} %get-tuple-element.26.two_pack), channel_id=1, source_target_pairs={{0,28},{4,8},{8,4},{12,16},{16,12},{20,24},{24,20},{28,0},{1,29},{... | collective-permute-start | bytes 61448 | tf_op jit(solution)/shard_map/ppermute | solution.py:520
  17.8 1.3 %collective-permute-start.4 = (f32[72,128]{1,0:T(8,128)S(1)}, f32[72,128]{1,0:T(8,128)S(1)}, u32[]{:S(2)}, u32[]{:S(2)}) collective-permute-start(f32[72,128]{1,0:T(8,128)S(1)} %get-tuple-element.27), channel_id=1, source_target_pairs={{0,1},{1,0},{2,3},{3,2},{4,5},{5,4},{6,7},{7,6},{8,9},{9,8},{10,11... | collective-permute-start | bytes 110600 | tf_op jit(solution)/shard_map/ppermute | solution.py:537
  19.1 3.4 %collective-permute-start.5 = (f32[72,128]{1,0:T(8,128)S(1)}, f32[72,128]{1,0:T(8,128)S(1)}, u32[]{:S(2)}, u32[]{:S(2)}) collective-permute-start(f32[72,128]{1,0:T(8,128)S(1)} %add.3.own.after), channel_id=1, source_target_pairs={{0,3},{1,2},{2,1},{3,0},{4,7},{5,6},{6,5},{7,4},{8,11},{9,10},{10,... | collective-permute-start | bytes 110600 | tf_op jit(solution)/shard_map/ppermute | solution.py:545
  19.5 3.4 %collective-permute-start.6 = (f32[72,128]{1,0:T(8,128)S(1)}, f32[72,128]{1,0:T(8,128)S(1)}, u32[]{:S(2)}, u32[]{:S(2)}) collective-permute-start(f32[72,128]{1,0:T(8,128)S(1)} %add.3.own.after), channel_id=1, source_target_pairs={{0,5},{1,4},{2,7},{3,6},{4,1},{5,0},{6,3},{7,2},{8,13},{9,12},{10,... | collective-permute-start | bytes 110600 | tf_op jit(solution)/shard_map/ppermute | solution.py:545
  19.5 4.5 %collective-permute-start.7 = (f32[72,128]{1,0:T(8,128)S(1)}, f32[72,128]{1,0:T(8,128)S(1)}, u32[]{:S(2)}, u32[]{:S(2)}) collective-permute-start(f32[72,128]{1,0:T(8,128)S(1)} %add.3.own.after), channel_id=1, source_target_pairs={{0,7},{1,6},{2,5},{3,4},{4,3},{5,2},{6,1},{7,0},{8,15},{9,14},{10,... | collective-permute-start | bytes 110600 | tf_op jit(solution)/shard_map/ppermute | solution.py:545
  22.1 9.2 %collective-permute-start.11 = (bf16[64,32,128]{2,1,0:T(8,128)(2,1)S(1)}, bf16[64,32,128]{2,1,0:T(8,128)(2,1)S(1)}, u32[]{:S(2)}, u32[]{:S(2)}) collective-permute-start(bf16[64,32,128]{2,1,0:T(8,128)(2,1)S(1)} %shard_map.66), channel_id=1, source_target_pairs={{0,4},{1,2},{2,1},{3,7},{4,0},{5,6},{6,5},{7,3},{8,12},{9,10},{10,... | collective-permute-start | bytes 1572872 | tf_op jit(solution)/shard_map/ppermute | solution.py:533
  24.0 4.5 %collective-permute-start.8 = (bf16[2,80,128]{2,1,0:T(8,128)(2,1)S(1)}, bf16[2,80,128]{2,1,0:T(8,128)(2,1)S(1)}, u32[]{:S(2)}, u32[]{:S(2)}) collective-permute-start(bf16[2,80,128]{2,1,0:T(8,128)(2,1)S(1)} %shard_map.64.pair.refs_0_), channel_id=1, source_target_pairs={{0,17},{1,24},{2,19},{3,26},{4,21},{5,28},{6,23},{7,30},{8,25},{9,... | collective-permute-start | bytes 122888 | tf_op jit(solution)/shard_map/ppermute | solution.py:567
  24.7 5.3 %collective-permute-start.9 = (bf16[2,80,128]{2,1,0:T(8,128)(2,1)S(1)}, bf16[2,80,128]{2,1,0:T(8,128)(2,1)S(1)}, u32[]{:S(2)}, u32[]{:S(2)}) collective-permute-start(bf16[2,80,128]{2,1,0:T(8,128)(2,1)S(1)} %shard_map.64.pair.refs_0_), channel_id=1, source_target_pairs={{0,9},{1,8},{2,11},{3,10},{4,13},{5,12},{6,15},{7,14},{8,1},{9,0},... | collective-permute-start | bytes 122888 | tf_op jit(solution)/shard_map/ppermute | solution.py:545
  28.5 1.8 %collective-permute-start.10 = (bf16[2,80,128]{2,1,0:T(8,128)(2,1)S(1)}, bf16[2,80,128]{2,1,0:T(8,128)(2,1)S(1)}, u32[]{:S(2)}, u32[]{:S(2)}) collective-permute-start(bf16[2,80,128]{2,1,0:T(8,128)(2,1)S(1)} %collective-permute-done.8.refs_1_), channel_id=1, source_target_pairs={{0,1},{1,0},{2,3},{3,2},{4,5},{5,4},{6,7},{7,6},{8,9},{9,8},{10,11... | collective-permute-start | bytes 122888 | tf_op jit(solution)/shard_map/ppermute | solution.py:537

commit v17 on v15

--- a/solution.py
+++ b/solution.py
@@ -6,8 +6,8 @@
 from jax.sharding import PartitionSpec as P
 
 CITERS = 2
-STEP = 16
-MODES = 8
+STEP = 32
+MODES = 16
 CHUNK = 16
 F32 = jnp.float32
 BF16 = jnp.bfloat16

time: 33 us -> 32.4 us (0.982)
  waiting for transfers between devices: 6.1 us -> 5.19 us
  starting transfers between devices: 14.7 us -> 15.6 us
  Pallas kernels: 11.2 us -> 10.6 us
    ppermute x1, waiting for transfers between devices: 2.33 us -> 1.58 us  [far_partner(): return lax.ppermute(value, ('sub', 'pln'), pairs)]
    ppermute x2, starting transfers between devices: 0.82 us -> 1.52 us  [exchanged(): lax.ppermute(value, axis, [(i, i ^ mask) for i in range(lax.axis_size(axi...]
    pallas_call x1, Pallas kernels: 1.17 us -> 0.76 us  [body(): call(outer_kernel, [shape((modes + 8, 2 * modes), F32), shape(plane, F32)...]
where the time goes in v17:
time: 32.4 us; the launch traced here: 32.3 us
  starting transfers between devices  15.6 us (48%)
  Pallas kernels  10.6 us (33%)
  waiting for transfers between devices  5.19 us (16%)
  between operations  0.77 us (2%)
    ppermute x3, starting transfers between devices, swapped(): return lax.ppermute(value, axis, pairs)  5.62 us
    pallas_call x1, Pallas kernels, body(): call(block_kernel, [shape((modes + 8, modes), F32), shape((7,) + plane, F...  3.41 us
    ppermute x4, starting transfers between devices, partner(): return lax.ppermute(value, ('sub', 'pln'), pairs)  3.31 us
    ppermute x2, starting transfers between devices, swapped_all(): return lax.ppermute(value, ('sub', 'pln'), pairs)  2.89 us
    pallas_call x1, Pallas kernels, body(): call(finish_kernel, [shape((1, modes), F32), shape(field, F32)], [VMEM] *...  2.71 us
    ppermute x1, starting transfers between devices, far_partner(): return lax.ppermute(value, ('sub', 'pln'), pairs)  2.3 us
    ppermute x4, waiting for transfers between devices, partner(): return lax.ppermute(value, ('sub', 'pln'), pairs)  1.75 us
    pallas_call x1, Pallas kernels, body(): call(stage_kernel, [shape((modes + 1, rows, layers), BF16), shape((modes...  1.6 us
  transfers between devices with their start and end apart: 12, of which 7 were waited for; matrix products, arithmetic and copies ran while one was open for 0% of the time, Pallas kernels for 17%

profile of v17, /device:TPU:0, one launch (start us, length us, event | category | flops | bytes accessed | tf_op | source)
XLA Modules:
  0.0 32.3 jit_solution(16556476155934805433)
XLA Ops:
  0.7 1.6 %shard_map.61 = (bf16[65,64,128]{2,1,0:T(8,128)(2,1)S(1)}, bf16[66,32,128]{2,1,0:T(8,128)(2,1)S(1)}) custom-call(s32[2,64,128]{2,1,0:T(8,128)} %labels_far.1, bf16[64,2,64,128]{3,2,1,0:T(8,128)(2,1)} %zvec.5), custom_call_target="tpu_custom_call" | custom-call | bytes 2097152 | tf_op jit(solution)/shard_map/pallas_call | solution.py:577
  2.3 0.5 %collective-permute-start = (bf16[65,64,128]{2,1,0:T(8,128)(2,1)S(1)}, bf16[65,64,128]{2,1,0:T(8,128)(2,1)S(1)}, u32[]{:S(2)}, u32[]{:S(2)}) collective-permute-start(bf16[65,64,128]{2,1,0:T(8,128)(2,1)S(1)} %get-tuple-element.23), channel_id=1, source_target_pairs={{0,1},{1,0},{2,3},{3,2},{4,5},{5,4},{6,7},{7,6},{8,9},{9,8},{10,11... | collective-permute-start | bytes 3194888 | tf_op jit(solution)/shard_map/ppermute | solution.py:520
  2.8 2.6 %collective-permute-start.1 = (bf16[66,32,128]{2,1,0:T(8,128)(2,1)S(1)}, bf16[66,32,128]{2,1,0:T(8,128)(2,1)S(1)}, u32[]{:S(2)}, u32[]{:S(2)}) collective-permute-start(bf16[66,32,128]{2,1,0:T(8,128)(2,1)S(1)} %get-tuple-element.25), channel_id=1, source_target_pairs={{0,4},{1,2},{2,1},{3,7},{4,0},{5,6},{6,5},{7,3},{8,12},{9,10},{10,... | collective-permute-start | bytes 1622024 | tf_op jit(solution)/shard_map/ppermute | solution.py:533
  5.4 0.7 %shard_map.59 = (bf16[64,32,128]{2,1,0:T(8,128)(2,1)S(1)}, bf16[80,128]{1,0:T(8,128)(2,1)S(1)}, bf16[80,128]{1,0:T(8,128)(2,1)S(1)}) custom-call(s32[2,64,128]{2,1,0:T(8,128)S(1)} %copy-done.1, bf16[64,2,64,128]{3,2,1,0:T(8,128)(2,1)S(1)} %copy-done), custom_call_target="tpu_custom_call" | custom-call | flops 10000000 | bytes 6291456 | tf_op jit(solution)/shard_map/pallas_call | solution.py:587
  6.1 0.4 %collective-permute-start.2 = (bf16[80,128]{1,0:T(8,128)(2,1)S(1)}, bf16[80,128]{1,0:T(8,128)(2,1)S(1)}, u32[]{:S(2)}, u32[]{:S(2)}) collective-permute-start(bf16[80,128]{1,0:T(8,128)(2,1)S(1)} %get-tuple-element.19.after.one_pack), channel_id=1, source_target_pairs={{0,4},{4,0},{8,12},{12,8},{16,20},{20,16},{24,28},{28,24},{1,5},{5... | collective-permute-start | bytes 61448 | tf_op jit(solution)/shard_map/ppermute | solution.py:520
  6.5 4.7 %collective-permute-start.3 = (bf16[80,128]{1,0:T(8,128)(2,1)S(1)}, bf16[80,128]{1,0:T(8,128)(2,1)S(1)}, u32[]{:S(2)}, u32[]{:S(2)}) collective-permute-start(bf16[80,128]{1,0:T(8,128)(2,1)S(1)} %get-tuple-element.26.two_pack), channel_id=1, source_target_pairs={{0,28},{4,8},{8,4},{12,16},{16,12},{20,24},{24,20},{28,0},{1,29},{... | collective-permute-start | bytes 61448 | tf_op jit(solution)/shard_map/ppermute | solution.py:520
  11.2 3.4 %shard_map.60 = (f32[72,64]{1,0:T(8,128)S(1)}, f32[7,64,128]{2,1,0:T(8,128)S(1)}, bf16[2,64,64,128]{3,2,1,0:T(8,128)(2,1)S(1)}) custom-call(f32[1,4]{1,0:T(1,128)S(1)} %bitcast.1, s32[2,64,128]{2,1,0:T(8,128)S(1)} %copy-done.1, f32[2,64,128]{2,1,0:T(8,128)S(1)} %copy-done.2, bf16[64,2,64,128]{3,2,1,0:T(8,128)(2,1)S(1)} %copy-done, ...), custom_call_target="tpu_custom_call" | custom-call | flops 400000000 | bytes 3145728 | tf_op jit(solution)/shard_map/pallas_call | solution.py:598
  14.6 0.0 collective-permute-done.inner_got
  14.6 0.7 %shard_map.62 = (f32[72,64]{1,0:T(8,128)S(1)}, f32[64,128]{1,0:T(8,128)S(1)}) custom-call(f32[1,4]{1,0:T(1,128)S(1)} %bitcast.2, f32[72,64]{1,0:T(8,128)S(1)} %get-tuple-element.20.partial, f32[7,64,128]{2,1,0:T(8,128)S(1)} %get-tuple-element.21.weights.refs_10_, bf16[2,64,64,128]{3,2,1,0:T(8,128)(2,1)S(1)} %get-tuple-element.22.here, ...), custom_call_target="tpu_custom_call" | custom-call | flops 100000000 | bytes 1048576 | tf_op jit(solution)/shard_map/pallas_call | solution.py:611
  15.3 0.0 collective-permute-done.2.one_got
  15.3 0.0 collective-permute-done.3.two_got
  15.3 0.0 collective-permute-done.1.outer_got
  15.3 0.8 %shard_map.63 = (f32[72,128]{1,0:T(8,128)S(1)}, f32[64,128]{1,0:T(8,128)S(1)}) custom-call(f32[1,4]{1,0:T(1,128)S(1)} %bitcast.3, f32[72,64]{1,0:T(8,128)S(1)} %get-tuple-element.24.partial, f32[7,64,128]{2,1,0:T(8,128)S(1)} %get-tuple-element.21.weights.refs_10_, bf16[2,64,64,128]{3,2,1,0:T(8,128)(2,1)S(1)} %get-tuple-element.22.here, ...), custom_call_target="tpu_custom_call" | custom-call | flops 100000000 | bytes 1048576 | tf_op jit(solution)/shard_map/pallas_call | solution.py:619
  16.1 0.1 collective-permute-start.4
  16.2 1.2 %collective-permute-done.4 = f32[72,128]{1,0:T(8,128)S(1)} collective-permute-done((f32[72,128]{1,0:T(8,128)S(1)}, f32[72,128]{1,0:T(8,128)S(1)}, u32[]{:S(2)}, u32[]{:S(2)}) %collective-permute-start.4) | collective-permute-done | bytes 36896 | tf_op jit(solution)/shard_map/ppermute | solution.py:537
  17.4 0.7 %collective-permute-start.5 = (f32[72,128]{1,0:T(8,128)S(1)}, f32[72,128]{1,0:T(8,128)S(1)}, u32[]{:S(2)}, u32[]{:S(2)}) collective-permute-start(f32[72,128]{1,0:T(8,128)S(1)} %add.3.own.after), channel_id=1, source_target_pairs={{0,3},{1,2},{2,1},{3,0},{4,7},{5,6},{6,5},{7,4},{8,11},{9,10},{10,... | collective-permute-start | bytes 110600 | tf_op jit(solution)/shard_map/ppermute | solution.py:545
  18.1 0.0 collective-permute-start.6
  18.1 2.3 %collective-permute-start.7 = (f32[72,128]{1,0:T(8,128)S(1)}, f32[72,128]{1,0:T(8,128)S(1)}, u32[]{:S(2)}, u32[]{:S(2)}) collective-permute-start(f32[72,128]{1,0:T(8,128)S(1)} %add.3.own.after), channel_id=1, source_target_pairs={{0,7},{1,6},{2,5},{3,4},{4,3},{5,2},{6,1},{7,0},{8,15},{9,14},{10,... | collective-permute-start | bytes 110600 | tf_op jit(solution)/shard_map/ppermute | solution.py:545
  20.4 0.3 collective-permute-start.11
  20.7 0.2 collective-permute-done.5.across
  20.8 0.7 %collective-permute-done.6.beside = f32[72,128]{1,0:T(8,128)S(1)} collective-permute-done((f32[72,128]{1,0:T(8,128)S(1)}, f32[72,128]{1,0:T(8,128)S(1)}, u32[]{:S(2)}, u32[]{:S(2)}) %collective-permute-start.6) | collective-permute-done | bytes 36896 | tf_op jit(solution)/shard_map/ppermute | solution.py:545
  21.5 0.9 %collective-permute-done.7.oblique = f32[72,128]{1,0:T(8,128)S(1)} collective-permute-done((f32[72,128]{1,0:T(8,128)S(1)}, f32[72,128]{1,0:T(8,128)S(1)}, u32[]{:S(2)}, u32[]{:S(2)}) %collective-permute-start.7) | collective-permute-done | bytes 36896 | tf_op jit(solution)/shard_map/ppermute | solution.py:545
  22.5 2.3 %collective-permute-start.8 = (bf16[2,80,128]{2,1,0:T(8,128)(2,1)S(1)}, bf16[2,80,128]{2,1,0:T(8,128)(2,1)S(1)}, u32[]{:S(2)}, u32[]{:S(2)}) collective-permute-start(bf16[2,80,128]{2,1,0:T(8,128)(2,1)S(1)} %shard_map.64.pair.refs_0_), channel_id=1, source_target_pairs={{0,17},{1,24},{2,19},{3,26},{4,21},{5,28},{6,23},{7,30},{8,25},{9,... | collective-permute-start | bytes 122888 | tf_op jit(solution)/shard_map/ppermute | solution.py:567
  24.8 0.3 %collective-permute-start.9 = (bf16[2,80,128]{2,1,0:T(8,128)(2,1)S(1)}, bf16[2,80,128]{2,1,0:T(8,128)(2,1)S(1)}, u32[]{:S(2)}, u32[]{:S(2)}) collective-permute-start(bf16[2,80,128]{2,1,0:T(8,128)(2,1)S(1)} %shard_map.64.pair.refs_0_), channel_id=1, source_target_pairs={{0,9},{1,8},{2,11},{3,10},{4,13},{5,12},{6,15},{7,14},{8,1},{9,0},... | collective-permute-start | bytes 122888 | tf_op jit(solution)/shard_map/ppermute | solution.py:545
  25.1 0.3 shard_map.67
  25.4 1.6 %collective-permute-done.8.refs_1_ = bf16[2,80,128]{2,1,0:T(8,128)(2,1)S(1)} collective-permute-done((bf16[2,80,128]{2,1,0:T(8,128)(2,1)S(1)}, bf16[2,80,128]{2,1,0:T(8,128)(2,1)S(1)}, u32[]{:S(2)}, u32[]{:S(2)}) %collective-permute-start.8) | collective-permute-done | bytes 40992 | tf_op jit(solution)/shard_map/ppermute | solution.py:567
  26.9 1.5 %collective-permute-start.10 = (bf16[2,80,128]{2,1,0:T(8,128)(2,1)S(1)}, bf16[2,80,128]{2,1,0:T(8,128)(2,1)S(1)}, u32[]{:S(2)}, u32[]{:S(2)}) collective-permute-start(bf16[2,80,128]{2,1,0:T(8,128)(2,1)S(1)} %collective-permute-done.8.refs_1_), channel_id=1, source_target_pairs={{0,1},{1,0},{2,3},{3,2},{4,5},{5,4},{6,7},{7,6},{8,9},{9,8},{10,11... | collective-permute-start | bytes 122888 | tf_op jit(solution)/shard_map/ppermute | solution.py:537
  28.4 0.5 %shard_map.65 = (f32[64,2,64,128]{3,2,1,0:T(8,128)S(1)}, f32[64,64,128]{2,1,0:T(8,128)S(1)}, f32[64,32,128]{2,1,0:T(8,128)S(1)}) custom-call(bf16[2,80,128]{2,1,0:T(8,128)(2,1)S(1)} %shard_map.64.pair.refs_0_, bf16[64,2,64,128]{3,2,1,0:T(8,128)(2,1)S(1)} %copy-done, bf16[65,64,128]{2,1,0:T(8,128)(2,1)S(1)} %collective-permute-done.inner_got, ...), custom_call_target="tpu_custom_call" | custom-call | flops 1073741824 | bytes 1048576 | tf_op jit(solution)/shard_map/pallas_call | solution.py:650
  28.9 0.0 collective-permute-done.9.refs_2_
  28.9 0.4 %collective-permute-done.10.refs_3_ = bf16[2,80,128]{2,1,0:T(8,128)(2,1)S(1)} collective-permute-done((bf16[2,80,128]{2,1,0:T(8,128)(2,1)S(1)}, bf16[2,80,128]{2,1,0:T(8,128)(2,1)S(1)}, u32[]{:S(2)}, u32[]{:S(2)}) %collective-permute-start.10) | collective-permute-done | bytes 40992 | tf_op jit(solution)/shard_map/ppermute | solution.py:537
  29.3 0.3 collective-permute-done.11.refs_7_
  29.5 2.7 %shard_map.68 = (f32[1,64]{1,0:T(1,128)}, f32[2,64,128]{2,1,0:T(8,128)}) custom-call(bf16[2,80,128]{2,1,0:T(8,128)(2,1)S(1)} %shard_map.64.pair.refs_0_, bf16[2,80,128]{2,1,0:T(8,128)(2,1)S(1)} %collective-permute-done.8.refs_1_, bf16[2,80,128]{2,1,0:T(8,128)(2,1)S(1)} %collective-permute-done.9.refs_2_, ...), custom_call_target="tpu_custom_call" | custom-call | flops 10000000 | bytes 5242880 | tf_op jit(solution)/shard_map/pallas_call | solution.py:662
  (11 shorter events, 0.1 us)
Async XLA Ops:
  0.6 4.8 %copy-start.1 = (s32[2,64,128]{2,1,0:T(8,128)S(1)}, s32[2,64,128]{2,1,0:T(8,128)}, u32[]{:S(2)}) copy-start(s32[2,64,128]{2,1,0:T(8,128)} %labels_far.1) | copy-start | bytes 196612
  0.6 4.7 %copy-start = (bf16[64,2,64,128]{3,2,1,0:T(8,128)(2,1)S(1)}, bf16[64,2,64,128]{3,2,1,0:T(8,128)(2,1)}, u32[]{:S(2)}) copy-start(bf16[64,2,64,128]{3,2,1,0:T(8,128)(2,1)} %zvec.5) | copy-start | bytes 6291460
  0.7 10.5 %copy-start.3 = (f32[4]{0:T(128)S(1)}, f32[4]{0:T(128)}, u32[]{:S(2)}) copy-start(f32[4]{0:T(128)} %param.5) | copy-start | bytes 52
  0.7 10.5 %copy-start.2 = (f32[2,64,128]{2,1,0:T(8,128)S(1)}, f32[2,64,128]{2,1,0:T(8,128)}, u32[]{:S(2)}) copy-start(f32[2,64,128]{2,1,0:T(8,128)} %refs_13_.1) | copy-start | bytes 196612
  2.3 12.3 %collective-permute-start = (bf16[65,64,128]{2,1,0:T(8,128)(2,1)S(1)}, bf16[65,64,128]{2,1,0:T(8,128)(2,1)S(1)}, u32[]{:S(2)}, u32[]{:S(2)}) collective-permute-start(bf16[65,64,128]{2,1,0:T(8,128)(2,1)S(1)} %get-tuple-element.23), channel_id=1, source_target_pairs={{0,1},{1,0},{2,3},{3,2},{4,5},{5,4},{6,7},{7,6},{8,9},{9,8},{10,11... | collective-permute-start | bytes 3194888 | tf_op jit(solution)/shard_map/ppermute | solution.py:520
  2.8 12.5 %collective-permute-start.1 = (bf16[66,32,128]{2,1,0:T(8,128)(2,1)S(1)}, bf16[66,32,128]{2,1,0:T(8,128)(2,1)S(1)}, u32[]{:S(2)}, u32[]{:S(2)}) collective-permute-start(bf16[66,32,128]{2,1,0:T(8,128)(2,1)S(1)} %get-tuple-element.25), channel_id=1, source_target_pairs={{0,4},{1,2},{2,1},{3,7},{4,0},{5,6},{6,5},{7,3},{8,12},{9,10},{10,... | collective-permute-start | bytes 1622024 | tf_op jit(solution)/shard_map/ppermute | solution.py:533
  6.1 9.2 %collective-permute-start.2 = (bf16[80,128]{1,0:T(8,128)(2,1)S(1)}, bf16[80,128]{1,0:T(8,128)(2,1)S(1)}, u32[]{:S(2)}, u32[]{:S(2)}) collective-permute-start(bf16[80,128]{1,0:T(8,128)(2,1)S(1)} %get-tuple-element.19.after.one_pack), channel_id=1, source_target_pairs={{0,4},{4,0},{8,12},{12,8},{16,20},{20,16},{24,28},{28,24},{1,5},{5... | collective-permute-start | bytes 61448 | tf_op jit(solution)/shard_map/ppermute | solution.py:520
  6.5 8.8 %collective-permute-start.3 = (bf16[80,128]{1,0:T(8,128)(2,1)S(1)}, bf16[80,128]{1,0:T(8,128)(2,1)S(1)}, u32[]{:S(2)}, u32[]{:S(2)}) collective-permute-start(bf16[80,128]{1,0:T(8,128)(2,1)S(1)} %get-tuple-element.26.two_pack), channel_id=1, source_target_pairs={{0,28},{4,8},{8,4},{12,16},{16,12},{20,24},{24,20},{28,0},{1,29},{... | collective-permute-start | bytes 61448 | tf_op jit(solution)/shard_map/ppermute | solution.py:520
  16.1 1.3 %collective-permute-start.4 = (f32[72,128]{1,0:T(8,128)S(1)}, f32[72,128]{1,0:T(8,128)S(1)}, u32[]{:S(2)}, u32[]{:S(2)}) collective-permute-start(f32[72,128]{1,0:T(8,128)S(1)} %get-tuple-element.27), channel_id=1, source_target_pairs={{0,1},{1,0},{2,3},{3,2},{4,5},{5,4},{6,7},{7,6},{8,9},{9,8},{10,11... | collective-permute-start | bytes 110600 | tf_op jit(solution)/shard_map/ppermute | solution.py:537
  17.4 3.4 %collective-permute-start.5 = (f32[72,128]{1,0:T(8,128)S(1)}, f32[72,128]{1,0:T(8,128)S(1)}, u32[]{:S(2)}, u32[]{:S(2)}) collective-permute-start(f32[72,128]{1,0:T(8,128)S(1)} %add.3.own.after), channel_id=1, source_target_pairs={{0,3},{1,2},{2,1},{3,0},{4,7},{5,6},{6,5},{7,4},{8,11},{9,10},{10,... | collective-permute-start | bytes 110600 | tf_op jit(solution)/shard_map/ppermute | solution.py:545
  18.1 3.4 %collective-permute-start.6 = (f32[72,128]{1,0:T(8,128)S(1)}, f32[72,128]{1,0:T(8,128)S(1)}, u32[]{:S(2)}, u32[]{:S(2)}) collective-permute-start(f32[72,128]{1,0:T(8,128)S(1)} %add.3.own.after), channel_id=1, source_target_pairs={{0,5},{1,4},{2,7},{3,6},{4,1},{5,0},{6,3},{7,2},{8,13},{9,12},{10,... | collective-permute-start | bytes 110600 | tf_op jit(solution)/shard_map/ppermute | solution.py:545
  18.1 4.3 %collective-permute-start.7 = (f32[72,128]{1,0:T(8,128)S(1)}, f32[72,128]{1,0:T(8,128)S(1)}, u32[]{:S(2)}, u32[]{:S(2)}) collective-permute-start(f32[72,128]{1,0:T(8,128)S(1)} %add.3.own.after), channel_id=1, source_target_pairs={{0,7},{1,6},{2,5},{3,4},{4,3},{5,2},{6,1},{7,0},{8,15},{9,14},{10,... | collective-permute-start | bytes 110600 | tf_op jit(solution)/shard_map/ppermute | solution.py:545
  20.4 9.2 %collective-permute-start.11 = (bf16[64,32,128]{2,1,0:T(8,128)(2,1)S(1)}, bf16[64,32,128]{2,1,0:T(8,128)(2,1)S(1)}, u32[]{:S(2)}, u32[]{:S(2)}) collective-permute-start(bf16[64,32,128]{2,1,0:T(8,128)(2,1)S(1)} %shard_map.66), channel_id=1, source_target_pairs={{0,4},{1,2},{2,1},{3,7},{4,0},{5,6},{6,5},{7,3},{8,12},{9,10},{10,... | collective-permute-start | bytes 1572872 | tf_op jit(solution)/shard_map/ppermute | solution.py:533
  22.5 4.5 %collective-permute-start.8 = (bf16[2,80,128]{2,1,0:T(8,128)(2,1)S(1)}, bf16[2,80,128]{2,1,0:T(8,128)(2,1)S(1)}, u32[]{:S(2)}, u32[]{:S(2)}) collective-permute-start(bf16[2,80,128]{2,1,0:T(8,128)(2,1)S(1)} %shard_map.64.pair.refs_0_), channel_id=1, source_target_pairs={{0,17},{1,24},{2,19},{3,26},{4,21},{5,28},{6,23},{7,30},{8,25},{9,... | collective-permute-start | bytes 122888 | tf_op jit(solution)/shard_map/ppermute | solution.py:567
  24.8 4.1 %collective-permute-start.9 = (bf16[2,80,128]{2,1,0:T(8,128)(2,1)S(1)}, bf16[2,80,128]{2,1,0:T(8,128)(2,1)S(1)}, u32[]{:S(2)}, u32[]{:S(2)}) collective-permute-start(bf16[2,80,128]{2,1,0:T(8,128)(2,1)S(1)} %shard_map.64.pair.refs_0_), channel_id=1, source_target_pairs={{0,9},{1,8},{2,11},{3,10},{4,13},{5,12},{6,15},{7,14},{8,1},{9,0},... | collective-permute-start | bytes 122888 | tf_op jit(solution)/shard_map/ppermute | solution.py:545
  26.9 2.3 %collective-permute-start.10 = (bf16[2,80,128]{2,1,0:T(8,128)(2,1)S(1)}, bf16[2,80,128]{2,1,0:T(8,128)(2,1)S(1)}, u32[]{:S(2)}, u32[]{:S(2)}) collective-permute-start(bf16[2,80,128]{2,1,0:T(8,128)(2,1)S(1)} %collective-permute-done.8.refs_1_), channel_id=1, source_target_pairs={{0,1},{1,0},{2,3},{3,2},{4,5},{5,4},{6,7},{7,6},{8,9},{9,8},{10,11... | collective-permute-start | bytes 122888 | tf_op jit(solution)/shard_map/ppermute | solution.py:537

commit v18 on v17

--- a/solution.py
+++ b/solution.py
@@ -165,7 +165,7 @@
                 image = (
                     half_diag[x, at, :] * wide[x]
                     - link_y[x, at, :] * up[x]
-                    - link_z[x, at, :] * pltpu.roll(wide[x], layers - 1, 1)
+                    - link_z[x, at, :] * pltpu.roll(here[x, y], layers - 1, 1).astype(F32)
                 )
                 if x == 0:
                     image = image - weights[0, at, :] * wide[1]

time: 32.4 us -> 32.4 us (level)
  no operation moved by 1% of the time
where the time goes in v18:
time: 32.4 us; the launch traced here: 32.2 us
  starting transfers between devices  15.5 us (48%)
  Pallas kernels  10.6 us (33%)
  waiting for transfers between devices  5.31 us (16%)
  between operations  0.77 us (2%)
    ppermute x3, starting transfers between devices, swapped(): return lax.ppermute(value, axis, pairs)  5.62 us
    pallas_call x1, Pallas kernels, body(): call(block_kernel, [shape((modes + 8, modes), F32), shape((7,) + plane, F...  3.41 us
    ppermute x4, starting transfers between devices, partner(): return lax.ppermute(value, ('sub', 'pln'), pairs)  3.31 us
    ppermute x2, starting transfers between devices, swapped_all(): return lax.ppermute(value, ('sub', 'pln'), pairs)  2.89 us
    pallas_call x1, Pallas kernels, body(): call(finish_kernel, [shape((1, modes), F32), shape(field, F32)], [VMEM] *...  2.71 us
    ppermute x1, starting transfers between devices, far_partner(): return lax.ppermute(value, ('sub', 'pln'), pairs)  2.31 us
    ppermute x4, waiting for transfers between devices, partner(): return lax.ppermute(value, ('sub', 'pln'), pairs)  1.75 us
    ppermute x1, waiting for transfers between devices, far_partner(): return lax.ppermute(value, ('sub', 'pln'), pairs)  1.66 us
  transfers between devices with their start and end apart: 12, of which 7 were waited for; matrix products, arithmetic and copies ran while one was open for 0% of the time, Pallas kernels for 17%

profile of v18, /device:TPU:0, one launch (start us, length us, event | category | flops | bytes accessed | tf_op | source)
XLA Modules:
  0.0 32.2 jit_solution(2942619879845394617)
XLA Ops:
  0.7 1.6 %shard_map.61 = (bf16[65,64,128]{2,1,0:T(8,128)(2,1)S(1)}, bf16[66,32,128]{2,1,0:T(8,128)(2,1)S(1)}) custom-call(s32[2,64,128]{2,1,0:T(8,128)} %labels_far.1, bf16[64,2,64,128]{3,2,1,0:T(8,128)(2,1)} %zvec.5), custom_call_target="tpu_custom_call" | custom-call | bytes 2097152 | tf_op jit(solution)/shard_map/pallas_call | solution.py:577
  2.3 0.5 %collective-permute-start = (bf16[65,64,128]{2,1,0:T(8,128)(2,1)S(1)}, bf16[65,64,128]{2,1,0:T(8,128)(2,1)S(1)}, u32[]{:S(2)}, u32[]{:S(2)}) collective-permute-start(bf16[65,64,128]{2,1,0:T(8,128)(2,1)S(1)} %get-tuple-element.23), channel_id=1, source_target_pairs={{0,1},{1,0},{2,3},{3,2},{4,5},{5,4},{6,7},{7,6},{8,9},{9,8},{10,11... | collective-permute-start | bytes 3194888 | tf_op jit(solution)/shard_map/ppermute | solution.py:520
  2.8 2.6 %collective-permute-start.1 = (bf16[66,32,128]{2,1,0:T(8,128)(2,1)S(1)}, bf16[66,32,128]{2,1,0:T(8,128)(2,1)S(1)}, u32[]{:S(2)}, u32[]{:S(2)}) collective-permute-start(bf16[66,32,128]{2,1,0:T(8,128)(2,1)S(1)} %get-tuple-element.25), channel_id=1, source_target_pairs={{0,4},{1,2},{2,1},{3,7},{4,0},{5,6},{6,5},{7,3},{8,12},{9,10},{10,... | collective-permute-start | bytes 1622024 | tf_op jit(solution)/shard_map/ppermute | solution.py:533
  5.4 0.7 %shard_map.59 = (bf16[64,32,128]{2,1,0:T(8,128)(2,1)S(1)}, bf16[80,128]{1,0:T(8,128)(2,1)S(1)}, bf16[80,128]{1,0:T(8,128)(2,1)S(1)}) custom-call(s32[2,64,128]{2,1,0:T(8,128)S(1)} %copy-done.1, bf16[64,2,64,128]{3,2,1,0:T(8,128)(2,1)S(1)} %copy-done), custom_call_target="tpu_custom_call" | custom-call | flops 10000000 | bytes 6291456 | tf_op jit(solution)/shard_map/pallas_call | solution.py:587
  6.1 0.4 %collective-permute-start.2 = (bf16[80,128]{1,0:T(8,128)(2,1)S(1)}, bf16[80,128]{1,0:T(8,128)(2,1)S(1)}, u32[]{:S(2)}, u32[]{:S(2)}) collective-permute-start(bf16[80,128]{1,0:T(8,128)(2,1)S(1)} %get-tuple-element.19.after.one_pack), channel_id=1, source_target_pairs={{0,4},{4,0},{8,12},{12,8},{16,20},{20,16},{24,28},{28,24},{1,5},{5... | collective-permute-start | bytes 61448 | tf_op jit(solution)/shard_map/ppermute | solution.py:520
  6.5 4.7 %collective-permute-start.3 = (bf16[80,128]{1,0:T(8,128)(2,1)S(1)}, bf16[80,128]{1,0:T(8,128)(2,1)S(1)}, u32[]{:S(2)}, u32[]{:S(2)}) collective-permute-start(bf16[80,128]{1,0:T(8,128)(2,1)S(1)} %get-tuple-element.26.two_pack), channel_id=1, source_target_pairs={{0,28},{4,8},{8,4},{12,16},{16,12},{20,24},{24,20},{28,0},{1,29},{... | collective-permute-start | bytes 61448 | tf_op jit(solution)/shard_map/ppermute | solution.py:520
  11.2 3.4 %shard_map.60 = (f32[72,64]{1,0:T(8,128)S(1)}, f32[7,64,128]{2,1,0:T(8,128)S(1)}, bf16[2,64,64,128]{3,2,1,0:T(8,128)(2,1)S(1)}) custom-call(f32[1,4]{1,0:T(1,128)S(1)} %bitcast.1, s32[2,64,128]{2,1,0:T(8,128)S(1)} %copy-done.1, f32[2,64,128]{2,1,0:T(8,128)S(1)} %copy-done.2, bf16[64,2,64,128]{3,2,1,0:T(8,128)(2,1)S(1)} %copy-done, ...), custom_call_target="tpu_custom_call" | custom-call | flops 400000000 | bytes 3145728 | tf_op jit(solution)/shard_map/pallas_call | solution.py:598
  14.6 0.0 collective-permute-done.inner_got
  14.6 0.7 %shard_map.62 = (f32[72,64]{1,0:T(8,128)S(1)}, f32[64,128]{1,0:T(8,128)S(1)}) custom-call(f32[1,4]{1,0:T(1,128)S(1)} %bitcast.2, f32[72,64]{1,0:T(8,128)S(1)} %get-tuple-element.20.partial, f32[7,64,128]{2,1,0:T(8,128)S(1)} %get-tuple-element.21.weights.refs_10_, bf16[2,64,64,128]{3,2,1,0:T(8,128)(2,1)S(1)} %get-tuple-element.22.here, ...), custom_call_target="tpu_custom_call" | custom-call | flops 100000000 | bytes 1048576 | tf_op jit(solution)/shard_map/pallas_call | solution.py:611
  15.3 0.0 collective-permute-done.2.one_got
  15.3 0.0 collective-permute-done.3.two_got
  15.3 0.0 collective-permute-done.1.outer_got
  15.3 0.8 %shard_map.63 = (f32[72,128]{1,0:T(8,128)S(1)}, f32[64,128]{1,0:T(8,128)S(1)}) custom-call(f32[1,4]{1,0:T(1,128)S(1)} %bitcast.3, f32[72,64]{1,0:T(8,128)S(1)} %get-tuple-element.24.partial, f32[7,64,128]{2,1,0:T(8,128)S(1)} %get-tuple-element.21.weights.refs_10_, bf16[2,64,64,128]{3,2,1,0:T(8,128)(2,1)S(1)} %get-tuple-element.22.here, ...), custom_call_target="tpu_custom_call" | custom-call | flops 100000000 | bytes 1048576 | tf_op jit(solution)/shard_map/pallas_call | solution.py:619
  16.1 0.1 collective-permute-start.4
  16.2 1.2 %collective-permute-done.4 = f32[72,128]{1,0:T(8,128)S(1)} collective-permute-done((f32[72,128]{1,0:T(8,128)S(1)}, f32[72,128]{1,0:T(8,128)S(1)}, u32[]{:S(2)}, u32[]{:S(2)}) %collective-permute-start.4) | collective-permute-done | bytes 36896 | tf_op jit(solution)/shard_map/ppermute | solution.py:537
  17.4 0.7 %collective-permute-start.5 = (f32[72,128]{1,0:T(8,128)S(1)}, f32[72,128]{1,0:T(8,128)S(1)}, u32[]{:S(2)}, u32[]{:S(2)}) collective-permute-start(f32[72,128]{1,0:T(8,128)S(1)} %add.3.own.after), channel_id=1, source_target_pairs={{0,3},{1,2},{2,1},{3,0},{4,7},{5,6},{6,5},{7,4},{8,11},{9,10},{10,... | collective-permute-start | bytes 110600 | tf_op jit(solution)/shard_map/ppermute | solution.py:545
  18.1 0.0 collective-permute-start.6
  18.1 2.3 %collective-permute-start.7 = (f32[72,128]{1,0:T(8,128)S(1)}, f32[72,128]{1,0:T(8,128)S(1)}, u32[]{:S(2)}, u32[]{:S(2)}) collective-permute-start(f32[72,128]{1,0:T(8,128)S(1)} %add.3.own.after), channel_id=1, source_target_pairs={{0,7},{1,6},{2,5},{3,4},{4,3},{5,2},{6,1},{7,0},{8,15},{9,14},{10,... | collective-permute-start | bytes 110600 | tf_op jit(solution)/shard_map/ppermute | solution.py:545
  20.4 0.3 collective-permute-start.11
  20.7 0.2 collective-permute-done.5.across
  20.8 0.7 %collective-permute-done.6.beside = f32[72,128]{1,0:T(8,128)S(1)} collective-permute-done((f32[72,128]{1,0:T(8,128)S(1)}, f32[72,128]{1,0:T(8,128)S(1)}, u32[]{:S(2)}, u32[]{:S(2)}) %collective-permute-start.6) | collective-permute-done | bytes 36896 | tf_op jit(solution)/shard_map/ppermute | solution.py:545
  21.5 0.9 %collective-permute-done.7.oblique = f32[72,128]{1,0:T(8,128)S(1)} collective-permute-done((f32[72,128]{1,0:T(8,128)S(1)}, f32[72,128]{1,0:T(8,128)S(1)}, u32[]{:S(2)}, u32[]{:S(2)}) %collective-permute-start.7) | collective-permute-done | bytes 36896 | tf_op jit(solution)/shard_map/ppermute | solution.py:545
  22.4 2.3 %collective-permute-start.8 = (bf16[2,80,128]{2,1,0:T(8,128)(2,1)S(1)}, bf16[2,80,128]{2,1,0:T(8,128)(2,1)S(1)}, u32[]{:S(2)}, u32[]{:S(2)}) collective-permute-start(bf16[2,80,128]{2,1,0:T(8,128)(2,1)S(1)} %shard_map.64.pair.refs_0_), channel_id=1, source_target_pairs={{0,17},{1,24},{2,19},{3,26},{4,21},{5,28},{6,23},{7,30},{8,25},{9,... | collective-permute-start | bytes 122888 | tf_op jit(solution)/shard_map/ppermute | solution.py:567
  24.8 0.3 %collective-permute-start.9 = (bf16[2,80,128]{2,1,0:T(8,128)(2,1)S(1)}, bf16[2,80,128]{2,1,0:T(8,128)(2,1)S(1)}, u32[]{:S(2)}, u32[]{:S(2)}) collective-permute-start(bf16[2,80,128]{2,1,0:T(8,128)(2,1)S(1)} %shard_map.64.pair.refs_0_), channel_id=1, source_target_pairs={{0,9},{1,8},{2,11},{3,10},{4,13},{5,12},{6,15},{7,14},{8,1},{9,0},... | collective-permute-start | bytes 122888 | tf_op jit(solution)/shard_map/ppermute | solution.py:545
  25.1 0.3 shard_map.67
  25.4 1.7 %collective-permute-done.8.refs_1_ = bf16[2,80,128]{2,1,0:T(8,128)(2,1)S(1)} collective-permute-done((bf16[2,80,128]{2,1,0:T(8,128)(2,1)S(1)}, bf16[2,80,128]{2,1,0:T(8,128)(2,1)S(1)}, u32[]{:S(2)}, u32[]{:S(2)}) %collective-permute-start.8) | collective-permute-done | bytes 40992 | tf_op jit(solution)/shard_map/ppermute | solution.py:567
  27.0 1.3 %collective-permute-start.10 = (bf16[2,80,128]{2,1,0:T(8,128)(2,1)S(1)}, bf16[2,80,128]{2,1,0:T(8,128)(2,1)S(1)}, u32[]{:S(2)}, u32[]{:S(2)}) collective-permute-start(bf16[2,80,128]{2,1,0:T(8,128)(2,1)S(1)} %collective-permute-done.8.refs_1_), channel_id=1, source_target_pairs={{0,1},{1,0},{2,3},{3,2},{4,5},{5,4},{6,7},{7,6},{8,9},{9,8},{10,11... | collective-permute-start | bytes 122888 | tf_op jit(solution)/shard_map/ppermute | solution.py:537
  28.3 0.5 %shard_map.65 = (f32[64,2,64,128]{3,2,1,0:T(8,128)S(1)}, f32[64,64,128]{2,1,0:T(8,128)S(1)}, f32[64,32,128]{2,1,0:T(8,128)S(1)}) custom-call(bf16[2,80,128]{2,1,0:T(8,128)(2,1)S(1)} %shard_map.64.pair.refs_0_, bf16[64,2,64,128]{3,2,1,0:T(8,128)(2,1)S(1)} %copy-done, bf16[65,64,128]{2,1,0:T(8,128)(2,1)S(1)} %collective-permute-done.inner_got, ...), custom_call_target="tpu_custom_call" | custom-call | flops 1073741824 | bytes 1048576 | tf_op jit(solution)/shard_map/pallas_call | solution.py:650
  28.8 0.0 collective-permute-done.9.refs_2_
  28.8 0.4 %collective-permute-done.10.refs_3_ = bf16[2,80,128]{2,1,0:T(8,128)(2,1)S(1)} collective-permute-done((bf16[2,80,128]{2,1,0:T(8,128)(2,1)S(1)}, bf16[2,80,128]{2,1,0:T(8,128)(2,1)S(1)}, u32[]{:S(2)}, u32[]{:S(2)}) %collective-permute-start.10) | collective-permute-done | bytes 40992 | tf_op jit(solution)/shard_map/ppermute | solution.py:537
  29.2 0.3 %collective-permute-done.11.refs_7_ = bf16[64,32,128]{2,1,0:T(8,128)(2,1)S(1)} collective-permute-done((bf16[64,32,128]{2,1,0:T(8,128)(2,1)S(1)}, bf16[64,32,128]{2,1,0:T(8,128)(2,1)S(1)}, u32[]{:S(2)}, u32[]{:S(2)}) %collective-permute-start.11) | collective-permute-done | bytes 524320 | tf_op jit(solution)/shard_map/ppermute | solution.py:533
  29.5 2.7 %shard_map.68 = (f32[1,64]{1,0:T(1,128)}, f32[2,64,128]{2,1,0:T(8,128)}) custom-call(bf16[2,80,128]{2,1,0:T(8,128)(2,1)S(1)} %shard_map.64.pair.refs_0_, bf16[2,80,128]{2,1,0:T(8,128)(2,1)S(1)} %collective-permute-done.8.refs_1_, bf16[2,80,128]{2,1,0:T(8,128)(2,1)S(1)} %collective-permute-done.9.refs_2_, ...), custom_call_target="tpu_custom_call" | custom-call | flops 10000000 | bytes 5242880 | tf_op jit(solution)/shard_map/pallas_call | solution.py:662
  (11 shorter events, 0.1 us)
Async XLA Ops:
  0.6 4.8 %copy-start.1 = (s32[2,64,128]{2,1,0:T(8,128)S(1)}, s32[2,64,128]{2,1,0:T(8,128)}, u32[]{:S(2)}) copy-start(s32[2,64,128]{2,1,0:T(8,128)} %labels_far.1) | copy-start | bytes 196612
  0.6 4.7 %copy-start = (bf16[64,2,64,128]{3,2,1,0:T(8,128)(2,1)S(1)}, bf16[64,2,64,128]{3,2,1,0:T(8,128)(2,1)}, u32[]{:S(2)}) copy-start(bf16[64,2,64,128]{3,2,1,0:T(8,128)(2,1)} %zvec.5) | copy-start | bytes 6291460
  0.7 10.5 %copy-start.3 = (f32[4]{0:T(128)S(1)}, f32[4]{0:T(128)}, u32[]{:S(2)}) copy-start(f32[4]{0:T(128)} %param.5) | copy-start | bytes 52
  0.7 10.5 %copy-start.2 = (f32[2,64,128]{2,1,0:T(8,128)S(1)}, f32[2,64,128]{2,1,0:T(8,128)}, u32[]{:S(2)}) copy-start(f32[2,64,128]{2,1,0:T(8,128)} %refs_13_.1) | copy-start | bytes 196612
  2.3 12.3 %collective-permute-start = (bf16[65,64,128]{2,1,0:T(8,128)(2,1)S(1)}, bf16[65,64,128]{2,1,0:T(8,128)(2,1)S(1)}, u32[]{:S(2)}, u32[]{:S(2)}) collective-permute-start(bf16[65,64,128]{2,1,0:T(8,128)(2,1)S(1)} %get-tuple-element.23), channel_id=1, source_target_pairs={{0,1},{1,0},{2,3},{3,2},{4,5},{5,4},{6,7},{7,6},{8,9},{9,8},{10,11... | collective-permute-start | bytes 3194888 | tf_op jit(solution)/shard_map/ppermute | solution.py:520
  2.8 12.5 %collective-permute-start.1 = (bf16[66,32,128]{2,1,0:T(8,128)(2,1)S(1)}, bf16[66,32,128]{2,1,0:T(8,128)(2,1)S(1)}, u32[]{:S(2)}, u32[]{:S(2)}) collective-permute-start(bf16[66,32,128]{2,1,0:T(8,128)(2,1)S(1)} %get-tuple-element.25), channel_id=1, source_target_pairs={{0,4},{1,2},{2,1},{3,7},{4,0},{5,6},{6,5},{7,3},{8,12},{9,10},{10,... | collective-permute-start | bytes 1622024 | tf_op jit(solution)/shard_map/ppermute | solution.py:533
  6.1 9.2 %collective-permute-start.2 = (bf16[80,128]{1,0:T(8,128)(2,1)S(1)}, bf16[80,128]{1,0:T(8,128)(2,1)S(1)}, u32[]{:S(2)}, u32[]{:S(2)}) collective-permute-start(bf16[80,128]{1,0:T(8,128)(2,1)S(1)} %get-tuple-element.19.after.one_pack), channel_id=1, source_target_pairs={{0,4},{4,0},{8,12},{12,8},{16,20},{20,16},{24,28},{28,24},{1,5},{5... | collective-permute-start | bytes 61448 | tf_op jit(solution)/shard_map/ppermute | solution.py:520
  6.5 8.8 %collective-permute-start.3 = (bf16[80,128]{1,0:T(8,128)(2,1)S(1)}, bf16[80,128]{1,0:T(8,128)(2,1)S(1)}, u32[]{:S(2)}, u32[]{:S(2)}) collective-permute-start(bf16[80,128]{1,0:T(8,128)(2,1)S(1)} %get-tuple-element.26.two_pack), channel_id=1, source_target_pairs={{0,28},{4,8},{8,4},{12,16},{16,12},{20,24},{24,20},{28,0},{1,29},{... | collective-permute-start | bytes 61448 | tf_op jit(solution)/shard_map/ppermute | solution.py:520
  16.1 1.3 %collective-permute-start.4 = (f32[72,128]{1,0:T(8,128)S(1)}, f32[72,128]{1,0:T(8,128)S(1)}, u32[]{:S(2)}, u32[]{:S(2)}) collective-permute-start(f32[72,128]{1,0:T(8,128)S(1)} %get-tuple-element.27), channel_id=1, source_target_pairs={{0,1},{1,0},{2,3},{3,2},{4,5},{5,4},{6,7},{7,6},{8,9},{9,8},{10,11... | collective-permute-start | bytes 110600 | tf_op jit(solution)/shard_map/ppermute | solution.py:537
  17.4 3.4 %collective-permute-start.5 = (f32[72,128]{1,0:T(8,128)S(1)}, f32[72,128]{1,0:T(8,128)S(1)}, u32[]{:S(2)}, u32[]{:S(2)}) collective-permute-start(f32[72,128]{1,0:T(8,128)S(1)} %add.3.own.after), channel_id=1, source_target_pairs={{0,3},{1,2},{2,1},{3,0},{4,7},{5,6},{6,5},{7,4},{8,11},{9,10},{10,... | collective-permute-start | bytes 110600 | tf_op jit(solution)/shard_map/ppermute | solution.py:545
  18.1 3.4 %collective-permute-start.6 = (f32[72,128]{1,0:T(8,128)S(1)}, f32[72,128]{1,0:T(8,128)S(1)}, u32[]{:S(2)}, u32[]{:S(2)}) collective-permute-start(f32[72,128]{1,0:T(8,128)S(1)} %add.3.own.after), channel_id=1, source_target_pairs={{0,5},{1,4},{2,7},{3,6},{4,1},{5,0},{6,3},{7,2},{8,13},{9,12},{10,... | collective-permute-start | bytes 110600 | tf_op jit(solution)/shard_map/ppermute | solution.py:545
  18.1 4.3 %collective-permute-start.7 = (f32[72,128]{1,0:T(8,128)S(1)}, f32[72,128]{1,0:T(8,128)S(1)}, u32[]{:S(2)}, u32[]{:S(2)}) collective-permute-start(f32[72,128]{1,0:T(8,128)S(1)} %add.3.own.after), channel_id=1, source_target_pairs={{0,7},{1,6},{2,5},{3,4},{4,3},{5,2},{6,1},{7,0},{8,15},{9,14},{10,... | collective-permute-start | bytes 110600 | tf_op jit(solution)/shard_map/ppermute | solution.py:545
  20.4 9.2 %collective-permute-start.11 = (bf16[64,32,128]{2,1,0:T(8,128)(2,1)S(1)}, bf16[64,32,128]{2,1,0:T(8,128)(2,1)S(1)}, u32[]{:S(2)}, u32[]{:S(2)}) collective-permute-start(bf16[64,32,128]{2,1,0:T(8,128)(2,1)S(1)} %shard_map.66), channel_id=1, source_target_pairs={{0,4},{1,2},{2,1},{3,7},{4,0},{5,6},{6,5},{7,3},{8,12},{9,10},{10,... | collective-permute-start | bytes 1572872 | tf_op jit(solution)/shard_map/ppermute | solution.py:533
  22.4 4.6 %collective-permute-start.8 = (bf16[2,80,128]{2,1,0:T(8,128)(2,1)S(1)}, bf16[2,80,128]{2,1,0:T(8,128)(2,1)S(1)}, u32[]{:S(2)}, u32[]{:S(2)}) collective-permute-start(bf16[2,80,128]{2,1,0:T(8,128)(2,1)S(1)} %shard_map.64.pair.refs_0_), channel_id=1, source_target_pairs={{0,17},{1,24},{2,19},{3,26},{4,21},{5,28},{6,23},{7,30},{8,25},{9,... | collective-permute-start | bytes 122888 | tf_op jit(solution)/shard_map/ppermute | solution.py:567
  24.8 4.1 %collective-permute-start.9 = (bf16[2,80,128]{2,1,0:T(8,128)(2,1)S(1)}, bf16[2,80,128]{2,1,0:T(8,128)(2,1)S(1)}, u32[]{:S(2)}, u32[]{:S(2)}) collective-permute-start(bf16[2,80,128]{2,1,0:T(8,128)(2,1)S(1)} %shard_map.64.pair.refs_0_), channel_id=1, source_target_pairs={{0,9},{1,8},{2,11},{3,10},{4,13},{5,12},{6,15},{7,14},{8,1},{9,0},... | collective-permute-start | bytes 122888 | tf_op jit(solution)/shard_map/ppermute | solution.py:545
  27.0 2.2 %collective-permute-start.10 = (bf16[2,80,128]{2,1,0:T(8,128)(2,1)S(1)}, bf16[2,80,128]{2,1,0:T(8,128)(2,1)S(1)}, u32[]{:S(2)}, u32[]{:S(2)}) collective-permute-start(bf16[2,80,128]{2,1,0:T(8,128)(2,1)S(1)} %collective-permute-done.8.refs_1_), channel_id=1, source_target_pairs={{0,1},{1,0},{2,3},{3,2},{4,5},{5,4},{6,7},{7,6},{8,9},{9,8},{10,11... | collective-permute-start | bytes 122888 | tf_op jit(solution)/shard_map/ppermute | solution.py:537

commit v19 on v18

--- a/solution.py
+++ b/solution.py
@@ -8,6 +8,7 @@
 CITERS = 2
 STEP = 32
 MODES = 16
+GROUP = 4
 CHUNK = 16
 F32 = jnp.float32
 BF16 = jnp.bfloat16
@@ -155,6 +156,7 @@
     def step(j, carry):
         total, wide = carry
         turn_rows(pl.multiple_of(jnp.minimum((j + 1) * STEP, rows - STEP), STEP))
+        left, right = [], []
         for u in range(STEP):
             y = j * STEP + u
             at = pl.ds(y, 1)
@@ -174,14 +176,18 @@
                 high = value.astype(BF16).astype(F32)
                 part = jnp.where(part_row == 0, high, jnp.where(part_row == 1, value - high, 0.0))
                 parts.append(part.astype(BF16))
-            total = total + lax.dot_general(
+            left.append(
                 jnp.concatenate(
                     [jnp.concatenate(images, axis=1), jnp.concatenate(parts, axis=1)], axis=0
-                ),
-                jnp.concatenate([here[0, y], here[1, y]], axis=1),
-                NT,
-                preferred_element_type=F32,
+                )
             )
+            right.append(jnp.concatenate([here[0, y], here[1, y]], axis=1))
+            if len(left) == GROUP:
+                total = total + lax.dot_general(
+                    jnp.concatenate(left, axis=1), jnp.concatenate(right, axis=1), NT,
+                    preferred_element_type=F32,
+                )
+                left, right = [], []
             wide = up
         return total, wide
 

time: 32.4 us -> 32.4 us (level)
  no operation moved by 1% of the time
where the time goes in v19:
time: 32.4 us; the launch traced here: 32.2 us
  starting transfers between devices  15.5 us (48%)
  Pallas kernels  10.6 us (33%)
  waiting for transfers between devices  5.31 us (16%)
  between operations  0.77 us (2%)
    ppermute x3, starting transfers between devices, swapped(): return lax.ppermute(value, axis, pairs)  5.62 us
    pallas_call x1, Pallas kernels, body(): call(block_kernel, [shape((modes + 8, modes), F32), shape((7,) + plane, F...  3.41 us
    ppermute x4, starting transfers between devices, partner(): return lax.ppermute(value, ('sub', 'pln'), pairs)  3.31 us
    ppermute x2, starting transfers between devices, swapped_all(): return lax.ppermute(value, ('sub', 'pln'), pairs)  2.89 us
    pallas_call x1, Pallas kernels, body(): call(finish_kernel, [shape((1, modes), F32), shape(field, F32)], [VMEM] *...  2.71 us
    ppermute x1, starting transfers between devices, far_partner(): return lax.ppermute(value, ('sub', 'pln'), pairs)  2.31 us
    ppermute x4, waiting for transfers between devices, partner(): return lax.ppermute(value, ('sub', 'pln'), pairs)  1.75 us
    ppermute x1, waiting for transfers between devices, far_partner(): return lax.ppermute(value, ('sub', 'pln'), pairs)  1.66 us
  transfers between devices with their start and end apart: 12, of which 7 were waited for; matrix products, arithmetic and copies ran while one was open for 0% of the time, Pallas kernels for 17%

profile of v19, /device:TPU:0, one launch (start us, length us, event | category | flops | bytes accessed | tf_op | source)
XLA Modules:
  0.0 32.2 jit_solution(2942619879845394617)
XLA Ops:
  0.7 1.6 %shard_map.61 = (bf16[65,64,128]{2,1,0:T(8,128)(2,1)S(1)}, bf16[66,32,128]{2,1,0:T(8,128)(2,1)S(1)}) custom-call(s32[2,64,128]{2,1,0:T(8,128)} %labels_far.1, bf16[64,2,64,128]{3,2,1,0:T(8,128)(2,1)} %zvec.5), custom_call_target="tpu_custom_call" | custom-call | bytes 2097152 | tf_op jit(solution)/shard_map/pallas_call | solution.py:583
  2.3 0.5 %collective-permute-start = (bf16[65,64,128]{2,1,0:T(8,128)(2,1)S(1)}, bf16[65,64,128]{2,1,0:T(8,128)(2,1)S(1)}, u32[]{:S(2)}, u32[]{:S(2)}) collective-permute-start(bf16[65,64,128]{2,1,0:T(8,128)(2,1)S(1)} %get-tuple-element.23), channel_id=1, source_target_pairs={{0,1},{1,0},{2,3},{3,2},{4,5},{5,4},{6,7},{7,6},{8,9},{9,8},{10,11... | collective-permute-start | bytes 3194888 | tf_op jit(solution)/shard_map/ppermute | solution.py:526
  2.8 2.6 %collective-permute-start.1 = (bf16[66,32,128]{2,1,0:T(8,128)(2,1)S(1)}, bf16[66,32,128]{2,1,0:T(8,128)(2,1)S(1)}, u32[]{:S(2)}, u32[]{:S(2)}) collective-permute-start(bf16[66,32,128]{2,1,0:T(8,128)(2,1)S(1)} %get-tuple-element.25), channel_id=1, source_target_pairs={{0,4},{1,2},{2,1},{3,7},{4,0},{5,6},{6,5},{7,3},{8,12},{9,10},{10,... | collective-permute-start | bytes 1622024 | tf_op jit(solution)/shard_map/ppermute | solution.py:539
  5.4 0.7 %shard_map.59 = (bf16[64,32,128]{2,1,0:T(8,128)(2,1)S(1)}, bf16[80,128]{1,0:T(8,128)(2,1)S(1)}, bf16[80,128]{1,0:T(8,128)(2,1)S(1)}) custom-call(s32[2,64,128]{2,1,0:T(8,128)S(1)} %copy-done.1, bf16[64,2,64,128]{3,2,1,0:T(8,128)(2,1)S(1)} %copy-done), custom_call_target="tpu_custom_call" | custom-call | flops 10000000 | bytes 6291456 | tf_op jit(solution)/shard_map/pallas_call | solution.py:593
  6.1 0.4 %collective-permute-start.2 = (bf16[80,128]{1,0:T(8,128)(2,1)S(1)}, bf16[80,128]{1,0:T(8,128)(2,1)S(1)}, u32[]{:S(2)}, u32[]{:S(2)}) collective-permute-start(bf16[80,128]{1,0:T(8,128)(2,1)S(1)} %get-tuple-element.19.after.one_pack), channel_id=1, source_target_pairs={{0,4},{4,0},{8,12},{12,8},{16,20},{20,16},{24,28},{28,24},{1,5},{5... | collective-permute-start | bytes 61448 | tf_op jit(solution)/shard_map/ppermute | solution.py:526
  6.5 4.7 %collective-permute-start.3 = (bf16[80,128]{1,0:T(8,128)(2,1)S(1)}, bf16[80,128]{1,0:T(8,128)(2,1)S(1)}, u32[]{:S(2)}, u32[]{:S(2)}) collective-permute-start(bf16[80,128]{1,0:T(8,128)(2,1)S(1)} %get-tuple-element.26.two_pack), channel_id=1, source_target_pairs={{0,28},{4,8},{8,4},{12,16},{16,12},{20,24},{24,20},{28,0},{1,29},{... | collective-permute-start | bytes 61448 | tf_op jit(solution)/shard_map/ppermute | solution.py:526
  11.2 3.4 %shard_map.60 = (f32[72,64]{1,0:T(8,128)S(1)}, f32[7,64,128]{2,1,0:T(8,128)S(1)}, bf16[2,64,64,128]{3,2,1,0:T(8,128)(2,1)S(1)}) custom-call(f32[1,4]{1,0:T(1,128)S(1)} %bitcast.1, s32[2,64,128]{2,1,0:T(8,128)S(1)} %copy-done.1, f32[2,64,128]{2,1,0:T(8,128)S(1)} %copy-done.2, bf16[64,2,64,128]{3,2,1,0:T(8,128)(2,1)S(1)} %copy-done, ...), custom_call_target="tpu_custom_call" | custom-call | flops 400000000 | bytes 3145728 | tf_op jit(solution)/shard_map/pallas_call | solution.py:604
  14.6 0.0 collective-permute-done.inner_got
  14.6 0.7 %shard_map.62 = (f32[72,64]{1,0:T(8,128)S(1)}, f32[64,128]{1,0:T(8,128)S(1)}) custom-call(f32[1,4]{1,0:T(1,128)S(1)} %bitcast.2, f32[72,64]{1,0:T(8,128)S(1)} %get-tuple-element.20.partial, f32[7,64,128]{2,1,0:T(8,128)S(1)} %get-tuple-element.21.weights.refs_10_, bf16[2,64,64,128]{3,2,1,0:T(8,128)(2,1)S(1)} %get-tuple-element.22.here, ...), custom_call_target="tpu_custom_call" | custom-call | flops 100000000 | bytes 1048576 | tf_op jit(solution)/shard_map/pallas_call | solution.py:617
  15.3 0.0 collective-permute-done.2.one_got
  15.3 0.0 collective-permute-done.3.two_got
  15.3 0.0 collective-permute-done.1.outer_got
  15.3 0.8 %shard_map.63 = (f32[72,128]{1,0:T(8,128)S(1)}, f32[64,128]{1,0:T(8,128)S(1)}) custom-call(f32[1,4]{1,0:T(1,128)S(1)} %bitcast.3, f32[72,64]{1,0:T(8,128)S(1)} %get-tuple-element.24.partial, f32[7,64,128]{2,1,0:T(8,128)S(1)} %get-tuple-element.21.weights.refs_10_, bf16[2,64,64,128]{3,2,1,0:T(8,128)(2,1)S(1)} %get-tuple-element.22.here, ...), custom_call_target="tpu_custom_call" | custom-call | flops 100000000 | bytes 1048576 | tf_op jit(solution)/shard_map/pallas_call | solution.py:625
  16.1 0.1 collective-permute-start.4
  16.2 1.2 %collective-permute-done.4 = f32[72,128]{1,0:T(8,128)S(1)} collective-permute-done((f32[72,128]{1,0:T(8,128)S(1)}, f32[72,128]{1,0:T(8,128)S(1)}, u32[]{:S(2)}, u32[]{:S(2)}) %collective-permute-start.4) | collective-permute-done | bytes 36896 | tf_op jit(solution)/shard_map/ppermute | solution.py:543
  17.4 0.7 %collective-permute-start.5 = (f32[72,128]{1,0:T(8,128)S(1)}, f32[72,128]{1,0:T(8,128)S(1)}, u32[]{:S(2)}, u32[]{:S(2)}) collective-permute-start(f32[72,128]{1,0:T(8,128)S(1)} %add.3.own.after), channel_id=1, source_target_pairs={{0,3},{1,2},{2,1},{3,0},{4,7},{5,6},{6,5},{7,4},{8,11},{9,10},{10,... | collective-permute-start | bytes 110600 | tf_op jit(solution)/shard_map/ppermute | solution.py:551
  18.1 0.0 collective-permute-start.6
  18.1 2.3 %collective-permute-start.7 = (f32[72,128]{1,0:T(8,128)S(1)}, f32[72,128]{1,0:T(8,128)S(1)}, u32[]{:S(2)}, u32[]{:S(2)}) collective-permute-start(f32[72,128]{1,0:T(8,128)S(1)} %add.3.own.after), channel_id=1, source_target_pairs={{0,7},{1,6},{2,5},{3,4},{4,3},{5,2},{6,1},{7,0},{8,15},{9,14},{10,... | collective-permute-start | bytes 110600 | tf_op jit(solution)/shard_map/ppermute | solution.py:551
  20.4 0.3 collective-permute-start.11
  20.7 0.2 collective-permute-done.5.across
  20.8 0.7 %collective-permute-done.6.beside = f32[72,128]{1,0:T(8,128)S(1)} collective-permute-done((f32[72,128]{1,0:T(8,128)S(1)}, f32[72,128]{1,0:T(8,128)S(1)}, u32[]{:S(2)}, u32[]{:S(2)}) %collective-permute-start.6) | collective-permute-done | bytes 36896 | tf_op jit(solution)/shard_map/ppermute | solution.py:551
  21.5 0.9 %collective-permute-done.7.oblique = f32[72,128]{1,0:T(8,128)S(1)} collective-permute-done((f32[72,128]{1,0:T(8,128)S(1)}, f32[72,128]{1,0:T(8,128)S(1)}, u32[]{:S(2)}, u32[]{:S(2)}) %collective-permute-start.7) | collective-permute-done | bytes 36896 | tf_op jit(solution)/shard_map/ppermute | solution.py:551
  22.4 2.3 %collective-permute-start.8 = (bf16[2,80,128]{2,1,0:T(8,128)(2,1)S(1)}, bf16[2,80,128]{2,1,0:T(8,128)(2,1)S(1)}, u32[]{:S(2)}, u32[]{:S(2)}) collective-permute-start(bf16[2,80,128]{2,1,0:T(8,128)(2,1)S(1)} %shard_map.64.pair.refs_0_), channel_id=1, source_target_pairs={{0,17},{1,24},{2,19},{3,26},{4,21},{5,28},{6,23},{7,30},{8,25},{9,... | collective-permute-start | bytes 122888 | tf_op jit(solution)/shard_map/ppermute | solution.py:573
  24.8 0.3 %collective-permute-start.9 = (bf16[2,80,128]{2,1,0:T(8,128)(2,1)S(1)}, bf16[2,80,128]{2,1,0:T(8,128)(2,1)S(1)}, u32[]{:S(2)}, u32[]{:S(2)}) collective-permute-start(bf16[2,80,128]{2,1,0:T(8,128)(2,1)S(1)} %shard_map.64.pair.refs_0_), channel_id=1, source_target_pairs={{0,9},{1,8},{2,11},{3,10},{4,13},{5,12},{6,15},{7,14},{8,1},{9,0},... | collective-permute-start | bytes 122888 | tf_op jit(solution)/shard_map/ppermute | solution.py:551
  25.1 0.3 shard_map.67
  25.4 1.7 %collective-permute-done.8.refs_1_ = bf16[2,80,128]{2,1,0:T(8,128)(2,1)S(1)} collective-permute-done((bf16[2,80,128]{2,1,0:T(8,128)(2,1)S(1)}, bf16[2,80,128]{2,1,0:T(8,128)(2,1)S(1)}, u32[]{:S(2)}, u32[]{:S(2)}) %collective-permute-start.8) | collective-permute-done | bytes 40992 | tf_op jit(solution)/shard_map/ppermute | solution.py:573
  27.0 1.3 %collective-permute-start.10 = (bf16[2,80,128]{2,1,0:T(8,128)(2,1)S(1)}, bf16[2,80,128]{2,1,0:T(8,128)(2,1)S(1)}, u32[]{:S(2)}, u32[]{:S(2)}) collective-permute-start(bf16[2,80,128]{2,1,0:T(8,128)(2,1)S(1)} %collective-permute-done.8.refs_1_), channel_id=1, source_target_pairs={{0,1},{1,0},{2,3},{3,2},{4,5},{5,4},{6,7},{7,6},{8,9},{9,8},{10,11... | collective-permute-start | bytes 122888 | tf_op jit(solution)/shard_map/ppermute | solution.py:543
  28.3 0.5 %shard_map.65 = (f32[64,2,64,128]{3,2,1,0:T(8,128)S(1)}, f32[64,64,128]{2,1,0:T(8,128)S(1)}, f32[64,32,128]{2,1,0:T(8,128)S(1)}) custom-call(bf16[2,80,128]{2,1,0:T(8,128)(2,1)S(1)} %shard_map.64.pair.refs_0_, bf16[64,2,64,128]{3,2,1,0:T(8,128)(2,1)S(1)} %copy-done, bf16[65,64,128]{2,1,0:T(8,128)(2,1)S(1)} %collective-permute-done.inner_got, ...), custom_call_target="tpu_custom_call" | custom-call | flops 1073741824 | bytes 1048576 | tf_op jit(solution)/shard_map/pallas_call | solution.py:656
  28.8 0.0 collective-permute-done.9.refs_2_
  28.8 0.4 %collective-permute-done.10.refs_3_ = bf16[2,80,128]{2,1,0:T(8,128)(2,1)S(1)} collective-permute-done((bf16[2,80,128]{2,1,0:T(8,128)(2,1)S(1)}, bf16[2,80,128]{2,1,0:T(8,128)(2,1)S(1)}, u32[]{:S(2)}, u32[]{:S(2)}) %collective-permute-start.10) | collective-permute-done | bytes 40992 | tf_op jit(solution)/shard_map/ppermute | solution.py:543
  29.2 0.3 %collective-permute-done.11.refs_7_ = bf16[64,32,128]{2,1,0:T(8,128)(2,1)S(1)} collective-permute-done((bf16[64,32,128]{2,1,0:T(8,128)(2,1)S(1)}, bf16[64,32,128]{2,1,0:T(8,128)(2,1)S(1)}, u32[]{:S(2)}, u32[]{:S(2)}) %collective-permute-start.11) | collective-permute-done | bytes 524320 | tf_op jit(solution)/shard_map/ppermute | solution.py:539
  29.5 2.7 %shard_map.68 = (f32[1,64]{1,0:T(1,128)}, f32[2,64,128]{2,1,0:T(8,128)}) custom-call(bf16[2,80,128]{2,1,0:T(8,128)(2,1)S(1)} %shard_map.64.pair.refs_0_, bf16[2,80,128]{2,1,0:T(8,128)(2,1)S(1)} %collective-permute-done.8.refs_1_, bf16[2,80,128]{2,1,0:T(8,128)(2,1)S(1)} %collective-permute-done.9.refs_2_, ...), custom_call_target="tpu_custom_call" | custom-call | flops 10000000 | bytes 5242880 | tf_op jit(solution)/shard_map/pallas_call | solution.py:668
  (11 shorter events, 0.1 us)
Async XLA Ops:
  0.6 4.8 %copy-start.1 = (s32[2,64,128]{2,1,0:T(8,128)S(1)}, s32[2,64,128]{2,1,0:T(8,128)}, u32[]{:S(2)}) copy-start(s32[2,64,128]{2,1,0:T(8,128)} %labels_far.1) | copy-start | bytes 196612
  0.6 4.7 %copy-start = (bf16[64,2,64,128]{3,2,1,0:T(8,128)(2,1)S(1)}, bf16[64,2,64,128]{3,2,1,0:T(8,128)(2,1)}, u32[]{:S(2)}) copy-start(bf16[64,2,64,128]{3,2,1,0:T(8,128)(2,1)} %zvec.5) | copy-start | bytes 6291460
  0.7 10.5 %copy-start.3 = (f32[4]{0:T(128)S(1)}, f32[4]{0:T(128)}, u32[]{:S(2)}) copy-start(f32[4]{0:T(128)} %param.5) | copy-start | bytes 52
  0.7 10.5 %copy-start.2 = (f32[2,64,128]{2,1,0:T(8,128)S(1)}, f32[2,64,128]{2,1,0:T(8,128)}, u32[]{:S(2)}) copy-start(f32[2,64,128]{2,1,0:T(8,128)} %refs_13_.1) | copy-start | bytes 196612
  2.3 12.3 %collective-permute-start = (bf16[65,64,128]{2,1,0:T(8,128)(2,1)S(1)}, bf16[65,64,128]{2,1,0:T(8,128)(2,1)S(1)}, u32[]{:S(2)}, u32[]{:S(2)}) collective-permute-start(bf16[65,64,128]{2,1,0:T(8,128)(2,1)S(1)} %get-tuple-element.23), channel_id=1, source_target_pairs={{0,1},{1,0},{2,3},{3,2},{4,5},{5,4},{6,7},{7,6},{8,9},{9,8},{10,11... | collective-permute-start | bytes 3194888 | tf_op jit(solution)/shard_map/ppermute | solution.py:526
  2.8 12.5 %collective-permute-start.1 = (bf16[66,32,128]{2,1,0:T(8,128)(2,1)S(1)}, bf16[66,32,128]{2,1,0:T(8,128)(2,1)S(1)}, u32[]{:S(2)}, u32[]{:S(2)}) collective-permute-start(bf16[66,32,128]{2,1,0:T(8,128)(2,1)S(1)} %get-tuple-element.25), channel_id=1, source_target_pairs={{0,4},{1,2},{2,1},{3,7},{4,0},{5,6},{6,5},{7,3},{8,12},{9,10},{10,... | collective-permute-start | bytes 1622024 | tf_op jit(solution)/shard_map/ppermute | solution.py:539
  6.1 9.2 %collective-permute-start.2 = (bf16[80,128]{1,0:T(8,128)(2,1)S(1)}, bf16[80,128]{1,0:T(8,128)(2,1)S(1)}, u32[]{:S(2)}, u32[]{:S(2)}) collective-permute-start(bf16[80,128]{1,0:T(8,128)(2,1)S(1)} %get-tuple-element.19.after.one_pack), channel_id=1, source_target_pairs={{0,4},{4,0},{8,12},{12,8},{16,20},{20,16},{24,28},{28,24},{1,5},{5... | collective-permute-start | bytes 61448 | tf_op jit(solution)/shard_map/ppermute | solution.py:526
  6.5 8.8 %collective-permute-start.3 = (bf16[80,128]{1,0:T(8,128)(2,1)S(1)}, bf16[80,128]{1,0:T(8,128)(2,1)S(1)}, u32[]{:S(2)}, u32[]{:S(2)}) collective-permute-start(bf16[80,128]{1,0:T(8,128)(2,1)S(1)} %get-tuple-element.26.two_pack), channel_id=1, source_target_pairs={{0,28},{4,8},{8,4},{12,16},{16,12},{20,24},{24,20},{28,0},{1,29},{... | collective-permute-start | bytes 61448 | tf_op jit(solution)/shard_map/ppermute | solution.py:526
  16.1 1.3 %collective-permute-start.4 = (f32[72,128]{1,0:T(8,128)S(1)}, f32[72,128]{1,0:T(8,128)S(1)}, u32[]{:S(2)}, u32[]{:S(2)}) collective-permute-start(f32[72,128]{1,0:T(8,128)S(1)} %get-tuple-element.27), channel_id=1, source_target_pairs={{0,1},{1,0},{2,3},{3,2},{4,5},{5,4},{6,7},{7,6},{8,9},{9,8},{10,11... | collective-permute-start | bytes 110600 | tf_op jit(solution)/shard_map/ppermute | solution.py:543
  17.4 3.4 %collective-permute-start.5 = (f32[72,128]{1,0:T(8,128)S(1)}, f32[72,128]{1,0:T(8,128)S(1)}, u32[]{:S(2)}, u32[]{:S(2)}) collective-permute-start(f32[72,128]{1,0:T(8,128)S(1)} %add.3.own.after), channel_id=1, source_target_pairs={{0,3},{1,2},{2,1},{3,0},{4,7},{5,6},{6,5},{7,4},{8,11},{9,10},{10,... | collective-permute-start | bytes 110600 | tf_op jit(solution)/shard_map/ppermute | solution.py:551
  18.1 3.4 %collective-permute-start.6 = (f32[72,128]{1,0:T(8,128)S(1)}, f32[72,128]{1,0:T(8,128)S(1)}, u32[]{:S(2)}, u32[]{:S(2)}) collective-permute-start(f32[72,128]{1,0:T(8,128)S(1)} %add.3.own.after), channel_id=1, source_target_pairs={{0,5},{1,4},{2,7},{3,6},{4,1},{5,0},{6,3},{7,2},{8,13},{9,12},{10,... | collective-permute-start | bytes 110600 | tf_op jit(solution)/shard_map/ppermute | solution.py:551
  18.1 4.3 %collective-permute-start.7 = (f32[72,128]{1,0:T(8,128)S(1)}, f32[72,128]{1,0:T(8,128)S(1)}, u32[]{:S(2)}, u32[]{:S(2)}) collective-permute-start(f32[72,128]{1,0:T(8,128)S(1)} %add.3.own.after), channel_id=1, source_target_pairs={{0,7},{1,6},{2,5},{3,4},{4,3},{5,2},{6,1},{7,0},{8,15},{9,14},{10,... | collective-permute-start | bytes 110600 | tf_op jit(solution)/shard_map/ppermute | solution.py:551
  20.4 9.2 %collective-permute-start.11 = (bf16[64,32,128]{2,1,0:T(8,128)(2,1)S(1)}, bf16[64,32,128]{2,1,0:T(8,128)(2,1)S(1)}, u32[]{:S(2)}, u32[]{:S(2)}) collective-permute-start(bf16[64,32,128]{2,1,0:T(8,128)(2,1)S(1)} %shard_map.66), channel_id=1, source_target_pairs={{0,4},{1,2},{2,1},{3,7},{4,0},{5,6},{6,5},{7,3},{8,12},{9,10},{10,... | collective-permute-start | bytes 1572872 | tf_op jit(solution)/shard_map/ppermute | solution.py:539
  22.4 4.6 %collective-permute-start.8 = (bf16[2,80,128]{2,1,0:T(8,128)(2,1)S(1)}, bf16[2,80,128]{2,1,0:T(8,128)(2,1)S(1)}, u32[]{:S(2)}, u32[]{:S(2)}) collective-permute-start(bf16[2,80,128]{2,1,0:T(8,128)(2,1)S(1)} %shard_map.64.pair.refs_0_), channel_id=1, source_target_pairs={{0,17},{1,24},{2,19},{3,26},{4,21},{5,28},{6,23},{7,30},{8,25},{9,... | collective-permute-start | bytes 122888 | tf_op jit(solution)/shard_map/ppermute | solution.py:573
  24.8 4.1 %collective-permute-start.9 = (bf16[2,80,128]{2,1,0:T(8,128)(2,1)S(1)}, bf16[2,80,128]{2,1,0:T(8,128)(2,1)S(1)}, u32[]{:S(2)}, u32[]{:S(2)}) collective-permute-start(bf16[2,80,128]{2,1,0:T(8,128)(2,1)S(1)} %shard_map.64.pair.refs_0_), channel_id=1, source_target_pairs={{0,9},{1,8},{2,11},{3,10},{4,13},{5,12},{6,15},{7,14},{8,1},{9,0},... | collective-permute-start | bytes 122888 | tf_op jit(solution)/shard_map/ppermute | solution.py:551
  27.0 2.2 %collective-permute-start.10 = (bf16[2,80,128]{2,1,0:T(8,128)(2,1)S(1)}, bf16[2,80,128]{2,1,0:T(8,128)(2,1)S(1)}, u32[]{:S(2)}, u32[]{:S(2)}) collective-permute-start(bf16[2,80,128]{2,1,0:T(8,128)(2,1)S(1)} %collective-permute-done.8.refs_1_), channel_id=1, source_target_pairs={{0,1},{1,0},{2,3},{3,2},{4,5},{5,4},{6,7},{7,6},{8,9},{9,8},{10,11... | collective-permute-start | bytes 122888 | tf_op jit(solution)/shard_map/ppermute | solution.py:543

commit v20 on v18

--- a/solution.py
+++ b/solution.py
@@ -19,12 +19,14 @@
 ANY = pl.BlockSpec(memory_space=pl.ANY)
 
 
-def call(kernel, outs, specs, scratch=(), flops=0, moved=0, limit=32, aliases=None):
+def call(kernel, outs, specs, scratch=(), flops=0, moved=0, limit=32, aliases=None, far=()):
     return pl.pallas_call(
         kernel,
         out_shape=outs,
         in_specs=specs,
-        out_specs=[ANY if at in (aliases or {}).values() else VMEM for at in range(len(outs))],
+        out_specs=[
+            HBM if at in far else ANY if at in (aliases or {}).values() else VMEM for at in range(len(outs))
+        ],
         input_output_aliases=aliases or {},
         scratch_shapes=list(scratch),
         cost_estimate=pl.CostEstimate(flops=flops, bytes_accessed=moved, transcendentals=0),
@@ -366,10 +368,10 @@
 
 
 def finish_kernel(*refs):
-    count = len(refs) - 15
+    count = len(refs) - 17
     blocks, refs = refs[:count], refs[count:]
     zvec, inner_got, outer_got, outer_last, picked, terms, middle, inner_face, outer_face, resid = refs[:10]
-    solution, deflated, direction_ref, spread, outer_field = refs[10:]
+    solution, deflated, direction_ref, spread, outer_field, staged, sems = refs[10:]
     subs = direction_ref.shape[0]
     modes, planes, rows, layers = zvec.shape
     half = rows // 2
@@ -495,6 +497,7 @@
     outer_field[pl.ds(pl.multiple_of((1 - side) * half, half), half), :] = last
     outside = (field[2], jnp.where(at_edge, 0.0, outer_field[...]))
     faces = (inner_face[...], outer_face[...])
+    copies = []
     for x in range(2):
         f = field[x]
         end_field = jnp.where(side == x, ends[1], ends[0])
@@ -508,7 +511,12 @@
             - terms[x, 4] * pltpu.roll(f, layers - 1, 1)
             - terms[x, 5] * end_field
         )
-        deflated[held[x]] = resid[held[x]] - image
+        staged[x] = resid[held[x]] - image
+        copy = pltpu.make_async_copy(staged.at[x], deflated.at[held[x]], sems.at[x])
+        copy.start()
+        copies.append(copy)
+    for copy in copies:
+        copy.wait()
 
 
 def swapped(value, axis, first):
@@ -667,7 +675,10 @@
                 pltpu.VMEM((subs, modes), F32),
                 pltpu.VMEM((modes, layers), F32),
                 pltpu.VMEM(plane, F32),
+                pltpu.VMEM(field, F32),
+                pltpu.SemaphoreType.DMA((2,)),
             ],
+            far=(1,),
             flops=10_000_000,
             moved=5 << 20,
         )(

time: 32.4 us -> 32.9 us (1.015)
  Pallas kernels: 10.6 us -> 11.1 us
    pallas_call x1, Pallas kernels: 2.71 us -> 3.23 us  [body(): call(finish_kernel, [shape((1, modes), F32), shape(field, F32)], [VMEM] *...]
where the time goes in v20:
time: 32.9 us; the launch traced here: 32.8 us
  starting transfers between devices  15.5 us (47%)
  Pallas kernels  11.1 us (34%)
  waiting for transfers between devices  5.31 us (16%)
  between operations  0.77 us (2%)
    ppermute x3, starting transfers between devices, swapped(): return lax.ppermute(value, axis, pairs)  5.62 us
    pallas_call x1, Pallas kernels, body(): call(block_kernel, [shape((modes + 8, modes), F32), shape((7,) + plane, F...  3.41 us
    ppermute x4, starting transfers between devices, partner(): return lax.ppermute(value, ('sub', 'pln'), pairs)  3.31 us
    pallas_call x1, Pallas kernels, body(): call(finish_kernel, [shape((1, modes), F32), shape(field, F32)], [VMEM] *...  3.23 us
    ppermute x2, starting transfers between devices, swapped_all(): return lax.ppermute(value, ('sub', 'pln'), pairs)  2.89 us
    ppermute x1, starting transfers between devices, far_partner(): return lax.ppermute(value, ('sub', 'pln'), pairs)  2.31 us
    ppermute x4, waiting for transfers between devices, partner(): return lax.ppermute(value, ('sub', 'pln'), pairs)  1.75 us
    ppermute x1, waiting for transfers between devices, far_partner(): return lax.ppermute(value, ('sub', 'pln'), pairs)  1.66 us
  transfers between devices with their start and end apart: 12, of which 7 were waited for; matrix products, arithmetic and copies ran while one was open for 0% of the time, Pallas kernels for 17%

profile of v20, /device:TPU:0, one launch (start us, length us, event | category | flops | bytes accessed | tf_op | source)
XLA Modules:
  0.0 32.8 jit_solution(15210773753521487623)
XLA Ops:
  0.7 1.6 %shard_map.61 = (bf16[65,64,128]{2,1,0:T(8,128)(2,1)S(1)}, bf16[66,32,128]{2,1,0:T(8,128)(2,1)S(1)}) custom-call(s32[2,64,128]{2,1,0:T(8,128)} %labels_far.1, bf16[64,2,64,128]{3,2,1,0:T(8,128)(2,1)} %zvec.5), custom_call_target="tpu_custom_call" | custom-call | bytes 2097152 | tf_op jit(solution)/shard_map/pallas_call | solution.py:585
  2.3 0.5 %collective-permute-start = (bf16[65,64,128]{2,1,0:T(8,128)(2,1)S(1)}, bf16[65,64,128]{2,1,0:T(8,128)(2,1)S(1)}, u32[]{:S(2)}, u32[]{:S(2)}) collective-permute-start(bf16[65,64,128]{2,1,0:T(8,128)(2,1)S(1)} %get-tuple-element.23), channel_id=1, source_target_pairs={{0,1},{1,0},{2,3},{3,2},{4,5},{5,4},{6,7},{7,6},{8,9},{9,8},{10,11... | collective-permute-start | bytes 3194888 | tf_op jit(solution)/shard_map/ppermute | solution.py:528
  2.8 2.6 %collective-permute-start.1 = (bf16[66,32,128]{2,1,0:T(8,128)(2,1)S(1)}, bf16[66,32,128]{2,1,0:T(8,128)(2,1)S(1)}, u32[]{:S(2)}, u32[]{:S(2)}) collective-permute-start(bf16[66,32,128]{2,1,0:T(8,128)(2,1)S(1)} %get-tuple-element.25), channel_id=1, source_target_pairs={{0,4},{1,2},{2,1},{3,7},{4,0},{5,6},{6,5},{7,3},{8,12},{9,10},{10,... | collective-permute-start | bytes 1622024 | tf_op jit(solution)/shard_map/ppermute | solution.py:541
  5.4 0.7 %shard_map.59 = (bf16[64,32,128]{2,1,0:T(8,128)(2,1)S(1)}, bf16[80,128]{1,0:T(8,128)(2,1)S(1)}, bf16[80,128]{1,0:T(8,128)(2,1)S(1)}) custom-call(s32[2,64,128]{2,1,0:T(8,128)S(1)} %copy-done.1, bf16[64,2,64,128]{3,2,1,0:T(8,128)(2,1)S(1)} %copy-done), custom_call_target="tpu_custom_call" | custom-call | flops 10000000 | bytes 6291456 | tf_op jit(solution)/shard_map/pallas_call | solution.py:595
  6.1 0.4 %collective-permute-start.2 = (bf16[80,128]{1,0:T(8,128)(2,1)S(1)}, bf16[80,128]{1,0:T(8,128)(2,1)S(1)}, u32[]{:S(2)}, u32[]{:S(2)}) collective-permute-start(bf16[80,128]{1,0:T(8,128)(2,1)S(1)} %get-tuple-element.19.after.one_pack), channel_id=1, source_target_pairs={{0,4},{4,0},{8,12},{12,8},{16,20},{20,16},{24,28},{28,24},{1,5},{5... | collective-permute-start | bytes 61448 | tf_op jit(solution)/shard_map/ppermute | solution.py:528
  6.5 4.7 %collective-permute-start.3 = (bf16[80,128]{1,0:T(8,128)(2,1)S(1)}, bf16[80,128]{1,0:T(8,128)(2,1)S(1)}, u32[]{:S(2)}, u32[]{:S(2)}) collective-permute-start(bf16[80,128]{1,0:T(8,128)(2,1)S(1)} %get-tuple-element.26.two_pack), channel_id=1, source_target_pairs={{0,28},{4,8},{8,4},{12,16},{16,12},{20,24},{24,20},{28,0},{1,29},{... | collective-permute-start | bytes 61448 | tf_op jit(solution)/shard_map/ppermute | solution.py:528
  11.2 3.4 %shard_map.60 = (f32[72,64]{1,0:T(8,128)S(1)}, f32[7,64,128]{2,1,0:T(8,128)S(1)}, bf16[2,64,64,128]{3,2,1,0:T(8,128)(2,1)S(1)}) custom-call(f32[1,4]{1,0:T(1,128)S(1)} %bitcast.1, s32[2,64,128]{2,1,0:T(8,128)S(1)} %copy-done.1, f32[2,64,128]{2,1,0:T(8,128)S(1)} %copy-done.2, bf16[64,2,64,128]{3,2,1,0:T(8,128)(2,1)S(1)} %copy-done, ...), custom_call_target="tpu_custom_call" | custom-call | flops 400000000 | bytes 3145728 | tf_op jit(solution)/shard_map/pallas_call | solution.py:606
  14.6 0.0 collective-permute-done.inner_got
  14.6 0.7 %shard_map.62 = (f32[72,64]{1,0:T(8,128)S(1)}, f32[64,128]{1,0:T(8,128)S(1)}) custom-call(f32[1,4]{1,0:T(1,128)S(1)} %bitcast.2, f32[72,64]{1,0:T(8,128)S(1)} %get-tuple-element.20.partial, f32[7,64,128]{2,1,0:T(8,128)S(1)} %get-tuple-element.21.weights.refs_10_, bf16[2,64,64,128]{3,2,1,0:T(8,128)(2,1)S(1)} %get-tuple-element.22.here, ...), custom_call_target="tpu_custom_call" | custom-call | flops 100000000 | bytes 1048576 | tf_op jit(solution)/shard_map/pallas_call | solution.py:619
  15.3 0.0 collective-permute-done.2.one_got
  15.3 0.0 collective-permute-done.3.two_got
  15.3 0.0 collective-permute-done.1.outer_got
  15.3 0.8 %shard_map.63 = (f32[72,128]{1,0:T(8,128)S(1)}, f32[64,128]{1,0:T(8,128)S(1)}) custom-call(f32[1,4]{1,0:T(1,128)S(1)} %bitcast.3, f32[72,64]{1,0:T(8,128)S(1)} %get-tuple-element.24.partial, f32[7,64,128]{2,1,0:T(8,128)S(1)} %get-tuple-element.21.weights.refs_10_, bf16[2,64,64,128]{3,2,1,0:T(8,128)(2,1)S(1)} %get-tuple-element.22.here, ...), custom_call_target="tpu_custom_call" | custom-call | flops 100000000 | bytes 1048576 | tf_op jit(solution)/shard_map/pallas_call | solution.py:627
  16.1 0.1 collective-permute-start.4
  16.2 1.2 %collective-permute-done.4 = f32[72,128]{1,0:T(8,128)S(1)} collective-permute-done((f32[72,128]{1,0:T(8,128)S(1)}, f32[72,128]{1,0:T(8,128)S(1)}, u32[]{:S(2)}, u32[]{:S(2)}) %collective-permute-start.4) | collective-permute-done | bytes 36896 | tf_op jit(solution)/shard_map/ppermute | solution.py:545
  17.4 0.7 %collective-permute-start.5 = (f32[72,128]{1,0:T(8,128)S(1)}, f32[72,128]{1,0:T(8,128)S(1)}, u32[]{:S(2)}, u32[]{:S(2)}) collective-permute-start(f32[72,128]{1,0:T(8,128)S(1)} %add.3.own.after), channel_id=1, source_target_pairs={{0,3},{1,2},{2,1},{3,0},{4,7},{5,6},{6,5},{7,4},{8,11},{9,10},{10,... | collective-permute-start | bytes 110600 | tf_op jit(solution)/shard_map/ppermute | solution.py:553
  18.1 0.0 collective-permute-start.6
  18.1 2.3 %collective-permute-start.7 = (f32[72,128]{1,0:T(8,128)S(1)}, f32[72,128]{1,0:T(8,128)S(1)}, u32[]{:S(2)}, u32[]{:S(2)}) collective-permute-start(f32[72,128]{1,0:T(8,128)S(1)} %add.3.own.after), channel_id=1, source_target_pairs={{0,7},{1,6},{2,5},{3,4},{4,3},{5,2},{6,1},{7,0},{8,15},{9,14},{10,... | collective-permute-start | bytes 110600 | tf_op jit(solution)/shard_map/ppermute | solution.py:553
  20.4 0.3 collective-permute-start.11
  20.7 0.2 collective-permute-done.5.across
  20.8 0.7 %collective-permute-done.6.beside = f32[72,128]{1,0:T(8,128)S(1)} collective-permute-done((f32[72,128]{1,0:T(8,128)S(1)}, f32[72,128]{1,0:T(8,128)S(1)}, u32[]{:S(2)}, u32[]{:S(2)}) %collective-permute-start.6) | collective-permute-done | bytes 36896 | tf_op jit(solution)/shard_map/ppermute | solution.py:553
  21.5 0.9 %collective-permute-done.7.oblique = f32[72,128]{1,0:T(8,128)S(1)} collective-permute-done((f32[72,128]{1,0:T(8,128)S(1)}, f32[72,128]{1,0:T(8,128)S(1)}, u32[]{:S(2)}, u32[]{:S(2)}) %collective-permute-start.7) | collective-permute-done | bytes 36896 | tf_op jit(solution)/shard_map/ppermute | solution.py:553
  22.4 2.3 %collective-permute-start.8 = (bf16[2,80,128]{2,1,0:T(8,128)(2,1)S(1)}, bf16[2,80,128]{2,1,0:T(8,128)(2,1)S(1)}, u32[]{:S(2)}, u32[]{:S(2)}) collective-permute-start(bf16[2,80,128]{2,1,0:T(8,128)(2,1)S(1)} %shard_map.64.pair.refs_0_), channel_id=1, source_target_pairs={{0,17},{1,24},{2,19},{3,26},{4,21},{5,28},{6,23},{7,30},{8,25},{9,... | collective-permute-start | bytes 122888 | tf_op jit(solution)/shard_map/ppermute | solution.py:575
  24.8 0.3 %collective-permute-start.9 = (bf16[2,80,128]{2,1,0:T(8,128)(2,1)S(1)}, bf16[2,80,128]{2,1,0:T(8,128)(2,1)S(1)}, u32[]{:S(2)}, u32[]{:S(2)}) collective-permute-start(bf16[2,80,128]{2,1,0:T(8,128)(2,1)S(1)} %shard_map.64.pair.refs_0_), channel_id=1, source_target_pairs={{0,9},{1,8},{2,11},{3,10},{4,13},{5,12},{6,15},{7,14},{8,1},{9,0},... | collective-permute-start | bytes 122888 | tf_op jit(solution)/shard_map/ppermute | solution.py:553
  25.1 0.3 shard_map.67
  25.4 1.7 %collective-permute-done.8.refs_1_ = bf16[2,80,128]{2,1,0:T(8,128)(2,1)S(1)} collective-permute-done((bf16[2,80,128]{2,1,0:T(8,128)(2,1)S(1)}, bf16[2,80,128]{2,1,0:T(8,128)(2,1)S(1)}, u32[]{:S(2)}, u32[]{:S(2)}) %collective-permute-start.8) | collective-permute-done | bytes 40992 | tf_op jit(solution)/shard_map/ppermute | solution.py:575
  27.0 1.3 %collective-permute-start.10 = (bf16[2,80,128]{2,1,0:T(8,128)(2,1)S(1)}, bf16[2,80,128]{2,1,0:T(8,128)(2,1)S(1)}, u32[]{:S(2)}, u32[]{:S(2)}) collective-permute-start(bf16[2,80,128]{2,1,0:T(8,128)(2,1)S(1)} %collective-permute-done.8.refs_1_), channel_id=1, source_target_pairs={{0,1},{1,0},{2,3},{3,2},{4,5},{5,4},{6,7},{7,6},{8,9},{9,8},{10,11... | collective-permute-start | bytes 122888 | tf_op jit(solution)/shard_map/ppermute | solution.py:545
  28.3 0.5 %shard_map.65 = (f32[64,2,64,128]{3,2,1,0:T(8,128)S(1)}, f32[64,64,128]{2,1,0:T(8,128)S(1)}, f32[64,32,128]{2,1,0:T(8,128)S(1)}) custom-call(bf16[2,80,128]{2,1,0:T(8,128)(2,1)S(1)} %shard_map.64.pair.refs_0_, bf16[64,2,64,128]{3,2,1,0:T(8,128)(2,1)S(1)} %copy-done, bf16[65,64,128]{2,1,0:T(8,128)(2,1)S(1)} %collective-permute-done.inner_got, ...), custom_call_target="tpu_custom_call" | custom-call | flops 1073741824 | bytes 1048576 | tf_op jit(solution)/shard_map/pallas_call | solution.py:658
  28.8 0.0 collective-permute-done.9.refs_2_
  28.8 0.4 %collective-permute-done.10.refs_3_ = bf16[2,80,128]{2,1,0:T(8,128)(2,1)S(1)} collective-permute-done((bf16[2,80,128]{2,1,0:T(8,128)(2,1)S(1)}, bf16[2,80,128]{2,1,0:T(8,128)(2,1)S(1)}, u32[]{:S(2)}, u32[]{:S(2)}) %collective-permute-start.10) | collective-permute-done | bytes 40992 | tf_op jit(solution)/shard_map/ppermute | solution.py:545
  29.2 0.3 %collective-permute-done.11.refs_7_ = bf16[64,32,128]{2,1,0:T(8,128)(2,1)S(1)} collective-permute-done((bf16[64,32,128]{2,1,0:T(8,128)(2,1)S(1)}, bf16[64,32,128]{2,1,0:T(8,128)(2,1)S(1)}, u32[]{:S(2)}, u32[]{:S(2)}) %collective-permute-start.11) | collective-permute-done | bytes 524320 | tf_op jit(solution)/shard_map/ppermute | solution.py:541
  29.5 3.2 %shard_map.68 = (f32[1,64]{1,0:T(1,128)}, f32[2,64,128]{2,1,0:T(8,128)}) custom-call(bf16[2,80,128]{2,1,0:T(8,128)(2,1)S(1)} %shard_map.64.pair.refs_0_, bf16[2,80,128]{2,1,0:T(8,128)(2,1)S(1)} %collective-permute-done.8.refs_1_, bf16[2,80,128]{2,1,0:T(8,128)(2,1)S(1)} %collective-permute-done.9.refs_2_, ...), custom_call_target="tpu_custom_call" | custom-call | flops 10000000 | bytes 5242880 | tf_op jit(solution)/shard_map/pallas_call | solution.py:670
  (11 shorter events, 0.1 us)
Async XLA Ops:
  0.6 4.8 %copy-start.1 = (s32[2,64,128]{2,1,0:T(8,128)S(1)}, s32[2,64,128]{2,1,0:T(8,128)}, u32[]{:S(2)}) copy-start(s32[2,64,128]{2,1,0:T(8,128)} %labels_far.1) | copy-start | bytes 196612
  0.6 4.7 %copy-start = (bf16[64,2,64,128]{3,2,1,0:T(8,128)(2,1)S(1)}, bf16[64,2,64,128]{3,2,1,0:T(8,128)(2,1)}, u32[]{:S(2)}) copy-start(bf16[64,2,64,128]{3,2,1,0:T(8,128)(2,1)} %zvec.5) | copy-start | bytes 6291460
  0.7 10.5 %copy-start.3 = (f32[4]{0:T(128)S(1)}, f32[4]{0:T(128)}, u32[]{:S(2)}) copy-start(f32[4]{0:T(128)} %param.5) | copy-start | bytes 52
  0.7 10.5 %copy-start.2 = (f32[2,64,128]{2,1,0:T(8,128)S(1)}, f32[2,64,128]{2,1,0:T(8,128)}, u32[]{:S(2)}) copy-start(f32[2,64,128]{2,1,0:T(8,128)} %refs_13_.1) | copy-start | bytes 196612
  2.3 12.3 %collective-permute-start = (bf16[65,64,128]{2,1,0:T(8,128)(2,1)S(1)}, bf16[65,64,128]{2,1,0:T(8,128)(2,1)S(1)}, u32[]{:S(2)}, u32[]{:S(2)}) collective-permute-start(bf16[65,64,128]{2,1,0:T(8,128)(2,1)S(1)} %get-tuple-element.23), channel_id=1, source_target_pairs={{0,1},{1,0},{2,3},{3,2},{4,5},{5,4},{6,7},{7,6},{8,9},{9,8},{10,11... | collective-permute-start | bytes 3194888 | tf_op jit(solution)/shard_map/ppermute | solution.py:528
  2.8 12.5 %collective-permute-start.1 = (bf16[66,32,128]{2,1,0:T(8,128)(2,1)S(1)}, bf16[66,32,128]{2,1,0:T(8,128)(2,1)S(1)}, u32[]{:S(2)}, u32[]{:S(2)}) collective-permute-start(bf16[66,32,128]{2,1,0:T(8,128)(2,1)S(1)} %get-tuple-element.25), channel_id=1, source_target_pairs={{0,4},{1,2},{2,1},{3,7},{4,0},{5,6},{6,5},{7,3},{8,12},{9,10},{10,... | collective-permute-start | bytes 1622024 | tf_op jit(solution)/shard_map/ppermute | solution.py:541
  6.1 9.2 %collective-permute-start.2 = (bf16[80,128]{1,0:T(8,128)(2,1)S(1)}, bf16[80,128]{1,0:T(8,128)(2,1)S(1)}, u32[]{:S(2)}, u32[]{:S(2)}) collective-permute-start(bf16[80,128]{1,0:T(8,128)(2,1)S(1)} %get-tuple-element.19.after.one_pack), channel_id=1, source_target_pairs={{0,4},{4,0},{8,12},{12,8},{16,20},{20,16},{24,28},{28,24},{1,5},{5... | collective-permute-start | bytes 61448 | tf_op jit(solution)/shard_map/ppermute | solution.py:528
  6.5 8.8 %collective-permute-start.3 = (bf16[80,128]{1,0:T(8,128)(2,1)S(1)}, bf16[80,128]{1,0:T(8,128)(2,1)S(1)}, u32[]{:S(2)}, u32[]{:S(2)}) collective-permute-start(bf16[80,128]{1,0:T(8,128)(2,1)S(1)} %get-tuple-element.26.two_pack), channel_id=1, source_target_pairs={{0,28},{4,8},{8,4},{12,16},{16,12},{20,24},{24,20},{28,0},{1,29},{... | collective-permute-start | bytes 61448 | tf_op jit(solution)/shard_map/ppermute | solution.py:528
  16.1 1.3 %collective-permute-start.4 = (f32[72,128]{1,0:T(8,128)S(1)}, f32[72,128]{1,0:T(8,128)S(1)}, u32[]{:S(2)}, u32[]{:S(2)}) collective-permute-start(f32[72,128]{1,0:T(8,128)S(1)} %get-tuple-element.27), channel_id=1, source_target_pairs={{0,1},{1,0},{2,3},{3,2},{4,5},{5,4},{6,7},{7,6},{8,9},{9,8},{10,11... | collective-permute-start | bytes 110600 | tf_op jit(solution)/shard_map/ppermute | solution.py:545
  17.4 3.4 %collective-permute-start.5 = (f32[72,128]{1,0:T(8,128)S(1)}, f32[72,128]{1,0:T(8,128)S(1)}, u32[]{:S(2)}, u32[]{:S(2)}) collective-permute-start(f32[72,128]{1,0:T(8,128)S(1)} %add.3.own.after), channel_id=1, source_target_pairs={{0,3},{1,2},{2,1},{3,0},{4,7},{5,6},{6,5},{7,4},{8,11},{9,10},{10,... | collective-permute-start | bytes 110600 | tf_op jit(solution)/shard_map/ppermute | solution.py:553
  18.1 3.4 %collective-permute-start.6 = (f32[72,128]{1,0:T(8,128)S(1)}, f32[72,128]{1,0:T(8,128)S(1)}, u32[]{:S(2)}, u32[]{:S(2)}) collective-permute-start(f32[72,128]{1,0:T(8,128)S(1)} %add.3.own.after), channel_id=1, source_target_pairs={{0,5},{1,4},{2,7},{3,6},{4,1},{5,0},{6,3},{7,2},{8,13},{9,12},{10,... | collective-permute-start | bytes 110600 | tf_op jit(solution)/shard_map/ppermute | solution.py:553
  18.1 4.3 %collective-permute-start.7 = (f32[72,128]{1,0:T(8,128)S(1)}, f32[72,128]{1,0:T(8,128)S(1)}, u32[]{:S(2)}, u32[]{:S(2)}) collective-permute-start(f32[72,128]{1,0:T(8,128)S(1)} %add.3.own.after), channel_id=1, source_target_pairs={{0,7},{1,6},{2,5},{3,4},{4,3},{5,2},{6,1},{7,0},{8,15},{9,14},{10,... | collective-permute-start | bytes 110600 | tf_op jit(solution)/shard_map/ppermute | solution.py:553
  20.4 9.2 %collective-permute-start.11 = (bf16[64,32,128]{2,1,0:T(8,128)(2,1)S(1)}, bf16[64,32,128]{2,1,0:T(8,128)(2,1)S(1)}, u32[]{:S(2)}, u32[]{:S(2)}) collective-permute-start(bf16[64,32,128]{2,1,0:T(8,128)(2,1)S(1)} %shard_map.66), channel_id=1, source_target_pairs={{0,4},{1,2},{2,1},{3,7},{4,0},{5,6},{6,5},{7,3},{8,12},{9,10},{10,... | collective-permute-start | bytes 1572872 | tf_op jit(solution)/shard_map/ppermute | solution.py:541
  22.4 4.6 %collective-permute-start.8 = (bf16[2,80,128]{2,1,0:T(8,128)(2,1)S(1)}, bf16[2,80,128]{2,1,0:T(8,128)(2,1)S(1)}, u32[]{:S(2)}, u32[]{:S(2)}) collective-permute-start(bf16[2,80,128]{2,1,0:T(8,128)(2,1)S(1)} %shard_map.64.pair.refs_0_), channel_id=1, source_target_pairs={{0,17},{1,24},{2,19},{3,26},{4,21},{5,28},{6,23},{7,30},{8,25},{9,... | collective-permute-start | bytes 122888 | tf_op jit(solution)/shard_map/ppermute | solution.py:575
  24.8 4.1 %collective-permute-start.9 = (bf16[2,80,128]{2,1,0:T(8,128)(2,1)S(1)}, bf16[2,80,128]{2,1,0:T(8,128)(2,1)S(1)}, u32[]{:S(2)}, u32[]{:S(2)}) collective-permute-start(bf16[2,80,128]{2,1,0:T(8,128)(2,1)S(1)} %shard_map.64.pair.refs_0_), channel_id=1, source_target_pairs={{0,9},{1,8},{2,11},{3,10},{4,13},{5,12},{6,15},{7,14},{8,1},{9,0},... | collective-permute-start | bytes 122888 | tf_op jit(solution)/shard_map/ppermute | solution.py:553
  27.0 2.2 %collective-permute-start.10 = (bf16[2,80,128]{2,1,0:T(8,128)(2,1)S(1)}, bf16[2,80,128]{2,1,0:T(8,128)(2,1)S(1)}, u32[]{:S(2)}, u32[]{:S(2)}) collective-permute-start(bf16[2,80,128]{2,1,0:T(8,128)(2,1)S(1)} %collective-permute-done.8.refs_1_), channel_id=1, source_target_pairs={{0,1},{1,0},{2,3},{3,2},{4,5},{5,4},{6,7},{7,6},{8,9},{9,8},{10,11... | collective-permute-start | bytes 122888 | tf_op jit(solution)/shard_map/ppermute | solution.py:545

commit v21 on v18

--- a/solution.py
+++ b/solution.py
@@ -416,14 +416,14 @@
 
     def in_parts(value):
         parts = []
-        for _ in range(3):
+        for _ in range(2):
             part = value.astype(BF16)
             parts.append(part.astype(F32))
             value = value - parts[-1]
         return jnp.concatenate(parts, axis=0).astype(BF16)
 
     def joined(value):
-        return (value[:subs] + value[subs:2 * subs]) + value[2 * subs:]
+        return value[:subs] + value[subs:]
 
     def coarse_apply(direction):
         pairs = in_parts(jnp.concatenate([direction, turned(direction, 1)], axis=1))

time: 32.4 us -> 32.4 us (level)
  no operation moved by 1% of the time
where the time goes in v21:
time: 32.4 us; the launch traced here: 32.2 us
  starting transfers between devices  15.5 us (48%)
  Pallas kernels  10.6 us (33%)
  waiting for transfers between devices  5.31 us (16%)
  between operations  0.77 us (2%)
    ppermute x3, starting transfers between devices, swapped(): return lax.ppermute(value, axis, pairs)  5.62 us
    pallas_call x1, Pallas kernels, body(): call(block_kernel, [shape((modes + 8, modes), F32), shape((7,) + plane, F...  3.41 us
    ppermute x4, starting transfers between devices, partner(): return lax.ppermute(value, ('sub', 'pln'), pairs)  3.31 us
    ppermute x2, starting transfers between devices, swapped_all(): return lax.ppermute(value, ('sub', 'pln'), pairs)  2.89 us
    pallas_call x1, Pallas kernels, body(): call(finish_kernel, [shape((1, modes), F32), shape(field, F32)], [VMEM] *...  2.7 us
    ppermute x1, starting transfers between devices, far_partner(): return lax.ppermute(value, ('sub', 'pln'), pairs)  2.31 us
    ppermute x4, waiting for transfers between devices, partner(): return lax.ppermute(value, ('sub', 'pln'), pairs)  1.75 us
    ppermute x1, waiting for transfers between devices, far_partner(): return lax.ppermute(value, ('sub', 'pln'), pairs)  1.66 us
  transfers between devices with their start and end apart: 12, of which 7 were waited for; matrix products, arithmetic and copies ran while one was open for 0% of the time, Pallas kernels for 17%

profile of v21, /device:TPU:0, one launch (start us, length us, event | category | flops | bytes accessed | tf_op | source)
XLA Modules:
  0.0 32.2 jit_solution(8234908028555251508)
XLA Ops:
  0.7 1.6 %shard_map.61 = (bf16[65,64,128]{2,1,0:T(8,128)(2,1)S(1)}, bf16[66,32,128]{2,1,0:T(8,128)(2,1)S(1)}) custom-call(s32[2,64,128]{2,1,0:T(8,128)} %labels_far.1, bf16[64,2,64,128]{3,2,1,0:T(8,128)(2,1)} %zvec.5), custom_call_target="tpu_custom_call" | custom-call | bytes 2097152 | tf_op jit(solution)/shard_map/pallas_call | solution.py:577
  2.3 0.5 %collective-permute-start = (bf16[65,64,128]{2,1,0:T(8,128)(2,1)S(1)}, bf16[65,64,128]{2,1,0:T(8,128)(2,1)S(1)}, u32[]{:S(2)}, u32[]{:S(2)}) collective-permute-start(bf16[65,64,128]{2,1,0:T(8,128)(2,1)S(1)} %get-tuple-element.23), channel_id=1, source_target_pairs={{0,1},{1,0},{2,3},{3,2},{4,5},{5,4},{6,7},{7,6},{8,9},{9,8},{10,11... | collective-permute-start | bytes 3194888 | tf_op jit(solution)/shard_map/ppermute | solution.py:520
  2.8 2.6 %collective-permute-start.1 = (bf16[66,32,128]{2,1,0:T(8,128)(2,1)S(1)}, bf16[66,32,128]{2,1,0:T(8,128)(2,1)S(1)}, u32[]{:S(2)}, u32[]{:S(2)}) collective-permute-start(bf16[66,32,128]{2,1,0:T(8,128)(2,1)S(1)} %get-tuple-element.25), channel_id=1, source_target_pairs={{0,4},{1,2},{2,1},{3,7},{4,0},{5,6},{6,5},{7,3},{8,12},{9,10},{10,... | collective-permute-start | bytes 1622024 | tf_op jit(solution)/shard_map/ppermute | solution.py:533
  5.4 0.7 %shard_map.59 = (bf16[64,32,128]{2,1,0:T(8,128)(2,1)S(1)}, bf16[80,128]{1,0:T(8,128)(2,1)S(1)}, bf16[80,128]{1,0:T(8,128)(2,1)S(1)}) custom-call(s32[2,64,128]{2,1,0:T(8,128)S(1)} %copy-done.1, bf16[64,2,64,128]{3,2,1,0:T(8,128)(2,1)S(1)} %copy-done), custom_call_target="tpu_custom_call" | custom-call | flops 10000000 | bytes 6291456 | tf_op jit(solution)/shard_map/pallas_call | solution.py:587
  6.1 0.4 %collective-permute-start.2 = (bf16[80,128]{1,0:T(8,128)(2,1)S(1)}, bf16[80,128]{1,0:T(8,128)(2,1)S(1)}, u32[]{:S(2)}, u32[]{:S(2)}) collective-permute-start(bf16[80,128]{1,0:T(8,128)(2,1)S(1)} %get-tuple-element.19.after.one_pack), channel_id=1, source_target_pairs={{0,4},{4,0},{8,12},{12,8},{16,20},{20,16},{24,28},{28,24},{1,5},{5... | collective-permute-start | bytes 61448 | tf_op jit(solution)/shard_map/ppermute | solution.py:520
  6.5 4.7 %collective-permute-start.3 = (bf16[80,128]{1,0:T(8,128)(2,1)S(1)}, bf16[80,128]{1,0:T(8,128)(2,1)S(1)}, u32[]{:S(2)}, u32[]{:S(2)}) collective-permute-start(bf16[80,128]{1,0:T(8,128)(2,1)S(1)} %get-tuple-element.26.two_pack), channel_id=1, source_target_pairs={{0,28},{4,8},{8,4},{12,16},{16,12},{20,24},{24,20},{28,0},{1,29},{... | collective-permute-start | bytes 61448 | tf_op jit(solution)/shard_map/ppermute | solution.py:520
  11.2 3.4 %shard_map.60 = (f32[72,64]{1,0:T(8,128)S(1)}, f32[7,64,128]{2,1,0:T(8,128)S(1)}, bf16[2,64,64,128]{3,2,1,0:T(8,128)(2,1)S(1)}) custom-call(f32[1,4]{1,0:T(1,128)S(1)} %bitcast.1, s32[2,64,128]{2,1,0:T(8,128)S(1)} %copy-done.1, f32[2,64,128]{2,1,0:T(8,128)S(1)} %copy-done.2, bf16[64,2,64,128]{3,2,1,0:T(8,128)(2,1)S(1)} %copy-done, ...), custom_call_target="tpu_custom_call" | custom-call | flops 400000000 | bytes 3145728 | tf_op jit(solution)/shard_map/pallas_call | solution.py:598
  14.6 0.0 collective-permute-done.inner_got
  14.6 0.7 %shard_map.62 = (f32[72,64]{1,0:T(8,128)S(1)}, f32[64,128]{1,0:T(8,128)S(1)}) custom-call(f32[1,4]{1,0:T(1,128)S(1)} %bitcast.2, f32[72,64]{1,0:T(8,128)S(1)} %get-tuple-element.20.partial, f32[7,64,128]{2,1,0:T(8,128)S(1)} %get-tuple-element.21.weights.refs_10_, bf16[2,64,64,128]{3,2,1,0:T(8,128)(2,1)S(1)} %get-tuple-element.22.here, ...), custom_call_target="tpu_custom_call" | custom-call | flops 100000000 | bytes 1048576 | tf_op jit(solution)/shard_map/pallas_call | solution.py:611
  15.3 0.0 collective-permute-done.2.one_got
  15.3 0.0 collective-permute-done.3.two_got
  15.3 0.0 collective-permute-done.1.outer_got
  15.3 0.8 %shard_map.63 = (f32[72,128]{1,0:T(8,128)S(1)}, f32[64,128]{1,0:T(8,128)S(1)}) custom-call(f32[1,4]{1,0:T(1,128)S(1)} %bitcast.3, f32[72,64]{1,0:T(8,128)S(1)} %get-tuple-element.24.partial, f32[7,64,128]{2,1,0:T(8,128)S(1)} %get-tuple-element.21.weights.refs_10_, bf16[2,64,64,128]{3,2,1,0:T(8,128)(2,1)S(1)} %get-tuple-element.22.here, ...), custom_call_target="tpu_custom_call" | custom-call | flops 100000000 | bytes 1048576 | tf_op jit(solution)/shard_map/pallas_call | solution.py:619
  16.1 0.1 collective-permute-start.4
  16.2 1.2 %collective-permute-done.4 = f32[72,128]{1,0:T(8,128)S(1)} collective-permute-done((f32[72,128]{1,0:T(8,128)S(1)}, f32[72,128]{1,0:T(8,128)S(1)}, u32[]{:S(2)}, u32[]{:S(2)}) %collective-permute-start.4) | collective-permute-done | bytes 36896 | tf_op jit(solution)/shard_map/ppermute | solution.py:537
  17.4 0.7 %collective-permute-start.5 = (f32[72,128]{1,0:T(8,128)S(1)}, f32[72,128]{1,0:T(8,128)S(1)}, u32[]{:S(2)}, u32[]{:S(2)}) collective-permute-start(f32[72,128]{1,0:T(8,128)S(1)} %add.3.own.after), channel_id=1, source_target_pairs={{0,3},{1,2},{2,1},{3,0},{4,7},{5,6},{6,5},{7,4},{8,11},{9,10},{10,... | collective-permute-start | bytes 110600 | tf_op jit(solution)/shard_map/ppermute | solution.py:545
  18.1 0.0 collective-permute-start.6
  18.1 2.3 %collective-permute-start.7 = (f32[72,128]{1,0:T(8,128)S(1)}, f32[72,128]{1,0:T(8,128)S(1)}, u32[]{:S(2)}, u32[]{:S(2)}) collective-permute-start(f32[72,128]{1,0:T(8,128)S(1)} %add.3.own.after), channel_id=1, source_target_pairs={{0,7},{1,6},{2,5},{3,4},{4,3},{5,2},{6,1},{7,0},{8,15},{9,14},{10,... | collective-permute-start | bytes 110600 | tf_op jit(solution)/shard_map/ppermute | solution.py:545
  20.4 0.3 collective-permute-start.11
  20.7 0.2 collective-permute-done.5.across
  20.8 0.7 %collective-permute-done.6.beside = f32[72,128]{1,0:T(8,128)S(1)} collective-permute-done((f32[72,128]{1,0:T(8,128)S(1)}, f32[72,128]{1,0:T(8,128)S(1)}, u32[]{:S(2)}, u32[]{:S(2)}) %collective-permute-start.6) | collective-permute-done | bytes 36896 | tf_op jit(solution)/shard_map/ppermute | solution.py:545
  21.5 0.9 %collective-permute-done.7.oblique = f32[72,128]{1,0:T(8,128)S(1)} collective-permute-done((f32[72,128]{1,0:T(8,128)S(1)}, f32[72,128]{1,0:T(8,128)S(1)}, u32[]{:S(2)}, u32[]{:S(2)}) %collective-permute-start.7) | collective-permute-done | bytes 36896 | tf_op jit(solution)/shard_map/ppermute | solution.py:545
  22.4 2.3 %collective-permute-start.8 = (bf16[2,80,128]{2,1,0:T(8,128)(2,1)S(1)}, bf16[2,80,128]{2,1,0:T(8,128)(2,1)S(1)}, u32[]{:S(2)}, u32[]{:S(2)}) collective-permute-start(bf16[2,80,128]{2,1,0:T(8,128)(2,1)S(1)} %shard_map.64.pair.refs_0_), channel_id=1, source_target_pairs={{0,17},{1,24},{2,19},{3,26},{4,21},{5,28},{6,23},{7,30},{8,25},{9,... | collective-permute-start | bytes 122888 | tf_op jit(solution)/shard_map/ppermute | solution.py:567
  24.8 0.3 %collective-permute-start.9 = (bf16[2,80,128]{2,1,0:T(8,128)(2,1)S(1)}, bf16[2,80,128]{2,1,0:T(8,128)(2,1)S(1)}, u32[]{:S(2)}, u32[]{:S(2)}) collective-permute-start(bf16[2,80,128]{2,1,0:T(8,128)(2,1)S(1)} %shard_map.64.pair.refs_0_), channel_id=1, source_target_pairs={{0,9},{1,8},{2,11},{3,10},{4,13},{5,12},{6,15},{7,14},{8,1},{9,0},... | collective-permute-start | bytes 122888 | tf_op jit(solution)/shard_map/ppermute | solution.py:545
  25.1 0.3 shard_map.67
  25.4 1.7 %collective-permute-done.8.refs_1_ = bf16[2,80,128]{2,1,0:T(8,128)(2,1)S(1)} collective-permute-done((bf16[2,80,128]{2,1,0:T(8,128)(2,1)S(1)}, bf16[2,80,128]{2,1,0:T(8,128)(2,1)S(1)}, u32[]{:S(2)}, u32[]{:S(2)}) %collective-permute-start.8) | collective-permute-done | bytes 40992 | tf_op jit(solution)/shard_map/ppermute | solution.py:567
  27.0 1.3 %collective-permute-start.10 = (bf16[2,80,128]{2,1,0:T(8,128)(2,1)S(1)}, bf16[2,80,128]{2,1,0:T(8,128)(2,1)S(1)}, u32[]{:S(2)}, u32[]{:S(2)}) collective-permute-start(bf16[2,80,128]{2,1,0:T(8,128)(2,1)S(1)} %collective-permute-done.8.refs_1_), channel_id=1, source_target_pairs={{0,1},{1,0},{2,3},{3,2},{4,5},{5,4},{6,7},{7,6},{8,9},{9,8},{10,11... | collective-permute-start | bytes 122888 | tf_op jit(solution)/shard_map/ppermute | solution.py:537
  28.3 0.5 %shard_map.65 = (f32[64,2,64,128]{3,2,1,0:T(8,128)S(1)}, f32[64,64,128]{2,1,0:T(8,128)S(1)}, f32[64,32,128]{2,1,0:T(8,128)S(1)}) custom-call(bf16[2,80,128]{2,1,0:T(8,128)(2,1)S(1)} %shard_map.64.pair.refs_0_, bf16[64,2,64,128]{3,2,1,0:T(8,128)(2,1)S(1)} %copy-done, bf16[65,64,128]{2,1,0:T(8,128)(2,1)S(1)} %collective-permute-done.inner_got, ...), custom_call_target="tpu_custom_call" | custom-call | flops 1073741824 | bytes 1048576 | tf_op jit(solution)/shard_map/pallas_call | solution.py:650
  28.8 0.0 collective-permute-done.9.refs_2_
  28.8 0.4 %collective-permute-done.10.refs_3_ = bf16[2,80,128]{2,1,0:T(8,128)(2,1)S(1)} collective-permute-done((bf16[2,80,128]{2,1,0:T(8,128)(2,1)S(1)}, bf16[2,80,128]{2,1,0:T(8,128)(2,1)S(1)}, u32[]{:S(2)}, u32[]{:S(2)}) %collective-permute-start.10) | collective-permute-done | bytes 40992 | tf_op jit(solution)/shard_map/ppermute | solution.py:537
  29.2 0.3 %collective-permute-done.11.refs_7_ = bf16[64,32,128]{2,1,0:T(8,128)(2,1)S(1)} collective-permute-done((bf16[64,32,128]{2,1,0:T(8,128)(2,1)S(1)}, bf16[64,32,128]{2,1,0:T(8,128)(2,1)S(1)}, u32[]{:S(2)}, u32[]{:S(2)}) %collective-permute-start.11) | collective-permute-done | bytes 524320 | tf_op jit(solution)/shard_map/ppermute | solution.py:533
  29.5 2.7 %shard_map.68 = (f32[1,64]{1,0:T(1,128)}, f32[2,64,128]{2,1,0:T(8,128)}) custom-call(bf16[2,80,128]{2,1,0:T(8,128)(2,1)S(1)} %shard_map.64.pair.refs_0_, bf16[2,80,128]{2,1,0:T(8,128)(2,1)S(1)} %collective-permute-done.8.refs_1_, bf16[2,80,128]{2,1,0:T(8,128)(2,1)S(1)} %collective-permute-done.9.refs_2_, ...), custom_call_target="tpu_custom_call" | custom-call | flops 10000000 | bytes 5242880 | tf_op jit(solution)/shard_map/pallas_call | solution.py:662
  (11 shorter events, 0.1 us)
Async XLA Ops:
  0.6 4.8 %copy-start.1 = (s32[2,64,128]{2,1,0:T(8,128)S(1)}, s32[2,64,128]{2,1,0:T(8,128)}, u32[]{:S(2)}) copy-start(s32[2,64,128]{2,1,0:T(8,128)} %labels_far.1) | copy-start | bytes 196612
  0.6 4.7 %copy-start = (bf16[64,2,64,128]{3,2,1,0:T(8,128)(2,1)S(1)}, bf16[64,2,64,128]{3,2,1,0:T(8,128)(2,1)}, u32[]{:S(2)}) copy-start(bf16[64,2,64,128]{3,2,1,0:T(8,128)(2,1)} %zvec.5) | copy-start | bytes 6291460
  0.7 10.5 %copy-start.3 = (f32[4]{0:T(128)S(1)}, f32[4]{0:T(128)}, u32[]{:S(2)}) copy-start(f32[4]{0:T(128)} %param.5) | copy-start | bytes 52
  0.7 10.5 %copy-start.2 = (f32[2,64,128]{2,1,0:T(8,128)S(1)}, f32[2,64,128]{2,1,0:T(8,128)}, u32[]{:S(2)}) copy-start(f32[2,64,128]{2,1,0:T(8,128)} %refs_13_.1) | copy-start | bytes 196612
  2.3 12.3 %collective-permute-start = (bf16[65,64,128]{2,1,0:T(8,128)(2,1)S(1)}, bf16[65,64,128]{2,1,0:T(8,128)(2,1)S(1)}, u32[]{:S(2)}, u32[]{:S(2)}) collective-permute-start(bf16[65,64,128]{2,1,0:T(8,128)(2,1)S(1)} %get-tuple-element.23), channel_id=1, source_target_pairs={{0,1},{1,0},{2,3},{3,2},{4,5},{5,4},{6,7},{7,6},{8,9},{9,8},{10,11... | collective-permute-start | bytes 3194888 | tf_op jit(solution)/shard_map/ppermute | solution.py:520
  2.8 12.5 %collective-permute-start.1 = (bf16[66,32,128]{2,1,0:T(8,128)(2,1)S(1)}, bf16[66,32,128]{2,1,0:T(8,128)(2,1)S(1)}, u32[]{:S(2)}, u32[]{:S(2)}) collective-permute-start(bf16[66,32,128]{2,1,0:T(8,128)(2,1)S(1)} %get-tuple-element.25), channel_id=1, source_target_pairs={{0,4},{1,2},{2,1},{3,7},{4,0},{5,6},{6,5},{7,3},{8,12},{9,10},{10,... | collective-permute-start | bytes 1622024 | tf_op jit(solution)/shard_map/ppermute | solution.py:533
  6.1 9.2 %collective-permute-start.2 = (bf16[80,128]{1,0:T(8,128)(2,1)S(1)}, bf16[80,128]{1,0:T(8,128)(2,1)S(1)}, u32[]{:S(2)}, u32[]{:S(2)}) collective-permute-start(bf16[80,128]{1,0:T(8,128)(2,1)S(1)} %get-tuple-element.19.after.one_pack), channel_id=1, source_target_pairs={{0,4},{4,0},{8,12},{12,8},{16,20},{20,16},{24,28},{28,24},{1,5},{5... | collective-permute-start | bytes 61448 | tf_op jit(solution)/shard_map/ppermute | solution.py:520
  6.5 8.8 %collective-permute-start.3 = (bf16[80,128]{1,0:T(8,128)(2,1)S(1)}, bf16[80,128]{1,0:T(8,128)(2,1)S(1)}, u32[]{:S(2)}, u32[]{:S(2)}) collective-permute-start(bf16[80,128]{1,0:T(8,128)(2,1)S(1)} %get-tuple-element.26.two_pack), channel_id=1, source_target_pairs={{0,28},{4,8},{8,4},{12,16},{16,12},{20,24},{24,20},{28,0},{1,29},{... | collective-permute-start | bytes 61448 | tf_op jit(solution)/shard_map/ppermute | solution.py:520
  16.1 1.3 %collective-permute-start.4 = (f32[72,128]{1,0:T(8,128)S(1)}, f32[72,128]{1,0:T(8,128)S(1)}, u32[]{:S(2)}, u32[]{:S(2)}) collective-permute-start(f32[72,128]{1,0:T(8,128)S(1)} %get-tuple-element.27), channel_id=1, source_target_pairs={{0,1},{1,0},{2,3},{3,2},{4,5},{5,4},{6,7},{7,6},{8,9},{9,8},{10,11... | collective-permute-start | bytes 110600 | tf_op jit(solution)/shard_map/ppermute | solution.py:537
  17.4 3.4 %collective-permute-start.5 = (f32[72,128]{1,0:T(8,128)S(1)}, f32[72,128]{1,0:T(8,128)S(1)}, u32[]{:S(2)}, u32[]{:S(2)}) collective-permute-start(f32[72,128]{1,0:T(8,128)S(1)} %add.3.own.after), channel_id=1, source_target_pairs={{0,3},{1,2},{2,1},{3,0},{4,7},{5,6},{6,5},{7,4},{8,11},{9,10},{10,... | collective-permute-start | bytes 110600 | tf_op jit(solution)/shard_map/ppermute | solution.py:545
  18.1 3.4 %collective-permute-start.6 = (f32[72,128]{1,0:T(8,128)S(1)}, f32[72,128]{1,0:T(8,128)S(1)}, u32[]{:S(2)}, u32[]{:S(2)}) collective-permute-start(f32[72,128]{1,0:T(8,128)S(1)} %add.3.own.after), channel_id=1, source_target_pairs={{0,5},{1,4},{2,7},{3,6},{4,1},{5,0},{6,3},{7,2},{8,13},{9,12},{10,... | collective-permute-start | bytes 110600 | tf_op jit(solution)/shard_map/ppermute | solution.py:545
  18.1 4.3 %collective-permute-start.7 = (f32[72,128]{1,0:T(8,128)S(1)}, f32[72,128]{1,0:T(8,128)S(1)}, u32[]{:S(2)}, u32[]{:S(2)}) collective-permute-start(f32[72,128]{1,0:T(8,128)S(1)} %add.3.own.after), channel_id=1, source_target_pairs={{0,7},{1,6},{2,5},{3,4},{4,3},{5,2},{6,1},{7,0},{8,15},{9,14},{10,... | collective-permute-start | bytes 110600 | tf_op jit(solution)/shard_map/ppermute | solution.py:545
  20.4 9.2 %collective-permute-start.11 = (bf16[64,32,128]{2,1,0:T(8,128)(2,1)S(1)}, bf16[64,32,128]{2,1,0:T(8,128)(2,1)S(1)}, u32[]{:S(2)}, u32[]{:S(2)}) collective-permute-start(bf16[64,32,128]{2,1,0:T(8,128)(2,1)S(1)} %shard_map.66), channel_id=1, source_target_pairs={{0,4},{1,2},{2,1},{3,7},{4,0},{5,6},{6,5},{7,3},{8,12},{9,10},{10,... | collective-permute-start | bytes 1572872 | tf_op jit(solution)/shard_map/ppermute | solution.py:533
  22.4 4.6 %collective-permute-start.8 = (bf16[2,80,128]{2,1,0:T(8,128)(2,1)S(1)}, bf16[2,80,128]{2,1,0:T(8,128)(2,1)S(1)}, u32[]{:S(2)}, u32[]{:S(2)}) collective-permute-start(bf16[2,80,128]{2,1,0:T(8,128)(2,1)S(1)} %shard_map.64.pair.refs_0_), channel_id=1, source_target_pairs={{0,17},{1,24},{2,19},{3,26},{4,21},{5,28},{6,23},{7,30},{8,25},{9,... | collective-permute-start | bytes 122888 | tf_op jit(solution)/shard_map/ppermute | solution.py:567
  24.8 4.1 %collective-permute-start.9 = (bf16[2,80,128]{2,1,0:T(8,128)(2,1)S(1)}, bf16[2,80,128]{2,1,0:T(8,128)(2,1)S(1)}, u32[]{:S(2)}, u32[]{:S(2)}) collective-permute-start(bf16[2,80,128]{2,1,0:T(8,128)(2,1)S(1)} %shard_map.64.pair.refs_0_), channel_id=1, source_target_pairs={{0,9},{1,8},{2,11},{3,10},{4,13},{5,12},{6,15},{7,14},{8,1},{9,0},... | collective-permute-start | bytes 122888 | tf_op jit(solution)/shard_map/ppermute | solution.py:545
  27.0 2.2 %collective-permute-start.10 = (bf16[2,80,128]{2,1,0:T(8,128)(2,1)S(1)}, bf16[2,80,128]{2,1,0:T(8,128)(2,1)S(1)}, u32[]{:S(2)}, u32[]{:S(2)}) collective-permute-start(bf16[2,80,128]{2,1,0:T(8,128)(2,1)S(1)} %collective-permute-done.8.refs_1_), channel_id=1, source_target_pairs={{0,1},{1,0},{2,3},{3,2},{4,5},{5,4},{6,7},{7,6},{8,9},{9,8},{10,11... | collective-permute-start | bytes 122888 | tf_op jit(solution)/shard_map/ppermute | solution.py:537
